TPU v7x, 256 devices: a whole 4x4x8 slice. The times are simulated.
256 devices in a mesh: batch: 16 (over z, x_lo), mp: 16 (over x_hi, y, core).
Axes of the slice: x: 4 (x_hi: 2, x_lo: 2; x = x_hi * 2 + x_lo), y: 4, z: 8, core: 2. Of those that a mesh axis runs over, the one named last changes fastest.
Arguments:
- hidden_in: bfloat16 [512, 16384], P('batch'), may hold values from -36 to 36
- queries: bfloat16 [512, 16384], P('batch', 'mp'), may hold values from -128 to 128
- key_cache: bfloat16 [512, 1024], P('batch'), may hold values from -4.5 to 4.5
- value_cache: bfloat16 [512, 1024], P('batch'), may hold values from -4 to 4
- question: int32 [128], P('batch'), may hold values from 0 to 15
- prefix_len: int32 [16], replicated, may hold values from 6 to 24, as said below
- norm_gain: float32 [16384], replicated, may hold values from 0.1 to 1.9
- gate_weight: bfloat16 [16384, 26624], P('batch', 'mp'), may hold values from -0.046875 to 0.046875
- up_weight: bfloat16 [16384, 26624], P('batch', 'mp'), may hold values from -0.046875 to 0.046875
- down_weight: bfloat16 [26624, 16384], P('mp', 'batch'), may hold values from -0.0390625 to 0.0390625
Outputs:
- layer_out: bfloat16 [512, 16384], P('mp', 'batch')
Inputs may be any that keep to these rules, and one draw needn't show every extreme that they name: `prefix_len`: some question has all 24 prefix tokens live, and another question has the fewest allowed.
All inputs are finite; a program needn't handle non-finite values.
Results may differ from a plain program's by a relative error of at most 0.0055.
Values may be sent and summed in bfloat16 or wider, within the bound.
No kernel may reach another device: no remote copies, remote signals or barrier semaphores. Data moves between devices by JAX's collectives and lax.ppermute only.
A program may use at most 64 MiB of HBM per device.

v0:
```python
import jax
import jax.numpy as jnp
from jax import lax
from jax.sharding import PartitionSpec as P

HEADS = 128
KV_HEADS = 8
HEAD_DIM = 128
PREFIX = 24
ROWS_DEV = 32


def attend(batch_index, first_group, query_block, key_cache, value_cache, question, prefix_len):
    group_size = HEADS // KV_HEADS
    local_heads = query_block.shape[1] // HEAD_DIM
    per_group = min(local_heads, group_size)
    group_count = local_heads // per_group
    total_rows = key_cache.shape[0]
    local_rows = jnp.arange(ROWS_DEV, dtype=jnp.int32)
    owner_rows = jnp.concatenate([jnp.zeros((PREFIX,), jnp.int32) + batch_index, question])
    owner_length = prefix_len[owner_rows]
    key_limit = jnp.where(
        local_rows < PREFIX, jnp.minimum(local_rows + 1, owner_length), owner_length
    )
    key_index = jnp.arange(total_rows, dtype=jnp.int32)
    key_batch = key_index // ROWS_DEV
    key_local = key_index % ROWS_DEV
    own_index = batch_index * ROWS_DEV + local_rows
    allowed = (key_batch[None, :] == owner_rows[:, None]) & (
        key_local[None, :] < key_limit[:, None]
    ) | (key_index[None, :] == own_index[:, None]) & (local_rows[:, None] >= PREFIX)
    key_heads = lax.dynamic_slice_in_dim(
        key_cache, first_group * HEAD_DIM, group_count * HEAD_DIM, 1
    ).reshape(total_rows, group_count, HEAD_DIM)
    value_heads = lax.dynamic_slice_in_dim(
        value_cache, first_group * HEAD_DIM, group_count * HEAD_DIM, 1
    ).reshape(total_rows, group_count, HEAD_DIM)
    query_heads = query_block.reshape(ROWS_DEV, group_count, per_group, HEAD_DIM)
    scores = jnp.einsum(
        "rgpd,kgd->gprk", query_heads, key_heads, preferred_element_type=jnp.float32
    ) / jnp.sqrt(jnp.float32(HEAD_DIM))
    scores = jnp.where(allowed[None, None], scores, jnp.float32(-1e30))
    row_peak = jnp.max(scores, axis=-1, keepdims=True)
    exponent = jnp.exp(scores - row_peak)
    attention = (exponent / jnp.sum(exponent, axis=-1, keepdims=True)).astype(jnp.bfloat16)
    context = jnp.einsum(
        "gprk,kgd->rgpd", attention, value_heads, preferred_element_type=jnp.float32
    )
    return context.reshape(ROWS_DEV, local_heads * HEAD_DIM).astype(jnp.bfloat16)


def body(
    hidden_in,
    queries,
    key_cache,
    value_cache,
    question,
    prefix_len,
    norm_gain,
    gate_weight,
    up_weight,
    down_weight,
):
    batch_index = lax.axis_index("batch")
    column_index = lax.axis_index("mp")
    all_keys, all_values = (
        lax.all_gather(key_cache, "batch", axis=0, tiled=True),
        lax.all_gather(value_cache, "batch", axis=0, tiled=True),
    )
    local_heads = queries.shape[1] // HEAD_DIM
    first_group = column_index * local_heads // (HEADS // KV_HEADS)
    context = attend(batch_index, first_group, queries, all_keys, all_values, question, prefix_len)
    full_context = lax.all_gather(context, "mp", axis=1, tiled=True)
    residual = (hidden_in.astype(jnp.float32) + full_context.astype(jnp.float32)).astype(
        jnp.bfloat16
    )
    widened = residual.astype(jnp.float32)
    mean_square = jnp.mean(widened * widened, axis=-1, keepdims=True)
    normed = (widened * lax.rsqrt(mean_square + 1e-05) * norm_gain).astype(jnp.bfloat16)
    normed_all, residual_all = (
        lax.all_to_all(normed, "batch", split_axis=1, concat_axis=0, tiled=True),
        lax.all_to_all(residual, "batch", split_axis=1, concat_axis=0, tiled=True),
    )
    total_rows = normed_all.shape[0]
    hidden_width = gate_weight.shape[1]
    gate_up = jnp.concatenate([gate_weight, up_weight], axis=1)
    out_rows = total_rows // lax.axis_size("mp")
    partial_sums = jnp.dot(normed_all, gate_up, preferred_element_type=jnp.float32)
    summed = lax.psum(partial_sums, "batch")
    hidden = (jax.nn.silu(summed[:, :hidden_width]) * summed[:, hidden_width:]).astype(jnp.bfloat16)
    branch_out = lax.psum_scatter(
        jnp.dot(hidden, down_weight, preferred_element_type=jnp.float32),
        "mp",
        scatter_dimension=0,
        tiled=True,
    )
    own_rows = lax.dynamic_slice_in_dim(residual_all, column_index * out_rows, out_rows, 0)
    return (own_rows.astype(jnp.float32) + branch_out).astype(jnp.bfloat16)


def solution(mesh):
    return jax.shard_map(
        body,
        mesh=mesh,
        in_specs=(
            P("batch", None),
            P("batch", "mp"),
            P("batch", None),
            P("batch", None),
            P("batch"),
            P(),
            P(),
            P("batch", "mp"),
            P("batch", "mp"),
            P("mp", "batch"),
        ),
        out_specs=P("mp", "batch"),
        check_vma=False,
    )
```

profile of v0, /device:TPU:32, one launch (start us, length us, event | category | flops | bytes accessed | tf_op | source)
XLA Modules:
  0.0 643.9 jit_solution(17211740097742198112)
XLA Ops:
  6.5 0.7 all-gather.6.cloned.1.call-update
  7.3 0.7 all-gather.4.cloned.1.call-update
  8.1 0.7 concatenate.6
  8.8 0.7 compare_select_fusion
  9.5 1.4 gather_fusion
  11.0 68.3 %all-gather.6.cloned.1.call-done = bf16[512,1024]{1,0:T(8,128)(2,1)} async-done(((bf16[32,1024]{1,0:T(8,128)(2,1)}), bf16[512,1024]{1,0:T(8,128)(2,1)}) %all-gather.6.cloned.1.call-update) | async-done | bytes 1048592 | tf_op jit(solution)/shard_map/all_gather | solution.py:67
  79.3 1.2 fusion.34
  80.6 0.8 copy-done.2
  81.6 68.8 %all-gather.4.cloned.1.call-done = bf16[512,1024]{1,0:T(8,128)(2,1)} async-done(((bf16[32,1024]{1,0:T(8,128)(2,1)}), bf16[512,1024]{1,0:T(8,128)(2,1)}) %all-gather.4.cloned.1.call-update) | async-done | bytes 1048592 | tf_op jit(solution)/shard_map/all_gather | solution.py:68
  150.4 1.4 fusion.12
  151.8 0.6 copy.32
  152.6 52.2 %all-gather.8.cloned.1.call-done = bf16[32,16384]{1,0:T(8,128)(2,1)} async-done(((bf16[32,1024]{1,0:T(8,128)(2,1)}), bf16[32,16384]{1,0:T(8,128)(2,1)}) %all-gather.8.cloned.1.call-update) | async-done | bytes 1048592 | tf_op jit(solution)/shard_map/all_gather | solution.py:73
  204.8 2.2 fusion.5
  207.0 0.9 copy-done.1
  207.9 0.3 fusion.7
  208.3 33.6 %all_to_all.38 = bf16[32,16,1024]{2,0,1:T(8,128)(2,1)S(1)} all-to-all(bf16[32,16,1024]{2,0,1:T(8,128)(2,1)S(1)} %bitcast.55), channel_id=1, replica_groups=mesh['batch'=16,'mp'=16] {'batch'}, dimensions={1} | all-to-all | bytes 2097152 | tf_op jit(solution)/shard_map/all_to_all | solution.py:81
  241.9 6.2 fusion
  248.2 301.4 %all-reduce.3.cloned.1.call-done = f32[512,3328]{1,0:T(8,128)} async-done(((f32[512,3328]{1,0:T(8,128)}), f32[512,3328]{1,0:T(8,128)}) %all-reduce.3.cloned.1.call-update) | async-done | bytes 6815760 | tf_op jit(solution)/shard_map/psum | solution.py:89
  549.6 6.5 %fusion.8 = f32[512,1024]{1,0:T(8,128)} fusion(bf16[1664,1024]{1,0:T(8,128)(2,1)S(1)} %copy-done, f32[512,3328]{1,0:T(8,128)} %all-reduce.3.cloned.1.call-done), kind=kOutput, calls=%fused_computation.13 | convolution fusion | flops 1749942272 | bytes 12320768 | tf_op jit(solution)/shard_map/dot_general | solution.py:92
  556.1 2.3 copy.31
  558.4 7.6 %all-to-all-start = ((bf16[32,16,1024]{2,0,1:T(8,128)(2,1)}), bf16[32,16,1024]{2,0,1:T(8,128)(2,1)}, u32[]{:S(2)}, u32[]{:S(2)}) async-start(bf16[32,16,1024]{2,0,1:T(8,128)(2,1)} %bitcast.54), calls=%async_computation | async-start | bytes 2097152 | tf_op jit(solution)/shard_map/all_to_all | solution.py:82
  566.0 25.7 %all-to-all-done = bf16[32,16,1024]{2,0,1:T(8,128)(2,1)} async-done(((bf16[32,16,1024]{2,0,1:T(8,128)(2,1)}), bf16[32,16,1024]{2,0,1:T(8,128)(2,1)}, u32[]{:S(2)}, u32[]{:S(2)}) %all-to-all-start) | async-done | bytes 1048608 | tf_op jit(solution)/shard_map/all_to_all | solution.py:82
  591.7 44.1 %reduce-scatter.2.cloned.1.call-done = f32[32,1024]{1,0:T(8,128)} async-done(((f32[512,1024]{1,0:T(8,128)}), f32[32,1024]{1,0:T(8,128)}) %reduce-scatter.2.cloned.1.call-update) | async-done | bytes 131088 | tf_op jit(solution)/shard_map/reduce_scatter | solution.py:91
  635.8 1.5 add_convert_fusion.1
  (27 shorter events, 0.7 us)
Async XLA Ops:
  6.5 543.0 %copy-start = (bf16[1664,1024]{1,0:T(8,128)(2,1)S(1)}, bf16[1664,1024]{1,0:T(8,128)(2,1)}, u32[]{:S(2)}) copy-start(bf16[1664,1024]{1,0:T(8,128)(2,1)} %param.19) | copy-start | bytes 10223620
  6.5 72.8 %all-gather.6.cloned.1.call-start = ((), (), s32[]{:S(2)}) async-start(), calls=%async_computation.4 | async-start | bytes 1114112 | tf_op jit(solution)/shard_map/all_gather | solution.py:67
  7.3 143.1 %all-gather.4.cloned.1.call-start = ((), (), s32[]{:S(2)}) async-start(), calls=%async_computation.3 | async-start | bytes 1114112 | tf_op jit(solution)/shard_map/all_gather | solution.py:68
  8.0 196.8 %all-gather.8.cloned.1.call-start = ((), (), s32[]{:S(2)}) async-start(), calls=%async_computation.5 | async-start | bytes 1114112 | tf_op jit(solution)/shard_map/all_gather | solution.py:73
  11.0 196.9 %copy-start.3 = (f32[16384]{0:T(1024)S(1)}, f32[16384]{0:T(1024)}, u32[]{:S(2)}) copy-start(f32[16384]{0:T(1024)} %param.16) | copy-start | bytes 196612
  80.6 0.8 copy-start.2
  152.5 397.1 %all-reduce.3.cloned.1.call-start = ((), (), s32[]{:S(2)}) async-start(), calls=%async_computation.6 | async-start | bytes 13631488 | tf_op jit(solution)/shard_map/psum | solution.py:89
  204.8 37.1 %copy-start.5 = (bf16[1024,1664]{1,0:T(8,128)(2,1)S(1)}, bf16[1024,1664]{1,0:T(8,128)(2,1)}, u32[]{:S(2)}) copy-start(bf16[1024,1664]{1,0:T(8,128)(2,1)} %param.17) | copy-start | bytes 10223620
  207.0 1.0 copy-start.1
  207.0 34.9 %copy-start.4 = (bf16[1024,1664]{1,0:T(8,128)(2,1)S(1)}, bf16[1024,1664]{1,0:T(8,128)(2,1)}, u32[]{:S(2)}) copy-start(bf16[1024,1664]{1,0:T(8,128)(2,1)} %param.18) | copy-start | bytes 10223620
  248.1 387.7 %reduce-scatter.2.cloned.1.call-start = ((), (), s32[]{:S(2)}) async-start(), calls=%async_computation.7 | async-start | bytes 2228224 | tf_op jit(solution)/shard_map/reduce_scatter | solution.py:91
  558.4 33.3 %all-to-all-start = ((bf16[32,16,1024]{2,0,1:T(8,128)(2,1)}), bf16[32,16,1024]{2,0,1:T(8,128)(2,1)}, u32[]{:S(2)}, u32[]{:S(2)}) async-start(bf16[32,16,1024]{2,0,1:T(8,128)(2,1)} %bitcast.54), calls=%async_computation | async-start | bytes 2097152 | tf_op jit(solution)/shard_map/all_to_all | solution.py:82
Sparse Core Ops, SparseCore 0:
  9.1 70.1 all-gather.5
  81.1 69.2 all-gather.3
  153.2 51.5 all-gather.7
  248.3 301.2 all-reduce.2
  556.2 79.5 reduce-scatter.1
where the time goes:
time: 644 us
  waiting for transfers between devices  562 us (87%)
  blocking collectives  33.6 us (5%)
  matrix products  15.3 us (2%)
  between operations  13.3 us (2%)
  starting transfers between devices  7.75 us (1%)
  local copies, waits for them, and re-layouts  6.92 us (1%)
    psum x1, waiting for transfers between devices, body(): summed = lax.psum(partial_sums, 'batch')  301 us
    all_gather x1, waiting for transfers between devices, body(): lax.all_gather(value_cache, 'batch', axis=0, tiled=True)  68.8 us
    all_gather x1, waiting for transfers between devices, body(): lax.all_gather(key_cache, 'batch', axis=0, tiled=True)  68.3 us
    all_gather x1, waiting for transfers between devices, body(): full_context = lax.all_gather(context, 'mp', axis=1, tiled=True)  52.2 us
    reduce_scatter x1, waiting for transfers between devices, body(): lax.psum_scatter(jnp.dot(hidden, down_weight, preferred_element_type=jnp....  44.1 us
    all_to_all x1, blocking collectives, body(): lax.all_to_all(normed, 'batch', split_axis=1, concat_axis=0, tiled=True)  33.6 us
    all_to_all x1, waiting for transfers between devices, body(): lax.all_to_all(residual, 'batch', split_axis=1, concat_axis=0, tiled=True)  25.7 us
  transfers between devices with their start and end apart: 6, of which 6 were waited for; matrix products, arithmetic and copies ran while one was open for 1% of the time, Pallas kernels for 0%

commit v1 on v0

v1 whole, which is shorter than its diff:
```python
import jax
import jax.numpy as jnp
from jax import lax
from jax.experimental import pallas as pl
from jax.experimental.pallas import tpu as pltpu
from jax.sharding import PartitionSpec as P

HEADS = 128
KV_HEADS = 8
HEAD_DIM = 128
PREFIX = 24
ROWS_DEV = 32
ZN = 8
LANE = 128
BF = jnp.bfloat16
F32 = jnp.float32
PLANE = [[2 * i + core for i in range(8)] for core in range(2)]
VMEM = pl.BlockSpec(memory_space=pltpu.VMEM)
SMEM = pl.BlockSpec(memory_space=pltpu.SMEM)
ANY = pl.BlockSpec(memory_space=pl.ANY)
PARAMS = pltpu.CompilerParams(vmem_limit_bytes=24 * 2**20)


def permute(value, axis, target, count=16):
    return lax.ppermute(value, axis, [(i, target(i)) for i in range(count)])


def along_z(value, step):
    return permute(value, "batch", lambda i: (i + 2 * step) % 16)


def x_pair(value):
    return permute(value, "batch", lambda i: i ^ 1)


def core_pair(value):
    return permute(value, "mp", lambda i: i ^ 1)


def transpose_mesh(value):
    return lax.ppermute(
        value,
        ("batch", "mp"),
        [(b * 16 + m, m * 16 + b) for b in range(16) for m in range(16)],
    )


def over_plane(value):
    return lax.all_to_all(value, "mp", 0, 0, axis_index_groups=PLANE, tiled=True)


def together(*pairs):
    values = lax.optimization_barrier(tuple(value for value, _ in pairs))
    sent = tuple(move(value) for value, (_, move) in zip(values, pairs))
    return lax.optimization_barrier(sent)


def in_vmem(*shapes):
    made = tuple(pltpu.VMEM(shape, dtype) for shape, dtype in shapes)
    return made if len(made) > 1 else made[0]


def pack_kernel(group_ref, key_ref, value_ref, out_ref, held, sems):
    at = pl.ds(pl.multiple_of(group_ref[0] * HEAD_DIM, HEAD_DIM), HEAD_DIM)
    first = pltpu.make_async_copy(key_ref.at[:, at], held.at[:, :HEAD_DIM], sems.at[0])
    second = pltpu.make_async_copy(value_ref.at[:, at], held.at[:, HEAD_DIM:], sems.at[1])
    first.start()
    second.start()
    first.wait()
    second.wait()
    for i in range(out_ref.shape[0]):
        out_ref[i] = held[...]


def pack(group, key_cache, value_cache):
    return pl.pallas_call(
        pack_kernel,
        out_shape=jax.ShapeDtypeStruct((16, ROWS_DEV, 2 * HEAD_DIM), BF),
        in_specs=[SMEM, ANY, ANY],
        out_specs=VMEM,
        scratch_shapes=[
            pltpu.VMEM((ROWS_DEV, 2 * HEAD_DIM), BF),
            pltpu.SemaphoreType.DMA((2,)),
        ],
        compiler_params=PARAMS,
    )(group.reshape(1), key_cache, value_cache)


def attend_kernel(place_ref, length_ref, question_ref, queries_ref, hidden_ref, pairs_ref, out_ref, held, sem):
    width = out_ref.shape[1]
    heads = width // HEAD_DIM
    total = pairs_ref.shape[0]
    own = place_ref[0]
    at = pl.ds(pl.multiple_of(place_ref[1] * width, width), width)
    fetch = pltpu.make_async_copy(hidden_ref.at[:, at], held, sem)
    fetch.start()
    shape = (ROWS_DEV, total)
    key_index = lax.broadcasted_iota(jnp.int32, shape, 1)
    row = lax.broadcasted_iota(jnp.int32, shape, 0)
    key_block = key_index >> 5
    key_local = key_index & (ROWS_DEV - 1)
    live = jnp.zeros(shape, jnp.int32)
    for block in range(total // ROWS_DEV):
        live = jnp.where(key_block == block, length_ref[block], live)
    owner = jnp.full(shape, own)
    for option in range(ROWS_DEV - PREFIX):
        owner = jnp.where(row == PREFIX + option, question_ref[option], owner)
    option = row >= PREFIX
    seen = (key_block == owner) & (key_local < live) & (option | (key_local <= row))
    seen = seen | (option & (key_index == own * ROWS_DEV + row))
    bias = jnp.where(seen, F32(0), F32(-1e30))
    bias = jnp.concatenate([bias] * heads, axis=0)
    queries = jnp.concatenate(
        [queries_ref[:, h * HEAD_DIM : (h + 1) * HEAD_DIM] for h in range(heads)], axis=0
    )
    scores = lax.dot_general(
        queries, pairs_ref[:, :HEAD_DIM], (((1,), (1,)), ((), ())), preferred_element_type=F32
    )
    scores = jnp.where(bias < 0, bias, scores * F32(HEAD_DIM**-0.5))
    exponent = jnp.exp(scores - jnp.max(scores, axis=1, keepdims=True))
    attention = (exponent / jnp.sum(exponent, axis=1, keepdims=True)).astype(BF)
    context = jnp.dot(attention, pairs_ref[:, HEAD_DIM:], preferred_element_type=F32).astype(BF)
    fetch.wait()
    for h in range(heads):
        columns = slice(h * HEAD_DIM, (h + 1) * HEAD_DIM)
        mine = context[h * ROWS_DEV : (h + 1) * ROWS_DEV].astype(F32)
        out_ref[:, columns] = (held[:, columns].astype(F32) + mine).astype(BF)


def attend(place, prefix_len, question, queries, hidden_in, pairs):
    return pl.pallas_call(
        attend_kernel,
        out_shape=in_vmem((queries.shape, BF)),
        in_specs=[SMEM, SMEM, SMEM, VMEM, ANY, VMEM],
        out_specs=VMEM,
        scratch_shapes=[pltpu.VMEM(queries.shape, BF), pltpu.SemaphoreType.DMA(())],
        compiler_params=PARAMS,
    )(place, prefix_len, question, queries, hidden_in, pairs)


FAR, KEEP = 4, 0


def project_kernel(tiles, early, place_ref, mine_ref, theirs_ref, gain_ref, gate_ref, up_ref, *refs):
    give, kept, far_low, far_high = refs[0:8], refs[8:15], refs[15], refs[16]
    rows, weights, sems, squares = refs[17:]
    n = ROWS_DEV
    width = mine_ref.shape[2]
    slots = weights.shape[0]
    wide = 2 * tiles + 1

    def copies(t, slot):
        at = pl.ds(pl.multiple_of(t * LANE, LANE), LANE)
        return (
            pltpu.make_async_copy(gate_ref.at[:, at], weights.at[slot, :, :LANE], sems.at[slot, 0]),
            pltpu.make_async_copy(up_ref.at[:, at], weights.at[slot, :, LANE:], sems.at[slot, 1]),
        )

    for t in range(slots - 1):
        for copy in copies(t, t):
            copy.start()

    def put(s, j, tile, value, is_early):
        if is_early:
            column = pl.multiple_of(tile * LANE, LANE)
            if j == 1:
                give[s][:, pl.ds(column, LANE)] = value
            elif s == FAR:
                far_low[:, pl.ds(column, LANE)] = value
            else:
                kept[s if s < FAR else s - 1][:, pl.ds(column, LANE)] = value
        else:
            late = tile - early + j * (wide - early)
            if s == FAR:
                far_high[:, pl.ds(pl.multiple_of(late * LANE, LANE), LANE)] = value
            else:
                column = pl.multiple_of((late + early) * LANE, LANE)
                kept[s if s < FAR else s - 1][:, pl.ds(column, LANE)] = value

    z, flip = place_ref[0], place_ref[1]
    gain = gain_ref[...]
    for s in range(ZN):
        source = (z + s) & (ZN - 1)
        for ref, j in ((mine_ref, flip), (theirs_ref, 1 - flip)):
            x = ref[source].astype(F32)
            rows[pl.ds(pl.multiple_of(s * 2 * n + j * n, n), n), :] = (x * gain).astype(BF)
            square = x * x
            total = square[:, :LANE]
            for k in range(1, width // LANE):
                total = total + square[:, k * LANE : (k + 1) * LANE]
            squares[pl.ds(pl.multiple_of(s * 2 * n + j * n, n), n), :] = total.astype(BF)
    for s in range(ZN):
        for j in range(2):
            put(s, j, wide - 1, squares[s * 2 * n + j * n : s * 2 * n + (j + 1) * n, :], False)

    def step(t, up_early):
        slot = lax.rem(t, slots)
        ahead = t + slots - 1

        @pl.when(ahead < tiles)
        def _():
            for copy in copies(ahead, lax.rem(ahead, slots)):
                copy.start()

        for copy in copies(t, slot):
            copy.wait()
        product = jnp.dot(rows[...], weights[slot], preferred_element_type=F32).astype(BF)
        for s in range(ZN):
            for j in range(2):
                part = product[s * 2 * n + j * n : s * 2 * n + (j + 1) * n]
                put(s, j, t, part[:, :LANE], True)
                put(s, j, tiles + t, part[:, LANE:], up_early)

    lax.fori_loop(0, early - tiles, lambda t, _: (step(t, True), 0)[1], 0)
    lax.fori_loop(early - tiles, tiles, lambda t, _: (step(t, False), 0)[1], 0)


def project(place, mine, theirs, gain, gate_weight, up_weight):
    width, hidden_width = gate_weight.shape
    tiles = hidden_width // LANE
    early = 2 * (2 * tiles + 1) // 3
    low = (ROWS_DEV, early * LANE)
    high = (ROWS_DEV, 2 * (2 * tiles + 1 - early) * LANE)
    whole = (ROWS_DEV, low[1] + high[1])
    n = 2 * ZN * ROWS_DEV
    refs = pl.pallas_call(
        lambda *refs: project_kernel(tiles, early, *refs),
        out_shape=in_vmem(*[(low, BF)] * 8, *[(whole, BF)] * 7, (low, BF), (high, BF)),
        in_specs=[SMEM, VMEM, VMEM, VMEM, ANY, ANY],
        out_specs=(VMEM,) * 17,
        scratch_shapes=[
            pltpu.VMEM((n, width), BF),
            pltpu.VMEM((3, width, 2 * LANE), BF),
            pltpu.SemaphoreType.DMA((3, 2)),
            pltpu.VMEM((n, LANE), BF),
        ],
        compiler_params=PARAMS,
    )(place, mine, theirs, gain, gate_weight, up_weight)
    kept = list(refs[8:15])
    return refs[:8], kept[:4] + [None] + kept[4:], refs[15], refs[16], early


def add_first_kernel(low_ref, x_ref, out_ref):
    out_ref[...] = (low_ref[...].astype(F32) + x_ref[...].astype(F32)).astype(BF)


def add_far_kernel(mine_up, mine_down, x_up, x_down, up, down, out_up, out_down):
    low = x_up.shape[1]
    out_up[:, :low] = (
        mine_up[:, :low].astype(F32) + x_up[...].astype(F32) + up[...].astype(F32)
    ).astype(BF)
    out_up[:, low:] = mine_up[:, low:]
    out_down[:, :low] = (mine_down[:, :low].astype(F32) + x_down[...].astype(F32)).astype(BF)
    out_down[:, low:] = (mine_down[:, low:].astype(F32) + down[...].astype(F32)).astype(BF)


def add_ring_kernel(mine_up, mine_down, x_up, x_down, up, down, out_up, out_down):
    low = x_up.shape[1]
    for mine, x, come, out in ((mine_up, x_up, up, out_up), (mine_down, x_down, down, out_down)):
        out[:, :low] = (
            mine[:, :low].astype(F32) + x[...].astype(F32) + come[:, :low].astype(F32)
        ).astype(BF)
        out[:, low:] = (mine[:, low:].astype(F32) + come[:, low:].astype(F32)).astype(BF)


def add_last_kernel(mine, x, up, down, keep, give):
    low, wide = x.shape[1], keep.shape[1]
    keep[:, :low] = (
        mine[:, :low].astype(F32)
        + x[...].astype(F32)
        + up[:, :low].astype(F32)
        + down[:, :low].astype(F32)
    )
    keep[:, low:] = (
        mine[:, low:wide].astype(F32) + up[:, low:wide].astype(F32) + down[:, low:wide].astype(F32)
    )
    give[...] = (
        mine[:, wide:].astype(F32) + up[:, wide:].astype(F32) + down[:, wide:].astype(F32)
    ).astype(BF)


def local(kernel, shapes, *args):
    return pl.pallas_call(
        kernel,
        out_shape=in_vmem(*shapes),
        in_specs=[VMEM] * len(args),
        out_specs=(VMEM,) * len(shapes) if len(shapes) > 1 else VMEM,
        compiler_params=PARAMS,
    )(*args)


def gated_kernel(keep, x, out):
    hidden_width = out.shape[1]
    wide = keep.shape[1]
    low = wide - x.shape[1]
    late = keep[:, low:] + x[...].astype(F32)
    squares = late[:, 2 * hidden_width - low :]
    scale = lax.rsqrt(jnp.sum(squares, axis=1, keepdims=True) * F32(1 / 16384) + 1e-05)
    gate = keep[:, :hidden_width] * scale
    lift = jnp.concatenate([keep[:, hidden_width:low], late[:, : 2 * hidden_width - low]], axis=1) * scale
    out[...] = (gate / (1 + jnp.exp(-gate)) * lift).astype(BF)


def down_kernel(place_ref, *refs):
    blocks, down_ref, give, keep = refs[:9], refs[9], refs[10], refs[11]
    rows, weights, sems = refs[12:]
    n = ROWS_DEV
    tiles = weights.shape[0]
    width = give.shape[2] // tiles
    copies = [
        pltpu.make_async_copy(down_ref.at[:, i * width : (i + 1) * width], weights.at[i], sems.at[i])
        for i in range(tiles)
    ]
    for copy in copies:
        copy.start()
    z, flip = place_ref[0], place_ref[1]
    for s in range(ZN):
        for j in range(2):
            if s == FAR:
                value = blocks[7 + j][0]
            else:
                value = blocks[s if s < FAR else s - 1][j]
            target = (z + s) & (ZN - 1)
            other = (flip + j) & 1
            at = (1 - other) * ZN * n + target * n
            rows[pl.ds(pl.multiple_of(at, n), n), :] = value
    for i in range(tiles):
        copies[i].wait()
        product = jnp.dot(rows[...], weights[i], preferred_element_type=F32)
        for target in range(ZN):
            give[target, :, i * width : (i + 1) * width] = product[target * n : (target + 1) * n].astype(BF)
            at = (ZN + target) * n
            keep[target, :, i * width : (i + 1) * width] = product[at : at + n]


def project_down(place, blocks, down_weight):
    hidden_width, width = down_weight.shape
    shape = (ZN, ROWS_DEV, width)
    return pl.pallas_call(
        down_kernel,
        out_shape=in_vmem((shape, BF), (shape, F32)),
        in_specs=[SMEM] + [VMEM] * 9 + [ANY],
        out_specs=(VMEM, VMEM),
        scratch_shapes=[
            pltpu.VMEM((2 * ZN * ROWS_DEV, hidden_width), BF),
            pltpu.VMEM((4, hidden_width, width // 4), BF),
            pltpu.SemaphoreType.DMA((4,)),
        ],
        compiler_params=PARAMS,
    )(place, *blocks, down_weight)


def add_core_kernel(keep, come, out):
    out[...] = (keep[...] + come[...].astype(F32)).astype(BF)


def finish_kernel(own, parts, out):
    total = own[...].astype(F32)
    for i in range(parts.shape[0]):
        total = total + parts[i].astype(F32)
    out[...] = total.astype(BF)


def ring(up, down, *more):
    return together(
        (up, lambda v: along_z(v, 1)), (down, lambda v: along_z(v, -1)), *more
    )


def body(
    hidden_in,
    queries,
    key_cache,
    value_cache,
    question,
    prefix_len,
    norm_gain,
    gate_weight,
    up_weight,
    down_weight,
):
    batch_index = lax.axis_index("batch")
    mp_index = lax.axis_index("mp")
    z, x_lo, core = batch_index >> 1, batch_index & 1, mp_index & 1
    rows, width = queries.shape
    hidden_width = gate_weight.shape[1]
    place = jnp.stack([z, x_lo ^ core])

    pairs = pack(mp_index >> 1, key_cache, value_cache)
    pairs = lax.all_to_all(pairs, "batch", 0, 0, tiled=True).reshape(16 * rows, 2 * HEAD_DIM)
    mine = attend(jnp.stack([batch_index, mp_index]), prefix_len, question, queries, hidden_in, pairs)

    own = transpose_mesh(mine)
    mine = over_plane(jnp.broadcast_to(own[None], (ZN, rows, width)))
    theirs = core_pair(mine)
    gain = lax.dynamic_slice_in_dim(norm_gain, batch_index * width, width, 0, allow_negative_indices=False)
    give, kept, far_low, far_high, early = project(
        place, mine, theirs, gain.reshape(1, width), gate_weight, up_weight
    )
    low, whole = far_low.shape, kept[0].shape

    def handed(s):
        return (give[s], x_pair)

    (x_far,) = together(handed(FAR))
    up, down, x_up, x_down = ring(
        local(add_first_kernel, [(low, BF)], far_low, x_far), far_high, handed(3), handed(5)
    )
    up, down = local(
        add_far_kernel, [(whole, BF)] * 2, kept[3], kept[5], x_up, x_down, up, down
    )
    up, down, x_up, x_down = ring(up, down, handed(2), handed(6))
    up, down = local(
        add_ring_kernel, [(whole, BF)] * 2, kept[2], kept[6], x_up, x_down, up, down
    )
    up, down, x_up, x_down = ring(up, down, handed(1), handed(7))
    up, down = local(
        add_ring_kernel, [(whole, BF)] * 2, kept[1], kept[7], x_up, x_down, up, down
    )
    up, down, x_own = ring(up, down, handed(0))
    late = whole[1] - 2 * hidden_width - LANE
    keep, last = local(
        add_last_kernel,
        [((rows, 2 * hidden_width + LANE), F32), ((rows, late), BF)],
        kept[0],
        x_own,
        up,
        down,
    )
    hidden = local(gated_kernel, [((rows, hidden_width), BF)], keep, x_pair(last))

    pair = jnp.stack([hidden, x_pair(hidden)])
    ups, downs = [pair], [pair]
    for _ in range(3):
        up, down = ring(ups[-1], downs[-1])
        ups.append(up)
        downs.append(down)
    up, down = ring(ups[-1][:1], downs[-1][1:])
    blocks = [pair, downs[1], downs[2], downs[3], ups[3], ups[2], ups[1], up, down]
    send, keep = project_down(place, blocks, down_weight)
    held = local(add_core_kernel, [(keep.shape, BF)], keep, core_pair(send))
    parts = over_plane(held)
    return pl.pallas_call(
        finish_kernel,
        out_shape=jax.ShapeDtypeStruct((rows, width), BF),
        in_specs=[VMEM, VMEM],
        out_specs=VMEM,
        compiler_params=PARAMS,
    )(own, parts)


def solution(mesh):
    return jax.shard_map(
        body,
        mesh=mesh,
        in_specs=(
            P("batch", None),
            P("batch", "mp"),
            P("batch", None),
            P("batch", None),
            P("batch"),
            P(),
            P(),
            P("batch", "mp"),
            P("batch", "mp"),
            P("mp", "batch"),
        ),
        out_specs=P("mp", "batch"),
        check_vma=False,
    )
```

time: 644 us -> 180 us (0.28)
  waiting for transfers between devices: 562 us -> 69.2 us
  starting transfers between devices: 7.75 us -> 45.5 us
  Pallas kernels: 0 us -> 17.4 us
  matrix products: 15.3 us -> 0 us
  between operations: 13.3 us -> 0.2 us
    psum x1 -> x0, waiting for transfers between devices: 301 us -> none  [body(): summed = lax.psum(partial_sums, 'batch')]
    all_gather x3 -> x0, waiting for transfers between devices: 189 us -> none  [the longest x1 68.8 us: body(): lax.all_gather(value_cache, 'batch', axis=0, tiled=True)]
    ppermute x0 -> x29, waiting for transfers between devices: none -> 58.6 us  [the longest x28 55.7 us: permute(): return lax.ppermute(value, axis, [(i, target(i)) for i in range(count)])]
    reduce_scatter x1 -> x0, waiting for transfers between devices: 44.1 us -> none  [body(): lax.psum_scatter(jnp.dot(hidden, down_weight, preferred_element_type=jnp....]
    ppermute x0 -> x29, starting transfers between devices: none -> 36 us  [the longest x28 31.5 us: permute(): return lax.ppermute(value, axis, [(i, target(i)) for i in range(count)])]
    pallas_call x0 -> x12, Pallas kernels: none -> 17.4 us  [the longest x1 8.66 us: project(): pl.pallas_call(lambda *refs: project_kernel(tiles, early, *refs), out_sha...]
    dot_general x4 -> x0, matrix products: 15.3 us -> none  [the longest x1 6.5 us: body(): jnp.dot(hidden, down_weight, preferred_element_type=jnp.float32)]
    all_to_all x1, waiting for transfers between devices: 25.7 us -> 10.6 us  [body(): lax.all_to_all(pairs, 'batch', 0, 0, tiled=True)]
  transfers between devices with their start and end apart: 6 -> 30, of which waited for: 6 -> 22; matrix products, arithmetic and copies ran while one was open for 1% -> 0% of each run, Pallas kernels for 0% -> 0%
where the time goes in v1:
time: 180 us; the launch traced here: 179 us
  waiting for transfers between devices  69.2 us (38%)
  starting transfers between devices  45.5 us (25%)
  blocking collectives  38.2 us (21%)
  Pallas kernels  17.4 us (10%)
  local copies, waits for them, and re-layouts  8.71 us (5%)
    ppermute x28, waiting for transfers between devices, permute(): return lax.ppermute(value, axis, [(i, target(i)) for i in range(count)])  55.7 us
    all_to_all x2, blocking collectives, over_plane(): lax.all_to_all(value, 'mp', 0, 0, axis_index_groups=PLANE, tiled=True)  38.2 us
    ppermute x28, starting transfers between devices, permute(): return lax.ppermute(value, axis, [(i, target(i)) for i in range(count)])  31.5 us
    all_to_all x1, waiting for transfers between devices, body(): lax.all_to_all(pairs, 'batch', 0, 0, tiled=True)  10.6 us
    all_to_all x1, starting transfers between devices, body(): lax.all_to_all(pairs, 'batch', 0, 0, tiled=True)  9.51 us
    pallas_call x1, Pallas kernels, project(): pl.pallas_call(lambda *refs: project_kernel(tiles, early, *refs), out_sha...  8.66 us
    unnamed x20, local copies, waits for them, and re-layouts  7.95 us
    pallas_call x1, Pallas kernels, project_down(): pl.pallas_call(down_kernel, out_shape=in_vmem((shape, BF), (shape, F32)),...  5.53 us
  transfers between devices with their start and end apart: 30, of which 22 were waited for; matrix products, arithmetic and copies ran while one was open for 0% of the time, Pallas kernels for 0%

profile of v1, /device:TPU:32, one launch (start us, length us, event | category | flops | bytes accessed | tf_op | source)
XLA Modules:
  0.0 179.4 jit_solution(2558884074880879501)
XLA Ops:
  2.7 9.5 %all-to-all-start = ((bf16[16,32,256]{2,1,0:T(8,128)(2,1)}), bf16[16,32,256]{2,1,0:T(8,128)(2,1)}, u32[]{:S(2)}, u32[]{:S(2)}) async-start(bf16[16,32,256]{2,1,0:T(8,128)(2,1)} %copy-done.4), calls=%async_computation | async-start | bytes 524288 | tf_op jit(solution)/shard_map/all_to_all | solution.py:390
  12.3 10.6 %all-to-all-done = bf16[16,32,256]{2,1,0:T(8,128)(2,1)} async-done(((bf16[16,32,256]{2,1,0:T(8,128)(2,1)}), bf16[16,32,256]{2,1,0:T(8,128)(2,1)}, u32[]{:S(2)}, u32[]{:S(2)}) %all-to-all-start) | async-done | bytes 262176 | tf_op jit(solution)/shard_map/all_to_all | solution.py:390
  27.9 4.4 %collective-permute-start = (bf16[32,1024]{1,0:T(8,128)(2,1)S(1)}, bf16[32,1024]{1,0:T(8,128)(2,1)S(1)}, u32[]{:S(2)}, u32[]{:S(2)}) collective-permute-start(bf16[32,1024]{1,0:T(8,128)(2,1)S(1)} %shard_map.101), channel_id=1, source_target_pairs={{0,0},{1,16},{2,32},{3,48},{4,64},{5,80},{6,96},{7,112},{8,128},{9... | collective-permute-start | bytes 196616 | tf_op jit(solution)/shard_map/ppermute | solution.py:41
  32.3 2.9 %collective-permute-done.own = bf16[32,1024]{1,0:T(8,128)(2,1)S(1)} collective-permute-done((bf16[32,1024]{1,0:T(8,128)(2,1)S(1)}, bf16[32,1024]{1,0:T(8,128)(2,1)S(1)}, u32[]{:S(2)}, u32[]{:S(2)}) %collective-permute-start) | collective-permute-done | bytes 65568 | tf_op jit(solution)/shard_map/ppermute | solution.py:41
  35.3 23.7 %all_to_all.15.refs_1_ = bf16[8,32,1024]{2,1,0:T(8,128)(2,1)} all-to-all(bf16[8,32,1024]{2,1,0:T(8,128)(2,1)S(1)} %broadcast_in_dim.2), channel_id=1, replica_groups={{0,2,4,6,8,10,12,14},{1,3,5,7,9,11,13,15},{16,18,20,22,24,26,28,30},{17..., dimensions={0} | all-to-all | bytes 1048576 | tf_op jit(solution)/shard_map/all_to_all | solution.py:49
  63.2 8.7 %shard_map.102 = (bf16[32,2304]{1,0:T(8,128)(2,1)S(1)}, bf16[32,2304]{1,0:T(8,128)(2,1)S(1)}, bf16[32,2304]{1,0:T(8,128)(2,1)S(1)}, bf16[32,2304]{1,0:T(8,128)(2...) custom-call(s32[2]{0:T(128)S(1)} %pad_add_fusion.1.refs_0_.place_ref, ...), custom_call_target="tpu_custom_call" | custom-call | tf_op jit(solution)/shard_map/pallas_call | solution.py:226
  72.0 5.9 %collective-permute-done.2.x_ref = bf16[32,2304]{1,0:T(8,128)(2,1)S(1)} collective-permute-done((bf16[32,2304]{1,0:T(8,128)(2,1)S(1)}, bf16[32,2304]{1,0:T(8,128)(2,1)S(1)}, u32[]{:S(2)}, u32[]{:S(2)}) %collective-permute-start.2) | collective-permute-done | bytes 147488 | tf_op jit(solution)/shard_map/ppermute | solution.py:25
  83.5 3.1 %collective-permute-done.5.x_up = bf16[32,2304]{1,0:T(8,128)(2,1)S(1)} collective-permute-done((bf16[32,2304]{1,0:T(8,128)(2,1)S(1)}, bf16[32,2304]{1,0:T(8,128)(2,1)S(1)}, u32[]{:S(2)}, u32[]{:S(2)}) %collective-permute-start.5) | collective-permute-done | bytes 147488 | tf_op jit(solution)/shard_map/ppermute | solution.py:25
  88.4 2.9 %collective-permute-start.8 = (bf16[32,4608]{1,0:T(8,128)(2,1)S(1)}, bf16[32,4608]{1,0:T(8,128)(2,1)S(1)}, u32[]{:S(2)}, u32[]{:S(2)}) collective-permute-start(bf16[32,4608]{1,0:T(8,128)(2,1)S(1)} %get-tuple-element.103), channel_id=1, source_target_pairs={{0,224},{16,240},{32,0},{48,16},{64,32},{80,48},{96,64},{112,80},{... | collective-permute-start | bytes 884744 | tf_op jit(solution)/shard_map/ppermute | solution.py:25
  93.4 3.1 %collective-permute-done.9.x_up = bf16[32,2304]{1,0:T(8,128)(2,1)S(1)} collective-permute-done((bf16[32,2304]{1,0:T(8,128)(2,1)S(1)}, bf16[32,2304]{1,0:T(8,128)(2,1)S(1)}, u32[]{:S(2)}, u32[]{:S(2)}) %collective-permute-start.9) | collective-permute-done | bytes 147488 | tf_op jit(solution)/shard_map/ppermute | solution.py:25
  98.3 3.2 %collective-permute-start.12 = (bf16[32,4608]{1,0:T(8,128)(2,1)S(1)}, bf16[32,4608]{1,0:T(8,128)(2,1)S(1)}, u32[]{:S(2)}, u32[]{:S(2)}) collective-permute-start(bf16[32,4608]{1,0:T(8,128)(2,1)S(1)} %get-tuple-element.115), channel_id=1, source_target_pairs={{0,224},{16,240},{32,0},{48,16},{64,32},{80,48},{96,64},{112,80},{... | collective-permute-start | bytes 884744 | tf_op jit(solution)/shard_map/ppermute | solution.py:25
  103.6 3.1 %collective-permute-done.13.x_up = bf16[32,2304]{1,0:T(8,128)(2,1)S(1)} collective-permute-done((bf16[32,2304]{1,0:T(8,128)(2,1)S(1)}, bf16[32,2304]{1,0:T(8,128)(2,1)S(1)}, u32[]{:S(2)}, u32[]{:S(2)}) %collective-permute-start.13) | collective-permute-done | bytes 147488 | tf_op jit(solution)/shard_map/ppermute | solution.py:25
  108.7 3.2 %collective-permute-start.16 = (bf16[32,4608]{1,0:T(8,128)(2,1)S(1)}, bf16[32,4608]{1,0:T(8,128)(2,1)S(1)}, u32[]{:S(2)}, u32[]{:S(2)}) collective-permute-start(bf16[32,4608]{1,0:T(8,128)(2,1)S(1)} %get-tuple-element.126), channel_id=1, source_target_pairs={{0,224},{16,240},{32,0},{48,16},{64,32},{80,48},{96,64},{112,80},{... | collective-permute-start | bytes 884744 | tf_op jit(solution)/shard_map/ppermute | solution.py:25
  112.4 4.7 %collective-permute-done.17.x = bf16[32,2304]{1,0:T(8,128)(2,1)S(1)} collective-permute-done((bf16[32,2304]{1,0:T(8,128)(2,1)S(1)}, bf16[32,2304]{1,0:T(8,128)(2,1)S(1)}, u32[]{:S(2)}, u32[]{:S(2)}) %collective-permute-start.17) | collective-permute-done | bytes 147488 | tf_op jit(solution)/shard_map/ppermute | solution.py:25
  117.8 3.9 %collective-permute-done.18.x = bf16[32,1152]{1,0:T(8,128)(2,1)S(1)} collective-permute-done((bf16[32,1152]{1,0:T(8,128)(2,1)S(1)}, bf16[32,1152]{1,0:T(8,128)(2,1)S(1)}, u32[]{:S(2)}, u32[]{:S(2)}) %collective-permute-start.18) | collective-permute-done | bytes 73760 | tf_op jit(solution)/shard_map/ppermute | solution.py:25
  122.4 4.3 %collective-permute-done.19 = bf16[32,1664]{1,0:T(8,128)(2,1)S(1)} collective-permute-done((bf16[32,1664]{1,0:T(8,128)(2,1)S(1)}, bf16[32,1664]{1,0:T(8,128)(2,1)S(1)}, u32[]{:S(2)}, u32[]{:S(2)}) %collective-permute-start.19) | collective-permute-done | bytes 106528 | tf_op jit(solution)/shard_map/ppermute | solution.py:25
  126.8 3.2 %collective-permute-start.21 = (bf16[2,32,1664]{2,1,0:T(8,128)(2,1)S(1)}, bf16[2,32,1664]{2,1,0:T(8,128)(2,1)S(1)}, u32[]{:S(2)}, u32[]{:S(2)}) collective-permute-start(bf16[2,32,1664]{2,1,0:T(8,128)(2,1)S(1)} %pad_maximum_fusion.refs_0_), channel_id=1, source_target_pairs={{0,224},{16,240},{32,0},{48,16},{64,32},{80,48},{96,64},{112,80},{... | collective-permute-start | bytes 638984 | tf_op jit(solution)/shard_map/ppermute | solution.py:25
  130.0 3.7 %collective-permute-done.20.refs_6_ = bf16[2,32,1664]{2,1,0:T(8,128)(2,1)S(1)} collective-permute-done((bf16[2,32,1664]{2,1,0:T(8,128)(2,1)S(1)}, bf16[2,32,1664]{2,1,0:T(8,128)(2,1)S(1)}, u32[]{:S(2)}, u32[]{:S(2)}) %collective-permute-start.20) | collective-permute-done | bytes 213024 | tf_op jit(solution)/shard_map/ppermute | solution.py:25
  136.9 3.8 %collective-permute-done.22.refs_5_ = bf16[2,32,1664]{2,1,0:T(8,128)(2,1)S(1)} collective-permute-done((bf16[2,32,1664]{2,1,0:T(8,128)(2,1)S(1)}, bf16[2,32,1664]{2,1,0:T(8,128)(2,1)S(1)}, u32[]{:S(2)}, u32[]{:S(2)}) %collective-permute-start.22) | collective-permute-done | bytes 213024 | tf_op jit(solution)/shard_map/ppermute | solution.py:25
  144.2 3.8 %collective-permute-done.24.refs_4_ = bf16[2,32,1664]{2,1,0:T(8,128)(2,1)S(1)} collective-permute-done((bf16[2,32,1664]{2,1,0:T(8,128)(2,1)S(1)}, bf16[2,32,1664]{2,1,0:T(8,128)(2,1)S(1)}, u32[]{:S(2)}, u32[]{:S(2)}) %collective-permute-start.24) | collective-permute-done | bytes 213024 | tf_op jit(solution)/shard_map/ppermute | solution.py:25
  149.7 2.1 %collective-permute-start.26 = (bf16[1,32,1664]{2,1,0:T(8,128)(2,1)S(1)}, bf16[1,32,1664]{2,1,0:T(8,128)(2,1)S(1)}, u32[]{:S(2)}, u32[]{:S(2)}) collective-permute-start(bf16[1,32,1664]{2,1,0:T(8,128)(2,1)S(1)} %slice.6), channel_id=1, source_target_pairs={{0,32},{16,48},{32,64},{48,80},{64,96},{80,112},{96,128},{112,144}... | collective-permute-start | bytes 319496 | tf_op jit(solution)/shard_map/ppermute | solution.py:25
  151.8 2.7 %collective-permute-done.26.refs_7_ = bf16[1,32,1664]{2,1,0:T(8,128)(2,1)S(1)} collective-permute-done((bf16[1,32,1664]{2,1,0:T(8,128)(2,1)S(1)}, bf16[1,32,1664]{2,1,0:T(8,128)(2,1)S(1)}, u32[]{:S(2)}, u32[]{:S(2)}) %collective-permute-start.26) | collective-permute-done | bytes 106528 | tf_op jit(solution)/shard_map/ppermute | solution.py:25
  156.5 5.5 %shard_map.109 = (bf16[8,32,1024]{2,1,0:T(8,128)(2,1)S(1)}, f32[8,32,1024]{2,1,0:T(8,128)S(1)}) custom-call(s32[2]{0:T(128)S(1)} %pad_add_fusion.1.refs_0_.place_ref, bf16[2,32,1664]{2,1,0:T(8,128)(2,1)S(1)} %pad_maximum_fusion.refs_0_, bf16[2,32,1664]{2,1,0:T(8,128)(2,1)S(1)} %collective-permute-done.21.refs_1_, ...), custom_call_target="tpu_custom_call" | custom-call | tf_op jit(solution)/shard_map/pallas_call | solution.py:339
  164.2 14.5 %all_to_all.16.parts = bf16[8,32,1024]{2,1,0:T(8,128)(2,1)S(1)} all-to-all(bf16[8,32,1024]{2,1,0:T(8,128)(2,1)S(1)} %shard_map.110), channel_id=1, replica_groups={{0,2,4,6,8,10,12,14},{1,3,5,7,9,11,13,15},{16,18,20,22,24,26,28,30},{17..., dimensions={0} | all-to-all | bytes 1048576 | tf_op jit(solution)/shard_map/all_to_all | solution.py:49
  (77 shorter events, 42.5 us)
Async XLA Ops:
  2.7 20.2 %all-to-all-start = ((bf16[16,32,256]{2,1,0:T(8,128)(2,1)}), bf16[16,32,256]{2,1,0:T(8,128)(2,1)}, u32[]{:S(2)}, u32[]{:S(2)}) async-start(bf16[16,32,256]{2,1,0:T(8,128)(2,1)} %copy-done.4), calls=%async_computation | async-start | bytes 524288 | tf_op jit(solution)/shard_map/all_to_all | solution.py:390
  27.9 7.4 %collective-permute-start = (bf16[32,1024]{1,0:T(8,128)(2,1)S(1)}, bf16[32,1024]{1,0:T(8,128)(2,1)S(1)}, u32[]{:S(2)}, u32[]{:S(2)}) collective-permute-start(bf16[32,1024]{1,0:T(8,128)(2,1)S(1)} %shard_map.101), channel_id=1, source_target_pairs={{0,0},{1,16},{2,32},{3,48},{4,64},{5,80},{6,96},{7,112},{8,128},{9... | collective-permute-start | bytes 196616 | tf_op jit(solution)/shard_map/ppermute | solution.py:41
  71.9 6.0 %collective-permute-start.2 = (bf16[32,2304]{1,0:T(8,128)(2,1)S(1)}, bf16[32,2304]{1,0:T(8,128)(2,1)S(1)}, u32[]{:S(2)}, u32[]{:S(2)}) collective-permute-start(bf16[32,2304]{1,0:T(8,128)(2,1)S(1)} %get-tuple-element.86), channel_id=1, source_target_pairs={{0,16},{16,0},{32,48},{48,32},{64,80},{80,64},{96,112},{112,96},{1... | collective-permute-start | bytes 442376 | tf_op jit(solution)/shard_map/ppermute | solution.py:25
  77.9 5.6 %collective-permute-start.3 = (bf16[32,2304]{1,0:T(8,128)(2,1)S(1)}, bf16[32,2304]{1,0:T(8,128)(2,1)S(1)}, u32[]{:S(2)}, u32[]{:S(2)}) collective-permute-start(bf16[32,2304]{1,0:T(8,128)(2,1)S(1)} %shard_map.103), channel_id=1, source_target_pairs={{0,32},{16,48},{32,64},{48,80},{64,96},{80,112},{96,128},{112,144}... | collective-permute-start | bytes 442376 | tf_op jit(solution)/shard_map/ppermute | solution.py:25
  78.3 5.2 %collective-permute-start.4 = (bf16[32,2304]{1,0:T(8,128)(2,1)S(1)}, bf16[32,2304]{1,0:T(8,128)(2,1)S(1)}, u32[]{:S(2)}, u32[]{:S(2)}) collective-permute-start(bf16[32,2304]{1,0:T(8,128)(2,1)S(1)} %get-tuple-element.91), channel_id=1, source_target_pairs={{0,224},{16,240},{32,0},{48,16},{64,32},{80,48},{96,64},{112,80},{... | collective-permute-start | bytes 442376 | tf_op jit(solution)/shard_map/ppermute | solution.py:25
  80.2 6.3 %collective-permute-start.5 = (bf16[32,2304]{1,0:T(8,128)(2,1)S(1)}, bf16[32,2304]{1,0:T(8,128)(2,1)S(1)}, u32[]{:S(2)}, u32[]{:S(2)}) collective-permute-start(bf16[32,2304]{1,0:T(8,128)(2,1)S(1)} %get-tuple-element.92), channel_id=1, source_target_pairs={{0,16},{16,0},{32,48},{48,32},{64,80},{80,64},{96,112},{112,96},{1... | collective-permute-start | bytes 442376 | tf_op jit(solution)/shard_map/ppermute | solution.py:25
  80.5 7.6 %collective-permute-start.6 = (bf16[32,2304]{1,0:T(8,128)(2,1)S(1)}, bf16[32,2304]{1,0:T(8,128)(2,1)S(1)}, u32[]{:S(2)}, u32[]{:S(2)}) collective-permute-start(bf16[32,2304]{1,0:T(8,128)(2,1)S(1)} %get-tuple-element.93), channel_id=1, source_target_pairs={{0,16},{16,0},{32,48},{48,32},{64,80},{80,64},{96,112},{112,96},{1... | collective-permute-start | bytes 442376 | tf_op jit(solution)/shard_map/ppermute | solution.py:25
  88.3 9.8 %collective-permute-start.7 = (bf16[32,4608]{1,0:T(8,128)(2,1)S(1)}, bf16[32,4608]{1,0:T(8,128)(2,1)S(1)}, u32[]{:S(2)}, u32[]{:S(2)}) collective-permute-start(bf16[32,4608]{1,0:T(8,128)(2,1)S(1)} %get-tuple-element.102), channel_id=1, source_target_pairs={{0,32},{16,48},{32,64},{48,80},{64,96},{80,112},{96,128},{112,144}... | collective-permute-start | bytes 884744 | tf_op jit(solution)/shard_map/ppermute | solution.py:25
  88.4 9.7 %collective-permute-start.8 = (bf16[32,4608]{1,0:T(8,128)(2,1)S(1)}, bf16[32,4608]{1,0:T(8,128)(2,1)S(1)}, u32[]{:S(2)}, u32[]{:S(2)}) collective-permute-start(bf16[32,4608]{1,0:T(8,128)(2,1)S(1)} %get-tuple-element.103), channel_id=1, source_target_pairs={{0,224},{16,240},{32,0},{48,16},{64,32},{80,48},{96,64},{112,80},{... | collective-permute-start | bytes 884744 | tf_op jit(solution)/shard_map/ppermute | solution.py:25
  91.3 5.1 %collective-permute-start.9 = (bf16[32,2304]{1,0:T(8,128)(2,1)S(1)}, bf16[32,2304]{1,0:T(8,128)(2,1)S(1)}, u32[]{:S(2)}, u32[]{:S(2)}) collective-permute-start(bf16[32,2304]{1,0:T(8,128)(2,1)S(1)} %get-tuple-element.104), channel_id=1, source_target_pairs={{0,16},{16,0},{32,48},{48,32},{64,80},{80,64},{96,112},{112,96},{1... | collective-permute-start | bytes 442376 | tf_op jit(solution)/shard_map/ppermute | solution.py:25
  91.8 6.3 %collective-permute-start.10 = (bf16[32,2304]{1,0:T(8,128)(2,1)S(1)}, bf16[32,2304]{1,0:T(8,128)(2,1)S(1)}, u32[]{:S(2)}, u32[]{:S(2)}) collective-permute-start(bf16[32,2304]{1,0:T(8,128)(2,1)S(1)} %get-tuple-element.105), channel_id=1, source_target_pairs={{0,16},{16,0},{32,48},{48,32},{64,80},{80,64},{96,112},{112,96},{1... | collective-permute-start | bytes 442376 | tf_op jit(solution)/shard_map/ppermute | solution.py:25
  98.2 10.0 %collective-permute-start.11 = (bf16[32,4608]{1,0:T(8,128)(2,1)S(1)}, bf16[32,4608]{1,0:T(8,128)(2,1)S(1)}, u32[]{:S(2)}, u32[]{:S(2)}) collective-permute-start(bf16[32,4608]{1,0:T(8,128)(2,1)S(1)} %get-tuple-element.114), channel_id=1, source_target_pairs={{0,32},{16,48},{32,64},{48,80},{64,96},{80,112},{96,128},{112,144}... | collective-permute-start | bytes 884744 | tf_op jit(solution)/shard_map/ppermute | solution.py:25
  98.3 10.0 %collective-permute-start.12 = (bf16[32,4608]{1,0:T(8,128)(2,1)S(1)}, bf16[32,4608]{1,0:T(8,128)(2,1)S(1)}, u32[]{:S(2)}, u32[]{:S(2)}) collective-permute-start(bf16[32,4608]{1,0:T(8,128)(2,1)S(1)} %get-tuple-element.115), channel_id=1, source_target_pairs={{0,224},{16,240},{32,0},{48,16},{64,32},{80,48},{96,64},{112,80},{... | collective-permute-start | bytes 884744 | tf_op jit(solution)/shard_map/ppermute | solution.py:25
  101.6 5.1 %collective-permute-start.13 = (bf16[32,2304]{1,0:T(8,128)(2,1)S(1)}, bf16[32,2304]{1,0:T(8,128)(2,1)S(1)}, u32[]{:S(2)}, u32[]{:S(2)}) collective-permute-start(bf16[32,2304]{1,0:T(8,128)(2,1)S(1)} %get-tuple-element.116), channel_id=1, source_target_pairs={{0,16},{16,0},{32,48},{48,32},{64,80},{80,64},{96,112},{112,96},{1... | collective-permute-start | bytes 442376 | tf_op jit(solution)/shard_map/ppermute | solution.py:25
  102.0 6.3 %collective-permute-start.14 = (bf16[32,2304]{1,0:T(8,128)(2,1)S(1)}, bf16[32,2304]{1,0:T(8,128)(2,1)S(1)}, u32[]{:S(2)}, u32[]{:S(2)}) collective-permute-start(bf16[32,2304]{1,0:T(8,128)(2,1)S(1)} %get-tuple-element.117), channel_id=1, source_target_pairs={{0,16},{16,0},{32,48},{48,32},{64,80},{80,64},{96,112},{112,96},{1... | collective-permute-start | bytes 442376 | tf_op jit(solution)/shard_map/ppermute | solution.py:25
  108.5 8.6 %collective-permute-start.15 = (bf16[32,4608]{1,0:T(8,128)(2,1)S(1)}, bf16[32,4608]{1,0:T(8,128)(2,1)S(1)}, u32[]{:S(2)}, u32[]{:S(2)}) collective-permute-start(bf16[32,4608]{1,0:T(8,128)(2,1)S(1)} %get-tuple-element.125), channel_id=1, source_target_pairs={{0,32},{16,48},{32,64},{48,80},{64,96},{80,112},{96,128},{112,144}... | collective-permute-start | bytes 884744 | tf_op jit(solution)/shard_map/ppermute | solution.py:25
  108.7 8.4 %collective-permute-start.16 = (bf16[32,4608]{1,0:T(8,128)(2,1)S(1)}, bf16[32,4608]{1,0:T(8,128)(2,1)S(1)}, u32[]{:S(2)}, u32[]{:S(2)}) collective-permute-start(bf16[32,4608]{1,0:T(8,128)(2,1)S(1)} %get-tuple-element.126), channel_id=1, source_target_pairs={{0,224},{16,240},{32,0},{48,16},{64,32},{80,48},{96,64},{112,80},{... | collective-permute-start | bytes 884744 | tf_op jit(solution)/shard_map/ppermute | solution.py:25
  112.0 5.1 %collective-permute-start.17 = (bf16[32,2304]{1,0:T(8,128)(2,1)S(1)}, bf16[32,2304]{1,0:T(8,128)(2,1)S(1)}, u32[]{:S(2)}, u32[]{:S(2)}) collective-permute-start(bf16[32,2304]{1,0:T(8,128)(2,1)S(1)} %get-tuple-element.127), channel_id=1, source_target_pairs={{0,16},{16,0},{32,48},{48,32},{64,80},{80,64},{96,112},{112,96},{1... | collective-permute-start | bytes 442376 | tf_op jit(solution)/shard_map/ppermute | solution.py:25
  126.7 7.0 %collective-permute-start.20 = (bf16[2,32,1664]{2,1,0:T(8,128)(2,1)S(1)}, bf16[2,32,1664]{2,1,0:T(8,128)(2,1)S(1)}, u32[]{:S(2)}, u32[]{:S(2)}) collective-permute-start(bf16[2,32,1664]{2,1,0:T(8,128)(2,1)S(1)} %pad_maximum_fusion.refs_0_), channel_id=1, source_target_pairs={{0,32},{16,48},{32,64},{48,80},{64,96},{80,112},{96,128},{112,144}... | collective-permute-start | bytes 638984 | tf_op jit(solution)/shard_map/ppermute | solution.py:25
  126.8 7.0 %collective-permute-start.21 = (bf16[2,32,1664]{2,1,0:T(8,128)(2,1)S(1)}, bf16[2,32,1664]{2,1,0:T(8,128)(2,1)S(1)}, u32[]{:S(2)}, u32[]{:S(2)}) collective-permute-start(bf16[2,32,1664]{2,1,0:T(8,128)(2,1)S(1)} %pad_maximum_fusion.refs_0_), channel_id=1, source_target_pairs={{0,224},{16,240},{32,0},{48,16},{64,32},{80,48},{96,64},{112,80},{... | collective-permute-start | bytes 638984 | tf_op jit(solution)/shard_map/ppermute | solution.py:25
  133.7 7.1 %collective-permute-start.22 = (bf16[2,32,1664]{2,1,0:T(8,128)(2,1)S(1)}, bf16[2,32,1664]{2,1,0:T(8,128)(2,1)S(1)}, u32[]{:S(2)}, u32[]{:S(2)}) collective-permute-start(bf16[2,32,1664]{2,1,0:T(8,128)(2,1)S(1)} %collective-permute-done.20.refs_6_), channel_id=1, source_target_pairs={{0,32},{16,48},{32,64},{48,80},{64,96},{80,112},{96,128},{112,144}... | collective-permute-start | bytes 638984 | tf_op jit(solution)/shard_map/ppermute | solution.py:25
  135.4 5.9 %collective-permute-start.23 = (bf16[2,32,1664]{2,1,0:T(8,128)(2,1)S(1)}, bf16[2,32,1664]{2,1,0:T(8,128)(2,1)S(1)}, u32[]{:S(2)}, u32[]{:S(2)}) collective-permute-start(bf16[2,32,1664]{2,1,0:T(8,128)(2,1)S(1)} %collective-permute-done.21.refs_1_), channel_id=1, source_target_pairs={{0,224},{16,240},{32,0},{48,16},{64,32},{80,48},{96,64},{112,80},{... | collective-permute-start | bytes 638984 | tf_op jit(solution)/shard_map/ppermute | solution.py:25
  141.3 6.7 %collective-permute-start.24 = (bf16[2,32,1664]{2,1,0:T(8,128)(2,1)S(1)}, bf16[2,32,1664]{2,1,0:T(8,128)(2,1)S(1)}, u32[]{:S(2)}, u32[]{:S(2)}) collective-permute-start(bf16[2,32,1664]{2,1,0:T(8,128)(2,1)S(1)} %collective-permute-done.22.refs_5_), channel_id=1, source_target_pairs={{0,32},{16,48},{32,64},{48,80},{64,96},{80,112},{96,128},{112,144}... | collective-permute-start | bytes 638984 | tf_op jit(solution)/shard_map/ppermute | solution.py:25
  143.3 6.4 %collective-permute-start.25 = (bf16[2,32,1664]{2,1,0:T(8,128)(2,1)S(1)}, bf16[2,32,1664]{2,1,0:T(8,128)(2,1)S(1)}, u32[]{:S(2)}, u32[]{:S(2)}) collective-permute-start(bf16[2,32,1664]{2,1,0:T(8,128)(2,1)S(1)} %collective-permute-done.23.refs_2_), channel_id=1, source_target_pairs={{0,224},{16,240},{32,0},{48,16},{64,32},{80,48},{96,64},{112,80},{... | collective-permute-start | bytes 638984 | tf_op jit(solution)/shard_map/ppermute | solution.py:25
  (16 other events, 170.8 us)

commit v2 on v1

v2 whole, which is shorter than its diff:
```python
import jax
import jax.numpy as jnp
from jax import lax
from jax.experimental import pallas as pl
from jax.experimental.pallas import tpu as pltpu
from jax.sharding import PartitionSpec as P

HEADS = 128
KV_HEADS = 8
HEAD_DIM = 128
PREFIX = 24
ROWS_DEV = 32
ZN = 8
LANE = 128
BF = jnp.bfloat16
F32 = jnp.float32
PLANE = [[2 * i + core for i in range(8)] for core in range(2)]
VMEM = pl.BlockSpec(memory_space=pltpu.VMEM)
SMEM = pl.BlockSpec(memory_space=pltpu.SMEM)
ANY = pl.BlockSpec(memory_space=pl.ANY)
HBM = pl.BlockSpec(memory_space=pltpu.HBM)
PARAMS = pltpu.CompilerParams(vmem_limit_bytes=24 * 2**20)


def permute(value, axis, target, count=16):
    return lax.ppermute(value, axis, [(i, target(i)) for i in range(count)])


def along_z(value, step):
    return permute(value, "batch", lambda i: (i + 2 * step) % 16)


def x_pair(value):
    return permute(value, "batch", lambda i: i ^ 1)


def core_pair(value):
    return permute(value, "mp", lambda i: i ^ 1)


def transpose_mesh(value):
    return lax.ppermute(
        value,
        ("batch", "mp"),
        [(b * 16 + m, m * 16 + b) for b in range(16) for m in range(16)],
    )


def over_plane(value):
    return lax.all_to_all(value, "mp", 0, 0, axis_index_groups=PLANE, tiled=True)


def together(*pairs):
    values = lax.optimization_barrier(tuple(value for value, _ in pairs))
    sent = tuple(move(value) for value, (_, move) in zip(values, pairs))
    return lax.optimization_barrier(sent)


def in_vmem(*shapes):
    made = tuple(pltpu.VMEM(shape, dtype) for shape, dtype in shapes)
    return made if len(made) > 1 else made[0]


def in_hbm(value):
    return pltpu.with_memory_space_constraint(value, pltpu.HBM)


def softmax(scores, seen):
    scores = jnp.where(seen, scores * F32(HEAD_DIM**-0.5), F32(-1e30))
    exponent = jnp.exp(scores - jnp.max(scores, axis=1, keepdims=True))
    return (exponent / jnp.sum(exponent, axis=1, keepdims=True)).astype(BF)


def scored(queries, keys):
    return lax.dot_general(queries, keys, (((1,), (1,)), ((), ())), preferred_element_type=F32)


def prepare_kernel(length_ref, question_ref, queries_ref, hidden_ref, key_ref, value_ref, out_ref, queries, hidden, pair, sems):
    width = queries.shape[1]
    heads = width // HEAD_DIM
    batch_index, mp_index = lax.axis_index("batch"), lax.axis_index("mp")
    head = pl.ds(pl.multiple_of((mp_index >> 1) * HEAD_DIM, HEAD_DIM), HEAD_DIM)
    at = pl.ds(pl.multiple_of(mp_index * width, width), width)
    copies = [
        pltpu.make_async_copy(source, target, sems.at[i])
        for i, (source, target) in enumerate(
            [
                (key_ref.at[:, head], pair.at[:, :HEAD_DIM]),
                (queries_ref, queries),
                (value_ref.at[:, head], pair.at[:, HEAD_DIM:]),
                (hidden_ref.at[:, at], hidden),
            ]
        )
    ]
    for copy in copies:
        copy.start()
    shape = (ROWS_DEV, ROWS_DEV)
    row = lax.broadcasted_iota(jnp.int32, shape, 0)
    key = lax.broadcasted_iota(jnp.int32, shape, 1)
    seen = (key <= row) & (key < length_ref[batch_index])
    seen = jnp.concatenate([seen.astype(F32)] * heads, axis=0) > 0
    shape = (16, LANE)
    option = lax.broadcasted_iota(jnp.int32, shape, 0) & (ROWS_DEV - PREFIX - 1)
    asked = jnp.zeros(shape, jnp.int32)
    for i in range(ROWS_DEV - PREFIX):
        asked = jnp.where(option == i, question_ref[i], asked)
    out_ref[32:, width:] = asked.astype(F32).astype(BF)
    out_ref[:32, width:] = jnp.zeros((ROWS_DEV, LANE), BF)
    copies[0].wait()
    copies[1].wait()
    stacked = jnp.concatenate(
        [queries[:, h * HEAD_DIM : (h + 1) * HEAD_DIM] for h in range(heads)], axis=0
    )
    attention = softmax(scored(stacked, pair[:, :HEAD_DIM]), seen)
    copies[2].wait()
    context = jnp.dot(attention, pair[:, HEAD_DIM:], preferred_element_type=F32).astype(BF)
    out_ref[32:, : 2 * HEAD_DIM] = pair[:16]
    out_ref[32:, 2 * HEAD_DIM : 4 * HEAD_DIM] = pair[16:]
    last = queries[16:].astype(F32)[PREFIX - 16 :]
    half = width // 2
    out_ref[32:, half:width] = jnp.concatenate([last[:, :half], last[:, half:]], axis=0).astype(BF)
    copies[3].wait()
    prefix = lax.broadcasted_iota(jnp.int32, (ROWS_DEV, HEAD_DIM), 0) < PREFIX
    for h in range(heads):
        columns = slice(h * HEAD_DIM, (h + 1) * HEAD_DIM)
        mine = context[h * ROWS_DEV : (h + 1) * ROWS_DEV].astype(F32)
        mine = jnp.where(prefix, mine, F32(0))
        out_ref[:32, columns] = (hidden[:, columns].astype(F32) + mine).astype(BF)


def prepare(prefix_len, question, queries, hidden_in, key_cache, value_cache):
    rows, width = queries.shape
    return pl.pallas_call(
        prepare_kernel,
        out_shape=in_vmem(((rows + 16, width + LANE), BF)),
        in_specs=[SMEM, SMEM, HBM, HBM, HBM, HBM],
        out_specs=VMEM,
        scratch_shapes=[
            pltpu.VMEM((rows, width), BF),
            pltpu.VMEM((rows, width), BF),
            pltpu.VMEM((rows, 2 * HEAD_DIM), BF),
            pltpu.SemaphoreType.DMA((4,)),
        ],
        compiler_params=PARAMS,
    )(prefix_len, question, in_hbm(queries), in_hbm(hidden_in), in_hbm(key_cache), in_hbm(value_cache))


FAR = 4


def project_kernel(tiles, early, length_ref, gain_ref, mine_ref, theirs_ref, gate_ref, up_ref, *refs):
    own_ref, give, kept, far_low, far_high = refs[0], refs[1:6], refs[6:13], refs[13], refs[14]
    residual, rows, squares, gain, sem = refs[15:]
    n = ROWS_DEV
    width = own_ref.shape[1]
    half = width // 2
    wide = 2 * tiles + 1
    batch_index, mp_index = lax.axis_index("batch"), lax.axis_index("mp")
    z, core = batch_index >> 1, mp_index & 1
    flip = (batch_index & 1) ^ core
    fetch = pltpu.make_async_copy(gain_ref.at[pl.ds(batch_index * width, width)], gain, sem)
    fetch.start()

    def put(s, j, tile, value):
        lanes = slice(tile * LANE, (tile + 1) * LANE)
        if tile < early:
            if j == 1 and s in (0, FAR):
                give[s][:, lanes] = value
            elif j == 1:
                give[min(s, ZN - s)][0 if s < FAR else 1, :, lanes] = value
            elif s == FAR:
                far_low[:, lanes] = value
            else:
                kept[s if s < FAR else s - 1][:, lanes] = value
        else:
            late = tile - early + j * (wide - early)
            if s == FAR:
                far_high[:, late * LANE : (late + 1) * LANE] = value
            else:
                late += early
                kept[s if s < FAR else s - 1][:, late * LANE : (late + 1) * LANE] = value

    blocks = [(ref, i) for ref in (mine_ref, theirs_ref) for i in range(ZN)]
    options = ROWS_DEV - PREFIX

    def gathered(lanes):
        return jnp.concatenate([ref[i, n:, lanes] for ref, i in blocks], axis=0)

    def unfolded(first):
        low, high = slice(first, first + HEAD_DIM), slice(first + 2 * HEAD_DIM, first + 3 * HEAD_DIM)
        return jnp.concatenate(
            [ref[i, n:, lanes] for ref, i in blocks for lanes in (low, high)], axis=0
        )

    keys, values = unfolded(0), unfolded(HEAD_DIM)
    shape = (16 * len(blocks), n * len(blocks))
    asked = gathered(slice(width, width + LANE)).astype(F32).astype(jnp.int32)
    asked = jnp.concatenate([asked] * (shape[1] // LANE), axis=1)
    place = lax.broadcasted_iota(jnp.int32, shape, 1)
    order = place >> 5
    row = lax.broadcasted_iota(jnp.int32, shape, 0)
    owner = ((order & (ZN - 1)) << 1) + ((order >> 3) ^ core)
    live = jnp.zeros(shape, jnp.int32)
    for i in range(len(blocks)):
        live = jnp.where(order == i, length_ref[((i & (ZN - 1)) << 1) + ((i >> 3) ^ core)], live)
    seen = (owner == asked) & ((place & (n - 1)) < live)
    seen = seen | (place == (row >> 4) * n + PREFIX + (row & (options - 1)))
    contexts = []
    for h in range(half // HEAD_DIM):
        queries = gathered(slice(half + h * HEAD_DIM, half + (h + 1) * HEAD_DIM))
        attention = softmax(scored(queries, keys), seen)
        context = jnp.dot(attention, values, preferred_element_type=F32)
        contexts.append(context.astype(BF).astype(F32))
    fetch.wait()
    scale = gain[...].reshape(1, width)
    for k, (ref, i) in enumerate(blocks):
        at = k * 16
        added = jnp.concatenate(
            [context[at : at + options] for context in contexts]
            + [context[at + options : at + 16] for context in contexts],
            axis=1,
        )
        added = jnp.concatenate([jnp.zeros((16 - options, width), F32), added], axis=0)
        first = ref[i, :16, :width]
        last = (ref[i, 16:n, :width].astype(F32) + added).astype(BF)
        if ref is mine_ref:
            residual[i, :16] = first
            residual[i, 16:] = last
        s = (i - z) & (ZN - 1)
        j = flip if ref is mine_ref else 1 - flip
        at = pl.multiple_of(s * 2 * n + j * n, n)
        for part, offset in ((first, 0), (last, 16)):
            x = part.astype(F32)
            into = pl.ds(pl.multiple_of(at + offset, 16), 16)
            rows[into, :] = (x * scale).astype(BF)
            square = x * x
            total = square[:, :LANE]
            for lane in range(1, width // LANE):
                total = total + square[:, lane * LANE : (lane + 1) * LANE]
            squares[into, :] = total.astype(BF)
    own_ref[...] = residual[mp_index >> 1]

    for first, ref, at in [
        (base + t, ref, t) for base, ref in ((0, gate_ref), (tiles, up_ref)) for t in range(0, tiles, 2)
    ] + [(wide - 1, None, 0)]:
        if ref is None:
            product = squares[...]
        else:
            lanes = slice(at * LANE, min(at + 2, tiles) * LANE)
            product = jnp.dot(rows[...], ref[:, lanes], preferred_element_type=F32).astype(BF)
        for t in range(product.shape[1] // LANE):
            for s in range(ZN):
                for j in range(2):
                    begin = (2 * s + j) * n
                    put(s, j, first + t, product[begin : begin + n, t * LANE : (t + 1) * LANE])


EARLY = 16


def project(prefix_len, norm_gain, mine, theirs, gate_weight, up_weight):
    width, hidden_width = gate_weight.shape
    tiles = hidden_width // LANE
    n = ROWS_DEV
    low = (n, EARLY * LANE)
    high = (n, 2 * (2 * tiles + 1 - EARLY) * LANE)
    whole = (n, low[1] + high[1])
    own = (n, width)
    refs = pl.pallas_call(
        lambda *refs: project_kernel(tiles, EARLY, *refs),
        out_shape=in_vmem(
            (own, BF), (low, BF), *[((2, *low), BF)] * 3, (low, BF), *[(whole, BF)] * 7, (low, BF), (high, BF)
        ),
        in_specs=[SMEM, HBM] + [VMEM] * 4,
        out_specs=(VMEM,) * 15,
        scratch_shapes=[
            pltpu.VMEM((ZN, n, width), BF),
            pltpu.VMEM((2 * ZN * n, width), BF),
            pltpu.VMEM((2 * ZN * n, LANE), BF),
            pltpu.VMEM((width,), F32),
            pltpu.SemaphoreType.DMA(()),
        ],
        compiler_params=PARAMS,
    )(prefix_len, in_hbm(norm_gain), mine, theirs, gate_weight, up_weight)
    kept = list(refs[6:13])
    return refs[0], refs[1:6], kept[:4] + [None] + kept[4:], refs[13], refs[14]


def add_first_kernel(low_ref, x_ref, out_ref):
    out_ref[...] = (low_ref[...].astype(F32) + x_ref[...].astype(F32)).astype(BF)


def add_far_kernel(mine_up, mine_down, x, up, down, out_up, out_down):
    low = x.shape[2]
    out_up[:, :low] = (
        mine_up[:, :low].astype(F32) + x[0].astype(F32) + up[...].astype(F32)
    ).astype(BF)
    out_up[:, low:] = mine_up[:, low:]
    out_down[:, :low] = (mine_down[:, :low].astype(F32) + x[1].astype(F32)).astype(BF)
    out_down[:, low:] = (mine_down[:, low:].astype(F32) + down[...].astype(F32)).astype(BF)


def add_ring_kernel(mine_up, mine_down, x, up, down, out_up, out_down):
    low = x.shape[2]
    for mine, i, come, out in ((mine_up, 0, up, out_up), (mine_down, 1, down, out_down)):
        out[:, :low] = (
            mine[:, :low].astype(F32) + x[i].astype(F32) + come[:, :low].astype(F32)
        ).astype(BF)
        out[:, low:] = (mine[:, low:].astype(F32) + come[:, low:].astype(F32)).astype(BF)


def add_last_kernel(mine, x, up, down, keep, give):
    low, wide = x.shape[1], keep.shape[1]
    keep[:, :low] = (
        mine[:, :low].astype(F32)
        + x[...].astype(F32)
        + up[:, :low].astype(F32)
        + down[:, :low].astype(F32)
    )
    keep[:, low:] = (
        mine[:, low:wide].astype(F32) + up[:, low:wide].astype(F32) + down[:, low:wide].astype(F32)
    )
    give[...] = (
        mine[:, wide:].astype(F32) + up[:, wide:].astype(F32) + down[:, wide:].astype(F32)
    ).astype(BF)


def local(kernel, shapes, *args):
    return pl.pallas_call(
        kernel,
        out_shape=in_vmem(*shapes),
        in_specs=[VMEM] * len(args),
        out_specs=(VMEM,) * len(shapes) if len(shapes) > 1 else VMEM,
        compiler_params=PARAMS,
    )(*args)


def gated_kernel(keep, x, out):
    hidden_width = out.shape[1]
    wide = keep.shape[1]
    low = wide - x.shape[1]
    late = keep[:, low:] + x[...].astype(F32)
    squares = late[:, 2 * hidden_width - low :]
    scale = lax.rsqrt(jnp.sum(squares, axis=1, keepdims=True) * F32(1 / 16384) + 1e-05)
    gate = keep[:, :hidden_width] * scale
    lift = jnp.concatenate([keep[:, hidden_width:low], late[:, : 2 * hidden_width - low]], axis=1) * scale
    out[...] = (gate / (1 + jnp.exp(-gate)) * lift).astype(BF)


def down_kernel(*refs):
    blocks, down_ref, give, keep, rows = refs[:9], refs[9], refs[10], refs[11], refs[12]
    n = ROWS_DEV
    batch_index, mp_index = lax.axis_index("batch"), lax.axis_index("mp")
    z, flip = batch_index >> 1, (batch_index ^ mp_index) & 1
    for s in range(ZN):
        for j in range(2):
            if s == FAR:
                value = blocks[7 + j][0]
            else:
                value = blocks[s if s < FAR else s - 1][j]
            target = (z + s) & (ZN - 1)
            other = (flip + j) & 1
            at = (1 - other) * ZN * n + target * n
            rows[pl.ds(pl.multiple_of(at, n), n), :] = value
    step = 2 * LANE
    for i in range(0, down_ref.shape[1], step):
        lanes = slice(i, i + step)
        product = jnp.dot(rows[...], down_ref[:, lanes], preferred_element_type=F32)
        for target in range(ZN):
            give[target, :, lanes] = product[target * n : (target + 1) * n].astype(BF)
            at = (ZN + target) * n
            keep[target, :, lanes] = product[at : at + n]


def project_down(blocks, down_weight):
    hidden_width, width = down_weight.shape
    shape = (ZN, ROWS_DEV, width)
    return pl.pallas_call(
        down_kernel,
        out_shape=in_vmem((shape, BF), (shape, F32)),
        in_specs=[VMEM] * 10,
        out_specs=(VMEM, VMEM),
        scratch_shapes=[pltpu.VMEM((2 * ZN * ROWS_DEV, hidden_width), BF)],
        compiler_params=PARAMS,
    )(*blocks, down_weight)


def add_core_kernel(keep, come, out):
    out[...] = (keep[...] + come[...].astype(F32)).astype(BF)


def finish_kernel(own, parts, out):
    total = own[...].astype(F32)
    for i in range(parts.shape[0]):
        total = total + parts[i].astype(F32)
    out[...] = total.astype(BF)


def ring(up, down, *more):
    return together(
        (up, lambda v: along_z(v, 1)), (down, lambda v: along_z(v, -1)), *more
    )


def body(
    hidden_in,
    queries,
    key_cache,
    value_cache,
    question,
    prefix_len,
    norm_gain,
    gate_weight,
    up_weight,
    down_weight,
):
    rows, width = queries.shape
    hidden_width = gate_weight.shape[1]

    sent = prepare(prefix_len, question, queries, hidden_in, key_cache, value_cache)
    came = transpose_mesh(sent)
    mine = over_plane(jnp.broadcast_to(came[None], (ZN, *came.shape)))
    theirs = core_pair(mine)
    own, give, kept, far_low, far_high = project(
        prefix_len, norm_gain, mine, theirs, gate_weight, up_weight
    )
    low, whole = far_low.shape, kept[0].shape

    (x,) = together((give[4], x_pair))
    up = local(add_first_kernel, [(low, BF)], far_low, x)
    up, down, x = ring(up, far_high, (give[3], x_pair))
    up, down = local(add_far_kernel, [(whole, BF)] * 2, kept[3], kept[5], x, up, down)
    up, down, x = ring(up, down, (give[2], x_pair))
    up, down = local(add_ring_kernel, [(whole, BF)] * 2, kept[2], kept[6], x, up, down)
    up, down, x = ring(up, down, (give[1], x_pair))
    up, down = local(add_ring_kernel, [(whole, BF)] * 2, kept[1], kept[7], x, up, down)
    up, down, x = ring(up, down, (give[0], x_pair))
    late = whole[1] - 2 * hidden_width - LANE
    keep, last = local(
        add_last_kernel,
        [((rows, 2 * hidden_width + LANE), F32), ((rows, late), BF)],
        kept[0],
        x,
        up,
        down,
    )
    hidden = local(gated_kernel, [((rows, hidden_width), BF)], keep, x_pair(last))

    pair = jnp.stack([hidden, x_pair(hidden)])
    ups, downs = [pair], [pair]
    for _ in range(3):
        up, down = ring(ups[-1], downs[-1])
        ups.append(up)
        downs.append(down)
    up, down = ring(ups[-1][:1], downs[-1][1:])
    blocks = [pair, downs[1], downs[2], downs[3], ups[3], ups[2], ups[1], up, down]
    send, keep = project_down(blocks, down_weight)
    held = local(add_core_kernel, [(keep.shape, BF)], keep, core_pair(send))
    parts = over_plane(held)
    return pl.pallas_call(
        finish_kernel,
        out_shape=jax.ShapeDtypeStruct((rows, width), BF),
        in_specs=[VMEM, VMEM],
        out_specs=VMEM,
        compiler_params=PARAMS,
    )(own, parts)


def solution(mesh):
    return jax.shard_map(
        body,
        mesh=mesh,
        in_specs=(
            P("batch", None),
            P("batch", "mp"),
            P("batch", None),
            P("batch", None),
            P("batch"),
            P(),
            P(),
            P("batch", "mp"),
            P("batch", "mp"),
            P("mp", "batch"),
        ),
        out_specs=P("mp", "batch"),
        check_vma=False,
    )
```

time: 180 us -> 158 us (0.88)
  starting transfers between devices: 45.5 us -> 32.6 us
  blocking collectives: 38.2 us -> 45.9 us
  waiting for transfers between devices: 69.2 us -> 63 us
  local copies, waits for them, and re-layouts: 8.71 us -> 3.68 us
  Pallas kernels: 17.4 us -> 12.6 us
    all_to_all x1 -> x0, waiting for transfers between devices: 10.6 us -> none  [body(): lax.all_to_all(pairs, 'batch', 0, 0, tiled=True)]
    all_to_all x1 -> x0, starting transfers between devices: 9.51 us -> none  [body(): lax.all_to_all(pairs, 'batch', 0, 0, tiled=True)]
    all_to_all x2, blocking collectives: 38.2 us -> 45.9 us  [over_plane(): lax.all_to_all(value, 'mp', 0, 0, axis_index_groups=PLANE, tiled=True)]
    unnamed x20 -> x10, local copies, waits for them, and re-layouts: 7.95 us -> 3.6 us
    pallas_call x1, Pallas kernels: 5.53 us -> 2.16 us  [project_down(): pl.pallas_call(down_kernel, out_shape=in_vmem((shape, BF), (shape, F32)),...]
    ppermute x1, waiting for transfers between devices: 2.92 us -> 5.62 us  [transpose_mesh(): lax.ppermute(value, ('batch', 'mp'), [(b * 16 + m, m * 16 + b) for b in r...]
    ppermute x28 -> x25, starting transfers between devices: 31.5 us -> 29.6 us  [permute(): return lax.ppermute(value, axis, [(i, target(i)) for i in range(count)])]
    ppermute x28 -> x25, waiting for transfers between devices: 55.7 us -> 57.4 us  [permute(): return lax.ppermute(value, axis, [(i, target(i)) for i in range(count)])]
  transfers between devices with their start and end apart: 30 -> 26, of which waited for: 22 -> 22; matrix products, arithmetic and copies ran while one was open for 0% -> 0% of each run, Pallas kernels for 0% -> 0%
where the time goes in v2:
time: 158 us
  waiting for transfers between devices  63 us (40%)
  blocking collectives  45.9 us (29%)
  starting transfers between devices  32.6 us (21%)
  Pallas kernels  12.6 us (8%)
  local copies, waits for them, and re-layouts  3.68 us (2%)
    ppermute x25, waiting for transfers between devices, permute(): return lax.ppermute(value, axis, [(i, target(i)) for i in range(count)])  57.4 us
    all_to_all x2, blocking collectives, over_plane(): lax.all_to_all(value, 'mp', 0, 0, axis_index_groups=PLANE, tiled=True)  45.9 us
    ppermute x25, starting transfers between devices, permute(): return lax.ppermute(value, axis, [(i, target(i)) for i in range(count)])  29.6 us
    pallas_call x1, Pallas kernels, project(): pl.pallas_call(lambda *refs: project_kernel(tiles, EARLY, *refs), out_sha...  6.9 us
    ppermute x1, waiting for transfers between devices, transpose_mesh(): lax.ppermute(value, ('batch', 'mp'), [(b * 16 + m, m * 16 + b) for b in r...  5.62 us
    unnamed x10, local copies, waits for them, and re-layouts  3.6 us
  transfers between devices with their start and end apart: 26, of which 22 were waited for; matrix products, arithmetic and copies ran while one was open for 0% of the time, Pallas kernels for 0%

profile of v2, /device:TPU:32, one launch (start us, length us, event | category | flops | bytes accessed | tf_op | source)
XLA Modules:
  0.0 157.9 jit_solution(14351923872922075133)
XLA Ops:
  3.6 3.0 %collective-permute-start = (bf16[48,1152]{1,0:T(8,128)(2,1)S(1)}, bf16[48,1152]{1,0:T(8,128)(2,1)S(1)}, u32[]{:S(2)}, u32[]{:S(2)}) collective-permute-start(bf16[48,1152]{1,0:T(8,128)(2,1)S(1)} %shard_map.100), channel_id=1, source_target_pairs={{0,0},{1,16},{2,32},{3,48},{4,64},{5,80},{6,96},{7,112},{8,128},{9... | collective-permute-start | bytes 331784 | tf_op jit(solution)/shard_map/ppermute | solution.py:42
  6.6 5.6 %collective-permute-done = bf16[48,1152]{1,0:T(8,128)(2,1)S(1)} collective-permute-done((bf16[48,1152]{1,0:T(8,128)(2,1)S(1)}, bf16[48,1152]{1,0:T(8,128)(2,1)S(1)}, u32[]{:S(2)}, u32[]{:S(2)}) %collective-permute-start) | collective-permute-done | bytes 110624 | tf_op jit(solution)/shard_map/ppermute | solution.py:42
  12.3 31.4 %all_to_all.10.refs_2_ = bf16[8,48,1152]{2,1,0:T(8,128)(2,1)S(1)} all-to-all(bf16[8,48,1152]{2,1,0:T(8,128)(2,1)S(1)} %broadcast_in_dim.2), channel_id=1, replica_groups={{0,2,4,6,8,10,12,14},{1,3,5,7,9,11,13,15},{16,18,20,22,24,26,28,30},{17..., dimensions={0} | all-to-all | bytes 1769472 | tf_op jit(solution)/shard_map/all_to_all | solution.py:50
  43.7 2.4 %collective-permute-done.1.refs_3_ = bf16[8,48,1152]{2,1,0:T(8,128)(2,1)S(1)} collective-permute-done((bf16[8,48,1152]{2,1,0:T(8,128)(2,1)S(1)}, bf16[8,48,1152]{2,1,0:T(8,128)(2,1)S(1)}, u32[]{:S(2)}, u32[]{:S(2)}) %collective-permute-start.1) | collective-permute-done | bytes 884768 | tf_op jit(solution)/shard_map/ppermute | solution.py:26
  48.1 6.9 %shard_map.101 = (bf16[32,1024]{1,0:T(8,128)(2,1)S(1)}, bf16[32,2048]{1,0:T(8,128)(2,1)S(1)}, bf16[2,32,2048]{2,1,0:T(8,128)(2,1)S(1)}, bf16[2,32,2048]{2,1,0:T(...) custom-call(s32[16]{0:T(128)S(1)} %copy-done.3, ...), custom_call_target="tpu_custom_call" | custom-call | tf_op jit(solution)/shard_map/pallas_call | solution.py:269
  55.0 2.6 %collective-permute-start.2 = (bf16[32,2048]{1,0:T(8,128)(2,1)S(1)}, bf16[32,2048]{1,0:T(8,128)(2,1)S(1)}, u32[]{:S(2)}, u32[]{:S(2)}) collective-permute-start(bf16[32,2048]{1,0:T(8,128)(2,1)S(1)} %get-tuple-element.79), channel_id=1, source_target_pairs={{0,16},{16,0},{32,48},{48,32},{64,80},{80,64},{96,112},{112,96},{1... | collective-permute-start | bytes 393224 | tf_op jit(solution)/shard_map/ppermute | solution.py:26
  57.6 3.8 %collective-permute-done.2.x_ref = bf16[32,2048]{1,0:T(8,128)(2,1)S(1)} collective-permute-done((bf16[32,2048]{1,0:T(8,128)(2,1)S(1)}, bf16[32,2048]{1,0:T(8,128)(2,1)S(1)}, u32[]{:S(2)}, u32[]{:S(2)}) %collective-permute-start.2) | collective-permute-done | bytes 131104 | tf_op jit(solution)/shard_map/ppermute | solution.py:26
  63.2 2.0 %collective-permute-start.3 = (bf16[32,2048]{1,0:T(8,128)(2,1)S(1)}, bf16[32,2048]{1,0:T(8,128)(2,1)S(1)}, u32[]{:S(2)}, u32[]{:S(2)}) collective-permute-start(bf16[32,2048]{1,0:T(8,128)(2,1)S(1)} %shard_map.102), channel_id=1, source_target_pairs={{0,32},{16,48},{32,64},{48,80},{64,96},{80,112},{96,128},{112,144}... | collective-permute-start | bytes 393224 | tf_op jit(solution)/shard_map/ppermute | solution.py:26
  65.3 2.9 %collective-permute-done.3.up = bf16[32,2048]{1,0:T(8,128)(2,1)S(1)} collective-permute-done((bf16[32,2048]{1,0:T(8,128)(2,1)S(1)}, bf16[32,2048]{1,0:T(8,128)(2,1)S(1)}, u32[]{:S(2)}, u32[]{:S(2)}) %collective-permute-start.3) | collective-permute-done | bytes 131104 | tf_op jit(solution)/shard_map/ppermute | solution.py:26
  73.3 4.6 %collective-permute-done.8.x = bf16[2,32,2048]{2,1,0:T(8,128)(2,1)S(1)} collective-permute-done((bf16[2,32,2048]{2,1,0:T(8,128)(2,1)S(1)}, bf16[2,32,2048]{2,1,0:T(8,128)(2,1)S(1)}, u32[]{:S(2)}, u32[]{:S(2)}) %collective-permute-start.8) | collective-permute-done | bytes 262176 | tf_op jit(solution)/shard_map/ppermute | solution.py:26
  78.1 3.0 %collective-permute-start.9 = (bf16[32,4864]{1,0:T(8,128)(2,1)S(1)}, bf16[32,4864]{1,0:T(8,128)(2,1)S(1)}, u32[]{:S(2)}, u32[]{:S(2)}) collective-permute-start(bf16[32,4864]{1,0:T(8,128)(2,1)S(1)} %get-tuple-element.100), channel_id=1, source_target_pairs={{0,32},{16,48},{32,64},{48,80},{64,96},{80,112},{96,128},{112,144}... | collective-permute-start | bytes 933896 | tf_op jit(solution)/shard_map/ppermute | solution.py:26
  83.1 4.6 %collective-permute-done.11.x = bf16[2,32,2048]{2,1,0:T(8,128)(2,1)S(1)} collective-permute-done((bf16[2,32,2048]{2,1,0:T(8,128)(2,1)S(1)}, bf16[2,32,2048]{2,1,0:T(8,128)(2,1)S(1)}, u32[]{:S(2)}, u32[]{:S(2)}) %collective-permute-start.11) | collective-permute-done | bytes 262176 | tf_op jit(solution)/shard_map/ppermute | solution.py:26
  89.2 2.1 %collective-permute-start.12 = (bf16[32,4864]{1,0:T(8,128)(2,1)S(1)}, bf16[32,4864]{1,0:T(8,128)(2,1)S(1)}, u32[]{:S(2)}, u32[]{:S(2)}) collective-permute-start(bf16[32,4864]{1,0:T(8,128)(2,1)S(1)} %get-tuple-element.109), channel_id=1, source_target_pairs={{0,32},{16,48},{32,64},{48,80},{64,96},{80,112},{96,128},{112,144}... | collective-permute-start | bytes 933896 | tf_op jit(solution)/shard_map/ppermute | solution.py:26
  93.0 3.2 %collective-permute-done.14.x = bf16[32,2048]{1,0:T(8,128)(2,1)S(1)} collective-permute-done((bf16[32,2048]{1,0:T(8,128)(2,1)S(1)}, bf16[32,2048]{1,0:T(8,128)(2,1)S(1)}, u32[]{:S(2)}, u32[]{:S(2)}) %collective-permute-start.14) | collective-permute-done | bytes 131104 | tf_op jit(solution)/shard_map/ppermute | solution.py:26
  96.3 2.7 %collective-permute-done.13.down = bf16[32,4864]{1,0:T(8,128)(2,1)S(1)} collective-permute-done((bf16[32,4864]{1,0:T(8,128)(2,1)S(1)}, bf16[32,4864]{1,0:T(8,128)(2,1)S(1)}, u32[]{:S(2)}, u32[]{:S(2)}) %collective-permute-start.13) | collective-permute-done | bytes 311328 | tf_op jit(solution)/shard_map/ppermute | solution.py:26
  100.1 3.6 %collective-permute-done.15.x = bf16[32,1408]{1,0:T(8,128)(2,1)S(1)} collective-permute-done((bf16[32,1408]{1,0:T(8,128)(2,1)S(1)}, bf16[32,1408]{1,0:T(8,128)(2,1)S(1)}, u32[]{:S(2)}, u32[]{:S(2)}) %collective-permute-start.15) | collective-permute-done | bytes 90144 | tf_op jit(solution)/shard_map/ppermute | solution.py:26
  104.9 3.8 %collective-permute-done.16 = bf16[32,1664]{1,0:T(8,128)(2,1)S(1)} collective-permute-done((bf16[32,1664]{1,0:T(8,128)(2,1)S(1)}, bf16[32,1664]{1,0:T(8,128)(2,1)S(1)}, u32[]{:S(2)}, u32[]{:S(2)}) %collective-permute-start.16) | collective-permute-done | bytes 106528 | tf_op jit(solution)/shard_map/ppermute | solution.py:26
  108.7 2.1 %collective-permute-start.17 = (bf16[2,32,1664]{2,1,0:T(8,128)(2,1)S(1)}, bf16[2,32,1664]{2,1,0:T(8,128)(2,1)S(1)}, u32[]{:S(2)}, u32[]{:S(2)}) collective-permute-start(bf16[2,32,1664]{2,1,0:T(8,128)(2,1)S(1)} %pad_maximum_fusion.refs_0_), channel_id=1, source_target_pairs={{0,32},{16,48},{32,64},{48,80},{64,96},{80,112},{96,128},{112,144}... | collective-permute-start | bytes 638984 | tf_op jit(solution)/shard_map/ppermute | solution.py:26
  110.8 5.1 %collective-permute-done.17.refs_6_ = bf16[2,32,1664]{2,1,0:T(8,128)(2,1)S(1)} collective-permute-done((bf16[2,32,1664]{2,1,0:T(8,128)(2,1)S(1)}, bf16[2,32,1664]{2,1,0:T(8,128)(2,1)S(1)}, u32[]{:S(2)}, u32[]{:S(2)}) %collective-permute-start.17) | collective-permute-done | bytes 213024 | tf_op jit(solution)/shard_map/ppermute | solution.py:26
  119.7 3.8 %collective-permute-done.19.refs_5_ = bf16[2,32,1664]{2,1,0:T(8,128)(2,1)S(1)} collective-permute-done((bf16[2,32,1664]{2,1,0:T(8,128)(2,1)S(1)}, bf16[2,32,1664]{2,1,0:T(8,128)(2,1)S(1)}, u32[]{:S(2)}, u32[]{:S(2)}) %collective-permute-start.19) | collective-permute-done | bytes 213024 | tf_op jit(solution)/shard_map/ppermute | solution.py:26
  127.6 3.8 %collective-permute-done.21.refs_4_ = bf16[2,32,1664]{2,1,0:T(8,128)(2,1)S(1)} collective-permute-done((bf16[2,32,1664]{2,1,0:T(8,128)(2,1)S(1)}, bf16[2,32,1664]{2,1,0:T(8,128)(2,1)S(1)}, u32[]{:S(2)}, u32[]{:S(2)}) %collective-permute-start.21) | collective-permute-done | bytes 213024 | tf_op jit(solution)/shard_map/ppermute | solution.py:26
  134.6 2.7 %collective-permute-done.23.refs_7_ = bf16[1,32,1664]{2,1,0:T(8,128)(2,1)S(1)} collective-permute-done((bf16[1,32,1664]{2,1,0:T(8,128)(2,1)S(1)}, bf16[1,32,1664]{2,1,0:T(8,128)(2,1)S(1)}, u32[]{:S(2)}, u32[]{:S(2)}) %collective-permute-start.23) | collective-permute-done | bytes 106528 | tf_op jit(solution)/shard_map/ppermute | solution.py:26
  138.4 2.2 %shard_map.108 = (bf16[8,32,1024]{2,1,0:T(8,128)(2,1)S(1)}, f32[8,32,1024]{2,1,0:T(8,128)S(1)}) custom-call(bf16[2,32,1664]{2,1,0:T(8,128)(2,1)S(1)} %pad_maximum_fusion.refs_0_, bf16[2,32,1664]{2,1,0:T(8,128)(2,1)S(1)} %collective-permute-done.18.refs_1_, bf16[2,32,1664]{2,1,0:T(8,128)(2,1)S(1)} %collective-permute-done.20.refs_2_, ...), custom_call_target="tpu_custom_call" | custom-call | tf_op jit(solution)/shard_map/pallas_call | solution.py:378
  142.7 14.5 %all_to_all.11.parts = bf16[8,32,1024]{2,1,0:T(8,128)(2,1)S(1)} all-to-all(bf16[8,32,1024]{2,1,0:T(8,128)(2,1)S(1)} %shard_map.109), channel_id=1, replica_groups={{0,2,4,6,8,10,12,14},{1,3,5,7,9,11,13,15},{16,18,20,22,24,26,28,30},{17..., dimensions={0} | all-to-all | bytes 1048576 | tf_op jit(solution)/shard_map/all_to_all | solution.py:50
  (55 shorter events, 35.2 us)
Async XLA Ops:
  3.6 8.7 %collective-permute-start = (bf16[48,1152]{1,0:T(8,128)(2,1)S(1)}, bf16[48,1152]{1,0:T(8,128)(2,1)S(1)}, u32[]{:S(2)}, u32[]{:S(2)}) collective-permute-start(bf16[48,1152]{1,0:T(8,128)(2,1)S(1)} %shard_map.100), channel_id=1, source_target_pairs={{0,0},{1,16},{2,32},{3,48},{4,64},{5,80},{6,96},{7,112},{8,128},{9... | collective-permute-start | bytes 331784 | tf_op jit(solution)/shard_map/ppermute | solution.py:42
  55.0 6.3 %collective-permute-start.2 = (bf16[32,2048]{1,0:T(8,128)(2,1)S(1)}, bf16[32,2048]{1,0:T(8,128)(2,1)S(1)}, u32[]{:S(2)}, u32[]{:S(2)}) collective-permute-start(bf16[32,2048]{1,0:T(8,128)(2,1)S(1)} %get-tuple-element.79), channel_id=1, source_target_pairs={{0,16},{16,0},{32,48},{48,32},{64,80},{80,64},{96,112},{112,96},{1... | collective-permute-start | bytes 393224 | tf_op jit(solution)/shard_map/ppermute | solution.py:26
  61.4 7.9 %collective-permute-start.5 = (bf16[2,32,2048]{2,1,0:T(8,128)(2,1)S(1)}, bf16[2,32,2048]{2,1,0:T(8,128)(2,1)S(1)}, u32[]{:S(2)}, u32[]{:S(2)}) collective-permute-start(bf16[2,32,2048]{2,1,0:T(8,128)(2,1)S(1)} %get-tuple-element.84), channel_id=1, source_target_pairs={{0,16},{16,0},{32,48},{48,32},{64,80},{80,64},{96,112},{112,96},{1... | collective-permute-start | bytes 786440 | tf_op jit(solution)/shard_map/ppermute | solution.py:26
  63.2 5.5 %collective-permute-start.4 = (bf16[32,2816]{1,0:T(8,128)(2,1)S(1)}, bf16[32,2816]{1,0:T(8,128)(2,1)S(1)}, u32[]{:S(2)}, u32[]{:S(2)}) collective-permute-start(bf16[32,2816]{1,0:T(8,128)(2,1)S(1)} %get-tuple-element.83), channel_id=1, source_target_pairs={{0,224},{16,240},{32,0},{48,16},{64,32},{80,48},{96,64},{112,80},{... | collective-permute-start | bytes 540680 | tf_op jit(solution)/shard_map/ppermute | solution.py:26
  63.2 5.0 %collective-permute-start.3 = (bf16[32,2048]{1,0:T(8,128)(2,1)S(1)}, bf16[32,2048]{1,0:T(8,128)(2,1)S(1)}, u32[]{:S(2)}, u32[]{:S(2)}) collective-permute-start(bf16[32,2048]{1,0:T(8,128)(2,1)S(1)} %shard_map.102), channel_id=1, source_target_pairs={{0,32},{16,48},{32,64},{48,80},{64,96},{80,112},{96,128},{112,144}... | collective-permute-start | bytes 393224 | tf_op jit(solution)/shard_map/ppermute | solution.py:26
  69.4 8.5 %collective-permute-start.6 = (bf16[32,4864]{1,0:T(8,128)(2,1)S(1)}, bf16[32,4864]{1,0:T(8,128)(2,1)S(1)}, u32[]{:S(2)}, u32[]{:S(2)}) collective-permute-start(bf16[32,4864]{1,0:T(8,128)(2,1)S(1)} %get-tuple-element.91), channel_id=1, source_target_pairs={{0,32},{16,48},{32,64},{48,80},{64,96},{80,112},{96,128},{112,144}... | collective-permute-start | bytes 933896 | tf_op jit(solution)/shard_map/ppermute | solution.py:26
  70.4 7.5 %collective-permute-start.7 = (bf16[32,4864]{1,0:T(8,128)(2,1)S(1)}, bf16[32,4864]{1,0:T(8,128)(2,1)S(1)}, u32[]{:S(2)}, u32[]{:S(2)}) collective-permute-start(bf16[32,4864]{1,0:T(8,128)(2,1)S(1)} %get-tuple-element.92), channel_id=1, source_target_pairs={{0,224},{16,240},{32,0},{48,16},{64,32},{80,48},{96,64},{112,80},{... | collective-permute-start | bytes 933896 | tf_op jit(solution)/shard_map/ppermute | solution.py:26
  71.5 6.4 %collective-permute-start.8 = (bf16[2,32,2048]{2,1,0:T(8,128)(2,1)S(1)}, bf16[2,32,2048]{2,1,0:T(8,128)(2,1)S(1)}, u32[]{:S(2)}, u32[]{:S(2)}) collective-permute-start(bf16[2,32,2048]{2,1,0:T(8,128)(2,1)S(1)} %get-tuple-element.93), channel_id=1, source_target_pairs={{0,16},{16,0},{32,48},{48,32},{64,80},{80,64},{96,112},{112,96},{1... | collective-permute-start | bytes 786440 | tf_op jit(solution)/shard_map/ppermute | solution.py:26
  78.1 9.7 %collective-permute-start.9 = (bf16[32,4864]{1,0:T(8,128)(2,1)S(1)}, bf16[32,4864]{1,0:T(8,128)(2,1)S(1)}, u32[]{:S(2)}, u32[]{:S(2)}) collective-permute-start(bf16[32,4864]{1,0:T(8,128)(2,1)S(1)} %get-tuple-element.100), channel_id=1, source_target_pairs={{0,32},{16,48},{32,64},{48,80},{64,96},{80,112},{96,128},{112,144}... | collective-permute-start | bytes 933896 | tf_op jit(solution)/shard_map/ppermute | solution.py:26
  81.1 7.8 %collective-permute-start.10 = (bf16[32,4864]{1,0:T(8,128)(2,1)S(1)}, bf16[32,4864]{1,0:T(8,128)(2,1)S(1)}, u32[]{:S(2)}, u32[]{:S(2)}) collective-permute-start(bf16[32,4864]{1,0:T(8,128)(2,1)S(1)} %get-tuple-element.101), channel_id=1, source_target_pairs={{0,224},{16,240},{32,0},{48,16},{64,32},{80,48},{96,64},{112,80},{... | collective-permute-start | bytes 933896 | tf_op jit(solution)/shard_map/ppermute | solution.py:26
  81.4 6.4 %collective-permute-start.11 = (bf16[2,32,2048]{2,1,0:T(8,128)(2,1)S(1)}, bf16[2,32,2048]{2,1,0:T(8,128)(2,1)S(1)}, u32[]{:S(2)}, u32[]{:S(2)}) collective-permute-start(bf16[2,32,2048]{2,1,0:T(8,128)(2,1)S(1)} %get-tuple-element.102), channel_id=1, source_target_pairs={{0,16},{16,0},{32,48},{48,32},{64,80},{80,64},{96,112},{112,96},{1... | collective-permute-start | bytes 786440 | tf_op jit(solution)/shard_map/ppermute | solution.py:26
  89.2 7.1 %collective-permute-start.12 = (bf16[32,4864]{1,0:T(8,128)(2,1)S(1)}, bf16[32,4864]{1,0:T(8,128)(2,1)S(1)}, u32[]{:S(2)}, u32[]{:S(2)}) collective-permute-start(bf16[32,4864]{1,0:T(8,128)(2,1)S(1)} %get-tuple-element.109), channel_id=1, source_target_pairs={{0,32},{16,48},{32,64},{48,80},{64,96},{80,112},{96,128},{112,144}... | collective-permute-start | bytes 933896 | tf_op jit(solution)/shard_map/ppermute | solution.py:26
  91.3 7.7 %collective-permute-start.13 = (bf16[32,4864]{1,0:T(8,128)(2,1)S(1)}, bf16[32,4864]{1,0:T(8,128)(2,1)S(1)}, u32[]{:S(2)}, u32[]{:S(2)}) collective-permute-start(bf16[32,4864]{1,0:T(8,128)(2,1)S(1)} %get-tuple-element.110), channel_id=1, source_target_pairs={{0,224},{16,240},{32,0},{48,16},{64,32},{80,48},{96,64},{112,80},{... | collective-permute-start | bytes 933896 | tf_op jit(solution)/shard_map/ppermute | solution.py:26
  91.3 5.0 %collective-permute-start.14 = (bf16[32,2048]{1,0:T(8,128)(2,1)S(1)}, bf16[32,2048]{1,0:T(8,128)(2,1)S(1)}, u32[]{:S(2)}, u32[]{:S(2)}) collective-permute-start(bf16[32,2048]{1,0:T(8,128)(2,1)S(1)} %get-tuple-element.111), channel_id=1, source_target_pairs={{0,16},{16,0},{32,48},{48,32},{64,80},{80,64},{96,112},{112,96},{1... | collective-permute-start | bytes 393224 | tf_op jit(solution)/shard_map/ppermute | solution.py:26
  99.1 4.6 %collective-permute-start.15 = (bf16[32,1408]{1,0:T(8,128)(2,1)S(1)}, bf16[32,1408]{1,0:T(8,128)(2,1)S(1)}, u32[]{:S(2)}, u32[]{:S(2)}) collective-permute-start(bf16[32,1408]{1,0:T(8,128)(2,1)S(1)} %get-tuple-element.116), channel_id=1, source_target_pairs={{0,16},{16,0},{32,48},{48,32},{64,80},{80,64},{96,112},{112,96},{1... | collective-permute-start | bytes 270344 | tf_op jit(solution)/shard_map/ppermute | solution.py:26
  103.9 4.8 %collective-permute-start.16 = (bf16[32,1664]{1,0:T(8,128)(2,1)S(1)}, bf16[32,1664]{1,0:T(8,128)(2,1)S(1)}, u32[]{:S(2)}, u32[]{:S(2)}) collective-permute-start(bf16[32,1664]{1,0:T(8,128)(2,1)S(1)} %shard_map.107), channel_id=1, source_target_pairs={{0,16},{16,0},{32,48},{48,32},{64,80},{80,64},{96,112},{112,96},{1... | collective-permute-start | bytes 319496 | tf_op jit(solution)/shard_map/ppermute | solution.py:26
  108.7 7.2 %collective-permute-start.17 = (bf16[2,32,1664]{2,1,0:T(8,128)(2,1)S(1)}, bf16[2,32,1664]{2,1,0:T(8,128)(2,1)S(1)}, u32[]{:S(2)}, u32[]{:S(2)}) collective-permute-start(bf16[2,32,1664]{2,1,0:T(8,128)(2,1)S(1)} %pad_maximum_fusion.refs_0_), channel_id=1, source_target_pairs={{0,32},{16,48},{32,64},{48,80},{64,96},{80,112},{96,128},{112,144}... | collective-permute-start | bytes 638984 | tf_op jit(solution)/shard_map/ppermute | solution.py:26
  110.8 6.9 %collective-permute-start.18 = (bf16[2,32,1664]{2,1,0:T(8,128)(2,1)S(1)}, bf16[2,32,1664]{2,1,0:T(8,128)(2,1)S(1)}, u32[]{:S(2)}, u32[]{:S(2)}) collective-permute-start(bf16[2,32,1664]{2,1,0:T(8,128)(2,1)S(1)} %pad_maximum_fusion.refs_0_), channel_id=1, source_target_pairs={{0,224},{16,240},{32,0},{48,16},{64,32},{80,48},{96,64},{112,80},{... | collective-permute-start | bytes 638984 | tf_op jit(solution)/shard_map/ppermute | solution.py:26
  117.7 5.8 %collective-permute-start.19 = (bf16[2,32,1664]{2,1,0:T(8,128)(2,1)S(1)}, bf16[2,32,1664]{2,1,0:T(8,128)(2,1)S(1)}, u32[]{:S(2)}, u32[]{:S(2)}) collective-permute-start(bf16[2,32,1664]{2,1,0:T(8,128)(2,1)S(1)} %collective-permute-done.17.refs_6_), channel_id=1, source_target_pairs={{0,32},{16,48},{32,64},{48,80},{64,96},{80,112},{96,128},{112,144}... | collective-permute-start | bytes 638984 | tf_op jit(solution)/shard_map/ppermute | solution.py:26
  119.4 6.2 %collective-permute-start.20 = (bf16[2,32,1664]{2,1,0:T(8,128)(2,1)S(1)}, bf16[2,32,1664]{2,1,0:T(8,128)(2,1)S(1)}, u32[]{:S(2)}, u32[]{:S(2)}) collective-permute-start(bf16[2,32,1664]{2,1,0:T(8,128)(2,1)S(1)} %collective-permute-done.18.refs_1_), channel_id=1, source_target_pairs={{0,224},{16,240},{32,0},{48,16},{64,32},{80,48},{96,64},{112,80},{... | collective-permute-start | bytes 638984 | tf_op jit(solution)/shard_map/ppermute | solution.py:26
  125.5 5.8 %collective-permute-start.21 = (bf16[2,32,1664]{2,1,0:T(8,128)(2,1)S(1)}, bf16[2,32,1664]{2,1,0:T(8,128)(2,1)S(1)}, u32[]{:S(2)}, u32[]{:S(2)}) collective-permute-start(bf16[2,32,1664]{2,1,0:T(8,128)(2,1)S(1)} %collective-permute-done.19.refs_5_), channel_id=1, source_target_pairs={{0,32},{16,48},{32,64},{48,80},{64,96},{80,112},{96,128},{112,144}... | collective-permute-start | bytes 638984 | tf_op jit(solution)/shard_map/ppermute | solution.py:26
  126.7 5.8 %collective-permute-start.22 = (bf16[2,32,1664]{2,1,0:T(8,128)(2,1)S(1)}, bf16[2,32,1664]{2,1,0:T(8,128)(2,1)S(1)}, u32[]{:S(2)}, u32[]{:S(2)}) collective-permute-start(bf16[2,32,1664]{2,1,0:T(8,128)(2,1)S(1)} %collective-permute-done.20.refs_2_), channel_id=1, source_target_pairs={{0,224},{16,240},{32,0},{48,16},{64,32},{80,48},{96,64},{112,80},{... | collective-permute-start | bytes 638984 | tf_op jit(solution)/shard_map/ppermute | solution.py:26
  132.5 4.8 %collective-permute-start.23 = (bf16[1,32,1664]{2,1,0:T(8,128)(2,1)S(1)}, bf16[1,32,1664]{2,1,0:T(8,128)(2,1)S(1)}, u32[]{:S(2)}, u32[]{:S(2)}) collective-permute-start(bf16[1,32,1664]{2,1,0:T(8,128)(2,1)S(1)} %slice.6), channel_id=1, source_target_pairs={{0,32},{16,48},{32,64},{48,80},{64,96},{80,112},{96,128},{112,144}... | collective-permute-start | bytes 319496 | tf_op jit(solution)/shard_map/ppermute | solution.py:26
  133.7 4.7 %collective-permute-start.24 = (bf16[1,32,1664]{2,1,0:T(8,128)(2,1)S(1)}, bf16[1,32,1664]{2,1,0:T(8,128)(2,1)S(1)}, u32[]{:S(2)}, u32[]{:S(2)}) collective-permute-start(bf16[1,32,1664]{2,1,0:T(8,128)(2,1)S(1)} %slice.7), channel_id=1, source_target_pairs={{0,224},{16,240},{32,0},{48,16},{64,32},{80,48},{96,64},{112,80},{... | collective-permute-start | bytes 319496 | tf_op jit(solution)/shard_map/ppermute | solution.py:26
  (7 other events, 131.2 us)

commit v3 on v2

--- a/solution.py
+++ b/solution.py
@@ -19,7 +19,7 @@
 SMEM = pl.BlockSpec(memory_space=pltpu.SMEM)
 ANY = pl.BlockSpec(memory_space=pl.ANY)
 HBM = pl.BlockSpec(memory_space=pltpu.HBM)
-PARAMS = pltpu.CompilerParams(vmem_limit_bytes=24 * 2**20)
+PARAMS = pltpu.CompilerParams(vmem_limit_bytes=28 * 2**20)
 
 
 def permute(value, axis, target, count=16):
@@ -50,12 +50,6 @@
     return lax.all_to_all(value, "mp", 0, 0, axis_index_groups=PLANE, tiled=True)
 
 
-def together(*pairs):
-    values = lax.optimization_barrier(tuple(value for value, _ in pairs))
-    sent = tuple(move(value) for value, (_, move) in zip(values, pairs))
-    return lax.optimization_barrier(sent)
-
-
 def in_vmem(*shapes):
     made = tuple(pltpu.VMEM(shape, dtype) for shape, dtype in shapes)
     return made if len(made) > 1 else made[0]
@@ -75,7 +69,7 @@
     return lax.dot_general(queries, keys, (((1,), (1,)), ((), ())), preferred_element_type=F32)
 
 
-def prepare_kernel(length_ref, question_ref, queries_ref, hidden_ref, key_ref, value_ref, out_ref, queries, hidden, pair, sems):
+def prepare_kernel(lengths, questions, queries_ref, hidden_ref, key_ref, value_ref, out_ref, queries, hidden, pair, length_ref, question_ref, sems):
     width = queries.shape[1]
     heads = width // HEAD_DIM
     batch_index, mp_index = lax.axis_index("batch"), lax.axis_index("mp")
@@ -89,11 +83,15 @@
                 (queries_ref, queries),
                 (value_ref.at[:, head], pair.at[:, HEAD_DIM:]),
                 (hidden_ref.at[:, at], hidden),
+                (lengths, length_ref),
+                (questions, question_ref),
             ]
         )
     ]
     for copy in copies:
         copy.start()
+    copies[4].wait()
+    copies[5].wait()
     shape = (ROWS_DEV, ROWS_DEV)
     row = lax.broadcasted_iota(jnp.int32, shape, 0)
     key = lax.broadcasted_iota(jnp.int32, shape, 1)
@@ -133,24 +131,26 @@
     return pl.pallas_call(
         prepare_kernel,
         out_shape=in_vmem(((rows + 16, width + LANE), BF)),
-        in_specs=[SMEM, SMEM, HBM, HBM, HBM, HBM],
+        in_specs=[HBM] * 6,
         out_specs=VMEM,
         scratch_shapes=[
             pltpu.VMEM((rows, width), BF),
             pltpu.VMEM((rows, width), BF),
             pltpu.VMEM((rows, 2 * HEAD_DIM), BF),
-            pltpu.SemaphoreType.DMA((4,)),
+            pltpu.SMEM(prefix_len.shape, jnp.int32),
+            pltpu.SMEM(question.shape, jnp.int32),
+            pltpu.SemaphoreType.DMA((6,)),
         ],
         compiler_params=PARAMS,
-    )(prefix_len, question, in_hbm(queries), in_hbm(hidden_in), in_hbm(key_cache), in_hbm(value_cache))
+    )(*map(in_hbm, (prefix_len, question, queries, hidden_in, key_cache, value_cache)))
 
 
 FAR = 4
 
 
-def project_kernel(tiles, early, length_ref, gain_ref, mine_ref, theirs_ref, gate_ref, up_ref, *refs):
+def project_kernel(tiles, early, length_ref, gain_ref, mine_ref, theirs_ref, gate_hbm, up_hbm, *refs):
     own_ref, give, kept, far_low, far_high = refs[0], refs[1:6], refs[6:13], refs[13], refs[14]
-    residual, rows, squares, gain, sem = refs[15:]
+    residual, rows, squares, gain, gate_ref, up_ref, sems = refs[15:]
     n = ROWS_DEV
     width = own_ref.shape[1]
     half = width // 2
@@ -158,8 +158,12 @@
     batch_index, mp_index = lax.axis_index("batch"), lax.axis_index("mp")
     z, core = batch_index >> 1, mp_index & 1
     flip = (batch_index & 1) ^ core
-    fetch = pltpu.make_async_copy(gain_ref.at[pl.ds(batch_index * width, width)], gain, sem)
+    fetch = pltpu.make_async_copy(gain_ref.at[pl.ds(batch_index * width, width)], gain, sems.at[0])
+    fetch_gate = pltpu.make_async_copy(gate_hbm, gate_ref, sems.at[1])
+    fetch_up = pltpu.make_async_copy(up_hbm, up_ref, sems.at[2])
     fetch.start()
+    fetch_gate.start()
+    fetch_up.start()
 
     def put(s, j, tile, value):
         lanes = slice(tile * LANE, (tile + 1) * LANE)
@@ -243,6 +247,8 @@
     for first, ref, at in [
         (base + t, ref, t) for base, ref in ((0, gate_ref), (tiles, up_ref)) for t in range(0, tiles, 2)
     ] + [(wide - 1, None, 0)]:
+        if at == 0 and ref is not None:
+            (fetch_gate if ref is gate_ref else fetch_up).wait()
         if ref is None:
             product = squares[...]
         else:
@@ -255,7 +261,7 @@
                     put(s, j, first + t, product[begin : begin + n, t * LANE : (t + 1) * LANE])
 
 
-EARLY = 16
+EARLY = 22
 
 
 def project(prefix_len, norm_gain, mine, theirs, gate_weight, up_weight):
@@ -271,17 +277,19 @@
         out_shape=in_vmem(
             (own, BF), (low, BF), *[((2, *low), BF)] * 3, (low, BF), *[(whole, BF)] * 7, (low, BF), (high, BF)
         ),
-        in_specs=[SMEM, HBM] + [VMEM] * 4,
+        in_specs=[SMEM, HBM, VMEM, VMEM, HBM, HBM],
         out_specs=(VMEM,) * 15,
         scratch_shapes=[
             pltpu.VMEM((ZN, n, width), BF),
             pltpu.VMEM((2 * ZN * n, width), BF),
             pltpu.VMEM((2 * ZN * n, LANE), BF),
             pltpu.VMEM((width,), F32),
-            pltpu.SemaphoreType.DMA(()),
+            pltpu.VMEM(gate_weight.shape, BF),
+            pltpu.VMEM(up_weight.shape, BF),
+            pltpu.SemaphoreType.DMA((3,)),
         ],
         compiler_params=PARAMS,
-    )(prefix_len, in_hbm(norm_gain), mine, theirs, gate_weight, up_weight)
+    )(prefix_len, in_hbm(norm_gain), mine, theirs, in_hbm(gate_weight), in_hbm(up_weight))
     kept = list(refs[6:13])
     return refs[0], refs[1:6], kept[:4] + [None] + kept[4:], refs[13], refs[14]
 
@@ -348,20 +356,23 @@
 
 
 def down_kernel(*refs):
-    blocks, down_ref, give, keep, rows = refs[:9], refs[9], refs[10], refs[11], refs[12]
+    own, up1, down1, up2, down2, up3, down3, up4, down4, x0, x1, x2, x3, x4, down_ref = refs[:15]
+    give, keep, rows = refs[15:]
     n = ROWS_DEV
     batch_index, mp_index = lax.axis_index("batch"), lax.axis_index("mp")
     z, flip = batch_index >> 1, (batch_index ^ mp_index) & 1
+    ours = {0: own, 1: down1, 2: down2, 3: down3, 5: up3, 6: up2, 7: up1}
+    partners = {0: x0, 7: x1.at[0], 1: x1.at[1], 6: x2.at[0], 2: x2.at[1], 5: x3.at[0], 3: x3.at[1], FAR: x4}
     for s in range(ZN):
-        for j in range(2):
-            if s == FAR:
-                value = blocks[7 + j][0]
-            else:
-                value = blocks[s if s < FAR else s - 1][j]
+        for j, found in enumerate((ours, partners)):
             target = (z + s) & (ZN - 1)
             other = (flip + j) & 1
-            at = (1 - other) * ZN * n + target * n
-            rows[pl.ds(pl.multiple_of(at, n), n), :] = value
+            at = pl.ds(pl.multiple_of((1 - other) * ZN * n + target * n, n), n)
+            if s in found:
+                rows[at, :] = found[s][...]
+            else:
+                rows[at, : up4.shape[1]] = up4[...]
+                rows[at, up4.shape[1] :] = down4[...]
     step = 2 * LANE
     for i in range(0, down_ref.shape[1], step):
         lanes = slice(i, i + step)
@@ -378,7 +389,7 @@
     return pl.pallas_call(
         down_kernel,
         out_shape=in_vmem((shape, BF), (shape, F32)),
-        in_specs=[VMEM] * 10,
+        in_specs=[VMEM] * (len(blocks) + 1),
         out_specs=(VMEM, VMEM),
         scratch_shapes=[pltpu.VMEM((2 * ZN * ROWS_DEV, hidden_width), BF)],
         compiler_params=PARAMS,
@@ -396,10 +407,8 @@
     out[...] = total.astype(BF)
 
 
-def ring(up, down, *more):
-    return together(
-        (up, lambda v: along_z(v, 1)), (down, lambda v: along_z(v, -1)), *more
-    )
+def after(*values):
+    return lax.optimization_barrier(values)
 
 
 def body(
@@ -426,15 +435,22 @@
     )
     low, whole = far_low.shape, kept[0].shape
 
-    (x,) = together((give[4], x_pair))
-    up = local(add_first_kernel, [(low, BF)], far_low, x)
-    up, down, x = ring(up, far_high, (give[3], x_pair))
+    far, ahead = after(give[4], give[3])
+    far, x = x_pair(far), x_pair(ahead)
+    up, down, ahead = after(local(add_first_kernel, [(low, BF)], far_low, far), far_high, give[2])
+    up, down, following = along_z(up, 1), along_z(down, -1), x_pair(ahead)
+    up, down, x = after(up, down, x)
     up, down = local(add_far_kernel, [(whole, BF)] * 2, kept[3], kept[5], x, up, down)
-    up, down, x = ring(up, down, (give[2], x_pair))
-    up, down = local(add_ring_kernel, [(whole, BF)] * 2, kept[2], kept[6], x, up, down)
-    up, down, x = ring(up, down, (give[1], x_pair))
-    up, down = local(add_ring_kernel, [(whole, BF)] * 2, kept[1], kept[7], x, up, down)
-    up, down, x = ring(up, down, (give[0], x_pair))
+    for step in (2, 1):
+        up, down, ahead = after(up, down, give[step - 1])
+        x = following
+        up, down, following = along_z(up, 1), along_z(down, -1), x_pair(ahead)
+        up, down, x = after(up, down, x)
+        up, down = local(
+            add_ring_kernel, [(whole, BF)] * 2, kept[step], kept[ZN - step], x, up, down
+        )
+    up, down = after(up, down)
+    up, down, x = after(along_z(up, 1), along_z(down, -1), following)
     late = whole[1] - 2 * hidden_width - LANE
     keep, last = local(
         add_last_kernel,
@@ -446,14 +462,21 @@
     )
     hidden = local(gated_kernel, [((rows, hidden_width), BF)], keep, x_pair(last))
 
-    pair = jnp.stack([hidden, x_pair(hidden)])
-    ups, downs = [pair], [pair]
-    for _ in range(3):
-        up, down = ring(ups[-1], downs[-1])
-        ups.append(up)
-        downs.append(down)
-    up, down = ring(ups[-1][:1], downs[-1][1:])
-    blocks = [pair, downs[1], downs[2], downs[3], ups[3], ups[2], ups[1], up, down]
+    up, down, across = hidden, hidden, hidden
+    blocks, partners = [hidden], []
+    for step in range(3):
+        up, down, across = after(up, down, across)
+        up, down, came = along_z(up, 1), along_z(down, -1), x_pair(across)
+        up, down = after(up, down)
+        partners.append(came)
+        blocks += [up, down]
+        across = jnp.stack([up, down])
+    half = (hidden_width // LANE + 1) // 2 * LANE
+    up, down, across = after(up[:, :half], down[:, half:], across)
+    up, down, came = along_z(up, 1), along_z(down, -1), x_pair(across)
+    up, down = after(up, down)
+    partners += [came, x_pair(jnp.concatenate([up, down], axis=1))]
+    blocks += [up, down, *partners]
     send, keep = project_down(blocks, down_weight)
     held = local(add_core_kernel, [(keep.shape, BF)], keep, core_pair(send))
     parts = over_plane(held)

time: 158 us -> 156 us (0.987)
  local copies, waits for them, and re-layouts: 3.68 us -> 0.08 us
  starting transfers between devices: 32.6 us -> 34.2 us
    unnamed x10 -> x4, local copies, waits for them, and re-layouts: 3.6 us -> 0.01 us
    ppermute x25 -> x29, starting transfers between devices: 29.6 us -> 31.2 us  [permute(): return lax.ppermute(value, axis, [(i, target(i)) for i in range(count)])]
    ppermute x25 -> x29, waiting for transfers between devices: 57.4 us -> 56.4 us  [permute(): return lax.ppermute(value, axis, [(i, target(i)) for i in range(count)])]
  transfers between devices with their start and end apart: 26 -> 30, of which waited for: 22 -> 24; matrix products, arithmetic and copies ran while one was open for 0% -> 0% of each run, Pallas kernels for 0% -> 0%
where the time goes in v3:
time: 156 us; the launch traced here: 155 us
  waiting for transfers between devices  62 us (40%)
  blocking collectives  45.9 us (29%)
  starting transfers between devices  34.2 us (22%)
  Pallas kernels  12.8 us (8%)
    ppermute x29, waiting for transfers between devices, permute(): return lax.ppermute(value, axis, [(i, target(i)) for i in range(count)])  56.4 us
    all_to_all x2, blocking collectives, over_plane(): lax.all_to_all(value, 'mp', 0, 0, axis_index_groups=PLANE, tiled=True)  45.9 us
    ppermute x29, starting transfers between devices, permute(): return lax.ppermute(value, axis, [(i, target(i)) for i in range(count)])  31.2 us
    pallas_call x1, Pallas kernels, project(): pl.pallas_call(lambda *refs: project_kernel(tiles, EARLY, *refs), out_sha...  7.61 us
    ppermute x1, waiting for transfers between devices, transpose_mesh(): lax.ppermute(value, ('batch', 'mp'), [(b * 16 + m, m * 16 + b) for b in r...  5.62 us
  transfers between devices with their start and end apart: 30, of which 24 were waited for; matrix products, arithmetic and copies ran while one was open for 0% of the time, Pallas kernels for 0%

profile of v3, /device:TPU:32, one launch (start us, length us, event | category | flops | bytes accessed | tf_op | source)
XLA Modules:
  0.0 155.3 jit_solution(3942651229013550469)
XLA Ops:
  1.4 3.0 %collective-permute-start = (bf16[48,1152]{1,0:T(8,128)(2,1)S(1)}, bf16[48,1152]{1,0:T(8,128)(2,1)S(1)}, u32[]{:S(2)}, u32[]{:S(2)}) collective-permute-start(bf16[48,1152]{1,0:T(8,128)(2,1)S(1)} %shard_map.100), channel_id=1, source_target_pairs={{0,0},{1,16},{2,32},{3,48},{4,64},{5,80},{6,96},{7,112},{8,128},{9... | collective-permute-start | bytes 331784 | tf_op jit(solution)/shard_map/ppermute | solution.py:42
  4.5 5.6 %collective-permute-done = bf16[48,1152]{1,0:T(8,128)(2,1)S(1)} collective-permute-done((bf16[48,1152]{1,0:T(8,128)(2,1)S(1)}, bf16[48,1152]{1,0:T(8,128)(2,1)S(1)}, u32[]{:S(2)}, u32[]{:S(2)}) %collective-permute-start) | collective-permute-done | bytes 110624 | tf_op jit(solution)/shard_map/ppermute | solution.py:42
  10.1 31.4 %all_to_all.10.refs_2_ = bf16[8,48,1152]{2,1,0:T(8,128)(2,1)S(1)} all-to-all(bf16[8,48,1152]{2,1,0:T(8,128)(2,1)S(1)} %broadcast_in_dim.2), channel_id=1, replica_groups={{0,2,4,6,8,10,12,14},{1,3,5,7,9,11,13,15},{16,18,20,22,24,26,28,30},{17..., dimensions={0} | all-to-all | bytes 1769472 | tf_op jit(solution)/shard_map/all_to_all | solution.py:50
  41.6 2.4 %collective-permute-done.1.refs_3_ = bf16[8,48,1152]{2,1,0:T(8,128)(2,1)S(1)} collective-permute-done((bf16[8,48,1152]{2,1,0:T(8,128)(2,1)S(1)}, bf16[8,48,1152]{2,1,0:T(8,128)(2,1)S(1)}, u32[]{:S(2)}, u32[]{:S(2)}) %collective-permute-start.1) | collective-permute-done | bytes 884768 | tf_op jit(solution)/shard_map/ppermute | solution.py:26
  44.0 7.6 %shard_map.101 = (bf16[32,1024]{1,0:T(8,128)(2,1)S(1)}, bf16[32,2816]{1,0:T(8,128)(2,1)S(1)}, bf16[2,32,2816]{2,1,0:T(8,128)(2,1)S(1)}, bf16[2,32,2816]{2,1,0:T(...) custom-call(s32[16]{0:T(128)S(1)} %copy-done.1, ...), custom_call_target="tpu_custom_call" | custom-call | tf_op jit(solution)/shard_map/pallas_call | solution.py:275
  51.6 2.5 %collective-permute-start.2 = (bf16[32,2816]{1,0:T(8,128)(2,1)S(1)}, bf16[32,2816]{1,0:T(8,128)(2,1)S(1)}, u32[]{:S(2)}, u32[]{:S(2)}) collective-permute-start(bf16[32,2816]{1,0:T(8,128)(2,1)S(1)} %get-tuple-element.84), channel_id=1, source_target_pairs={{0,16},{16,0},{32,48},{48,32},{64,80},{80,64},{96,112},{112,96},{1... | collective-permute-start | bytes 540680 | tf_op jit(solution)/shard_map/ppermute | solution.py:26
  54.3 5.2 %collective-permute-done.2.x_ref = bf16[32,2816]{1,0:T(8,128)(2,1)S(1)} collective-permute-done((bf16[32,2816]{1,0:T(8,128)(2,1)S(1)}, bf16[32,2816]{1,0:T(8,128)(2,1)S(1)}, u32[]{:S(2)}, u32[]{:S(2)}) %collective-permute-start.2) | collective-permute-done | bytes 180256 | tf_op jit(solution)/shard_map/ppermute | solution.py:26
  63.7 3.0 %collective-permute-done.4.down = bf16[32,1280]{1,0:T(8,128)(2,1)S(1)} collective-permute-done((bf16[32,1280]{1,0:T(8,128)(2,1)S(1)}, bf16[32,1280]{1,0:T(8,128)(2,1)S(1)}, u32[]{:S(2)}, u32[]{:S(2)}) %collective-permute-start.4) | collective-permute-done | bytes 81952 | tf_op jit(solution)/shard_map/ppermute | solution.py:26
  71.5 3.4 %collective-permute-done.8.x = bf16[2,32,2816]{2,1,0:T(8,128)(2,1)S(1)} collective-permute-done((bf16[2,32,2816]{2,1,0:T(8,128)(2,1)S(1)}, bf16[2,32,2816]{2,1,0:T(8,128)(2,1)S(1)}, u32[]{:S(2)}, u32[]{:S(2)}) %collective-permute-start.8) | collective-permute-done | bytes 360480 | tf_op jit(solution)/shard_map/ppermute | solution.py:26
  76.9 2.1 %collective-permute-start.9 = (bf16[32,4096]{1,0:T(8,128)(2,1)S(1)}, bf16[32,4096]{1,0:T(8,128)(2,1)S(1)}, u32[]{:S(2)}, u32[]{:S(2)}) collective-permute-start(bf16[32,4096]{1,0:T(8,128)(2,1)S(1)} %get-tuple-element.105), channel_id=1, source_target_pairs={{0,32},{16,48},{32,64},{48,80},{64,96},{80,112},{96,128},{112,144}... | collective-permute-start | bytes 786440 | tf_op jit(solution)/shard_map/ppermute | solution.py:26
  79.0 3.2 %collective-permute-done.11.x = bf16[2,32,2816]{2,1,0:T(8,128)(2,1)S(1)} collective-permute-done((bf16[2,32,2816]{2,1,0:T(8,128)(2,1)S(1)}, bf16[2,32,2816]{2,1,0:T(8,128)(2,1)S(1)}, u32[]{:S(2)}, u32[]{:S(2)}) %collective-permute-start.11) | collective-permute-done | bytes 360480 | tf_op jit(solution)/shard_map/ppermute | solution.py:26
  83.3 2.6 %collective-permute-done.10.down = bf16[32,4096]{1,0:T(8,128)(2,1)S(1)} collective-permute-done((bf16[32,4096]{1,0:T(8,128)(2,1)S(1)}, bf16[32,4096]{1,0:T(8,128)(2,1)S(1)}, u32[]{:S(2)}, u32[]{:S(2)}) %collective-permute-start.10) | collective-permute-done | bytes 262176 | tf_op jit(solution)/shard_map/ppermute | solution.py:26
  86.1 2.1 %collective-permute-start.12 = (bf16[32,4096]{1,0:T(8,128)(2,1)S(1)}, bf16[32,4096]{1,0:T(8,128)(2,1)S(1)}, u32[]{:S(2)}, u32[]{:S(2)}) collective-permute-start(bf16[32,4096]{1,0:T(8,128)(2,1)S(1)} %get-tuple-element.111), channel_id=1, source_target_pairs={{0,32},{16,48},{32,64},{48,80},{64,96},{80,112},{96,128},{112,144}... | collective-permute-start | bytes 786440 | tf_op jit(solution)/shard_map/ppermute | solution.py:26
  90.0 4.0 %collective-permute-done.14.x = bf16[32,2816]{1,0:T(8,128)(2,1)S(1)} collective-permute-done((bf16[32,2816]{1,0:T(8,128)(2,1)S(1)}, bf16[32,2816]{1,0:T(8,128)(2,1)S(1)}, u32[]{:S(2)}, u32[]{:S(2)}) %collective-permute-start.14) | collective-permute-done | bytes 180256 | tf_op jit(solution)/shard_map/ppermute | solution.py:26
  96.6 3.1 %collective-permute-done.15.x = bf16[32,640]{1,0:T(8,128)(2,1)S(1)} collective-permute-done((bf16[32,640]{1,0:T(8,128)(2,1)S(1)}, bf16[32,640]{1,0:T(8,128)(2,1)S(1)}, u32[]{:S(2)}, u32[]{:S(2)}) %collective-permute-start.15) | collective-permute-done | bytes 40992 | tf_op jit(solution)/shard_map/ppermute | solution.py:26
  99.8 2.1 %collective-permute-start.16 = (bf16[32,1664]{1,0:T(8,128)(2,1)S(1)}, bf16[32,1664]{1,0:T(8,128)(2,1)S(1)}, u32[]{:S(2)}, u32[]{:S(2)}) collective-permute-start(bf16[32,1664]{1,0:T(8,128)(2,1)S(1)} %shard_map.107.refs_0_), channel_id=1, source_target_pairs={{0,32},{16,48},{32,64},{48,80},{64,96},{80,112},{96,128},{112,144}... | collective-permute-start | bytes 319496 | tf_op jit(solution)/shard_map/ppermute | solution.py:26
  102.0 2.8 %collective-permute-done.16.refs_1_ = bf16[32,1664]{1,0:T(8,128)(2,1)S(1)} collective-permute-done((bf16[32,1664]{1,0:T(8,128)(2,1)S(1)}, bf16[32,1664]{1,0:T(8,128)(2,1)S(1)}, u32[]{:S(2)}, u32[]{:S(2)}) %collective-permute-start.16) | collective-permute-done | bytes 106528 | tf_op jit(solution)/shard_map/ppermute | solution.py:26
  104.8 2.8 %collective-permute-done.17.refs_2_ = bf16[32,1664]{1,0:T(8,128)(2,1)S(1)} collective-permute-done((bf16[32,1664]{1,0:T(8,128)(2,1)S(1)}, bf16[32,1664]{1,0:T(8,128)(2,1)S(1)}, u32[]{:S(2)}, u32[]{:S(2)}) %collective-permute-start.17) | collective-permute-done | bytes 106528 | tf_op jit(solution)/shard_map/ppermute | solution.py:26
  109.7 3.0 %collective-permute-done.18.refs_3_ = bf16[32,1664]{1,0:T(8,128)(2,1)S(1)} collective-permute-done((bf16[32,1664]{1,0:T(8,128)(2,1)S(1)}, bf16[32,1664]{1,0:T(8,128)(2,1)S(1)}, u32[]{:S(2)}, u32[]{:S(2)}) %collective-permute-start.18) | collective-permute-done | bytes 106528 | tf_op jit(solution)/shard_map/ppermute | solution.py:26
  116.2 2.7 %collective-permute-done.20.refs_5_ = bf16[32,1664]{1,0:T(8,128)(2,1)S(1)} collective-permute-done((bf16[32,1664]{1,0:T(8,128)(2,1)S(1)}, bf16[32,1664]{1,0:T(8,128)(2,1)S(1)}, u32[]{:S(2)}, u32[]{:S(2)}) %collective-permute-start.20) | collective-permute-done | bytes 106528 | tf_op jit(solution)/shard_map/ppermute | solution.py:26
  130.1 2.3 %collective-permute-done.26.refs_11_ = bf16[2,32,1664]{2,1,0:T(8,128)(2,1)S(1)} collective-permute-done((bf16[2,32,1664]{2,1,0:T(8,128)(2,1)S(1)}, bf16[2,32,1664]{2,1,0:T(8,128)(2,1)S(1)}, u32[]{:S(2)}, u32[]{:S(2)}) %collective-permute-start.26) | collective-permute-done | bytes 213024 | tf_op jit(solution)/shard_map/ppermute | solution.py:26
  132.4 3.4 %collective-permute-done.28.refs_13_ = bf16[32,1664]{1,0:T(8,128)(2,1)S(1)} collective-permute-done((bf16[32,1664]{1,0:T(8,128)(2,1)S(1)}, bf16[32,1664]{1,0:T(8,128)(2,1)S(1)}, u32[]{:S(2)}, u32[]{:S(2)}) %collective-permute-start.28) | collective-permute-done | bytes 106528 | tf_op jit(solution)/shard_map/ppermute | solution.py:26
  135.8 2.2 %shard_map.108 = (bf16[8,32,1024]{2,1,0:T(8,128)(2,1)S(1)}, f32[8,32,1024]{2,1,0:T(8,128)S(1)}) custom-call(bf16[32,1664]{1,0:T(8,128)(2,1)S(1)} %shard_map.107.refs_0_, bf16[32,1664]{1,0:T(8,128)(2,1)S(1)} %collective-permute-done.16.refs_1_, bf16[32,1664]{1,0:T(8,128)(2,1)S(1)} %collective-permute-done.17.refs_2_, ...), custom_call_target="tpu_custom_call" | custom-call | tf_op jit(solution)/shard_map/pallas_call | solution.py:389
  140.1 14.5 %all_to_all.11.parts = bf16[8,32,1024]{2,1,0:T(8,128)(2,1)S(1)} all-to-all(bf16[8,32,1024]{2,1,0:T(8,128)(2,1)S(1)} %shard_map.109), channel_id=1, replica_groups={{0,2,4,6,8,10,12,14},{1,3,5,7,9,11,13,15},{16,18,20,22,24,26,28,30},{17..., dimensions={0} | all-to-all | bytes 1048576 | tf_op jit(solution)/shard_map/all_to_all | solution.py:50
  (60 shorter events, 38.0 us)
Async XLA Ops:
  1.4 8.7 %collective-permute-start = (bf16[48,1152]{1,0:T(8,128)(2,1)S(1)}, bf16[48,1152]{1,0:T(8,128)(2,1)S(1)}, u32[]{:S(2)}, u32[]{:S(2)}) collective-permute-start(bf16[48,1152]{1,0:T(8,128)(2,1)S(1)} %shard_map.100), channel_id=1, source_target_pairs={{0,0},{1,16},{2,32},{3,48},{4,64},{5,80},{6,96},{7,112},{8,128},{9... | collective-permute-start | bytes 331784 | tf_op jit(solution)/shard_map/ppermute | solution.py:42
  51.6 7.9 %collective-permute-start.2 = (bf16[32,2816]{1,0:T(8,128)(2,1)S(1)}, bf16[32,2816]{1,0:T(8,128)(2,1)S(1)}, u32[]{:S(2)}, u32[]{:S(2)}) collective-permute-start(bf16[32,2816]{1,0:T(8,128)(2,1)S(1)} %get-tuple-element.84), channel_id=1, source_target_pairs={{0,16},{16,0},{32,48},{48,32},{64,80},{80,64},{96,112},{112,96},{1... | collective-permute-start | bytes 540680 | tf_op jit(solution)/shard_map/ppermute | solution.py:26
  54.2 13.1 %collective-permute-start.5 = (bf16[2,32,2816]{2,1,0:T(8,128)(2,1)S(1)}, bf16[2,32,2816]{2,1,0:T(8,128)(2,1)S(1)}, u32[]{:S(2)}, u32[]{:S(2)}) collective-permute-start(bf16[2,32,2816]{2,1,0:T(8,128)(2,1)S(1)} %get-tuple-element.89), channel_id=1, source_target_pairs={{0,16},{16,0},{32,48},{48,32},{64,80},{80,64},{96,112},{112,96},{1... | collective-permute-start | bytes 1081352 | tf_op jit(solution)/shard_map/ppermute | solution.py:26
  59.6 7.7 %collective-permute-start.3 = (bf16[32,2816]{1,0:T(8,128)(2,1)S(1)}, bf16[32,2816]{1,0:T(8,128)(2,1)S(1)}, u32[]{:S(2)}, u32[]{:S(2)}) collective-permute-start(bf16[32,2816]{1,0:T(8,128)(2,1)S(1)} %shard_map.102), channel_id=1, source_target_pairs={{0,32},{16,48},{32,64},{48,80},{64,96},{80,112},{96,128},{112,144}... | collective-permute-start | bytes 540680 | tf_op jit(solution)/shard_map/ppermute | solution.py:26
  61.0 14.0 %collective-permute-start.8 = (bf16[2,32,2816]{2,1,0:T(8,128)(2,1)S(1)}, bf16[2,32,2816]{2,1,0:T(8,128)(2,1)S(1)}, u32[]{:S(2)}, u32[]{:S(2)}) collective-permute-start(bf16[2,32,2816]{2,1,0:T(8,128)(2,1)S(1)} %get-tuple-element.98), channel_id=1, source_target_pairs={{0,16},{16,0},{32,48},{48,32},{64,80},{80,64},{96,112},{112,96},{1... | collective-permute-start | bytes 1081352 | tf_op jit(solution)/shard_map/ppermute | solution.py:26
  67.4 7.6 %collective-permute-start.6 = (bf16[32,4096]{1,0:T(8,128)(2,1)S(1)}, bf16[32,4096]{1,0:T(8,128)(2,1)S(1)}, u32[]{:S(2)}, u32[]{:S(2)}) collective-permute-start(bf16[32,4096]{1,0:T(8,128)(2,1)S(1)} %get-tuple-element.96), channel_id=1, source_target_pairs={{0,32},{16,48},{32,64},{48,80},{64,96},{80,112},{96,128},{112,144}... | collective-permute-start | bytes 786440 | tf_op jit(solution)/shard_map/ppermute | solution.py:26
  69.1 7.6 %collective-permute-start.7 = (bf16[32,4096]{1,0:T(8,128)(2,1)S(1)}, bf16[32,4096]{1,0:T(8,128)(2,1)S(1)}, u32[]{:S(2)}, u32[]{:S(2)}) collective-permute-start(bf16[32,4096]{1,0:T(8,128)(2,1)S(1)} %get-tuple-element.97), channel_id=1, source_target_pairs={{0,224},{16,240},{32,0},{48,16},{64,32},{80,48},{96,64},{112,80},{... | collective-permute-start | bytes 786440 | tf_op jit(solution)/shard_map/ppermute | solution.py:26
  69.5 12.7 %collective-permute-start.11 = (bf16[2,32,2816]{2,1,0:T(8,128)(2,1)S(1)}, bf16[2,32,2816]{2,1,0:T(8,128)(2,1)S(1)}, u32[]{:S(2)}, u32[]{:S(2)}) collective-permute-start(bf16[2,32,2816]{2,1,0:T(8,128)(2,1)S(1)} %get-tuple-element.107), channel_id=1, source_target_pairs={{0,16},{16,0},{32,48},{48,32},{64,80},{80,64},{96,112},{112,96},{1... | collective-permute-start | bytes 1081352 | tf_op jit(solution)/shard_map/ppermute | solution.py:26
  76.9 6.4 %collective-permute-start.9 = (bf16[32,4096]{1,0:T(8,128)(2,1)S(1)}, bf16[32,4096]{1,0:T(8,128)(2,1)S(1)}, u32[]{:S(2)}, u32[]{:S(2)}) collective-permute-start(bf16[32,4096]{1,0:T(8,128)(2,1)S(1)} %get-tuple-element.105), channel_id=1, source_target_pairs={{0,32},{16,48},{32,64},{48,80},{64,96},{80,112},{96,128},{112,144}... | collective-permute-start | bytes 786440 | tf_op jit(solution)/shard_map/ppermute | solution.py:26
  79.0 6.9 %collective-permute-start.10 = (bf16[32,4096]{1,0:T(8,128)(2,1)S(1)}, bf16[32,4096]{1,0:T(8,128)(2,1)S(1)}, u32[]{:S(2)}, u32[]{:S(2)}) collective-permute-start(bf16[32,4096]{1,0:T(8,128)(2,1)S(1)} %get-tuple-element.106), channel_id=1, source_target_pairs={{0,224},{16,240},{32,0},{48,16},{64,32},{80,48},{96,64},{112,80},{... | collective-permute-start | bytes 786440 | tf_op jit(solution)/shard_map/ppermute | solution.py:26
  86.1 7.9 %collective-permute-start.12 = (bf16[32,4096]{1,0:T(8,128)(2,1)S(1)}, bf16[32,4096]{1,0:T(8,128)(2,1)S(1)}, u32[]{:S(2)}, u32[]{:S(2)}) collective-permute-start(bf16[32,4096]{1,0:T(8,128)(2,1)S(1)} %get-tuple-element.111), channel_id=1, source_target_pairs={{0,32},{16,48},{32,64},{48,80},{64,96},{80,112},{96,128},{112,144}... | collective-permute-start | bytes 786440 | tf_op jit(solution)/shard_map/ppermute | solution.py:26
  88.2 7.3 %collective-permute-start.13 = (bf16[32,4096]{1,0:T(8,128)(2,1)S(1)}, bf16[32,4096]{1,0:T(8,128)(2,1)S(1)}, u32[]{:S(2)}, u32[]{:S(2)}) collective-permute-start(bf16[32,4096]{1,0:T(8,128)(2,1)S(1)} %get-tuple-element.112), channel_id=1, source_target_pairs={{0,224},{16,240},{32,0},{48,16},{64,32},{80,48},{96,64},{112,80},{... | collective-permute-start | bytes 786440 | tf_op jit(solution)/shard_map/ppermute | solution.py:26
  88.2 5.8 %collective-permute-start.14 = (bf16[32,2816]{1,0:T(8,128)(2,1)S(1)}, bf16[32,2816]{1,0:T(8,128)(2,1)S(1)}, u32[]{:S(2)}, u32[]{:S(2)}) collective-permute-start(bf16[32,2816]{1,0:T(8,128)(2,1)S(1)} %get-tuple-element.113), channel_id=1, source_target_pairs={{0,16},{16,0},{32,48},{48,32},{64,80},{80,64},{96,112},{112,96},{1... | collective-permute-start | bytes 540680 | tf_op jit(solution)/shard_map/ppermute | solution.py:26
  99.8 4.9 %collective-permute-start.16 = (bf16[32,1664]{1,0:T(8,128)(2,1)S(1)}, bf16[32,1664]{1,0:T(8,128)(2,1)S(1)}, u32[]{:S(2)}, u32[]{:S(2)}) collective-permute-start(bf16[32,1664]{1,0:T(8,128)(2,1)S(1)} %shard_map.107.refs_0_), channel_id=1, source_target_pairs={{0,32},{16,48},{32,64},{48,80},{64,96},{80,112},{96,128},{112,144}... | collective-permute-start | bytes 319496 | tf_op jit(solution)/shard_map/ppermute | solution.py:26
  101.9 5.6 %collective-permute-start.17 = (bf16[32,1664]{1,0:T(8,128)(2,1)S(1)}, bf16[32,1664]{1,0:T(8,128)(2,1)S(1)}, u32[]{:S(2)}, u32[]{:S(2)}) collective-permute-start(bf16[32,1664]{1,0:T(8,128)(2,1)S(1)} %shard_map.107.refs_0_), channel_id=1, source_target_pairs={{0,224},{16,240},{32,0},{48,16},{64,32},{80,48},{96,64},{112,80},{... | collective-permute-start | bytes 319496 | tf_op jit(solution)/shard_map/ppermute | solution.py:26
  107.6 5.1 %collective-permute-start.18 = (bf16[32,1664]{1,0:T(8,128)(2,1)S(1)}, bf16[32,1664]{1,0:T(8,128)(2,1)S(1)}, u32[]{:S(2)}, u32[]{:S(2)}) collective-permute-start(bf16[32,1664]{1,0:T(8,128)(2,1)S(1)} %collective-permute-done.16.refs_1_), channel_id=1, source_target_pairs={{0,32},{16,48},{32,64},{48,80},{64,96},{80,112},{96,128},{112,144}... | collective-permute-start | bytes 319496 | tf_op jit(solution)/shard_map/ppermute | solution.py:26
  109.2 4.9 %collective-permute-start.19 = (bf16[32,1664]{1,0:T(8,128)(2,1)S(1)}, bf16[32,1664]{1,0:T(8,128)(2,1)S(1)}, u32[]{:S(2)}, u32[]{:S(2)}) collective-permute-start(bf16[32,1664]{1,0:T(8,128)(2,1)S(1)} %collective-permute-done.17.refs_2_), channel_id=1, source_target_pairs={{0,224},{16,240},{32,0},{48,16},{64,32},{80,48},{96,64},{112,80},{... | collective-permute-start | bytes 319496 | tf_op jit(solution)/shard_map/ppermute | solution.py:26
  114.1 4.8 %collective-permute-start.20 = (bf16[32,1664]{1,0:T(8,128)(2,1)S(1)}, bf16[32,1664]{1,0:T(8,128)(2,1)S(1)}, u32[]{:S(2)}, u32[]{:S(2)}) collective-permute-start(bf16[32,1664]{1,0:T(8,128)(2,1)S(1)} %collective-permute-done.18.refs_3_), channel_id=1, source_target_pairs={{0,32},{16,48},{32,64},{48,80},{64,96},{80,112},{96,128},{112,144}... | collective-permute-start | bytes 319496 | tf_op jit(solution)/shard_map/ppermute | solution.py:26
  121.0 6.2 %collective-permute-start.22 = (bf16[32,896]{1,0:T(8,128)(2,1)S(1)}, bf16[32,896]{1,0:T(8,128)(2,1)S(1)}, u32[]{:S(2)}, u32[]{:S(2)}) collective-permute-start(bf16[32,896]{1,0:T(8,128)(2,1)S(1)} %slice.6), channel_id=1, source_target_pairs={{0,32},{16,48},{32,64},{48,80},{64,96},{80,112},{96,128},{112,144}... | collective-permute-start | bytes 172040 | tf_op jit(solution)/shard_map/ppermute | solution.py:26
  123.1 5.6 %collective-permute-start.24 = (bf16[32,1664]{1,0:T(8,128)(2,1)S(1)}, bf16[32,1664]{1,0:T(8,128)(2,1)S(1)}, u32[]{:S(2)}, u32[]{:S(2)}) collective-permute-start(bf16[32,1664]{1,0:T(8,128)(2,1)S(1)} %shard_map.107.refs_0_), channel_id=1, source_target_pairs={{0,16},{16,0},{32,48},{48,32},{64,80},{80,64},{96,112},{112,96},{1... | collective-permute-start | bytes 319496 | tf_op jit(solution)/shard_map/ppermute | solution.py:26
  123.7 6.4 %collective-permute-start.25 = (bf16[2,32,1664]{2,1,0:T(8,128)(2,1)S(1)}, bf16[2,32,1664]{2,1,0:T(8,128)(2,1)S(1)}, u32[]{:S(2)}, u32[]{:S(2)}) collective-permute-start(bf16[2,32,1664]{2,1,0:T(8,128)(2,1)S(1)} %pad_maximum_fusion), channel_id=1, source_target_pairs={{0,16},{16,0},{32,48},{48,32},{64,80},{80,64},{96,112},{112,96},{1... | collective-permute-start | bytes 638984 | tf_op jit(solution)/shard_map/ppermute | solution.py:26
  125.1 7.2 %collective-permute-start.26 = (bf16[2,32,1664]{2,1,0:T(8,128)(2,1)S(1)}, bf16[2,32,1664]{2,1,0:T(8,128)(2,1)S(1)}, u32[]{:S(2)}, u32[]{:S(2)}) collective-permute-start(bf16[2,32,1664]{2,1,0:T(8,128)(2,1)S(1)} %pad_maximum_fusion.1), channel_id=1, source_target_pairs={{0,16},{16,0},{32,48},{48,32},{64,80},{80,64},{96,112},{112,96},{1... | collective-permute-start | bytes 638984 | tf_op jit(solution)/shard_map/ppermute | solution.py:26
  126.6 9.2 %collective-permute-start.27 = (bf16[2,32,1664]{2,1,0:T(8,128)(2,1)S(1)}, bf16[2,32,1664]{2,1,0:T(8,128)(2,1)S(1)}, u32[]{:S(2)}, u32[]{:S(2)}) collective-permute-start(bf16[2,32,1664]{2,1,0:T(8,128)(2,1)S(1)} %pad_maximum_fusion.2), channel_id=1, source_target_pairs={{0,16},{16,0},{32,48},{48,32},{64,80},{80,64},{96,112},{112,96},{1... | collective-permute-start | bytes 638984 | tf_op jit(solution)/shard_map/ppermute | solution.py:26
  127.2 8.6 %collective-permute-start.28 = (bf16[32,1664]{1,0:T(8,128)(2,1)S(1)}, bf16[32,1664]{1,0:T(8,128)(2,1)S(1)}, u32[]{:S(2)}, u32[]{:S(2)}) collective-permute-start(bf16[32,1664]{1,0:T(8,128)(2,1)S(1)} %pad_maximum_fusion.3), channel_id=1, source_target_pairs={{0,16},{16,0},{32,48},{48,32},{64,80},{80,64},{96,112},{112,96},{1... | collective-permute-start | bytes 319496 | tf_op jit(solution)/shard_map/ppermute | solution.py:26
  (8 other events, 134.3 us)

commit v4 on v3

--- a/solution.py
+++ b/solution.py
@@ -467,14 +467,17 @@
     for step in range(3):
         up, down, across = after(up, down, across)
         up, down, came = along_z(up, 1), along_z(down, -1), x_pair(across)
-        up, down = after(up, down)
+        if partners:
+            up, down, partners[-1] = after(up, down, partners[-1])
+        else:
+            up, down = after(up, down)
         partners.append(came)
         blocks += [up, down]
         across = jnp.stack([up, down])
     half = (hidden_width // LANE + 1) // 2 * LANE
     up, down, across = after(up[:, :half], down[:, half:], across)
     up, down, came = along_z(up, 1), along_z(down, -1), x_pair(across)
-    up, down = after(up, down)
+    up, down, partners[-1] = after(up, down, partners[-1])
     partners += [came, x_pair(jnp.concatenate([up, down], axis=1))]
     blocks += [up, down, *partners]
     send, keep = project_down(blocks, down_weight)

time: 156 us -> 151 us (0.968)
  waiting for transfers between devices: 62 us -> 59.1 us
    ppermute x29, waiting for transfers between devices: 56.4 us -> 53.5 us  [permute(): return lax.ppermute(value, axis, [(i, target(i)) for i in range(count)])]
  transfers between devices with their start and end apart: 30 -> 30, of which waited for: 24 -> 22; matrix products, arithmetic and copies ran while one was open for 0% -> 0% of each run, Pallas kernels for 0% -> 0%
where the time goes in v4:
time: 151 us
  waiting for transfers between devices  59.1 us (39%)
  blocking collectives  45.9 us (30%)
  starting transfers between devices  32.7 us (22%)
  Pallas kernels  12.8 us (8%)
    ppermute x29, waiting for transfers between devices, permute(): return lax.ppermute(value, axis, [(i, target(i)) for i in range(count)])  53.5 us
    all_to_all x2, blocking collectives, over_plane(): lax.all_to_all(value, 'mp', 0, 0, axis_index_groups=PLANE, tiled=True)  45.9 us
    ppermute x29, starting transfers between devices, permute(): return lax.ppermute(value, axis, [(i, target(i)) for i in range(count)])  29.7 us
    pallas_call x1, Pallas kernels, project(): pl.pallas_call(lambda *refs: project_kernel(tiles, EARLY, *refs), out_sha...  7.61 us
    ppermute x1, waiting for transfers between devices, transpose_mesh(): lax.ppermute(value, ('batch', 'mp'), [(b * 16 + m, m * 16 + b) for b in r...  5.62 us
    ppermute x1, starting transfers between devices, transpose_mesh(): lax.ppermute(value, ('batch', 'mp'), [(b * 16 + m, m * 16 + b) for b in r...  3.03 us
  transfers between devices with their start and end apart: 30, of which 22 were waited for; matrix products, arithmetic and copies ran while one was open for 0% of the time, Pallas kernels for 0%

profile of v4, /device:TPU:32, one launch (start us, length us, event | category | flops | bytes accessed | tf_op | source)
XLA Modules:
  0.0 150.9 jit_solution(2409664170867202629)
XLA Ops:
  1.4 3.0 %collective-permute-start = (bf16[48,1152]{1,0:T(8,128)(2,1)S(1)}, bf16[48,1152]{1,0:T(8,128)(2,1)S(1)}, u32[]{:S(2)}, u32[]{:S(2)}) collective-permute-start(bf16[48,1152]{1,0:T(8,128)(2,1)S(1)} %shard_map.100), channel_id=1, source_target_pairs={{0,0},{1,16},{2,32},{3,48},{4,64},{5,80},{6,96},{7,112},{8,128},{9... | collective-permute-start | bytes 331784 | tf_op jit(solution)/shard_map/ppermute | solution.py:42
  4.5 5.6 %collective-permute-done = bf16[48,1152]{1,0:T(8,128)(2,1)S(1)} collective-permute-done((bf16[48,1152]{1,0:T(8,128)(2,1)S(1)}, bf16[48,1152]{1,0:T(8,128)(2,1)S(1)}, u32[]{:S(2)}, u32[]{:S(2)}) %collective-permute-start) | collective-permute-done | bytes 110624 | tf_op jit(solution)/shard_map/ppermute | solution.py:42
  10.1 31.4 %all_to_all.10.refs_2_ = bf16[8,48,1152]{2,1,0:T(8,128)(2,1)S(1)} all-to-all(bf16[8,48,1152]{2,1,0:T(8,128)(2,1)S(1)} %broadcast_in_dim.2), channel_id=1, replica_groups={{0,2,4,6,8,10,12,14},{1,3,5,7,9,11,13,15},{16,18,20,22,24,26,28,30},{17..., dimensions={0} | all-to-all | bytes 1769472 | tf_op jit(solution)/shard_map/all_to_all | solution.py:50
  41.6 2.4 %collective-permute-done.1.refs_3_ = bf16[8,48,1152]{2,1,0:T(8,128)(2,1)S(1)} collective-permute-done((bf16[8,48,1152]{2,1,0:T(8,128)(2,1)S(1)}, bf16[8,48,1152]{2,1,0:T(8,128)(2,1)S(1)}, u32[]{:S(2)}, u32[]{:S(2)}) %collective-permute-start.1) | collective-permute-done | bytes 884768 | tf_op jit(solution)/shard_map/ppermute | solution.py:26
  44.0 7.6 %shard_map.101 = (bf16[32,1024]{1,0:T(8,128)(2,1)S(1)}, bf16[32,2816]{1,0:T(8,128)(2,1)S(1)}, bf16[2,32,2816]{2,1,0:T(8,128)(2,1)S(1)}, bf16[2,32,2816]{2,1,0:T(...) custom-call(s32[16]{0:T(128)S(1)} %copy-done.1, ...), custom_call_target="tpu_custom_call" | custom-call | tf_op jit(solution)/shard_map/pallas_call | solution.py:275
  51.6 2.5 %collective-permute-start.2 = (bf16[32,2816]{1,0:T(8,128)(2,1)S(1)}, bf16[32,2816]{1,0:T(8,128)(2,1)S(1)}, u32[]{:S(2)}, u32[]{:S(2)}) collective-permute-start(bf16[32,2816]{1,0:T(8,128)(2,1)S(1)} %get-tuple-element.87), channel_id=1, source_target_pairs={{0,16},{16,0},{32,48},{48,32},{64,80},{80,64},{96,112},{112,96},{1... | collective-permute-start | bytes 540680 | tf_op jit(solution)/shard_map/ppermute | solution.py:26
  54.3 5.2 %collective-permute-done.2.x_ref = bf16[32,2816]{1,0:T(8,128)(2,1)S(1)} collective-permute-done((bf16[32,2816]{1,0:T(8,128)(2,1)S(1)}, bf16[32,2816]{1,0:T(8,128)(2,1)S(1)}, u32[]{:S(2)}, u32[]{:S(2)}) %collective-permute-start.2) | collective-permute-done | bytes 180256 | tf_op jit(solution)/shard_map/ppermute | solution.py:26
  63.7 3.0 %collective-permute-done.4.down = bf16[32,1280]{1,0:T(8,128)(2,1)S(1)} collective-permute-done((bf16[32,1280]{1,0:T(8,128)(2,1)S(1)}, bf16[32,1280]{1,0:T(8,128)(2,1)S(1)}, u32[]{:S(2)}, u32[]{:S(2)}) %collective-permute-start.4) | collective-permute-done | bytes 81952 | tf_op jit(solution)/shard_map/ppermute | solution.py:26
  69.5 2.1 %collective-permute-start.11 = (bf16[2,32,2816]{2,1,0:T(8,128)(2,1)S(1)}, bf16[2,32,2816]{2,1,0:T(8,128)(2,1)S(1)}, u32[]{:S(2)}, u32[]{:S(2)}) collective-permute-start(bf16[2,32,2816]{2,1,0:T(8,128)(2,1)S(1)} %get-tuple-element.110), channel_id=1, source_target_pairs={{0,16},{16,0},{32,48},{48,32},{64,80},{80,64},{96,112},{112,96},{1... | collective-permute-start | bytes 1081352 | tf_op jit(solution)/shard_map/ppermute | solution.py:26
  71.5 3.4 %collective-permute-done.8.x = bf16[2,32,2816]{2,1,0:T(8,128)(2,1)S(1)} collective-permute-done((bf16[2,32,2816]{2,1,0:T(8,128)(2,1)S(1)}, bf16[2,32,2816]{2,1,0:T(8,128)(2,1)S(1)}, u32[]{:S(2)}, u32[]{:S(2)}) %collective-permute-start.8) | collective-permute-done | bytes 360480 | tf_op jit(solution)/shard_map/ppermute | solution.py:26
  76.9 2.1 %collective-permute-start.9 = (bf16[32,4096]{1,0:T(8,128)(2,1)S(1)}, bf16[32,4096]{1,0:T(8,128)(2,1)S(1)}, u32[]{:S(2)}, u32[]{:S(2)}) collective-permute-start(bf16[32,4096]{1,0:T(8,128)(2,1)S(1)} %get-tuple-element.108), channel_id=1, source_target_pairs={{0,32},{16,48},{32,64},{48,80},{64,96},{80,112},{96,128},{112,144}... | collective-permute-start | bytes 786440 | tf_op jit(solution)/shard_map/ppermute | solution.py:26
  79.0 3.2 %collective-permute-done.11.x = bf16[2,32,2816]{2,1,0:T(8,128)(2,1)S(1)} collective-permute-done((bf16[2,32,2816]{2,1,0:T(8,128)(2,1)S(1)}, bf16[2,32,2816]{2,1,0:T(8,128)(2,1)S(1)}, u32[]{:S(2)}, u32[]{:S(2)}) %collective-permute-start.11) | collective-permute-done | bytes 360480 | tf_op jit(solution)/shard_map/ppermute | solution.py:26
  83.3 2.6 %collective-permute-done.10.down = bf16[32,4096]{1,0:T(8,128)(2,1)S(1)} collective-permute-done((bf16[32,4096]{1,0:T(8,128)(2,1)S(1)}, bf16[32,4096]{1,0:T(8,128)(2,1)S(1)}, u32[]{:S(2)}, u32[]{:S(2)}) %collective-permute-start.10) | collective-permute-done | bytes 262176 | tf_op jit(solution)/shard_map/ppermute | solution.py:26
  86.1 2.1 %collective-permute-start.12 = (bf16[32,4096]{1,0:T(8,128)(2,1)S(1)}, bf16[32,4096]{1,0:T(8,128)(2,1)S(1)}, u32[]{:S(2)}, u32[]{:S(2)}) collective-permute-start(bf16[32,4096]{1,0:T(8,128)(2,1)S(1)} %get-tuple-element.114), channel_id=1, source_target_pairs={{0,32},{16,48},{32,64},{48,80},{64,96},{80,112},{96,128},{112,144}... | collective-permute-start | bytes 786440 | tf_op jit(solution)/shard_map/ppermute | solution.py:26
  90.0 4.0 %collective-permute-done.14.x = bf16[32,2816]{1,0:T(8,128)(2,1)S(1)} collective-permute-done((bf16[32,2816]{1,0:T(8,128)(2,1)S(1)}, bf16[32,2816]{1,0:T(8,128)(2,1)S(1)}, u32[]{:S(2)}, u32[]{:S(2)}) %collective-permute-start.14) | collective-permute-done | bytes 180256 | tf_op jit(solution)/shard_map/ppermute | solution.py:26
  96.6 3.5 %collective-permute-done.15.x = bf16[32,640]{1,0:T(8,128)(2,1)S(1)} collective-permute-done((bf16[32,640]{1,0:T(8,128)(2,1)S(1)}, bf16[32,640]{1,0:T(8,128)(2,1)S(1)}, u32[]{:S(2)}, u32[]{:S(2)}) %collective-permute-start.15) | collective-permute-done | bytes 40992 | tf_op jit(solution)/shard_map/ppermute | solution.py:26
  100.2 2.1 %collective-permute-start.16 = (bf16[32,1664]{1,0:T(8,128)(2,1)S(1)}, bf16[32,1664]{1,0:T(8,128)(2,1)S(1)}, u32[]{:S(2)}, u32[]{:S(2)}) collective-permute-start(bf16[32,1664]{1,0:T(8,128)(2,1)S(1)} %shard_map.107.refs_0_), channel_id=1, source_target_pairs={{0,32},{16,48},{32,64},{48,80},{64,96},{80,112},{96,128},{112,144}... | collective-permute-start | bytes 319496 | tf_op jit(solution)/shard_map/ppermute | solution.py:26
  105.1 2.9 %collective-permute-done.17.refs_2_ = bf16[32,1664]{1,0:T(8,128)(2,1)S(1)} collective-permute-done((bf16[32,1664]{1,0:T(8,128)(2,1)S(1)}, bf16[32,1664]{1,0:T(8,128)(2,1)S(1)}, u32[]{:S(2)}, u32[]{:S(2)}) %collective-permute-start.17) | collective-permute-done | bytes 106528 | tf_op jit(solution)/shard_map/ppermute | solution.py:26
  110.7 2.2 %collective-permute-done.18.refs_3_ = bf16[32,1664]{1,0:T(8,128)(2,1)S(1)} collective-permute-done((bf16[32,1664]{1,0:T(8,128)(2,1)S(1)}, bf16[32,1664]{1,0:T(8,128)(2,1)S(1)}, u32[]{:S(2)}, u32[]{:S(2)}) %collective-permute-start.18) | collective-permute-done | bytes 106528 | tf_op jit(solution)/shard_map/ppermute | solution.py:26
  117.1 2.3 %collective-permute-done.21.refs_5_ = bf16[32,1664]{1,0:T(8,128)(2,1)S(1)} collective-permute-done((bf16[32,1664]{1,0:T(8,128)(2,1)S(1)}, bf16[32,1664]{1,0:T(8,128)(2,1)S(1)}, u32[]{:S(2)}, u32[]{:S(2)}) %collective-permute-start.21) | collective-permute-done | bytes 106528 | tf_op jit(solution)/shard_map/ppermute | solution.py:26
  123.7 2.9 %collective-permute-done.25.refs_8_ = bf16[32,768]{1,0:T(8,128)(2,1)S(1)} collective-permute-done((bf16[32,768]{1,0:T(8,128)(2,1)S(1)}, bf16[32,768]{1,0:T(8,128)(2,1)S(1)}, u32[]{:S(2)}, u32[]{:S(2)}) %collective-permute-start.25) | collective-permute-done | bytes 49184 | tf_op jit(solution)/shard_map/ppermute | solution.py:26
  127.3 4.1 %collective-permute-done.28.refs_13_ = bf16[32,1664]{1,0:T(8,128)(2,1)S(1)} collective-permute-done((bf16[32,1664]{1,0:T(8,128)(2,1)S(1)}, bf16[32,1664]{1,0:T(8,128)(2,1)S(1)}, u32[]{:S(2)}, u32[]{:S(2)}) %collective-permute-start.28) | collective-permute-done | bytes 106528 | tf_op jit(solution)/shard_map/ppermute | solution.py:26
  131.4 2.2 %shard_map.108 = (bf16[8,32,1024]{2,1,0:T(8,128)(2,1)S(1)}, f32[8,32,1024]{2,1,0:T(8,128)S(1)}) custom-call(bf16[32,1664]{1,0:T(8,128)(2,1)S(1)} %shard_map.107.refs_0_, bf16[32,1664]{1,0:T(8,128)(2,1)S(1)} %collective-permute-done.16.refs_1_, bf16[32,1664]{1,0:T(8,128)(2,1)S(1)} %collective-permute-done.17.refs_2_, ...), custom_call_target="tpu_custom_call" | custom-call | tf_op jit(solution)/shard_map/pallas_call | solution.py:389
  135.7 14.5 %all_to_all.11.parts = bf16[8,32,1024]{2,1,0:T(8,128)(2,1)S(1)} all-to-all(bf16[8,32,1024]{2,1,0:T(8,128)(2,1)S(1)} %shard_map.109), channel_id=1, replica_groups={{0,2,4,6,8,10,12,14},{1,3,5,7,9,11,13,15},{16,18,20,22,24,26,28,30},{17..., dimensions={0} | all-to-all | bytes 1048576 | tf_op jit(solution)/shard_map/all_to_all | solution.py:50
  (60 shorter events, 33.8 us)
Async XLA Ops:
  1.4 8.7 %collective-permute-start = (bf16[48,1152]{1,0:T(8,128)(2,1)S(1)}, bf16[48,1152]{1,0:T(8,128)(2,1)S(1)}, u32[]{:S(2)}, u32[]{:S(2)}) collective-permute-start(bf16[48,1152]{1,0:T(8,128)(2,1)S(1)} %shard_map.100), channel_id=1, source_target_pairs={{0,0},{1,16},{2,32},{3,48},{4,64},{5,80},{6,96},{7,112},{8,128},{9... | collective-permute-start | bytes 331784 | tf_op jit(solution)/shard_map/ppermute | solution.py:42
  51.6 7.9 %collective-permute-start.2 = (bf16[32,2816]{1,0:T(8,128)(2,1)S(1)}, bf16[32,2816]{1,0:T(8,128)(2,1)S(1)}, u32[]{:S(2)}, u32[]{:S(2)}) collective-permute-start(bf16[32,2816]{1,0:T(8,128)(2,1)S(1)} %get-tuple-element.87), channel_id=1, source_target_pairs={{0,16},{16,0},{32,48},{48,32},{64,80},{80,64},{96,112},{112,96},{1... | collective-permute-start | bytes 540680 | tf_op jit(solution)/shard_map/ppermute | solution.py:26
  54.2 13.1 %collective-permute-start.5 = (bf16[2,32,2816]{2,1,0:T(8,128)(2,1)S(1)}, bf16[2,32,2816]{2,1,0:T(8,128)(2,1)S(1)}, u32[]{:S(2)}, u32[]{:S(2)}) collective-permute-start(bf16[2,32,2816]{2,1,0:T(8,128)(2,1)S(1)} %get-tuple-element.92), channel_id=1, source_target_pairs={{0,16},{16,0},{32,48},{48,32},{64,80},{80,64},{96,112},{112,96},{1... | collective-permute-start | bytes 1081352 | tf_op jit(solution)/shard_map/ppermute | solution.py:26
  59.6 7.7 %collective-permute-start.3 = (bf16[32,2816]{1,0:T(8,128)(2,1)S(1)}, bf16[32,2816]{1,0:T(8,128)(2,1)S(1)}, u32[]{:S(2)}, u32[]{:S(2)}) collective-permute-start(bf16[32,2816]{1,0:T(8,128)(2,1)S(1)} %shard_map.102), channel_id=1, source_target_pairs={{0,32},{16,48},{32,64},{48,80},{64,96},{80,112},{96,128},{112,144}... | collective-permute-start | bytes 540680 | tf_op jit(solution)/shard_map/ppermute | solution.py:26
  61.0 14.0 %collective-permute-start.8 = (bf16[2,32,2816]{2,1,0:T(8,128)(2,1)S(1)}, bf16[2,32,2816]{2,1,0:T(8,128)(2,1)S(1)}, u32[]{:S(2)}, u32[]{:S(2)}) collective-permute-start(bf16[2,32,2816]{2,1,0:T(8,128)(2,1)S(1)} %get-tuple-element.101), channel_id=1, source_target_pairs={{0,16},{16,0},{32,48},{48,32},{64,80},{80,64},{96,112},{112,96},{1... | collective-permute-start | bytes 1081352 | tf_op jit(solution)/shard_map/ppermute | solution.py:26
  67.4 7.6 %collective-permute-start.6 = (bf16[32,4096]{1,0:T(8,128)(2,1)S(1)}, bf16[32,4096]{1,0:T(8,128)(2,1)S(1)}, u32[]{:S(2)}, u32[]{:S(2)}) collective-permute-start(bf16[32,4096]{1,0:T(8,128)(2,1)S(1)} %get-tuple-element.99), channel_id=1, source_target_pairs={{0,32},{16,48},{32,64},{48,80},{64,96},{80,112},{96,128},{112,144}... | collective-permute-start | bytes 786440 | tf_op jit(solution)/shard_map/ppermute | solution.py:26
  69.1 7.6 %collective-permute-start.7 = (bf16[32,4096]{1,0:T(8,128)(2,1)S(1)}, bf16[32,4096]{1,0:T(8,128)(2,1)S(1)}, u32[]{:S(2)}, u32[]{:S(2)}) collective-permute-start(bf16[32,4096]{1,0:T(8,128)(2,1)S(1)} %get-tuple-element.100), channel_id=1, source_target_pairs={{0,224},{16,240},{32,0},{48,16},{64,32},{80,48},{96,64},{112,80},{... | collective-permute-start | bytes 786440 | tf_op jit(solution)/shard_map/ppermute | solution.py:26
  69.5 12.7 %collective-permute-start.11 = (bf16[2,32,2816]{2,1,0:T(8,128)(2,1)S(1)}, bf16[2,32,2816]{2,1,0:T(8,128)(2,1)S(1)}, u32[]{:S(2)}, u32[]{:S(2)}) collective-permute-start(bf16[2,32,2816]{2,1,0:T(8,128)(2,1)S(1)} %get-tuple-element.110), channel_id=1, source_target_pairs={{0,16},{16,0},{32,48},{48,32},{64,80},{80,64},{96,112},{112,96},{1... | collective-permute-start | bytes 1081352 | tf_op jit(solution)/shard_map/ppermute | solution.py:26
  76.9 6.4 %collective-permute-start.9 = (bf16[32,4096]{1,0:T(8,128)(2,1)S(1)}, bf16[32,4096]{1,0:T(8,128)(2,1)S(1)}, u32[]{:S(2)}, u32[]{:S(2)}) collective-permute-start(bf16[32,4096]{1,0:T(8,128)(2,1)S(1)} %get-tuple-element.108), channel_id=1, source_target_pairs={{0,32},{16,48},{32,64},{48,80},{64,96},{80,112},{96,128},{112,144}... | collective-permute-start | bytes 786440 | tf_op jit(solution)/shard_map/ppermute | solution.py:26
  79.0 6.9 %collective-permute-start.10 = (bf16[32,4096]{1,0:T(8,128)(2,1)S(1)}, bf16[32,4096]{1,0:T(8,128)(2,1)S(1)}, u32[]{:S(2)}, u32[]{:S(2)}) collective-permute-start(bf16[32,4096]{1,0:T(8,128)(2,1)S(1)} %get-tuple-element.109), channel_id=1, source_target_pairs={{0,224},{16,240},{32,0},{48,16},{64,32},{80,48},{96,64},{112,80},{... | collective-permute-start | bytes 786440 | tf_op jit(solution)/shard_map/ppermute | solution.py:26
  86.1 7.9 %collective-permute-start.12 = (bf16[32,4096]{1,0:T(8,128)(2,1)S(1)}, bf16[32,4096]{1,0:T(8,128)(2,1)S(1)}, u32[]{:S(2)}, u32[]{:S(2)}) collective-permute-start(bf16[32,4096]{1,0:T(8,128)(2,1)S(1)} %get-tuple-element.114), channel_id=1, source_target_pairs={{0,32},{16,48},{32,64},{48,80},{64,96},{80,112},{96,128},{112,144}... | collective-permute-start | bytes 786440 | tf_op jit(solution)/shard_map/ppermute | solution.py:26
  88.2 7.3 %collective-permute-start.13 = (bf16[32,4096]{1,0:T(8,128)(2,1)S(1)}, bf16[32,4096]{1,0:T(8,128)(2,1)S(1)}, u32[]{:S(2)}, u32[]{:S(2)}) collective-permute-start(bf16[32,4096]{1,0:T(8,128)(2,1)S(1)} %get-tuple-element.115), channel_id=1, source_target_pairs={{0,224},{16,240},{32,0},{48,16},{64,32},{80,48},{96,64},{112,80},{... | collective-permute-start | bytes 786440 | tf_op jit(solution)/shard_map/ppermute | solution.py:26
  88.2 5.8 %collective-permute-start.14 = (bf16[32,2816]{1,0:T(8,128)(2,1)S(1)}, bf16[32,2816]{1,0:T(8,128)(2,1)S(1)}, u32[]{:S(2)}, u32[]{:S(2)}) collective-permute-start(bf16[32,2816]{1,0:T(8,128)(2,1)S(1)} %get-tuple-element.116), channel_id=1, source_target_pairs={{0,16},{16,0},{32,48},{48,32},{64,80},{80,64},{96,112},{112,96},{1... | collective-permute-start | bytes 540680 | tf_op jit(solution)/shard_map/ppermute | solution.py:26
  100.2 4.8 %collective-permute-start.16 = (bf16[32,1664]{1,0:T(8,128)(2,1)S(1)}, bf16[32,1664]{1,0:T(8,128)(2,1)S(1)}, u32[]{:S(2)}, u32[]{:S(2)}) collective-permute-start(bf16[32,1664]{1,0:T(8,128)(2,1)S(1)} %shard_map.107.refs_0_), channel_id=1, source_target_pairs={{0,32},{16,48},{32,64},{48,80},{64,96},{80,112},{96,128},{112,144}... | collective-permute-start | bytes 319496 | tf_op jit(solution)/shard_map/ppermute | solution.py:26
  102.3 5.7 %collective-permute-start.17 = (bf16[32,1664]{1,0:T(8,128)(2,1)S(1)}, bf16[32,1664]{1,0:T(8,128)(2,1)S(1)}, u32[]{:S(2)}, u32[]{:S(2)}) collective-permute-start(bf16[32,1664]{1,0:T(8,128)(2,1)S(1)} %shard_map.107.refs_0_), channel_id=1, source_target_pairs={{0,224},{16,240},{32,0},{48,16},{64,32},{80,48},{96,64},{112,80},{... | collective-permute-start | bytes 319496 | tf_op jit(solution)/shard_map/ppermute | solution.py:26
  102.3 8.4 %collective-permute-start.20 = (bf16[32,1664]{1,0:T(8,128)(2,1)S(1)}, bf16[32,1664]{1,0:T(8,128)(2,1)S(1)}, u32[]{:S(2)}, u32[]{:S(2)}) collective-permute-start(bf16[32,1664]{1,0:T(8,128)(2,1)S(1)} %shard_map.107.refs_0_), channel_id=1, source_target_pairs={{0,16},{16,0},{32,48},{48,32},{64,80},{80,64},{96,112},{112,96},{1... | collective-permute-start | bytes 319496 | tf_op jit(solution)/shard_map/ppermute | solution.py:26
  108.0 4.9 %collective-permute-start.18 = (bf16[32,1664]{1,0:T(8,128)(2,1)S(1)}, bf16[32,1664]{1,0:T(8,128)(2,1)S(1)}, u32[]{:S(2)}, u32[]{:S(2)}) collective-permute-start(bf16[32,1664]{1,0:T(8,128)(2,1)S(1)} %collective-permute-done.16.refs_1_), channel_id=1, source_target_pairs={{0,32},{16,48},{32,64},{48,80},{64,96},{80,112},{96,128},{112,144}... | collective-permute-start | bytes 319496 | tf_op jit(solution)/shard_map/ppermute | solution.py:26
  109.9 4.7 %collective-permute-start.19 = (bf16[32,1664]{1,0:T(8,128)(2,1)S(1)}, bf16[32,1664]{1,0:T(8,128)(2,1)S(1)}, u32[]{:S(2)}, u32[]{:S(2)}) collective-permute-start(bf16[32,1664]{1,0:T(8,128)(2,1)S(1)} %collective-permute-done.17.refs_2_), channel_id=1, source_target_pairs={{0,224},{16,240},{32,0},{48,16},{64,32},{80,48},{96,64},{112,80},{... | collective-permute-start | bytes 319496 | tf_op jit(solution)/shard_map/ppermute | solution.py:26
  110.1 10.8 %collective-permute-start.23 = (bf16[2,32,1664]{2,1,0:T(8,128)(2,1)S(1)}, bf16[2,32,1664]{2,1,0:T(8,128)(2,1)S(1)}, u32[]{:S(2)}, u32[]{:S(2)}) collective-permute-start(bf16[2,32,1664]{2,1,0:T(8,128)(2,1)S(1)} %pad_maximum_fusion), channel_id=1, source_target_pairs={{0,16},{16,0},{32,48},{48,32},{64,80},{80,64},{96,112},{112,96},{1... | collective-permute-start | bytes 638984 | tf_op jit(solution)/shard_map/ppermute | solution.py:26
  114.6 4.8 %collective-permute-start.21 = (bf16[32,1664]{1,0:T(8,128)(2,1)S(1)}, bf16[32,1664]{1,0:T(8,128)(2,1)S(1)}, u32[]{:S(2)}, u32[]{:S(2)}) collective-permute-start(bf16[32,1664]{1,0:T(8,128)(2,1)S(1)} %collective-permute-done.18.refs_3_), channel_id=1, source_target_pairs={{0,32},{16,48},{32,64},{48,80},{64,96},{80,112},{96,128},{112,144}... | collective-permute-start | bytes 319496 | tf_op jit(solution)/shard_map/ppermute | solution.py:26
  116.7 9.9 %collective-permute-start.26 = (bf16[2,32,1664]{2,1,0:T(8,128)(2,1)S(1)}, bf16[2,32,1664]{2,1,0:T(8,128)(2,1)S(1)}, u32[]{:S(2)}, u32[]{:S(2)}) collective-permute-start(bf16[2,32,1664]{2,1,0:T(8,128)(2,1)S(1)} %pad_maximum_fusion.1), channel_id=1, source_target_pairs={{0,16},{16,0},{32,48},{48,32},{64,80},{80,64},{96,112},{112,96},{1... | collective-permute-start | bytes 638984 | tf_op jit(solution)/shard_map/ppermute | solution.py:26
  121.0 5.6 %collective-permute-start.24 = (bf16[32,896]{1,0:T(8,128)(2,1)S(1)}, bf16[32,896]{1,0:T(8,128)(2,1)S(1)}, u32[]{:S(2)}, u32[]{:S(2)}) collective-permute-start(bf16[32,896]{1,0:T(8,128)(2,1)S(1)} %slice.6), channel_id=1, source_target_pairs={{0,32},{16,48},{32,64},{48,80},{64,96},{80,112},{96,128},{112,144}... | collective-permute-start | bytes 172040 | tf_op jit(solution)/shard_map/ppermute | solution.py:26
  123.1 8.3 %collective-permute-start.27 = (bf16[2,32,1664]{2,1,0:T(8,128)(2,1)S(1)}, bf16[2,32,1664]{2,1,0:T(8,128)(2,1)S(1)}, u32[]{:S(2)}, u32[]{:S(2)}) collective-permute-start(bf16[2,32,1664]{2,1,0:T(8,128)(2,1)S(1)} %pad_maximum_fusion.2), channel_id=1, source_target_pairs={{0,16},{16,0},{32,48},{48,32},{64,80},{80,64},{96,112},{112,96},{1... | collective-permute-start | bytes 638984 | tf_op jit(solution)/shard_map/ppermute | solution.py:26
  126.6 4.8 %collective-permute-start.28 = (bf16[32,1664]{1,0:T(8,128)(2,1)S(1)}, bf16[32,1664]{1,0:T(8,128)(2,1)S(1)}, u32[]{:S(2)}, u32[]{:S(2)}) collective-permute-start(bf16[32,1664]{1,0:T(8,128)(2,1)S(1)} %pad_maximum_fusion.3), channel_id=1, source_target_pairs={{0,16},{16,0},{32,48},{48,32},{64,80},{80,64},{96,112},{112,96},{1... | collective-permute-start | bytes 319496 | tf_op jit(solution)/shard_map/ppermute | solution.py:26
  (8 other events, 130.3 us)

commit v5 on v4

--- a/solution.py
+++ b/solution.py
@@ -69,92 +69,129 @@
     return lax.dot_general(queries, keys, (((1,), (1,)), ((), ())), preferred_element_type=F32)
 
 
-def prepare_kernel(lengths, questions, queries_ref, hidden_ref, key_ref, value_ref, out_ref, queries, hidden, pair, length_ref, question_ref, sems):
+def head_copies(key_ref, value_ref, pair, sems):
+    at = pl.ds(pl.multiple_of((lax.axis_index("mp") >> 1) * HEAD_DIM, HEAD_DIM), HEAD_DIM)
+    return (
+        pltpu.make_async_copy(key_ref.at[:, at], pair.at[:, :HEAD_DIM], sems.at[0]),
+        pltpu.make_async_copy(value_ref.at[:, at], pair.at[:, HEAD_DIM:], sems.at[1]),
+    )
+
+
+def option_kernel(questions, queries_ref, key_ref, value_ref, out_ref, queries, pair, question_ref, sems):
     width = queries.shape[1]
-    heads = width // HEAD_DIM
-    batch_index, mp_index = lax.axis_index("batch"), lax.axis_index("mp")
-    head = pl.ds(pl.multiple_of((mp_index >> 1) * HEAD_DIM, HEAD_DIM), HEAD_DIM)
-    at = pl.ds(pl.multiple_of(mp_index * width, width), width)
-    copies = [
-        pltpu.make_async_copy(source, target, sems.at[i])
-        for i, (source, target) in enumerate(
-            [
-                (key_ref.at[:, head], pair.at[:, :HEAD_DIM]),
-                (queries_ref, queries),
-                (value_ref.at[:, head], pair.at[:, HEAD_DIM:]),
-                (hidden_ref.at[:, at], hidden),
-                (lengths, length_ref),
-                (questions, question_ref),
-            ]
-        )
-    ]
+    copies = (
+        *head_copies(key_ref, value_ref, pair, sems),
+        pltpu.make_async_copy(queries_ref.at[16:], queries, sems.at[2]),
+        pltpu.make_async_copy(questions, question_ref, sems.at[3]),
+    )
     for copy in copies:
         copy.start()
-    copies[4].wait()
-    copies[5].wait()
-    shape = (ROWS_DEV, ROWS_DEV)
-    row = lax.broadcasted_iota(jnp.int32, shape, 0)
-    key = lax.broadcasted_iota(jnp.int32, shape, 1)
-    seen = (key <= row) & (key < length_ref[batch_index])
-    seen = jnp.concatenate([seen.astype(F32)] * heads, axis=0) > 0
+    for copy in copies:
+        copy.wait()
     shape = (16, LANE)
     option = lax.broadcasted_iota(jnp.int32, shape, 0) & (ROWS_DEV - PREFIX - 1)
     asked = jnp.zeros(shape, jnp.int32)
     for i in range(ROWS_DEV - PREFIX):
         asked = jnp.where(option == i, question_ref[i], asked)
-    out_ref[32:, width:] = asked.astype(F32).astype(BF)
-    out_ref[:32, width:] = jnp.zeros((ROWS_DEV, LANE), BF)
-    copies[0].wait()
-    copies[1].wait()
+    out_ref[:, width:] = asked.astype(F32).astype(BF)
+    out_ref[:, : 2 * HEAD_DIM] = pair[:16]
+    out_ref[:, 2 * HEAD_DIM : 4 * HEAD_DIM] = pair[16:]
+    last = queries[...].astype(F32)[PREFIX - 16 :]
+    half = width // 2
+    out_ref[:, half:width] = jnp.concatenate([last[:, :half], last[:, half:]], axis=0).astype(BF)
+
+
+def prepare_options(question, queries, key_cache, value_cache):
+    rows, width = queries.shape
+    return pl.pallas_call(
+        option_kernel,
+        out_shape=in_vmem(((16, width + LANE), BF)),
+        in_specs=[HBM] * 4,
+        out_specs=VMEM,
+        scratch_shapes=[
+            pltpu.VMEM((16, width), BF),
+            pltpu.VMEM((rows, 2 * HEAD_DIM), BF),
+            pltpu.SMEM(question.shape, jnp.int32),
+            pltpu.SemaphoreType.DMA((4,)),
+        ],
+        compiler_params=PARAMS,
+    )(*map(in_hbm, (question, queries, key_cache, value_cache)))
+
+
+def prefix_kernel(lengths, queries_ref, hidden_ref, key_ref, value_ref, out_ref, queries, hidden, pair, length_ref, sems):
+    width = queries.shape[1]
+    heads = width // HEAD_DIM
+    at = pl.ds(pl.multiple_of(lax.axis_index("mp") * width, width), width)
+    copies = (
+        *head_copies(key_ref, value_ref, pair, sems),
+        pltpu.make_async_copy(queries_ref, queries, sems.at[2]),
+        pltpu.make_async_copy(lengths, length_ref, sems.at[3]),
+        pltpu.make_async_copy(hidden_ref.at[:, at], hidden, sems.at[4]),
+    )
+    for copy in copies:
+        copy.start()
+    for copy in copies:
+        copy.wait()
+    shape = (ROWS_DEV, ROWS_DEV)
+    row = lax.broadcasted_iota(jnp.int32, shape, 0)
+    key = lax.broadcasted_iota(jnp.int32, shape, 1)
+    seen = (key <= row) & (key < length_ref[lax.axis_index("batch")])
+    seen = jnp.concatenate([seen.astype(F32)] * heads, axis=0) > 0
     stacked = jnp.concatenate(
         [queries[:, h * HEAD_DIM : (h + 1) * HEAD_DIM] for h in range(heads)], axis=0
     )
     attention = softmax(scored(stacked, pair[:, :HEAD_DIM]), seen)
-    copies[2].wait()
     context = jnp.dot(attention, pair[:, HEAD_DIM:], preferred_element_type=F32).astype(BF)
-    out_ref[32:, : 2 * HEAD_DIM] = pair[:16]
-    out_ref[32:, 2 * HEAD_DIM : 4 * HEAD_DIM] = pair[16:]
-    last = queries[16:].astype(F32)[PREFIX - 16 :]
-    half = width // 2
-    out_ref[32:, half:width] = jnp.concatenate([last[:, :half], last[:, half:]], axis=0).astype(BF)
-    copies[3].wait()
     prefix = lax.broadcasted_iota(jnp.int32, (ROWS_DEV, HEAD_DIM), 0) < PREFIX
     for h in range(heads):
         columns = slice(h * HEAD_DIM, (h + 1) * HEAD_DIM)
         mine = context[h * ROWS_DEV : (h + 1) * ROWS_DEV].astype(F32)
         mine = jnp.where(prefix, mine, F32(0))
-        out_ref[:32, columns] = (hidden[:, columns].astype(F32) + mine).astype(BF)
-
-
-def prepare(prefix_len, question, queries, hidden_in, key_cache, value_cache):
+        out_ref[:, columns] = (hidden[:, columns].astype(F32) + mine).astype(BF)
+
+
+def prepare_rows(prefix_len, queries, hidden_in, key_cache, value_cache):
     rows, width = queries.shape
     return pl.pallas_call(
-        prepare_kernel,
-        out_shape=in_vmem(((rows + 16, width + LANE), BF)),
-        in_specs=[HBM] * 6,
+        prefix_kernel,
+        out_shape=in_vmem(((rows, width), BF)),
+        in_specs=[HBM] * 5,
         out_specs=VMEM,
         scratch_shapes=[
             pltpu.VMEM((rows, width), BF),
             pltpu.VMEM((rows, width), BF),
             pltpu.VMEM((rows, 2 * HEAD_DIM), BF),
             pltpu.SMEM(prefix_len.shape, jnp.int32),
-            pltpu.SMEM(question.shape, jnp.int32),
-            pltpu.SemaphoreType.DMA((6,)),
+            pltpu.SemaphoreType.DMA((5,)),
         ],
         compiler_params=PARAMS,
-    )(*map(in_hbm, (prefix_len, question, queries, hidden_in, key_cache, value_cache)))
+    )(*map(in_hbm, (prefix_len, queries, hidden_in, key_cache, value_cache)))
 
 
 FAR = 4
 
 
-def project_kernel(tiles, early, length_ref, gain_ref, mine_ref, theirs_ref, gate_hbm, up_hbm, *refs):
-    own_ref, give, kept, far_low, far_high = refs[0], refs[1:6], refs[6:13], refs[13], refs[14]
-    residual, rows, squares, gain, gate_ref, up_ref, sems = refs[15:]
+ORDER = (0, 1, 2, 3, 5, 6, 7, FAR)
+
+
+def products(rows, squares, gate_ref, up_ref, ready):
+    tiles = gate_ref.shape[1] // LANE
+    for base, ref in ((0, gate_ref), (tiles, up_ref)):
+        ready(ref)
+        for t in range(0, tiles, 2):
+            lanes = slice(t * LANE, min(t + 2, tiles) * LANE)
+            product = jnp.dot(rows[...], ref[:, lanes], preferred_element_type=F32).astype(BF)
+            for i in range(product.shape[1] // LANE):
+                yield base + t + i, product[:, i * LANE : (i + 1) * LANE]
+    yield 2 * tiles, squares[...]
+
+
+def far_kernel(early, length_ref, gain_ref, options, their_options, mine_ref, theirs_ref, gate_hbm, up_hbm, *refs):
+    own_ref, rows, squares, gate_ref, up_ref, give, low, high, residual, gain, sems = refs
     n = ROWS_DEV
     width = own_ref.shape[1]
     half = width // 2
-    wide = 2 * tiles + 1
+    wide = 2 * (gate_ref.shape[1] // LANE) + 1
     batch_index, mp_index = lax.axis_index("batch"), lax.axis_index("mp")
     z, core = batch_index >> 1, mp_index & 1
     flip = (batch_index & 1) ^ core
@@ -165,36 +202,15 @@
     fetch_gate.start()
     fetch_up.start()
 
-    def put(s, j, tile, value):
-        lanes = slice(tile * LANE, (tile + 1) * LANE)
-        if tile < early:
-            if j == 1 and s in (0, FAR):
-                give[s][:, lanes] = value
-            elif j == 1:
-                give[min(s, ZN - s)][0 if s < FAR else 1, :, lanes] = value
-            elif s == FAR:
-                far_low[:, lanes] = value
-            else:
-                kept[s if s < FAR else s - 1][:, lanes] = value
-        else:
-            late = tile - early + j * (wide - early)
-            if s == FAR:
-                far_high[:, late * LANE : (late + 1) * LANE] = value
-            else:
-                late += early
-                kept[s if s < FAR else s - 1][:, late * LANE : (late + 1) * LANE] = value
-
-    blocks = [(ref, i) for ref in (mine_ref, theirs_ref) for i in range(ZN)]
-    options = ROWS_DEV - PREFIX
+    blocks = [(ref, i) for ref in (options, their_options) for i in range(ZN)]
+    count = ROWS_DEV - PREFIX
 
     def gathered(lanes):
-        return jnp.concatenate([ref[i, n:, lanes] for ref, i in blocks], axis=0)
+        return jnp.concatenate([ref[i, :, lanes] for ref, i in blocks], axis=0)
 
     def unfolded(first):
-        low, high = slice(first, first + HEAD_DIM), slice(first + 2 * HEAD_DIM, first + 3 * HEAD_DIM)
-        return jnp.concatenate(
-            [ref[i, n:, lanes] for ref, i in blocks for lanes in (low, high)], axis=0
-        )
+        lower, upper = slice(first, first + HEAD_DIM), slice(first + 2 * HEAD_DIM, first + 3 * HEAD_DIM)
+        return jnp.concatenate([ref[i, :, lanes] for ref, i in blocks for lanes in (lower, upper)], axis=0)
 
     keys, values = unfolded(0), unfolded(HEAD_DIM)
     shape = (16 * len(blocks), n * len(blocks))
@@ -208,7 +224,7 @@
     for i in range(len(blocks)):
         live = jnp.where(order == i, length_ref[((i & (ZN - 1)) << 1) + ((i >> 3) ^ core)], live)
     seen = (owner == asked) & ((place & (n - 1)) < live)
-    seen = seen | (place == (row >> 4) * n + PREFIX + (row & (options - 1)))
+    seen = seen | (place == (row >> 4) * n + PREFIX + (row & (count - 1)))
     contexts = []
     for h in range(half // HEAD_DIM):
         queries = gathered(slice(half + h * HEAD_DIM, half + (h + 1) * HEAD_DIM))
@@ -217,22 +233,23 @@
         contexts.append(context.astype(BF).astype(F32))
     fetch.wait()
     scale = gain[...].reshape(1, width)
-    for k, (ref, i) in enumerate(blocks):
+    for k, (ref, i) in enumerate((ref, i) for ref in (mine_ref, theirs_ref) for i in range(ZN)):
         at = k * 16
         added = jnp.concatenate(
-            [context[at : at + options] for context in contexts]
-            + [context[at + options : at + 16] for context in contexts],
+            [context[at : at + count] for context in contexts]
+            + [context[at + count : at + 16] for context in contexts],
             axis=1,
         )
-        added = jnp.concatenate([jnp.zeros((16 - options, width), F32), added], axis=0)
-        first = ref[i, :16, :width]
-        last = (ref[i, 16:n, :width].astype(F32) + added).astype(BF)
+        added = jnp.concatenate([jnp.zeros((16 - count, width), F32), added], axis=0)
+        first = ref[i, :16, :]
+        last = (ref[i, 16:, :].astype(F32) + added).astype(BF)
         if ref is mine_ref:
             residual[i, :16] = first
             residual[i, 16:] = last
         s = (i - z) & (ZN - 1)
         j = flip if ref is mine_ref else 1 - flip
-        at = pl.multiple_of(s * 2 * n + j * n, n)
+        position = jnp.where(s == FAR, ZN - 1, s - (s > FAR).astype(jnp.int32))
+        at = pl.multiple_of(position * 2 * n + j * n, n)
         for part, offset in ((first, 0), (last, 16)):
             x = part.astype(F32)
             into = pl.ds(pl.multiple_of(at + offset, 16), 16)
@@ -244,54 +261,82 @@
             squares[into, :] = total.astype(BF)
     own_ref[...] = residual[mp_index >> 1]
 
-    for first, ref, at in [
-        (base + t, ref, t) for base, ref in ((0, gate_ref), (tiles, up_ref)) for t in range(0, tiles, 2)
-    ] + [(wide - 1, None, 0)]:
-        if at == 0 and ref is not None:
-            (fetch_gate if ref is gate_ref else fetch_up).wait()
-        if ref is None:
-            product = squares[...]
+    begin = (ZN - 1) * 2 * n
+    far = slice(begin, begin + 2 * n)
+    ready = lambda ref: (fetch_gate if ref is gate_ref else fetch_up).wait()
+    for tile, value in products(rows.at[far], squares.at[far], gate_ref, up_ref, ready):
+        if tile < early:
+            low[:, tile * LANE : (tile + 1) * LANE] = value[:n]
+            give[:, tile * LANE : (tile + 1) * LANE] = value[n:]
         else:
-            lanes = slice(at * LANE, min(at + 2, tiles) * LANE)
-            product = jnp.dot(rows[...], ref[:, lanes], preferred_element_type=F32).astype(BF)
-        for t in range(product.shape[1] // LANE):
-            for s in range(ZN):
-                for j in range(2):
-                    begin = (2 * s + j) * n
-                    put(s, j, first + t, product[begin : begin + n, t * LANE : (t + 1) * LANE])
+            for j in range(2):
+                late = tile - early + j * (wide - early)
+                high[:, late * LANE : (late + 1) * LANE] = value[j * n : (j + 1) * n]
+
+
+def near_kernel(early, rows, squares, gate_ref, up_ref, *refs):
+    give, kept = refs[:4], refs[4:]
+    n = ROWS_DEV
+    wide = 2 * (gate_ref.shape[1] // LANE) + 1
+    near = slice(0, (ZN - 1) * 2 * n)
+    for tile, value in products(rows.at[near], squares.at[near], gate_ref, up_ref, lambda ref: None):
+        for k, s in enumerate(ORDER[:-1]):
+            for j in range(2):
+                part = value[(2 * k + j) * n : (2 * k + j + 1) * n]
+                if tile >= early:
+                    late = tile + j * (wide - early)
+                    kept[k][:, late * LANE : (late + 1) * LANE] = part
+                elif j == 0:
+                    kept[k][:, tile * LANE : (tile + 1) * LANE] = part
+                elif s == 0:
+                    give[0][:, tile * LANE : (tile + 1) * LANE] = part
+                else:
+                    into = give[min(s, ZN - s)]
+                    into[0 if s < FAR else 1, :, tile * LANE : (tile + 1) * LANE] = part
 
 
 EARLY = 22
 
 
-def project(prefix_len, norm_gain, mine, theirs, gate_weight, up_weight):
+def project(prefix_len, norm_gain, options, mine, gate_weight, up_weight):
     width, hidden_width = gate_weight.shape
-    tiles = hidden_width // LANE
+    wide = 2 * (hidden_width // LANE) + 1
     n = ROWS_DEV
     low = (n, EARLY * LANE)
-    high = (n, 2 * (2 * tiles + 1 - EARLY) * LANE)
+    high = (n, 2 * (wide - EARLY) * LANE)
     whole = (n, low[1] + high[1])
-    own = (n, width)
-    refs = pl.pallas_call(
-        lambda *refs: project_kernel(tiles, EARLY, *refs),
+    all_rows = 2 * ZN * n
+    own, rows, squares, gate, up, far_give, far_low, far_high = pl.pallas_call(
+        lambda *refs: far_kernel(EARLY, *refs),
         out_shape=in_vmem(
-            (own, BF), (low, BF), *[((2, *low), BF)] * 3, (low, BF), *[(whole, BF)] * 7, (low, BF), (high, BF)
+            ((n, width), BF),
+            ((all_rows, width), BF),
+            ((all_rows, LANE), BF),
+            (gate_weight.shape, BF),
+            (up_weight.shape, BF),
+            (low, BF),
+            (low, BF),
+            (high, BF),
         ),
-        in_specs=[SMEM, HBM, VMEM, VMEM, HBM, HBM],
-        out_specs=(VMEM,) * 15,
+        in_specs=[SMEM, HBM] + [VMEM] * 4 + [HBM, HBM],
+        out_specs=(VMEM,) * 8,
         scratch_shapes=[
             pltpu.VMEM((ZN, n, width), BF),
-            pltpu.VMEM((2 * ZN * n, width), BF),
-            pltpu.VMEM((2 * ZN * n, LANE), BF),
             pltpu.VMEM((width,), F32),
-            pltpu.VMEM(gate_weight.shape, BF),
-            pltpu.VMEM(up_weight.shape, BF),
             pltpu.SemaphoreType.DMA((3,)),
         ],
         compiler_params=PARAMS,
-    )(prefix_len, in_hbm(norm_gain), mine, theirs, in_hbm(gate_weight), in_hbm(up_weight))
-    kept = list(refs[6:13])
-    return refs[0], refs[1:6], kept[:4] + [None] + kept[4:], refs[13], refs[14]
+    )(prefix_len, in_hbm(norm_gain), *options, *mine, in_hbm(gate_weight), in_hbm(up_weight))
+    refs = local(
+        lambda *refs: near_kernel(EARLY, *refs),
+        [(low, BF), *[((2, *low), BF)] * 3, *[(whole, BF)] * 7],
+        rows,
+        squares,
+        gate,
+        up,
+    )
+    kept = list(refs[4:])
+    return own, [*refs[:4], far_give], kept[:4] + [None] + kept[4:], far_low, far_high
 
 
 def add_first_kernel(low_ref, x_ref, out_ref):
@@ -426,20 +471,26 @@
     rows, width = queries.shape
     hidden_width = gate_weight.shape[1]
 
-    sent = prepare(prefix_len, question, queries, hidden_in, key_cache, value_cache)
-    came = transpose_mesh(sent)
-    mine = over_plane(jnp.broadcast_to(came[None], (ZN, *came.shape)))
-    theirs = core_pair(mine)
+    options = transpose_mesh(prepare_options(question, queries, key_cache, value_cache))
+    mine = transpose_mesh(prepare_rows(prefix_len, queries, hidden_in, key_cache, value_cache))
+    options = over_plane(jnp.broadcast_to(options[None], (ZN, *options.shape)))
+    options, mine = after(options, mine)
+    mine = over_plane(jnp.broadcast_to(mine[None], (ZN, *mine.shape)))
     own, give, kept, far_low, far_high = project(
-        prefix_len, norm_gain, mine, theirs, gate_weight, up_weight
+        prefix_len,
+        norm_gain,
+        (options, core_pair(options)),
+        (mine, core_pair(mine)),
+        gate_weight,
+        up_weight,
     )
     low, whole = far_low.shape, kept[0].shape
 
-    far, ahead = after(give[4], give[3])
-    far, x = x_pair(far), x_pair(ahead)
-    up, down, ahead = after(local(add_first_kernel, [(low, BF)], far_low, far), far_high, give[2])
-    up, down, following = along_z(up, 1), along_z(down, -1), x_pair(ahead)
-    up, down, x = after(up, down, x)
+    up = local(add_first_kernel, [(low, BF)], far_low, x_pair(give[4]))
+    up, down, x = after(up, far_high, give[3])
+    x, up, down = x_pair(x), along_z(up, 1), along_z(down, -1)
+    up, down, x, ahead = after(up, down, x, give[2])
+    following = x_pair(ahead)
     up, down = local(add_far_kernel, [(whole, BF)] * 2, kept[3], kept[5], x, up, down)
     for step in (2, 1):
         up, down, ahead = after(up, down, give[step - 1])

time: 151 us -> 165 us (1.093)
  starting transfers between devices: 32.7 us -> 48.5 us
  blocking collectives: 45.9 us -> 39.1 us
  Pallas kernels: 12.8 us -> 15.3 us
  waiting for transfers between devices: 59.1 us -> 60.9 us
    all_to_all x0 -> x1, starting transfers between devices: none -> 13.4 us  [over_plane(): lax.all_to_all(value, 'mp', 0, 0, axis_index_groups=PLANE, tiled=True)]
    all_to_all x2, blocking collectives: 45.9 us -> 39.1 us  [over_plane(): lax.all_to_all(value, 'mp', 0, 0, axis_index_groups=PLANE, tiled=True)]
    pallas_call x7 -> x8, Pallas kernels: 0.89 us -> 4.39 us  [local(): pl.pallas_call(kernel, out_shape=in_vmem(*shapes), in_specs=[VMEM] * len(...]
    ppermute x1 -> x2, starting transfers between devices: 3.03 us -> 6.45 us  [transpose_mesh(): lax.ppermute(value, ('batch', 'mp'), [(b * 16 + m, m * 16 + b) for b in r...]
    ppermute x1 -> x2, waiting for transfers between devices: 5.62 us -> 7.54 us  [transpose_mesh(): lax.ppermute(value, ('batch', 'mp'), [(b * 16 + m, m * 16 + b) for b in r...]
    ppermute x29 -> x30, starting transfers between devices: 29.7 us -> 28.7 us  [permute(): return lax.ppermute(value, axis, [(i, target(i)) for i in range(count)])]
    pallas_call x2 -> x3, Pallas kernels: 9.03 us -> 8.04 us  [the longest x1 5.78 us: project(): pl.pallas_call(lambda *refs: far_kernel(EARLY, *refs), out_shape=in_vmem(...]
    ppermute x29 -> x30, waiting for transfers between devices: 53.5 us -> 52.9 us  [permute(): return lax.ppermute(value, axis, [(i, target(i)) for i in range(count)])]
  transfers between devices with their start and end apart: 30 -> 33, of which waited for: 22 -> 26; matrix products, arithmetic and copies ran while one was open for 0% -> 0% of each run, Pallas kernels for 0% -> 3%
where the time goes in v5:
time: 165 us
  waiting for transfers between devices  60.9 us (37%)
  starting transfers between devices  48.5 us (29%)
  blocking collectives  39.1 us (24%)
  Pallas kernels  15.3 us (9%)
    ppermute x30, waiting for transfers between devices, permute(): return lax.ppermute(value, axis, [(i, target(i)) for i in range(count)])  52.9 us
    all_to_all x2, blocking collectives, over_plane(): lax.all_to_all(value, 'mp', 0, 0, axis_index_groups=PLANE, tiled=True)  39.1 us
    ppermute x30, starting transfers between devices, permute(): return lax.ppermute(value, axis, [(i, target(i)) for i in range(count)])  28.7 us
    all_to_all x1, starting transfers between devices, over_plane(): lax.all_to_all(value, 'mp', 0, 0, axis_index_groups=PLANE, tiled=True)  13.4 us
    ppermute x2, waiting for transfers between devices, transpose_mesh(): lax.ppermute(value, ('batch', 'mp'), [(b * 16 + m, m * 16 + b) for b in r...  7.54 us
    ppermute x2, starting transfers between devices, transpose_mesh(): lax.ppermute(value, ('batch', 'mp'), [(b * 16 + m, m * 16 + b) for b in r...  6.45 us
    pallas_call x1, Pallas kernels, project(): pl.pallas_call(lambda *refs: far_kernel(EARLY, *refs), out_shape=in_vmem(...  5.78 us
    pallas_call x8, Pallas kernels, local(): pl.pallas_call(kernel, out_shape=in_vmem(*shapes), in_specs=[VMEM] * len(...  4.39 us
  transfers between devices with their start and end apart: 33, of which 26 were waited for; matrix products, arithmetic and copies ran while one was open for 0% of the time, Pallas kernels for 3%

profile of v5, /device:TPU:32, one launch (start us, length us, event | category | flops | bytes accessed | tf_op | source)
XLA Modules:
  0.0 164.8 jit_solution(2606762549259823306)
XLA Ops:
  0.9 3.0 %collective-permute-start = (bf16[16,1152]{1,0:T(8,128)(2,1)S(1)}, bf16[16,1152]{1,0:T(8,128)(2,1)S(1)}, u32[]{:S(2)}, u32[]{:S(2)}) collective-permute-start(bf16[16,1152]{1,0:T(8,128)(2,1)S(1)} %shard_map.100), channel_id=1, source_target_pairs={{0,0},{1,16},{2,32},{3,48},{4,64},{5,80},{6,96},{7,112},{8,128},{9... | collective-permute-start | bytes 110600 | tf_op jit(solution)/shard_map/ppermute | solution.py:42
  3.9 3.9 %collective-permute-done = bf16[16,1152]{1,0:T(8,128)(2,1)S(1)} collective-permute-done((bf16[16,1152]{1,0:T(8,128)(2,1)S(1)}, bf16[16,1152]{1,0:T(8,128)(2,1)S(1)}, u32[]{:S(2)}, u32[]{:S(2)}) %collective-permute-start) | collective-permute-done | bytes 36896 | tf_op jit(solution)/shard_map/ppermute | solution.py:42
  8.5 13.4 %all-to-all-start = ((bf16[8,16,1152]{2,1,0:T(8,128)(2,1)}), bf16[8,16,1152]{2,1,0:T(8,128)(2,1)S(1)}, u32[]{:S(2)}, u32[]{:S(2)}) async-start(bf16[8,16,1152]{2,1,0:T(8,128)(2,1)} %broadcast_in_dim.4), calls=%async_computation | async-start | bytes 589824 | tf_op jit(solution)/shard_map/all_to_all | solution.py:50
  23.3 3.4 %collective-permute-start.1 = (bf16[32,1024]{1,0:T(8,128)(2,1)S(1)}, bf16[32,1024]{1,0:T(8,128)(2,1)S(1)}, u32[]{:S(2)}, u32[]{:S(2)}) collective-permute-start(bf16[32,1024]{1,0:T(8,128)(2,1)S(1)} %shard_map.101), channel_id=1, source_target_pairs={{0,0},{1,16},{2,32},{3,48},{4,64},{5,80},{6,96},{7,112},{8,128},{9... | collective-permute-start | bytes 196616 | tf_op jit(solution)/shard_map/ppermute | solution.py:42
  26.7 3.6 %collective-permute-done.1 = bf16[32,1024]{1,0:T(8,128)(2,1)S(1)} collective-permute-done((bf16[32,1024]{1,0:T(8,128)(2,1)S(1)}, bf16[32,1024]{1,0:T(8,128)(2,1)S(1)}, u32[]{:S(2)}, u32[]{:S(2)}) %collective-permute-start.1) | collective-permute-done | bytes 65568 | tf_op jit(solution)/shard_map/ppermute | solution.py:42
  30.8 24.6 %all_to_all.15.refs_4_ = bf16[8,32,1024]{2,1,0:T(8,128)(2,1)S(1)} all-to-all(bf16[8,32,1024]{2,1,0:T(8,128)(2,1)S(1)} %broadcast_in_dim.5), channel_id=1, replica_groups={{0,2,4,6,8,10,12,14},{1,3,5,7,9,11,13,15},{16,18,20,22,24,26,28,30},{17..., dimensions={0} | all-to-all | bytes 1048576 | tf_op jit(solution)/shard_map/all_to_all | solution.py:50
  57.7 5.8 %shard_map.102 = (bf16[32,1024]{1,0:T(8,128)(2,1)S(1)}, bf16[512,1024]{1,0:T(8,128)(2,1)S(1)}, bf16[512,128]{1,0:T(8,128)(2,1)S(1)}, bf16[1024,1664]{1,0:T(8,128...) custom-call(s32[16]{0:T(128)S(1)} %copy-done.1, ...), custom_call_target="tpu_custom_call" | custom-call | tf_op jit(solution)/shard_map/pallas_call | solution.py:309
  63.5 2.5 %collective-permute-start.4 = (bf16[32,2816]{1,0:T(8,128)(2,1)S(1)}, bf16[32,2816]{1,0:T(8,128)(2,1)S(1)}, u32[]{:S(2)}, u32[]{:S(2)}) collective-permute-start(bf16[32,2816]{1,0:T(8,128)(2,1)S(1)} %get-tuple-element.96), channel_id=1, source_target_pairs={{0,16},{16,0},{32,48},{48,32},{64,80},{80,64},{96,112},{112,96},{1... | collective-permute-start | bytes 540680 | tf_op jit(solution)/shard_map/ppermute | solution.py:26
  66.0 3.5 %shard_map.103 = (bf16[32,2816]{1,0:T(8,128)(2,1)S(1)}, bf16[2,32,2816]{2,1,0:T(8,128)(2,1)S(1)}, bf16[2,32,2816]{2,1,0:T(8,128)(2,1)S(1)}, bf16[2,32,2816]{2,1,...) custom-call(bf16[512,1024]{1,0:T(8,128)(2,1)S(1)} %get-tuple-element, ...), custom_call_target="tpu_custom_call" | custom-call | tf_op jit(solution)/shard_map/pallas_call | solution.py:382
  74.7 2.4 %collective-permute-done.6.down = bf16[32,1280]{1,0:T(8,128)(2,1)S(1)} collective-permute-done((bf16[32,1280]{1,0:T(8,128)(2,1)S(1)}, bf16[32,1280]{1,0:T(8,128)(2,1)S(1)}, u32[]{:S(2)}, u32[]{:S(2)}) %collective-permute-start.6) | collective-permute-done | bytes 81952 | tf_op jit(solution)/shard_map/ppermute | solution.py:26
  78.2 2.7 %collective-permute-done.7.x = bf16[2,32,2816]{2,1,0:T(8,128)(2,1)S(1)} collective-permute-done((bf16[2,32,2816]{2,1,0:T(8,128)(2,1)S(1)}, bf16[2,32,2816]{2,1,0:T(8,128)(2,1)S(1)}, u32[]{:S(2)}, u32[]{:S(2)}) %collective-permute-start.7) | collective-permute-done | bytes 360480 | tf_op jit(solution)/shard_map/ppermute | solution.py:26
  85.2 3.7 %collective-permute-done.8.up = bf16[32,4096]{1,0:T(8,128)(2,1)S(1)} collective-permute-done((bf16[32,4096]{1,0:T(8,128)(2,1)S(1)}, bf16[32,4096]{1,0:T(8,128)(2,1)S(1)}, u32[]{:S(2)}, u32[]{:S(2)}) %collective-permute-start.8) | collective-permute-done | bytes 262176 | tf_op jit(solution)/shard_map/ppermute | solution.py:26
  89.0 3.3 %collective-permute-done.10.x = bf16[2,32,2816]{2,1,0:T(8,128)(2,1)S(1)} collective-permute-done((bf16[2,32,2816]{2,1,0:T(8,128)(2,1)S(1)}, bf16[2,32,2816]{2,1,0:T(8,128)(2,1)S(1)}, u32[]{:S(2)}, u32[]{:S(2)}) %collective-permute-start.10) | collective-permute-done | bytes 360480 | tf_op jit(solution)/shard_map/ppermute | solution.py:26
  94.5 3.1 %collective-permute-done.13.x = bf16[2,32,2816]{2,1,0:T(8,128)(2,1)S(1)} collective-permute-done((bf16[2,32,2816]{2,1,0:T(8,128)(2,1)S(1)}, bf16[2,32,2816]{2,1,0:T(8,128)(2,1)S(1)}, u32[]{:S(2)}, u32[]{:S(2)}) %collective-permute-start.13) | collective-permute-done | bytes 360480 | tf_op jit(solution)/shard_map/ppermute | solution.py:26
  102.0 2.1 %collective-permute-start.16 = (bf16[32,2816]{1,0:T(8,128)(2,1)S(1)}, bf16[32,2816]{1,0:T(8,128)(2,1)S(1)}, u32[]{:S(2)}, u32[]{:S(2)}) collective-permute-start(bf16[32,2816]{1,0:T(8,128)(2,1)S(1)} %get-tuple-element.126), channel_id=1, source_target_pairs={{0,16},{16,0},{32,48},{48,32},{64,80},{80,64},{96,112},{112,96},{1... | collective-permute-start | bytes 540680 | tf_op jit(solution)/shard_map/ppermute | solution.py:26
  104.1 3.5 %collective-permute-done.16.x = bf16[32,2816]{1,0:T(8,128)(2,1)S(1)} collective-permute-done((bf16[32,2816]{1,0:T(8,128)(2,1)S(1)}, bf16[32,2816]{1,0:T(8,128)(2,1)S(1)}, u32[]{:S(2)}, u32[]{:S(2)}) %collective-permute-start.16) | collective-permute-done | bytes 180256 | tf_op jit(solution)/shard_map/ppermute | solution.py:26
  109.9 4.0 %collective-permute-done.17.x = bf16[32,640]{1,0:T(8,128)(2,1)S(1)} collective-permute-done((bf16[32,640]{1,0:T(8,128)(2,1)S(1)}, bf16[32,640]{1,0:T(8,128)(2,1)S(1)}, u32[]{:S(2)}, u32[]{:S(2)}) %collective-permute-start.17) | collective-permute-done | bytes 40992 | tf_op jit(solution)/shard_map/ppermute | solution.py:26
  114.0 2.1 %collective-permute-start.18 = (bf16[32,1664]{1,0:T(8,128)(2,1)S(1)}, bf16[32,1664]{1,0:T(8,128)(2,1)S(1)}, u32[]{:S(2)}, u32[]{:S(2)}) collective-permute-start(bf16[32,1664]{1,0:T(8,128)(2,1)S(1)} %shard_map.109.refs_0_), channel_id=1, source_target_pairs={{0,32},{16,48},{32,64},{48,80},{64,96},{80,112},{96,128},{112,144}... | collective-permute-start | bytes 319496 | tf_op jit(solution)/shard_map/ppermute | solution.py:26
  118.8 2.4 %collective-permute-done.19.refs_2_ = bf16[32,1664]{1,0:T(8,128)(2,1)S(1)} collective-permute-done((bf16[32,1664]{1,0:T(8,128)(2,1)S(1)}, bf16[32,1664]{1,0:T(8,128)(2,1)S(1)}, u32[]{:S(2)}, u32[]{:S(2)}) %collective-permute-start.19) | collective-permute-done | bytes 106528 | tf_op jit(solution)/shard_map/ppermute | solution.py:26
  130.6 2.4 %collective-permute-done.23.refs_5_ = bf16[32,1664]{1,0:T(8,128)(2,1)S(1)} collective-permute-done((bf16[32,1664]{1,0:T(8,128)(2,1)S(1)}, bf16[32,1664]{1,0:T(8,128)(2,1)S(1)}, u32[]{:S(2)}, u32[]{:S(2)}) %collective-permute-start.23) | collective-permute-done | bytes 106528 | tf_op jit(solution)/shard_map/ppermute | solution.py:26
  137.2 3.4 %collective-permute-done.27.refs_8_ = bf16[32,768]{1,0:T(8,128)(2,1)S(1)} collective-permute-done((bf16[32,768]{1,0:T(8,128)(2,1)S(1)}, bf16[32,768]{1,0:T(8,128)(2,1)S(1)}, u32[]{:S(2)}, u32[]{:S(2)}) %collective-permute-start.27) | collective-permute-done | bytes 49184 | tf_op jit(solution)/shard_map/ppermute | solution.py:26
  140.7 4.7 %collective-permute-done.30.refs_13_ = bf16[32,1664]{1,0:T(8,128)(2,1)S(1)} collective-permute-done((bf16[32,1664]{1,0:T(8,128)(2,1)S(1)}, bf16[32,1664]{1,0:T(8,128)(2,1)S(1)}, u32[]{:S(2)}, u32[]{:S(2)}) %collective-permute-start.30) | collective-permute-done | bytes 106528 | tf_op jit(solution)/shard_map/ppermute | solution.py:26
  145.4 2.2 %shard_map.110 = (bf16[8,32,1024]{2,1,0:T(8,128)(2,1)S(1)}, f32[8,32,1024]{2,1,0:T(8,128)S(1)}) custom-call(bf16[32,1664]{1,0:T(8,128)(2,1)S(1)} %shard_map.109.refs_0_, bf16[32,1664]{1,0:T(8,128)(2,1)S(1)} %collective-permute-done.18.refs_1_, bf16[32,1664]{1,0:T(8,128)(2,1)S(1)} %collective-permute-done.19.refs_2_, ...), custom_call_target="tpu_custom_call" | custom-call | tf_op jit(solution)/shard_map/pallas_call | solution.py:434
  149.6 14.5 %all_to_all.16.parts = bf16[8,32,1024]{2,1,0:T(8,128)(2,1)S(1)} all-to-all(bf16[8,32,1024]{2,1,0:T(8,128)(2,1)S(1)} %shard_map.111), channel_id=1, replica_groups={{0,2,4,6,8,10,12,14},{1,3,5,7,9,11,13,15},{16,18,20,22,24,26,28,30},{17..., dimensions={0} | all-to-all | bytes 1048576 | tf_op jit(solution)/shard_map/all_to_all | solution.py:50
  (69 shorter events, 44.5 us)
Async XLA Ops:
  0.9 6.9 %collective-permute-start = (bf16[16,1152]{1,0:T(8,128)(2,1)S(1)}, bf16[16,1152]{1,0:T(8,128)(2,1)S(1)}, u32[]{:S(2)}, u32[]{:S(2)}) collective-permute-start(bf16[16,1152]{1,0:T(8,128)(2,1)S(1)} %shard_map.100), channel_id=1, source_target_pairs={{0,0},{1,16},{2,32},{3,48},{4,64},{5,80},{6,96},{7,112},{8,128},{9... | collective-permute-start | bytes 110600 | tf_op jit(solution)/shard_map/ppermute | solution.py:42
  8.5 22.2 %all-to-all-start = ((bf16[8,16,1152]{2,1,0:T(8,128)(2,1)}), bf16[8,16,1152]{2,1,0:T(8,128)(2,1)S(1)}, u32[]{:S(2)}, u32[]{:S(2)}) async-start(bf16[8,16,1152]{2,1,0:T(8,128)(2,1)} %broadcast_in_dim.4), calls=%async_computation | async-start | bytes 589824 | tf_op jit(solution)/shard_map/all_to_all | solution.py:50
  23.3 7.1 %collective-permute-start.1 = (bf16[32,1024]{1,0:T(8,128)(2,1)S(1)}, bf16[32,1024]{1,0:T(8,128)(2,1)S(1)}, u32[]{:S(2)}, u32[]{:S(2)}) collective-permute-start(bf16[32,1024]{1,0:T(8,128)(2,1)S(1)} %shard_map.101), channel_id=1, source_target_pairs={{0,0},{1,16},{2,32},{3,48},{4,64},{5,80},{6,96},{7,112},{8,128},{9... | collective-permute-start | bytes 196616 | tf_op jit(solution)/shard_map/ppermute | solution.py:42
  63.5 7.3 %collective-permute-start.4 = (bf16[32,2816]{1,0:T(8,128)(2,1)S(1)}, bf16[32,2816]{1,0:T(8,128)(2,1)S(1)}, u32[]{:S(2)}, u32[]{:S(2)}) collective-permute-start(bf16[32,2816]{1,0:T(8,128)(2,1)S(1)} %get-tuple-element.96), channel_id=1, source_target_pairs={{0,16},{16,0},{32,48},{48,32},{64,80},{80,64},{96,112},{112,96},{1... | collective-permute-start | bytes 540680 | tf_op jit(solution)/shard_map/ppermute | solution.py:26
  70.9 10.0 %collective-permute-start.7 = (bf16[2,32,2816]{2,1,0:T(8,128)(2,1)S(1)}, bf16[2,32,2816]{2,1,0:T(8,128)(2,1)S(1)}, u32[]{:S(2)}, u32[]{:S(2)}) collective-permute-start(bf16[2,32,2816]{2,1,0:T(8,128)(2,1)S(1)} %get-tuple-element.101), channel_id=1, source_target_pairs={{0,16},{16,0},{32,48},{48,32},{64,80},{80,64},{96,112},{112,96},{1... | collective-permute-start | bytes 1081352 | tf_op jit(solution)/shard_map/ppermute | solution.py:26
  72.7 5.5 %collective-permute-start.5 = (bf16[32,2816]{1,0:T(8,128)(2,1)S(1)}, bf16[32,2816]{1,0:T(8,128)(2,1)S(1)}, u32[]{:S(2)}, u32[]{:S(2)}) collective-permute-start(bf16[32,2816]{1,0:T(8,128)(2,1)S(1)} %shard_map.104), channel_id=1, source_target_pairs={{0,32},{16,48},{32,64},{48,80},{64,96},{80,112},{96,128},{112,144}... | collective-permute-start | bytes 540680 | tf_op jit(solution)/shard_map/ppermute | solution.py:26
  80.9 11.3 %collective-permute-start.10 = (bf16[2,32,2816]{2,1,0:T(8,128)(2,1)S(1)}, bf16[2,32,2816]{2,1,0:T(8,128)(2,1)S(1)}, u32[]{:S(2)}, u32[]{:S(2)}) collective-permute-start(bf16[2,32,2816]{2,1,0:T(8,128)(2,1)S(1)} %get-tuple-element.111), channel_id=1, source_target_pairs={{0,16},{16,0},{32,48},{48,32},{64,80},{80,64},{96,112},{112,96},{1... | collective-permute-start | bytes 1081352 | tf_op jit(solution)/shard_map/ppermute | solution.py:26
  82.5 6.4 %collective-permute-start.8 = (bf16[32,4096]{1,0:T(8,128)(2,1)S(1)}, bf16[32,4096]{1,0:T(8,128)(2,1)S(1)}, u32[]{:S(2)}, u32[]{:S(2)}) collective-permute-start(bf16[32,4096]{1,0:T(8,128)(2,1)S(1)} %get-tuple-element.109), channel_id=1, source_target_pairs={{0,32},{16,48},{32,64},{48,80},{64,96},{80,112},{96,128},{112,144}... | collective-permute-start | bytes 786440 | tf_op jit(solution)/shard_map/ppermute | solution.py:26
  82.5 6.4 %collective-permute-start.9 = (bf16[32,4096]{1,0:T(8,128)(2,1)S(1)}, bf16[32,4096]{1,0:T(8,128)(2,1)S(1)}, u32[]{:S(2)}, u32[]{:S(2)}) collective-permute-start(bf16[32,4096]{1,0:T(8,128)(2,1)S(1)} %get-tuple-element.110), channel_id=1, source_target_pairs={{0,224},{16,240},{32,0},{48,16},{64,32},{80,48},{96,64},{112,80},{... | collective-permute-start | bytes 786440 | tf_op jit(solution)/shard_map/ppermute | solution.py:26
  84.6 13.1 %collective-permute-start.13 = (bf16[2,32,2816]{2,1,0:T(8,128)(2,1)S(1)}, bf16[2,32,2816]{2,1,0:T(8,128)(2,1)S(1)}, u32[]{:S(2)}, u32[]{:S(2)}) collective-permute-start(bf16[2,32,2816]{2,1,0:T(8,128)(2,1)S(1)} %get-tuple-element.120), channel_id=1, source_target_pairs={{0,16},{16,0},{32,48},{48,32},{64,80},{80,64},{96,112},{112,96},{1... | collective-permute-start | bytes 1081352 | tf_op jit(solution)/shard_map/ppermute | solution.py:26
  92.4 6.9 %collective-permute-start.11 = (bf16[32,4096]{1,0:T(8,128)(2,1)S(1)}, bf16[32,4096]{1,0:T(8,128)(2,1)S(1)}, u32[]{:S(2)}, u32[]{:S(2)}) collective-permute-start(bf16[32,4096]{1,0:T(8,128)(2,1)S(1)} %get-tuple-element.118), channel_id=1, source_target_pairs={{0,32},{16,48},{32,64},{48,80},{64,96},{80,112},{96,128},{112,144}... | collective-permute-start | bytes 786440 | tf_op jit(solution)/shard_map/ppermute | solution.py:26
  92.5 6.9 %collective-permute-start.12 = (bf16[32,4096]{1,0:T(8,128)(2,1)S(1)}, bf16[32,4096]{1,0:T(8,128)(2,1)S(1)}, u32[]{:S(2)}, u32[]{:S(2)}) collective-permute-start(bf16[32,4096]{1,0:T(8,128)(2,1)S(1)} %get-tuple-element.119), channel_id=1, source_target_pairs={{0,224},{16,240},{32,0},{48,16},{64,32},{80,48},{96,64},{112,80},{... | collective-permute-start | bytes 786440 | tf_op jit(solution)/shard_map/ppermute | solution.py:26
  99.6 8.0 %collective-permute-start.14 = (bf16[32,4096]{1,0:T(8,128)(2,1)S(1)}, bf16[32,4096]{1,0:T(8,128)(2,1)S(1)}, u32[]{:S(2)}, u32[]{:S(2)}) collective-permute-start(bf16[32,4096]{1,0:T(8,128)(2,1)S(1)} %get-tuple-element.124), channel_id=1, source_target_pairs={{0,32},{16,48},{32,64},{48,80},{64,96},{80,112},{96,128},{112,144}... | collective-permute-start | bytes 786440 | tf_op jit(solution)/shard_map/ppermute | solution.py:26
  101.3 8.3 %collective-permute-start.15 = (bf16[32,4096]{1,0:T(8,128)(2,1)S(1)}, bf16[32,4096]{1,0:T(8,128)(2,1)S(1)}, u32[]{:S(2)}, u32[]{:S(2)}) collective-permute-start(bf16[32,4096]{1,0:T(8,128)(2,1)S(1)} %get-tuple-element.125), channel_id=1, source_target_pairs={{0,224},{16,240},{32,0},{48,16},{64,32},{80,48},{96,64},{112,80},{... | collective-permute-start | bytes 786440 | tf_op jit(solution)/shard_map/ppermute | solution.py:26
  102.0 5.6 %collective-permute-start.16 = (bf16[32,2816]{1,0:T(8,128)(2,1)S(1)}, bf16[32,2816]{1,0:T(8,128)(2,1)S(1)}, u32[]{:S(2)}, u32[]{:S(2)}) collective-permute-start(bf16[32,2816]{1,0:T(8,128)(2,1)S(1)} %get-tuple-element.126), channel_id=1, source_target_pairs={{0,16},{16,0},{32,48},{48,32},{64,80},{80,64},{96,112},{112,96},{1... | collective-permute-start | bytes 540680 | tf_op jit(solution)/shard_map/ppermute | solution.py:26
  116.1 5.1 %collective-permute-start.19 = (bf16[32,1664]{1,0:T(8,128)(2,1)S(1)}, bf16[32,1664]{1,0:T(8,128)(2,1)S(1)}, u32[]{:S(2)}, u32[]{:S(2)}) collective-permute-start(bf16[32,1664]{1,0:T(8,128)(2,1)S(1)} %shard_map.109.refs_0_), channel_id=1, source_target_pairs={{0,224},{16,240},{32,0},{48,16},{64,32},{80,48},{96,64},{112,80},{... | collective-permute-start | bytes 319496 | tf_op jit(solution)/shard_map/ppermute | solution.py:26
  116.1 8.2 %collective-permute-start.22 = (bf16[32,1664]{1,0:T(8,128)(2,1)S(1)}, bf16[32,1664]{1,0:T(8,128)(2,1)S(1)}, u32[]{:S(2)}, u32[]{:S(2)}) collective-permute-start(bf16[32,1664]{1,0:T(8,128)(2,1)S(1)} %shard_map.109.refs_0_), channel_id=1, source_target_pairs={{0,16},{16,0},{32,48},{48,32},{64,80},{80,64},{96,112},{112,96},{1... | collective-permute-start | bytes 319496 | tf_op jit(solution)/shard_map/ppermute | solution.py:26
  121.3 5.0 %collective-permute-start.20 = (bf16[32,1664]{1,0:T(8,128)(2,1)S(1)}, bf16[32,1664]{1,0:T(8,128)(2,1)S(1)}, u32[]{:S(2)}, u32[]{:S(2)}) collective-permute-start(bf16[32,1664]{1,0:T(8,128)(2,1)S(1)} %collective-permute-done.18.refs_1_), channel_id=1, source_target_pairs={{0,32},{16,48},{32,64},{48,80},{64,96},{80,112},{96,128},{112,144}... | collective-permute-start | bytes 319496 | tf_op jit(solution)/shard_map/ppermute | solution.py:26
  122.3 5.8 %collective-permute-start.21 = (bf16[32,1664]{1,0:T(8,128)(2,1)S(1)}, bf16[32,1664]{1,0:T(8,128)(2,1)S(1)}, u32[]{:S(2)}, u32[]{:S(2)}) collective-permute-start(bf16[32,1664]{1,0:T(8,128)(2,1)S(1)} %collective-permute-done.19.refs_2_), channel_id=1, source_target_pairs={{0,224},{16,240},{32,0},{48,16},{64,32},{80,48},{96,64},{112,80},{... | collective-permute-start | bytes 319496 | tf_op jit(solution)/shard_map/ppermute | solution.py:26
  123.4 11.6 %collective-permute-start.25 = (bf16[2,32,1664]{2,1,0:T(8,128)(2,1)S(1)}, bf16[2,32,1664]{2,1,0:T(8,128)(2,1)S(1)}, u32[]{:S(2)}, u32[]{:S(2)}) collective-permute-start(bf16[2,32,1664]{2,1,0:T(8,128)(2,1)S(1)} %pad_maximum_fusion), channel_id=1, source_target_pairs={{0,16},{16,0},{32,48},{48,32},{64,80},{80,64},{96,112},{112,96},{1... | collective-permute-start | bytes 638984 | tf_op jit(solution)/shard_map/ppermute | solution.py:26
  130.3 10.3 %collective-permute-start.28 = (bf16[2,32,1664]{2,1,0:T(8,128)(2,1)S(1)}, bf16[2,32,1664]{2,1,0:T(8,128)(2,1)S(1)}, u32[]{:S(2)}, u32[]{:S(2)}) collective-permute-start(bf16[2,32,1664]{2,1,0:T(8,128)(2,1)S(1)} %pad_maximum_fusion.1), channel_id=1, source_target_pairs={{0,16},{16,0},{32,48},{48,32},{64,80},{80,64},{96,112},{112,96},{1... | collective-permute-start | bytes 638984 | tf_op jit(solution)/shard_map/ppermute | solution.py:26
  135.1 5.5 %collective-permute-start.26 = (bf16[32,896]{1,0:T(8,128)(2,1)S(1)}, bf16[32,896]{1,0:T(8,128)(2,1)S(1)}, u32[]{:S(2)}, u32[]{:S(2)}) collective-permute-start(bf16[32,896]{1,0:T(8,128)(2,1)S(1)} %slice.6), channel_id=1, source_target_pairs={{0,32},{16,48},{32,64},{48,80},{64,96},{80,112},{96,128},{112,144}... | collective-permute-start | bytes 172040 | tf_op jit(solution)/shard_map/ppermute | solution.py:26
  137.2 8.2 %collective-permute-start.29 = (bf16[2,32,1664]{2,1,0:T(8,128)(2,1)S(1)}, bf16[2,32,1664]{2,1,0:T(8,128)(2,1)S(1)}, u32[]{:S(2)}, u32[]{:S(2)}) collective-permute-start(bf16[2,32,1664]{2,1,0:T(8,128)(2,1)S(1)} %pad_maximum_fusion.2), channel_id=1, source_target_pairs={{0,16},{16,0},{32,48},{48,32},{64,80},{80,64},{96,112},{112,96},{1... | collective-permute-start | bytes 638984 | tf_op jit(solution)/shard_map/ppermute | solution.py:26
  140.6 4.8 %collective-permute-start.30 = (bf16[32,1664]{1,0:T(8,128)(2,1)S(1)}, bf16[32,1664]{1,0:T(8,128)(2,1)S(1)}, u32[]{:S(2)}, u32[]{:S(2)}) collective-permute-start(bf16[32,1664]{1,0:T(8,128)(2,1)S(1)} %pad_maximum_fusion.3), channel_id=1, source_target_pairs={{0,16},{16,0},{32,48},{48,32},{64,80},{80,64},{96,112},{112,96},{1... | collective-permute-start | bytes 319496 | tf_op jit(solution)/shard_map/ppermute | solution.py:26
  (11 other events, 154.3 us)

commit v6 on v3

--- a/solution.py
+++ b/solution.py
@@ -36,6 +36,14 @@
 
 def core_pair(value):
     return permute(value, "mp", lambda i: i ^ 1)
+
+
+def by_core(value, target, cores):
+    return lax.ppermute(
+        value,
+        ("batch", "mp"),
+        [(b * 16 + m, target(b, m % 2) * 16 + m) for b in range(16) for m in range(16) if m % 2 in cores],
+    )
 
 
 def transpose_mesh(value):
@@ -355,49 +363,44 @@
     out[...] = (gate / (1 + jnp.exp(-gate)) * lift).astype(BF)
 
 
-def down_kernel(*refs):
-    own, up1, down1, up2, down2, up3, down3, up4, down4, x0, x1, x2, x3, x4, down_ref = refs[:15]
-    give, keep, rows = refs[15:]
+def down_kernel(own, near1, near2, near3, far, x0, x1, x2, x3, x4, down_ref, their_down, give, keep, rows):
     n = ROWS_DEV
+    width = down_ref.shape[0]
     batch_index, mp_index = lax.axis_index("batch"), lax.axis_index("mp")
-    z, flip = batch_index >> 1, (batch_index ^ mp_index) & 1
-    ours = {0: own, 1: down1, 2: down2, 3: down3, 5: up3, 6: up2, 7: up1}
-    partners = {0: x0, 7: x1.at[0], 1: x1.at[1], 6: x2.at[0], 2: x2.at[1], 5: x3.at[0], 3: x3.at[1], FAR: x4}
-    for s in range(ZN):
-        for j, found in enumerate((ours, partners)):
-            target = (z + s) & (ZN - 1)
-            other = (flip + j) & 1
-            at = pl.ds(pl.multiple_of((1 - other) * ZN * n + target * n, n), n)
-            if s in found:
-                rows[at, :] = found[s][...]
-            else:
-                rows[at, : up4.shape[1]] = up4[...]
-                rows[at, up4.shape[1] :] = down4[...]
+    core = mp_index & 1
+    flip = (batch_index & 1) ^ core
+    for j, found in enumerate(((near1, near2, near3, far, own), (x1, x2, x3, x4, x0))):
+        first = ((flip + j) & 1) * 4 * n
+        for i in range(3):
+            rows[pl.ds(pl.multiple_of(first + i * n, n), n), :] = found[i][...]
+        last = pl.ds(pl.multiple_of(first + 3 * n, n), n)
+
+        @pl.when(core == 0)
+        def _():
+            rows[last, :] = found[3][...]
+
+        @pl.when(core == 1)
+        def _():
+            rows[last, :] = found[4][...]
+
     step = 2 * LANE
     for i in range(0, down_ref.shape[1], step):
         lanes = slice(i, i + step)
-        product = jnp.dot(rows[...], down_ref[:, lanes], preferred_element_type=F32)
-        for target in range(ZN):
-            give[target, :, lanes] = product[target * n : (target + 1) * n].astype(BF)
-            at = (ZN + target) * n
-            keep[target, :, lanes] = product[at : at + n]
-
-
-def project_down(blocks, down_weight):
-    hidden_width, width = down_weight.shape
-    shape = (ZN, ROWS_DEV, width)
-    return pl.pallas_call(
-        down_kernel,
-        out_shape=in_vmem((shape, BF), (shape, F32)),
-        in_specs=[VMEM] * (len(blocks) + 1),
-        out_specs=(VMEM, VMEM),
-        scratch_shapes=[pltpu.VMEM((2 * ZN * ROWS_DEV, hidden_width), BF)],
-        compiler_params=PARAMS,
-    )(*blocks, down_weight)
-
-
-def add_core_kernel(keep, come, out):
-    out[...] = (keep[...] + come[...].astype(F32)).astype(BF)
+        product = jnp.dot(rows[:, :width], down_ref[:, lanes], preferred_element_type=F32)
+        product = product + jnp.dot(rows[:, width:], their_down[:, lanes], preferred_element_type=F32)
+        product = product.astype(BF)
+        for k in range(4):
+            keep[k, :, lanes] = product[k * n : (k + 1) * n]
+            give[k, :, lanes] = product[(4 + k) * n : (5 + k) * n]
+
+
+def place_kernel(keep, come, out):
+    z, core = lax.axis_index("batch") >> 1, lax.axis_index("mp") & 1
+    for parts, side in ((keep, core), (come, 1 - core)):
+        sign = 2 * side - 1
+        for k in range(4):
+            distance = sign * (k + 1) if k < 3 else (1 - side) * FAR
+            out[(z + distance) & (ZN - 1)] = parts[k]
 
 
 def finish_kernel(own, parts, out):
@@ -427,7 +430,9 @@
     hidden_width = gate_weight.shape[1]
 
     sent = prepare(prefix_len, question, queries, hidden_in, key_cache, value_cache)
-    came = transpose_mesh(sent)
+    sent, down_weight = after(sent, down_weight)
+    their_down = core_pair(down_weight)
+    came, their_down = after(transpose_mesh(sent), their_down)
     mine = over_plane(jnp.broadcast_to(came[None], (ZN, *came.shape)))
     theirs = core_pair(mine)
     own, give, kept, far_low, far_high = project(
@@ -462,23 +467,28 @@
     )
     hidden = local(gated_kernel, [((rows, hidden_width), BF)], keep, x_pair(last))
 
-    up, down, across = hidden, hidden, hidden
-    blocks, partners = [hidden], []
-    for step in range(3):
-        up, down, across = after(up, down, across)
-        up, down, came = along_z(up, 1), along_z(down, -1), x_pair(across)
-        up, down = after(up, down)
+    near = jnp.concatenate([hidden, core_pair(hidden)], axis=1)
+    blocks, partners = [near], []
+    for step in range(4):
+        across = blocks[-1]
+        near, across = after(across, across)
+        near = by_core(near, lambda i, core: (i + 2 - 4 * core) % 16, (0,) if step == 3 else (0, 1))
+        came = by_core(across, lambda i, core: i ^ 1, (1,) if step == 0 else (0, 1))
+        if partners:
+            near, partners[-1] = after(near, partners[-1])
         partners.append(came)
-        blocks += [up, down]
-        across = jnp.stack([up, down])
-    half = (hidden_width // LANE + 1) // 2 * LANE
-    up, down, across = after(up[:, :half], down[:, half:], across)
-    up, down, came = along_z(up, 1), along_z(down, -1), x_pair(across)
-    up, down = after(up, down)
-    partners += [came, x_pair(jnp.concatenate([up, down], axis=1))]
-    blocks += [up, down, *partners]
-    send, keep = project_down(blocks, down_weight)
-    held = local(add_core_kernel, [(keep.shape, BF)], keep, core_pair(send))
+        blocks.append(near)
+    partners.append(by_core(near, lambda i, core: i ^ 1, (0,)))
+    shape = (4, rows, width)
+    keep, send = pl.pallas_call(
+        lambda *refs: down_kernel(*refs[:12], refs[13], refs[12], refs[14]),
+        out_shape=in_vmem((shape, BF), (shape, BF)),
+        in_specs=[VMEM] * 12,
+        out_specs=(VMEM, VMEM),
+        scratch_shapes=[pltpu.VMEM((8 * rows, 2 * hidden_width), BF)],
+        compiler_params=PARAMS,
+    )(*blocks, *partners, down_weight, their_down)
+    held = local(place_kernel, [((ZN, rows, width), BF)], keep, core_pair(send))
     parts = over_plane(held)
     return pl.pallas_call(
         finish_kernel,

time: 156 us -> 158 us (1.013); the launches traced: 155 us -> 155 us
  waiting for transfers between devices: 62 us -> 58.8 us
  starting transfers between devices: 34.2 us -> 36.3 us
    ppermute x29 -> x18, waiting for transfers between devices: 56.4 us -> 34.6 us  [permute(): return lax.ppermute(value, axis, [(i, target(i)) for i in range(count)])]
    ppermute x0 -> x9, waiting for transfers between devices: none -> 18.6 us  [by_core(): lax.ppermute(value, ('batch', 'mp'), [(b * 16 + m, target(b, m % 2) * 16...]
    ppermute x0 -> x9, starting transfers between devices: none -> 15.7 us  [by_core(): lax.ppermute(value, ('batch', 'mp'), [(b * 16 + m, target(b, m % 2) * 16...]
    ppermute x29 -> x18, starting transfers between devices: 31.2 us -> 17.6 us  [permute(): return lax.ppermute(value, axis, [(i, target(i)) for i in range(count)])]
  transfers between devices with their start and end apart: 30 -> 28, of which waited for: 24 -> 20; matrix products, arithmetic and copies ran while one was open for 0% -> 0% of each run, Pallas kernels for 0% -> 0%
where the time goes in v6:
time: 158 us; the launch traced here: 155 us
  waiting for transfers between devices  58.8 us (37%)
  blocking collectives  46.9 us (30%)
  starting transfers between devices  36.3 us (23%)
  Pallas kernels  12.8 us (8%)
    all_to_all x2, blocking collectives, over_plane(): lax.all_to_all(value, 'mp', 0, 0, axis_index_groups=PLANE, tiled=True)  46.9 us
    ppermute x18, waiting for transfers between devices, permute(): return lax.ppermute(value, axis, [(i, target(i)) for i in range(count)])  34.6 us
    ppermute x9, waiting for transfers between devices, by_core(): lax.ppermute(value, ('batch', 'mp'), [(b * 16 + m, target(b, m % 2) * 16...  18.6 us
    ppermute x18, starting transfers between devices, permute(): return lax.ppermute(value, axis, [(i, target(i)) for i in range(count)])  17.6 us
    ppermute x9, starting transfers between devices, by_core(): lax.ppermute(value, ('batch', 'mp'), [(b * 16 + m, target(b, m % 2) * 16...  15.7 us
    pallas_call x1, Pallas kernels, project(): pl.pallas_call(lambda *refs: project_kernel(tiles, EARLY, *refs), out_sha...  7.61 us
    ppermute x1, waiting for transfers between devices, transpose_mesh(): lax.ppermute(value, ('batch', 'mp'), [(b * 16 + m, m * 16 + b) for b in r...  5.51 us
  transfers between devices with their start and end apart: 28, of which 20 were waited for; matrix products, arithmetic and copies ran while one was open for 0% of the time, Pallas kernels for 0%

profile of v6, /device:TPU:32, one launch (start us, length us, event | category | flops | bytes accessed | tf_op | source)
XLA Modules:
  0.0 155.0 jit_solution(2867960419685786220)
XLA Ops:
  1.5 3.0 %collective-permute-start = (bf16[48,1152]{1,0:T(8,128)(2,1)S(1)}, bf16[48,1152]{1,0:T(8,128)(2,1)S(1)}, u32[]{:S(2)}, u32[]{:S(2)}) collective-permute-start(bf16[48,1152]{1,0:T(8,128)(2,1)S(1)} %shard_map.100), channel_id=1, source_target_pairs={{0,0},{1,16},{2,32},{3,48},{4,64},{5,80},{6,96},{7,112},{8,128},{9... | collective-permute-start | bytes 331784 | tf_op jit(solution)/shard_map/ppermute | solution.py:50
  4.6 5.5 %collective-permute-done = bf16[48,1152]{1,0:T(8,128)(2,1)S(1)} collective-permute-done((bf16[48,1152]{1,0:T(8,128)(2,1)S(1)}, bf16[48,1152]{1,0:T(8,128)(2,1)S(1)}, u32[]{:S(2)}, u32[]{:S(2)}) %collective-permute-start) | collective-permute-done | bytes 110624 | tf_op jit(solution)/shard_map/ppermute | solution.py:50
  10.1 32.2 %all_to_all.10.refs_2_ = bf16[8,48,1152]{2,1,0:T(8,128)(2,1)S(1)} all-to-all(bf16[8,48,1152]{2,1,0:T(8,128)(2,1)S(1)} %broadcast_in_dim.2), channel_id=1, replica_groups={{0,2,4,6,8,10,12,14},{1,3,5,7,9,11,13,15},{16,18,20,22,24,26,28,30},{17..., dimensions={0} | all-to-all | bytes 1769472 | tf_op jit(solution)/shard_map/all_to_all | solution.py:58
  42.4 2.4 %collective-permute-done.2.refs_3_ = bf16[8,48,1152]{2,1,0:T(8,128)(2,1)S(1)} collective-permute-done((bf16[8,48,1152]{2,1,0:T(8,128)(2,1)S(1)}, bf16[8,48,1152]{2,1,0:T(8,128)(2,1)S(1)}, u32[]{:S(2)}, u32[]{:S(2)}) %collective-permute-start.2) | collective-permute-done | bytes 884768 | tf_op jit(solution)/shard_map/ppermute | solution.py:26
  44.8 7.6 %shard_map.101 = (bf16[32,1024]{1,0:T(8,128)(2,1)S(1)}, bf16[32,2816]{1,0:T(8,128)(2,1)S(1)}, bf16[2,32,2816]{2,1,0:T(8,128)(2,1)S(1)}, bf16[2,32,2816]{2,1,0:T(...) custom-call(s32[16]{0:T(128)S(1)} %copy-done.1, ...), custom_call_target="tpu_custom_call" | custom-call | tf_op jit(solution)/shard_map/pallas_call | solution.py:283
  52.4 2.3 %collective-permute-start.3 = (bf16[32,2816]{1,0:T(8,128)(2,1)S(1)}, bf16[32,2816]{1,0:T(8,128)(2,1)S(1)}, u32[]{:S(2)}, u32[]{:S(2)}) collective-permute-start(bf16[32,2816]{1,0:T(8,128)(2,1)S(1)} %get-tuple-element.85), channel_id=1, source_target_pairs={{0,16},{16,0},{32,48},{48,32},{64,80},{80,64},{96,112},{112,96},{1... | collective-permute-start | bytes 540680 | tf_op jit(solution)/shard_map/ppermute | solution.py:26
  54.8 5.2 %collective-permute-done.3.x_ref = bf16[32,2816]{1,0:T(8,128)(2,1)S(1)} collective-permute-done((bf16[32,2816]{1,0:T(8,128)(2,1)S(1)}, bf16[32,2816]{1,0:T(8,128)(2,1)S(1)}, u32[]{:S(2)}, u32[]{:S(2)}) %collective-permute-start.3) | collective-permute-done | bytes 180256 | tf_op jit(solution)/shard_map/ppermute | solution.py:26
  64.3 2.7 %collective-permute-done.5.down = bf16[32,1280]{1,0:T(8,128)(2,1)S(1)} collective-permute-done((bf16[32,1280]{1,0:T(8,128)(2,1)S(1)}, bf16[32,1280]{1,0:T(8,128)(2,1)S(1)}, u32[]{:S(2)}, u32[]{:S(2)}) %collective-permute-start.5) | collective-permute-done | bytes 81952 | tf_op jit(solution)/shard_map/ppermute | solution.py:26
  72.1 3.4 %collective-permute-done.9.x = bf16[2,32,2816]{2,1,0:T(8,128)(2,1)S(1)} collective-permute-done((bf16[2,32,2816]{2,1,0:T(8,128)(2,1)S(1)}, bf16[2,32,2816]{2,1,0:T(8,128)(2,1)S(1)}, u32[]{:S(2)}, u32[]{:S(2)}) %collective-permute-start.9) | collective-permute-done | bytes 360480 | tf_op jit(solution)/shard_map/ppermute | solution.py:26
  77.5 2.1 %collective-permute-start.10 = (bf16[32,4096]{1,0:T(8,128)(2,1)S(1)}, bf16[32,4096]{1,0:T(8,128)(2,1)S(1)}, u32[]{:S(2)}, u32[]{:S(2)}) collective-permute-start(bf16[32,4096]{1,0:T(8,128)(2,1)S(1)} %get-tuple-element.106), channel_id=1, source_target_pairs={{0,32},{16,48},{32,64},{48,80},{64,96},{80,112},{96,128},{112,144}... | collective-permute-start | bytes 786440 | tf_op jit(solution)/shard_map/ppermute | solution.py:26
  79.6 3.1 %collective-permute-done.12.x = bf16[2,32,2816]{2,1,0:T(8,128)(2,1)S(1)} collective-permute-done((bf16[2,32,2816]{2,1,0:T(8,128)(2,1)S(1)}, bf16[2,32,2816]{2,1,0:T(8,128)(2,1)S(1)}, u32[]{:S(2)}, u32[]{:S(2)}) %collective-permute-start.12) | collective-permute-done | bytes 360480 | tf_op jit(solution)/shard_map/ppermute | solution.py:26
  84.0 2.4 %collective-permute-done.11.down = bf16[32,4096]{1,0:T(8,128)(2,1)S(1)} collective-permute-done((bf16[32,4096]{1,0:T(8,128)(2,1)S(1)}, bf16[32,4096]{1,0:T(8,128)(2,1)S(1)}, u32[]{:S(2)}, u32[]{:S(2)}) %collective-permute-start.11) | collective-permute-done | bytes 262176 | tf_op jit(solution)/shard_map/ppermute | solution.py:26
  90.1 4.4 %collective-permute-done.15.x = bf16[32,2816]{1,0:T(8,128)(2,1)S(1)} collective-permute-done((bf16[32,2816]{1,0:T(8,128)(2,1)S(1)}, bf16[32,2816]{1,0:T(8,128)(2,1)S(1)}, u32[]{:S(2)}, u32[]{:S(2)}) %collective-permute-start.15) | collective-permute-done | bytes 180256 | tf_op jit(solution)/shard_map/ppermute | solution.py:26
  96.7 3.2 %collective-permute-done.16.x = bf16[32,640]{1,0:T(8,128)(2,1)S(1)} collective-permute-done((bf16[32,640]{1,0:T(8,128)(2,1)S(1)}, bf16[32,640]{1,0:T(8,128)(2,1)S(1)}, u32[]{:S(2)}, u32[]{:S(2)}) %collective-permute-start.16) | collective-permute-done | bytes 40992 | tf_op jit(solution)/shard_map/ppermute | solution.py:26
  101.4 2.1 %collective-permute-start.18 = (bf16[32,3328]{1,0:T(8,128)(2,1)S(1)}, bf16[32,3328]{1,0:T(8,128)(2,1)S(1)}, u32[]{:S(2)}, u32[]{:S(2)}) collective-permute-start(bf16[32,3328]{1,0:T(8,128)(2,1)S(1)} %pad_maximum_fusion.refs_0_), channel_id=1, source_target_pairs={{0,32},{1,225},{2,34},{3,227},{4,36},{5,229},{6,38},{7,231},{8,40}... | collective-permute-start | bytes 638984 | tf_op jit(solution)/shard_map/ppermute | solution.py:42
  104.2 3.2 %collective-permute-done.18.refs_1_ = bf16[32,3328]{1,0:T(8,128)(2,1)S(1)} collective-permute-done((bf16[32,3328]{1,0:T(8,128)(2,1)S(1)}, bf16[32,3328]{1,0:T(8,128)(2,1)S(1)}, u32[]{:S(2)}, u32[]{:S(2)}) %collective-permute-start.18) | collective-permute-done | bytes 213024 | tf_op jit(solution)/shard_map/ppermute | solution.py:42
  109.9 3.2 %collective-permute-done.19.refs_2_ = bf16[32,3328]{1,0:T(8,128)(2,1)S(1)} collective-permute-done((bf16[32,3328]{1,0:T(8,128)(2,1)S(1)}, bf16[32,3328]{1,0:T(8,128)(2,1)S(1)}, u32[]{:S(2)}, u32[]{:S(2)}) %collective-permute-start.19) | collective-permute-done | bytes 213024 | tf_op jit(solution)/shard_map/ppermute | solution.py:42
  115.8 3.2 %collective-permute-done.21.refs_3_ = bf16[32,3328]{1,0:T(8,128)(2,1)S(1)} collective-permute-done((bf16[32,3328]{1,0:T(8,128)(2,1)S(1)}, bf16[32,3328]{1,0:T(8,128)(2,1)S(1)}, u32[]{:S(2)}, u32[]{:S(2)}) %collective-permute-start.21) | collective-permute-done | bytes 213024 | tf_op jit(solution)/shard_map/ppermute | solution.py:42
  119.1 3.9 %collective-permute-start.23 = (bf16[32,3328]{1,0:T(8,128)(2,1)S(1)}, bf16[32,3328]{1,0:T(8,128)(2,1)S(1)}, u32[]{:S(2)}, u32[]{:S(2)}) collective-permute-start(bf16[32,3328]{1,0:T(8,128)(2,1)S(1)} %collective-permute-done.21.refs_3_), channel_id=1, source_target_pairs={{0,32},{2,34},{4,36},{6,38},{8,40},{10,42},{12,44},{14,46},{16,48}... | collective-permute-start | bytes 638984 | tf_op jit(solution)/shard_map/ppermute | solution.py:42
  123.6 4.4 %collective-permute-done.23.refs_4_ = bf16[32,3328]{1,0:T(8,128)(2,1)S(1)} collective-permute-done((bf16[32,3328]{1,0:T(8,128)(2,1)S(1)}, bf16[32,3328]{1,0:T(8,128)(2,1)S(1)}, u32[]{:S(2)}, u32[]{:S(2)}) %collective-permute-start.23) | collective-permute-done | bytes 213024 | tf_op jit(solution)/shard_map/ppermute | solution.py:42
  128.0 3.1 %collective-permute-start.26 = (bf16[32,3328]{1,0:T(8,128)(2,1)S(1)}, bf16[32,3328]{1,0:T(8,128)(2,1)S(1)}, u32[]{:S(2)}, u32[]{:S(2)}) collective-permute-start(bf16[32,3328]{1,0:T(8,128)(2,1)S(1)} %collective-permute-done.23.refs_4_), channel_id=1, source_target_pairs={{0,16},{2,18},{4,20},{6,22},{8,24},{10,26},{12,28},{14,30},{16,0},... | collective-permute-start | bytes 638984 | tf_op jit(solution)/shard_map/ppermute | solution.py:42
  131.1 4.6 %collective-permute-done.26.refs_9_ = bf16[32,3328]{1,0:T(8,128)(2,1)S(1)} collective-permute-done((bf16[32,3328]{1,0:T(8,128)(2,1)S(1)}, bf16[32,3328]{1,0:T(8,128)(2,1)S(1)}, u32[]{:S(2)}, u32[]{:S(2)}) %collective-permute-start.26) | collective-permute-done | bytes 213024 | tf_op jit(solution)/shard_map/ppermute | solution.py:42
  135.7 2.2 %shard_map.108 = (bf16[4,32,1024]{2,1,0:T(8,128)(2,1)S(1)}, bf16[4,32,1024]{2,1,0:T(8,128)(2,1)S(1)}) custom-call(bf16[32,3328]{1,0:T(8,128)(2,1)S(1)} %pad_maximum_fusion.refs_0_, bf16[32,3328]{1,0:T(8,128)(2,1)S(1)} %collective-permute-done.18.refs_1_, bf16[32,3328]{1,0:T(8,128)(2,1)S(1)} %collective-permute-done.19.refs_2_, ...), custom_call_target="tpu_custom_call" | custom-call | tf_op jit(solution)/shard_map/pallas_call | solution.py:483
  139.6 14.7 %all_to_all.11.parts = bf16[8,32,1024]{2,1,0:T(8,128)(2,1)S(1)} all-to-all(bf16[8,32,1024]{2,1,0:T(8,128)(2,1)S(1)} %shard_map.109), channel_id=1, replica_groups={{0,2,4,6,8,10,12,14},{1,3,5,7,9,11,13,15},{16,18,20,22,24,26,28,30},{17..., dimensions={0} | all-to-all | bytes 1048576 | tf_op jit(solution)/shard_map/all_to_all | solution.py:58
  (51 shorter events, 30.7 us)
Async XLA Ops:
  1.4 8.6 %collective-permute-start.1 = (bf16[1664,1024]{1,0:T(8,128)(2,1)}, bf16[1664,1024]{1,0:T(8,128)(2,1)S(1)}, u32[]{:S(2)}, u32[]{:S(2)}) collective-permute-start(bf16[1664,1024]{1,0:T(8,128)(2,1)} %refs_10_), channel_id=1, source_target_pairs={{0,1},{1,0},{2,3},{3,2},{4,5},{5,4},{6,7},{7,6},{8,9},{9,8},{10,11... | collective-permute-start | bytes 10223624 | tf_op jit(solution)/shard_map/ppermute | solution.py:26
  1.5 8.5 %collective-permute-start = (bf16[48,1152]{1,0:T(8,128)(2,1)S(1)}, bf16[48,1152]{1,0:T(8,128)(2,1)S(1)}, u32[]{:S(2)}, u32[]{:S(2)}) collective-permute-start(bf16[48,1152]{1,0:T(8,128)(2,1)S(1)} %shard_map.100), channel_id=1, source_target_pairs={{0,0},{1,16},{2,32},{3,48},{4,64},{5,80},{6,96},{7,112},{8,128},{9... | collective-permute-start | bytes 331784 | tf_op jit(solution)/shard_map/ppermute | solution.py:50
  52.4 7.6 %collective-permute-start.3 = (bf16[32,2816]{1,0:T(8,128)(2,1)S(1)}, bf16[32,2816]{1,0:T(8,128)(2,1)S(1)}, u32[]{:S(2)}, u32[]{:S(2)}) collective-permute-start(bf16[32,2816]{1,0:T(8,128)(2,1)S(1)} %get-tuple-element.85), channel_id=1, source_target_pairs={{0,16},{16,0},{32,48},{48,32},{64,80},{80,64},{96,112},{112,96},{1... | collective-permute-start | bytes 540680 | tf_op jit(solution)/shard_map/ppermute | solution.py:26
  54.7 13.1 %collective-permute-start.6 = (bf16[2,32,2816]{2,1,0:T(8,128)(2,1)S(1)}, bf16[2,32,2816]{2,1,0:T(8,128)(2,1)S(1)}, u32[]{:S(2)}, u32[]{:S(2)}) collective-permute-start(bf16[2,32,2816]{2,1,0:T(8,128)(2,1)S(1)} %get-tuple-element.90), channel_id=1, source_target_pairs={{0,16},{16,0},{32,48},{48,32},{64,80},{80,64},{96,112},{112,96},{1... | collective-permute-start | bytes 1081352 | tf_op jit(solution)/shard_map/ppermute | solution.py:26
  60.1 6.8 %collective-permute-start.4 = (bf16[32,2816]{1,0:T(8,128)(2,1)S(1)}, bf16[32,2816]{1,0:T(8,128)(2,1)S(1)}, u32[]{:S(2)}, u32[]{:S(2)}) collective-permute-start(bf16[32,2816]{1,0:T(8,128)(2,1)S(1)} %shard_map.102), channel_id=1, source_target_pairs={{0,32},{16,48},{32,64},{48,80},{64,96},{80,112},{96,128},{112,144}... | collective-permute-start | bytes 540680 | tf_op jit(solution)/shard_map/ppermute | solution.py:26
  61.4 14.1 %collective-permute-start.9 = (bf16[2,32,2816]{2,1,0:T(8,128)(2,1)S(1)}, bf16[2,32,2816]{2,1,0:T(8,128)(2,1)S(1)}, u32[]{:S(2)}, u32[]{:S(2)}) collective-permute-start(bf16[2,32,2816]{2,1,0:T(8,128)(2,1)S(1)} %get-tuple-element.99), channel_id=1, source_target_pairs={{0,16},{16,0},{32,48},{48,32},{64,80},{80,64},{96,112},{112,96},{1... | collective-permute-start | bytes 1081352 | tf_op jit(solution)/shard_map/ppermute | solution.py:26
  62.5 4.4 %collective-permute-start.5 = (bf16[32,1280]{1,0:T(8,128)(2,1)S(1)}, bf16[32,1280]{1,0:T(8,128)(2,1)S(1)}, u32[]{:S(2)}, u32[]{:S(2)}) collective-permute-start(bf16[32,1280]{1,0:T(8,128)(2,1)S(1)} %get-tuple-element.89), channel_id=1, source_target_pairs={{0,224},{16,240},{32,0},{48,16},{64,32},{80,48},{96,64},{112,80},{... | collective-permute-start | bytes 245768 | tf_op jit(solution)/shard_map/ppermute | solution.py:26
  67.9 7.6 %collective-permute-start.7 = (bf16[32,4096]{1,0:T(8,128)(2,1)S(1)}, bf16[32,4096]{1,0:T(8,128)(2,1)S(1)}, u32[]{:S(2)}, u32[]{:S(2)}) collective-permute-start(bf16[32,4096]{1,0:T(8,128)(2,1)S(1)} %get-tuple-element.97), channel_id=1, source_target_pairs={{0,32},{16,48},{32,64},{48,80},{64,96},{80,112},{96,128},{112,144}... | collective-permute-start | bytes 786440 | tf_op jit(solution)/shard_map/ppermute | solution.py:26
  69.7 7.6 %collective-permute-start.8 = (bf16[32,4096]{1,0:T(8,128)(2,1)S(1)}, bf16[32,4096]{1,0:T(8,128)(2,1)S(1)}, u32[]{:S(2)}, u32[]{:S(2)}) collective-permute-start(bf16[32,4096]{1,0:T(8,128)(2,1)S(1)} %get-tuple-element.98), channel_id=1, source_target_pairs={{0,224},{16,240},{32,0},{48,16},{64,32},{80,48},{96,64},{112,80},{... | collective-permute-start | bytes 786440 | tf_op jit(solution)/shard_map/ppermute | solution.py:26
  70.0 12.7 %collective-permute-start.12 = (bf16[2,32,2816]{2,1,0:T(8,128)(2,1)S(1)}, bf16[2,32,2816]{2,1,0:T(8,128)(2,1)S(1)}, u32[]{:S(2)}, u32[]{:S(2)}) collective-permute-start(bf16[2,32,2816]{2,1,0:T(8,128)(2,1)S(1)} %get-tuple-element.108), channel_id=1, source_target_pairs={{0,16},{16,0},{32,48},{48,32},{64,80},{80,64},{96,112},{112,96},{1... | collective-permute-start | bytes 1081352 | tf_op jit(solution)/shard_map/ppermute | solution.py:26
  77.5 6.4 %collective-permute-start.10 = (bf16[32,4096]{1,0:T(8,128)(2,1)S(1)}, bf16[32,4096]{1,0:T(8,128)(2,1)S(1)}, u32[]{:S(2)}, u32[]{:S(2)}) collective-permute-start(bf16[32,4096]{1,0:T(8,128)(2,1)S(1)} %get-tuple-element.106), channel_id=1, source_target_pairs={{0,32},{16,48},{32,64},{48,80},{64,96},{80,112},{96,128},{112,144}... | collective-permute-start | bytes 786440 | tf_op jit(solution)/shard_map/ppermute | solution.py:26
  79.6 6.7 %collective-permute-start.11 = (bf16[32,4096]{1,0:T(8,128)(2,1)S(1)}, bf16[32,4096]{1,0:T(8,128)(2,1)S(1)}, u32[]{:S(2)}, u32[]{:S(2)}) collective-permute-start(bf16[32,4096]{1,0:T(8,128)(2,1)S(1)} %get-tuple-element.107), channel_id=1, source_target_pairs={{0,224},{16,240},{32,0},{48,16},{64,32},{80,48},{96,64},{112,80},{... | collective-permute-start | bytes 786440 | tf_op jit(solution)/shard_map/ppermute | solution.py:26
  86.5 8.0 %collective-permute-start.13 = (bf16[32,4096]{1,0:T(8,128)(2,1)S(1)}, bf16[32,4096]{1,0:T(8,128)(2,1)S(1)}, u32[]{:S(2)}, u32[]{:S(2)}) collective-permute-start(bf16[32,4096]{1,0:T(8,128)(2,1)S(1)} %get-tuple-element.112), channel_id=1, source_target_pairs={{0,32},{16,48},{32,64},{48,80},{64,96},{80,112},{96,128},{112,144}... | collective-permute-start | bytes 786440 | tf_op jit(solution)/shard_map/ppermute | solution.py:26
  88.6 7.0 %collective-permute-start.14 = (bf16[32,4096]{1,0:T(8,128)(2,1)S(1)}, bf16[32,4096]{1,0:T(8,128)(2,1)S(1)}, u32[]{:S(2)}, u32[]{:S(2)}) collective-permute-start(bf16[32,4096]{1,0:T(8,128)(2,1)S(1)} %get-tuple-element.113), channel_id=1, source_target_pairs={{0,224},{16,240},{32,0},{48,16},{64,32},{80,48},{96,64},{112,80},{... | collective-permute-start | bytes 786440 | tf_op jit(solution)/shard_map/ppermute | solution.py:26
  88.6 5.9 %collective-permute-start.15 = (bf16[32,2816]{1,0:T(8,128)(2,1)S(1)}, bf16[32,2816]{1,0:T(8,128)(2,1)S(1)}, u32[]{:S(2)}, u32[]{:S(2)}) collective-permute-start(bf16[32,2816]{1,0:T(8,128)(2,1)S(1)} %get-tuple-element.114), channel_id=1, source_target_pairs={{0,16},{16,0},{32,48},{48,32},{64,80},{80,64},{96,112},{112,96},{1... | collective-permute-start | bytes 540680 | tf_op jit(solution)/shard_map/ppermute | solution.py:26
  101.4 5.9 %collective-permute-start.18 = (bf16[32,3328]{1,0:T(8,128)(2,1)S(1)}, bf16[32,3328]{1,0:T(8,128)(2,1)S(1)}, u32[]{:S(2)}, u32[]{:S(2)}) collective-permute-start(bf16[32,3328]{1,0:T(8,128)(2,1)S(1)} %pad_maximum_fusion.refs_0_), channel_id=1, source_target_pairs={{0,32},{1,225},{2,34},{3,227},{4,36},{5,229},{6,38},{7,231},{8,40}... | collective-permute-start | bytes 638984 | tf_op jit(solution)/shard_map/ppermute | solution.py:42
  103.5 6.5 %collective-permute-start.20 = (bf16[32,3328]{1,0:T(8,128)(2,1)S(1)}, bf16[32,3328]{1,0:T(8,128)(2,1)S(1)}, u32[]{:S(2)}, u32[]{:S(2)}) collective-permute-start(bf16[32,3328]{1,0:T(8,128)(2,1)S(1)} %pad_maximum_fusion.refs_0_), channel_id=1, source_target_pairs={{1,17},{3,19},{5,21},{7,23},{9,25},{11,27},{13,29},{15,31},{17,1},... | collective-permute-start | bytes 638984 | tf_op jit(solution)/shard_map/ppermute | solution.py:42
  107.3 5.8 %collective-permute-start.19 = (bf16[32,3328]{1,0:T(8,128)(2,1)S(1)}, bf16[32,3328]{1,0:T(8,128)(2,1)S(1)}, u32[]{:S(2)}, u32[]{:S(2)}) collective-permute-start(bf16[32,3328]{1,0:T(8,128)(2,1)S(1)} %collective-permute-done.18.refs_1_), channel_id=1, source_target_pairs={{0,32},{1,225},{2,34},{3,227},{4,36},{5,229},{6,38},{7,231},{8,40}... | collective-permute-start | bytes 638984 | tf_op jit(solution)/shard_map/ppermute | solution.py:42
  109.3 6.5 %collective-permute-start.22 = (bf16[32,3328]{1,0:T(8,128)(2,1)S(1)}, bf16[32,3328]{1,0:T(8,128)(2,1)S(1)}, u32[]{:S(2)}, u32[]{:S(2)}) collective-permute-start(bf16[32,3328]{1,0:T(8,128)(2,1)S(1)} %collective-permute-done.18.refs_1_), channel_id=1, source_target_pairs={{0,16},{1,17},{2,18},{3,19},{4,20},{5,21},{6,22},{7,23},{8,24},{9,... | collective-permute-start | bytes 638984 | tf_op jit(solution)/shard_map/ppermute | solution.py:42
  113.2 5.9 %collective-permute-start.21 = (bf16[32,3328]{1,0:T(8,128)(2,1)S(1)}, bf16[32,3328]{1,0:T(8,128)(2,1)S(1)}, u32[]{:S(2)}, u32[]{:S(2)}) collective-permute-start(bf16[32,3328]{1,0:T(8,128)(2,1)S(1)} %collective-permute-done.19.refs_2_), channel_id=1, source_target_pairs={{0,32},{1,225},{2,34},{3,227},{4,36},{5,229},{6,38},{7,231},{8,40}... | collective-permute-start | bytes 638984 | tf_op jit(solution)/shard_map/ppermute | solution.py:42
  115.2 8.4 %collective-permute-start.24 = (bf16[32,3328]{1,0:T(8,128)(2,1)S(1)}, bf16[32,3328]{1,0:T(8,128)(2,1)S(1)}, u32[]{:S(2)}, u32[]{:S(2)}) collective-permute-start(bf16[32,3328]{1,0:T(8,128)(2,1)S(1)} %collective-permute-done.19.refs_2_), channel_id=1, source_target_pairs={{0,16},{1,17},{2,18},{3,19},{4,20},{5,21},{6,22},{7,23},{8,24},{9,... | collective-permute-start | bytes 638984 | tf_op jit(solution)/shard_map/ppermute | solution.py:42
  119.1 8.9 %collective-permute-start.23 = (bf16[32,3328]{1,0:T(8,128)(2,1)S(1)}, bf16[32,3328]{1,0:T(8,128)(2,1)S(1)}, u32[]{:S(2)}, u32[]{:S(2)}) collective-permute-start(bf16[32,3328]{1,0:T(8,128)(2,1)S(1)} %collective-permute-done.21.refs_3_), channel_id=1, source_target_pairs={{0,32},{2,34},{4,36},{6,38},{8,40},{10,42},{12,44},{14,46},{16,48}... | collective-permute-start | bytes 638984 | tf_op jit(solution)/shard_map/ppermute | solution.py:42
  122.9 8.2 %collective-permute-start.25 = (bf16[32,3328]{1,0:T(8,128)(2,1)S(1)}, bf16[32,3328]{1,0:T(8,128)(2,1)S(1)}, u32[]{:S(2)}, u32[]{:S(2)}) collective-permute-start(bf16[32,3328]{1,0:T(8,128)(2,1)S(1)} %collective-permute-done.21.refs_3_), channel_id=1, source_target_pairs={{0,16},{1,17},{2,18},{3,19},{4,20},{5,21},{6,22},{7,23},{8,24},{9,... | collective-permute-start | bytes 638984 | tf_op jit(solution)/shard_map/ppermute | solution.py:42
  128.0 7.7 %collective-permute-start.26 = (bf16[32,3328]{1,0:T(8,128)(2,1)S(1)}, bf16[32,3328]{1,0:T(8,128)(2,1)S(1)}, u32[]{:S(2)}, u32[]{:S(2)}) collective-permute-start(bf16[32,3328]{1,0:T(8,128)(2,1)S(1)} %collective-permute-done.23.refs_4_), channel_id=1, source_target_pairs={{0,16},{2,18},{4,20},{6,22},{8,24},{10,26},{12,28},{14,30},{16,0},... | collective-permute-start | bytes 638984 | tf_op jit(solution)/shard_map/ppermute | solution.py:42
  (6 other events, 137.7 us)

commit v7 on v4

--- a/solution.py
+++ b/solution.py
@@ -148,13 +148,26 @@
 FAR = 4
 
 
-def project_kernel(tiles, early, length_ref, gain_ref, mine_ref, theirs_ref, gate_hbm, up_hbm, *refs):
-    own_ref, give, kept, far_low, far_high = refs[0], refs[1:6], refs[6:13], refs[13], refs[14]
-    residual, rows, squares, gain, gate_ref, up_ref, sems = refs[15:]
+ORDER = [(s, 1) for s in (FAR, 3, 5, 2, 6, 1, 7, 0)] + [(s, 0) for s in range(ZN)]
+FIRST = 3
+
+
+def products(rows, squares, gate_ref, up_ref, ready):
+    tiles = gate_ref.shape[1] // LANE
+    for base, ref in ((0, gate_ref), (tiles, up_ref)):
+        ready(ref)
+        for t in range(0, tiles, 2):
+            lanes = slice(t * LANE, min(t + 2, tiles) * LANE)
+            product = jnp.dot(rows[...], ref[:, lanes], preferred_element_type=F32).astype(BF)
+            yield slice((base + t) * LANE, (base + t) * LANE + product.shape[1]), product
+    yield slice(2 * tiles * LANE, (2 * tiles + 1) * LANE), squares[...]
+
+
+def first_kernel(length_ref, gain_ref, mine_ref, theirs_ref, gate_hbm, up_hbm, *refs):
+    own_ref, rows, squares, gate_ref, up_ref, far_ref, next_ref, residual, gain, sems = refs
     n = ROWS_DEV
     width = own_ref.shape[1]
     half = width // 2
-    wide = 2 * tiles + 1
     batch_index, mp_index = lax.axis_index("batch"), lax.axis_index("mp")
     z, core = batch_index >> 1, mp_index & 1
     flip = (batch_index & 1) ^ core
@@ -164,25 +177,6 @@
     fetch.start()
     fetch_gate.start()
     fetch_up.start()
-
-    def put(s, j, tile, value):
-        lanes = slice(tile * LANE, (tile + 1) * LANE)
-        if tile < early:
-            if j == 1 and s in (0, FAR):
-                give[s][:, lanes] = value
-            elif j == 1:
-                give[min(s, ZN - s)][0 if s < FAR else 1, :, lanes] = value
-            elif s == FAR:
-                far_low[:, lanes] = value
-            else:
-                kept[s if s < FAR else s - 1][:, lanes] = value
-        else:
-            late = tile - early + j * (wide - early)
-            if s == FAR:
-                far_high[:, late * LANE : (late + 1) * LANE] = value
-            else:
-                late += early
-                kept[s if s < FAR else s - 1][:, late * LANE : (late + 1) * LANE] = value
 
     blocks = [(ref, i) for ref in (mine_ref, theirs_ref) for i in range(ZN)]
     options = ROWS_DEV - PREFIX
@@ -232,7 +226,10 @@
             residual[i, 16:] = last
         s = (i - z) & (ZN - 1)
         j = flip if ref is mine_ref else 1 - flip
-        at = pl.multiple_of(s * 2 * n + j * n, n)
+        position = ZN + s
+        for index, (target, _) in enumerate(ORDER[:ZN]):
+            position = jnp.where((s == target) & (j == 1), index, position)
+        at = pl.multiple_of(position * n, n)
         for part, offset in ((first, 0), (last, 16)):
             x = part.astype(F32)
             into = pl.ds(pl.multiple_of(at + offset, 16), 16)
@@ -243,116 +240,115 @@
                 total = total + square[:, lane * LANE : (lane + 1) * LANE]
             squares[into, :] = total.astype(BF)
     own_ref[...] = residual[mp_index >> 1]
-
-    for first, ref, at in [
-        (base + t, ref, t) for base, ref in ((0, gate_ref), (tiles, up_ref)) for t in range(0, tiles, 2)
-    ] + [(wide - 1, None, 0)]:
-        if at == 0 and ref is not None:
-            (fetch_gate if ref is gate_ref else fetch_up).wait()
-        if ref is None:
-            product = squares[...]
-        else:
-            lanes = slice(at * LANE, min(at + 2, tiles) * LANE)
-            product = jnp.dot(rows[...], ref[:, lanes], preferred_element_type=F32).astype(BF)
-        for t in range(product.shape[1] // LANE):
-            for s in range(ZN):
-                for j in range(2):
-                    begin = (2 * s + j) * n
-                    put(s, j, first + t, product[begin : begin + n, t * LANE : (t + 1) * LANE])
-
-
-EARLY = 22
+    early = slice(0, FIRST * n)
+    ready = lambda ref: (fetch_gate if ref is gate_ref else fetch_up).wait()
+    for lanes, value in products(rows.at[early], squares.at[early], gate_ref, up_ref, ready):
+        far_ref[:, lanes] = value[:n]
+        next_ref[0, :, lanes] = value[n : 2 * n]
+        next_ref[1, :, lanes] = value[2 * n :]
+
+
+def rest_kernel(rows, squares, gate_ref, up_ref, give2, give1, give0, *kept):
+    n = ROWS_DEV
+    into = [give2.at[0], give2.at[1], give1.at[0], give1.at[1], give0, *kept]
+    late = slice(FIRST * n, len(ORDER) * n)
+    for lanes, value in products(rows.at[late], squares.at[late], gate_ref, up_ref, lambda ref: None):
+        for i, ref in enumerate(into):
+            ref[:, lanes] = value[i * n : (i + 1) * n]
 
 
 def project(prefix_len, norm_gain, mine, theirs, gate_weight, up_weight):
     width, hidden_width = gate_weight.shape
-    tiles = hidden_width // LANE
     n = ROWS_DEV
-    low = (n, EARLY * LANE)
-    high = (n, 2 * (2 * tiles + 1 - EARLY) * LANE)
-    whole = (n, low[1] + high[1])
-    own = (n, width)
-    refs = pl.pallas_call(
-        lambda *refs: project_kernel(tiles, EARLY, *refs),
+    part = (n, 2 * hidden_width + LANE)
+    all_rows = len(ORDER) * n
+    own, rows, squares, gate, up, far, following = pl.pallas_call(
+        first_kernel,
         out_shape=in_vmem(
-            (own, BF), (low, BF), *[((2, *low), BF)] * 3, (low, BF), *[(whole, BF)] * 7, (low, BF), (high, BF)
+            ((n, width), BF),
+            ((all_rows, width), BF),
+            ((all_rows, LANE), BF),
+            (gate_weight.shape, BF),
+            (up_weight.shape, BF),
+            (part, BF),
+            ((2, *part), BF),
         ),
         in_specs=[SMEM, HBM, VMEM, VMEM, HBM, HBM],
-        out_specs=(VMEM,) * 15,
+        out_specs=(VMEM,) * 7,
         scratch_shapes=[
             pltpu.VMEM((ZN, n, width), BF),
-            pltpu.VMEM((2 * ZN * n, width), BF),
-            pltpu.VMEM((2 * ZN * n, LANE), BF),
             pltpu.VMEM((width,), F32),
-            pltpu.VMEM(gate_weight.shape, BF),
-            pltpu.VMEM(up_weight.shape, BF),
             pltpu.SemaphoreType.DMA((3,)),
         ],
         compiler_params=PARAMS,
     )(prefix_len, in_hbm(norm_gain), mine, theirs, in_hbm(gate_weight), in_hbm(up_weight))
-    kept = list(refs[6:13])
-    return refs[0], refs[1:6], kept[:4] + [None] + kept[4:], refs[13], refs[14]
-
-
-def add_first_kernel(low_ref, x_ref, out_ref):
-    out_ref[...] = (low_ref[...].astype(F32) + x_ref[...].astype(F32)).astype(BF)
+    give2, give1, give0, *kept = local(
+        rest_kernel,
+        [((2, *part), BF)] * 2 + [(part, BF)] * 9,
+        rows,
+        squares,
+        gate,
+        up,
+        cost=cost((len(ORDER) - FIRST) * n, width, part[1]),
+    )
+    return own, [give0, give1, give2, following, far], kept
+
+
+def summed(*refs):
+    total = refs[0].astype(F32)
+    for ref in refs[1:]:
+        total = total + ref.astype(F32)
+    return total.astype(BF)
+
+
+def add_first_kernel(mine, x, out_up, out_down):
+    low = out_up.shape[1]
+    out_up[...] = summed(mine[:, :low], x[:, :low])
+    out_down[...] = summed(mine[:, low:], x[:, low:])
 
 
 def add_far_kernel(mine_up, mine_down, x, up, down, out_up, out_down):
-    low = x.shape[2]
-    out_up[:, :low] = (
-        mine_up[:, :low].astype(F32) + x[0].astype(F32) + up[...].astype(F32)
-    ).astype(BF)
-    out_up[:, low:] = mine_up[:, low:]
-    out_down[:, :low] = (mine_down[:, :low].astype(F32) + x[1].astype(F32)).astype(BF)
-    out_down[:, low:] = (mine_down[:, low:].astype(F32) + down[...].astype(F32)).astype(BF)
+    low = up.shape[1]
+    out_up[:, :low] = summed(mine_up[:, :low], x[0, :, :low], up[...])
+    out_up[:, low:] = summed(mine_up[:, low:], x[0, :, low:])
+    out_down[:, :low] = summed(mine_down[:, :low], x[1, :, :low])
+    out_down[:, low:] = summed(mine_down[:, low:], x[1, :, low:], down[...])
 
 
 def add_ring_kernel(mine_up, mine_down, x, up, down, out_up, out_down):
-    low = x.shape[2]
-    for mine, i, come, out in ((mine_up, 0, up, out_up), (mine_down, 1, down, out_down)):
-        out[:, :low] = (
-            mine[:, :low].astype(F32) + x[i].astype(F32) + come[:, :low].astype(F32)
-        ).astype(BF)
-        out[:, low:] = (mine[:, low:].astype(F32) + come[:, low:].astype(F32)).astype(BF)
-
-
-def add_last_kernel(mine, x, up, down, keep, give):
-    low, wide = x.shape[1], keep.shape[1]
-    keep[:, :low] = (
-        mine[:, :low].astype(F32)
-        + x[...].astype(F32)
-        + up[:, :low].astype(F32)
-        + down[:, :low].astype(F32)
+    out_up[...] = summed(mine_up[...], x[0], up[...])
+    out_down[...] = summed(mine_down[...], x[1], down[...])
+
+
+def gated_kernel(mine, x, up, down, out):
+    width = out.shape[1]
+
+    def total(lanes):
+        parts = [ref[:, lanes].astype(F32) for ref in (mine, x, up, down)]
+        return (parts[0] + parts[1]) + (parts[2] + parts[3])
+
+    squares = total(slice(2 * width, 2 * width + LANE))
+    scale = lax.rsqrt(jnp.sum(squares, axis=1, keepdims=True) * F32(1 / 16384) + 1e-05)
+    gate = total(slice(0, width)) * scale
+    lift = total(slice(width, 2 * width)) * scale
+    out[...] = (gate / (1 + jnp.exp(-gate)) * lift).astype(BF)
+
+
+def cost(rows, depth, columns):
+    return pl.CostEstimate(
+        flops=2 * rows * depth * columns, bytes_accessed=2 * depth * columns, transcendentals=0
     )
-    keep[:, low:] = (
-        mine[:, low:wide].astype(F32) + up[:, low:wide].astype(F32) + down[:, low:wide].astype(F32)
-    )
-    give[...] = (
-        mine[:, wide:].astype(F32) + up[:, wide:].astype(F32) + down[:, wide:].astype(F32)
-    ).astype(BF)
-
-
-def local(kernel, shapes, *args):
+
+
+def local(kernel, shapes, *args, cost=None):
     return pl.pallas_call(
         kernel,
         out_shape=in_vmem(*shapes),
         in_specs=[VMEM] * len(args),
         out_specs=(VMEM,) * len(shapes) if len(shapes) > 1 else VMEM,
         compiler_params=PARAMS,
+        cost_estimate=cost,
     )(*args)
-
-
-def gated_kernel(keep, x, out):
-    hidden_width = out.shape[1]
-    wide = keep.shape[1]
-    low = wide - x.shape[1]
-    late = keep[:, low:] + x[...].astype(F32)
-    squares = late[:, 2 * hidden_width - low :]
-    scale = lax.rsqrt(jnp.sum(squares, axis=1, keepdims=True) * F32(1 / 16384) + 1e-05)
-    gate = keep[:, :hidden_width] * scale
-    lift = jnp.concatenate([keep[:, hidden_width:low], late[:, : 2 * hidden_width - low]], axis=1) * scale
-    out[...] = (gate / (1 + jnp.exp(-gate)) * lift).astype(BF)
 
 
 def down_kernel(*refs):
@@ -430,37 +426,32 @@
     came = transpose_mesh(sent)
     mine = over_plane(jnp.broadcast_to(came[None], (ZN, *came.shape)))
     theirs = core_pair(mine)
-    own, give, kept, far_low, far_high = project(
-        prefix_len, norm_gain, mine, theirs, gate_weight, up_weight
-    )
-    low, whole = far_low.shape, kept[0].shape
+    own, give, kept = project(prefix_len, norm_gain, mine, theirs, gate_weight, up_weight)
+    part = kept[0].shape
+    half = (part[1] // LANE) // 2 * LANE
+    ends = [((rows, half), BF), ((rows, part[1] - half), BF)]
 
     far, ahead = after(give[4], give[3])
-    far, x = x_pair(far), x_pair(ahead)
-    up, down, ahead = after(local(add_first_kernel, [(low, BF)], far_low, far), far_high, give[2])
-    up, down, following = along_z(up, 1), along_z(down, -1), x_pair(ahead)
-    up, down, x = after(up, down, x)
-    up, down = local(add_far_kernel, [(whole, BF)] * 2, kept[3], kept[5], x, up, down)
-    for step in (2, 1):
-        up, down, ahead = after(up, down, give[step - 1])
+    far, following = x_pair(far), x_pair(ahead)
+    up, down = local(add_first_kernel, ends, kept[4], far)
+    for step in (4, 3, 2, 1):
+        up, down, ahead = after(up, down, give[step - 2] if step > 1 else give[0])
         x = following
-        up, down, following = along_z(up, 1), along_z(down, -1), x_pair(ahead)
+        if step > 1:
+            following = x_pair(ahead)
+        up, down = along_z(up, 1), along_z(down, -1)
         up, down, x = after(up, down, x)
-        up, down = local(
-            add_ring_kernel, [(whole, BF)] * 2, kept[step], kept[ZN - step], x, up, down
-        )
-    up, down = after(up, down)
-    up, down, x = after(along_z(up, 1), along_z(down, -1), following)
-    late = whole[1] - 2 * hidden_width - LANE
-    keep, last = local(
-        add_last_kernel,
-        [((rows, 2 * hidden_width + LANE), F32), ((rows, late), BF)],
-        kept[0],
-        x,
-        up,
-        down,
-    )
-    hidden = local(gated_kernel, [((rows, hidden_width), BF)], keep, x_pair(last))
+        if step > 1:
+            up, down = local(
+                add_far_kernel if step == 4 else add_ring_kernel,
+                [(part, BF)] * 2,
+                kept[step - 1],
+                kept[ZN + 1 - step],
+                x,
+                up,
+                down,
+            )
+    hidden = local(gated_kernel, [((rows, hidden_width), BF)], kept[0], x, up, down)
 
     up, down, across = hidden, hidden, hidden
     blocks, partners = [hidden], []

time: 151 us -> 148 us (0.980)
  starting transfers between devices: 32.7 us -> 31 us
    pallas_call x7, Pallas kernels: 0.89 us -> 4.15 us  [local(): pl.pallas_call(kernel, out_shape=in_vmem(*shapes), in_specs=[VMEM] * len(...]
    pallas_call x1, Pallas kernels: 7.61 us -> 4.36 us  [project(): pl.pallas_call(first_kernel, out_shape=in_vmem(((n, width), BF), ((all_ro...]
    ppermute x29 -> x28, starting transfers between devices: 29.7 us -> 28 us  [permute(): return lax.ppermute(value, axis, [(i, target(i)) for i in range(count)])]
    ppermute x29 -> x28, waiting for transfers between devices: 53.5 us -> 52.1 us  [permute(): return lax.ppermute(value, axis, [(i, target(i)) for i in range(count)])]
  transfers between devices with their start and end apart: 30 -> 29, of which waited for: 22 -> 22; matrix products, arithmetic and copies ran while one was open for 0% -> 0% of each run, Pallas kernels for 0% -> 3%
where the time goes in v7:
time: 148 us
  waiting for transfers between devices  57.7 us (39%)
  blocking collectives  45.9 us (31%)
  starting transfers between devices  31 us (21%)
  Pallas kernels  12.8 us (9%)
    ppermute x28, waiting for transfers between devices, permute(): return lax.ppermute(value, axis, [(i, target(i)) for i in range(count)])  52.1 us
    all_to_all x2, blocking collectives, over_plane(): lax.all_to_all(value, 'mp', 0, 0, axis_index_groups=PLANE, tiled=True)  45.9 us
    ppermute x28, starting transfers between devices, permute(): return lax.ppermute(value, axis, [(i, target(i)) for i in range(count)])  28 us
    ppermute x1, waiting for transfers between devices, transpose_mesh(): lax.ppermute(value, ('batch', 'mp'), [(b * 16 + m, m * 16 + b) for b in r...  5.62 us
    pallas_call x1, Pallas kernels, project(): pl.pallas_call(first_kernel, out_shape=in_vmem(((n, width), BF), ((all_ro...  4.36 us
    pallas_call x7, Pallas kernels, local(): pl.pallas_call(kernel, out_shape=in_vmem(*shapes), in_specs=[VMEM] * len(...  4.15 us
    ppermute x1, starting transfers between devices, transpose_mesh(): lax.ppermute(value, ('batch', 'mp'), [(b * 16 + m, m * 16 + b) for b in r...  3.03 us
  transfers between devices with their start and end apart: 29, of which 22 were waited for; matrix products, arithmetic and copies ran while one was open for 0% of the time, Pallas kernels for 3%

profile of v7, /device:TPU:32, one launch (start us, length us, event | category | flops | bytes accessed | tf_op | source)
XLA Modules:
  0.0 147.7 jit_solution(17549784962714491213)
XLA Ops:
  1.4 3.0 %collective-permute-start = (bf16[48,1152]{1,0:T(8,128)(2,1)S(1)}, bf16[48,1152]{1,0:T(8,128)(2,1)S(1)}, u32[]{:S(2)}, u32[]{:S(2)}) collective-permute-start(bf16[48,1152]{1,0:T(8,128)(2,1)S(1)} %shard_map.100), channel_id=1, source_target_pairs={{0,0},{1,16},{2,32},{3,48},{4,64},{5,80},{6,96},{7,112},{8,128},{9... | collective-permute-start | bytes 331784 | tf_op jit(solution)/shard_map/ppermute | solution.py:42
  4.5 5.6 %collective-permute-done = bf16[48,1152]{1,0:T(8,128)(2,1)S(1)} collective-permute-done((bf16[48,1152]{1,0:T(8,128)(2,1)S(1)}, bf16[48,1152]{1,0:T(8,128)(2,1)S(1)}, u32[]{:S(2)}, u32[]{:S(2)}) %collective-permute-start) | collective-permute-done | bytes 110624 | tf_op jit(solution)/shard_map/ppermute | solution.py:42
  10.1 31.4 %all_to_all.10.mine_ref = bf16[8,48,1152]{2,1,0:T(8,128)(2,1)S(1)} all-to-all(bf16[8,48,1152]{2,1,0:T(8,128)(2,1)S(1)} %broadcast_in_dim.2), channel_id=1, replica_groups={{0,2,4,6,8,10,12,14},{1,3,5,7,9,11,13,15},{16,18,20,22,24,26,28,30},{17..., dimensions={0} | all-to-all | bytes 1769472 | tf_op jit(solution)/shard_map/all_to_all | solution.py:50
  41.6 2.4 %collective-permute-done.1.theirs_ref = bf16[8,48,1152]{2,1,0:T(8,128)(2,1)S(1)} collective-permute-done((bf16[8,48,1152]{2,1,0:T(8,128)(2,1)S(1)}, bf16[8,48,1152]{2,1,0:T(8,128)(2,1)S(1)}, u32[]{:S(2)}, u32[]{:S(2)}) %collective-permute-start.1) | collective-permute-done | bytes 884768 | tf_op jit(solution)/shard_map/ppermute | solution.py:26
  44.0 4.4 %shard_map.101 = (bf16[32,1024]{1,0:T(8,128)(2,1)S(1)}, bf16[512,1024]{1,0:T(8,128)(2,1)S(1)}, bf16[512,128]{1,0:T(8,128)(2,1)S(1)}, bf16[1024,1664]{1,0:T(8,128...) custom-call(s32[16]{0:T(128)S(1)} %copy-done.1, ...), custom_call_target="tpu_custom_call" | custom-call | tf_op jit(solution)/shard_map/pallas_call | solution.py:265
  48.4 2.5 %collective-permute-start.2 = (bf16[32,3456]{1,0:T(8,128)(2,1)S(1)}, bf16[32,3456]{1,0:T(8,128)(2,1)S(1)}, u32[]{:S(2)}, u32[]{:S(2)}) collective-permute-start(bf16[32,3456]{1,0:T(8,128)(2,1)S(1)} %get-tuple-element.96), channel_id=1, source_target_pairs={{0,16},{16,0},{32,48},{48,32},{64,80},{80,64},{96,112},{112,96},{1... | collective-permute-start | bytes 663560 | tf_op jit(solution)/shard_map/ppermute | solution.py:26
  51.0 3.3 %shard_map.102 = (bf16[2,32,3456]{2,1,0:T(8,128)(2,1)S(1)}, bf16[2,32,3456]{2,1,0:T(8,128)(2,1)S(1)}, bf16[32,3456]{1,0:T(8,128)(2,1)S(1)}, bf16[32,3456]{1,0:T(...) custom-call(bf16[512,1024]{1,0:T(8,128)(2,1)S(1)} %get-tuple-element, ...), custom_call_target="tpu_custom_call" | custom-call | flops 2944401408 | bytes 7077888 | tf_op jit(solution)/shard_map/pallas_call | solution.py:344
  54.3 2.8 %collective-permute-done.2.x = bf16[32,3456]{1,0:T(8,128)(2,1)S(1)} collective-permute-done((bf16[32,3456]{1,0:T(8,128)(2,1)S(1)}, bf16[32,3456]{1,0:T(8,128)(2,1)S(1)}, u32[]{:S(2)}, u32[]{:S(2)}) %collective-permute-start.2) | collective-permute-done | bytes 221216 | tf_op jit(solution)/shard_map/ppermute | solution.py:26
  57.2 2.1 %collective-permute-start.8 = (bf16[2,32,3456]{2,1,0:T(8,128)(2,1)S(1)}, bf16[2,32,3456]{2,1,0:T(8,128)(2,1)S(1)}, u32[]{:S(2)}, u32[]{:S(2)}) collective-permute-start(bf16[2,32,3456]{2,1,0:T(8,128)(2,1)S(1)} %get-tuple-element.111), channel_id=1, source_target_pairs={{0,16},{16,0},{32,48},{48,32},{64,80},{80,64},{96,112},{112,96},{1... | collective-permute-start | bytes 1327112 | tf_op jit(solution)/shard_map/ppermute | solution.py:26
  61.4 2.7 %collective-permute-done.3.up = bf16[32,1664]{1,0:T(8,128)(2,1)S(1)} collective-permute-done((bf16[32,1664]{1,0:T(8,128)(2,1)S(1)}, bf16[32,1664]{1,0:T(8,128)(2,1)S(1)}, u32[]{:S(2)}, u32[]{:S(2)}) %collective-permute-start.3) | collective-permute-done | bytes 106528 | tf_op jit(solution)/shard_map/ppermute | solution.py:26
  64.1 2.5 %collective-permute-done.5.x = bf16[2,32,3456]{2,1,0:T(8,128)(2,1)S(1)} collective-permute-done((bf16[2,32,3456]{2,1,0:T(8,128)(2,1)S(1)}, bf16[2,32,3456]{2,1,0:T(8,128)(2,1)S(1)}, u32[]{:S(2)}, u32[]{:S(2)}) %collective-permute-start.5) | collective-permute-done | bytes 442400 | tf_op jit(solution)/shard_map/ppermute | solution.py:26
  68.9 2.1 %collective-permute-start.11 = (bf16[2,32,3456]{2,1,0:T(8,128)(2,1)S(1)}, bf16[2,32,3456]{2,1,0:T(8,128)(2,1)S(1)}, u32[]{:S(2)}, u32[]{:S(2)}) collective-permute-start(bf16[2,32,3456]{2,1,0:T(8,128)(2,1)S(1)} %get-tuple-element.120), channel_id=1, source_target_pairs={{0,16},{16,0},{32,48},{48,32},{64,80},{80,64},{96,112},{112,96},{1... | collective-permute-start | bytes 1327112 | tf_op jit(solution)/shard_map/ppermute | solution.py:26
  70.9 2.4 %collective-permute-done.6.up = bf16[32,3456]{1,0:T(8,128)(2,1)S(1)} collective-permute-done((bf16[32,3456]{1,0:T(8,128)(2,1)S(1)}, bf16[32,3456]{1,0:T(8,128)(2,1)S(1)}, u32[]{:S(2)}, u32[]{:S(2)}) %collective-permute-start.6) | collective-permute-done | bytes 221216 | tf_op jit(solution)/shard_map/ppermute | solution.py:26
  80.6 5.0 %collective-permute-done.11.x = bf16[2,32,3456]{2,1,0:T(8,128)(2,1)S(1)} collective-permute-done((bf16[2,32,3456]{2,1,0:T(8,128)(2,1)S(1)}, bf16[2,32,3456]{2,1,0:T(8,128)(2,1)S(1)}, u32[]{:S(2)}, u32[]{:S(2)}) %collective-permute-start.11) | collective-permute-done | bytes 442400 | tf_op jit(solution)/shard_map/ppermute | solution.py:26
  89.8 2.5 %collective-permute-done.12.up = bf16[32,3456]{1,0:T(8,128)(2,1)S(1)} collective-permute-done((bf16[32,3456]{1,0:T(8,128)(2,1)S(1)}, bf16[32,3456]{1,0:T(8,128)(2,1)S(1)}, u32[]{:S(2)}, u32[]{:S(2)}) %collective-permute-start.12) | collective-permute-done | bytes 221216 | tf_op jit(solution)/shard_map/ppermute | solution.py:26
  94.0 2.1 %collective-permute-start.15 = (bf16[32,1664]{1,0:T(8,128)(2,1)S(1)}, bf16[32,1664]{1,0:T(8,128)(2,1)S(1)}, u32[]{:S(2)}, u32[]{:S(2)}) collective-permute-start(bf16[32,1664]{1,0:T(8,128)(2,1)S(1)} %shard_map.107.refs_0_), channel_id=1, source_target_pairs={{0,32},{16,48},{32,64},{48,80},{64,96},{80,112},{96,128},{112,144}... | collective-permute-start | bytes 319496 | tf_op jit(solution)/shard_map/ppermute | solution.py:26
  98.8 3.2 %collective-permute-done.16.refs_2_ = bf16[32,1664]{1,0:T(8,128)(2,1)S(1)} collective-permute-done((bf16[32,1664]{1,0:T(8,128)(2,1)S(1)}, bf16[32,1664]{1,0:T(8,128)(2,1)S(1)}, u32[]{:S(2)}, u32[]{:S(2)}) %collective-permute-start.16) | collective-permute-done | bytes 106528 | tf_op jit(solution)/shard_map/ppermute | solution.py:26
  102.1 2.1 %collective-permute-start.17 = (bf16[32,1664]{1,0:T(8,128)(2,1)S(1)}, bf16[32,1664]{1,0:T(8,128)(2,1)S(1)}, u32[]{:S(2)}, u32[]{:S(2)}) collective-permute-start(bf16[32,1664]{1,0:T(8,128)(2,1)S(1)} %collective-permute-done.15.refs_1_), channel_id=1, source_target_pairs={{0,32},{16,48},{32,64},{48,80},{64,96},{80,112},{96,128},{112,144}... | collective-permute-start | bytes 319496 | tf_op jit(solution)/shard_map/ppermute | solution.py:26
  106.8 4.3 %collective-permute-done.18.refs_4_ = bf16[32,1664]{1,0:T(8,128)(2,1)S(1)} collective-permute-done((bf16[32,1664]{1,0:T(8,128)(2,1)S(1)}, bf16[32,1664]{1,0:T(8,128)(2,1)S(1)}, u32[]{:S(2)}, u32[]{:S(2)}) %collective-permute-start.18) | collective-permute-done | bytes 106528 | tf_op jit(solution)/shard_map/ppermute | solution.py:26
  113.3 2.7 %collective-permute-done.20.refs_5_ = bf16[32,1664]{1,0:T(8,128)(2,1)S(1)} collective-permute-done((bf16[32,1664]{1,0:T(8,128)(2,1)S(1)}, bf16[32,1664]{1,0:T(8,128)(2,1)S(1)}, u32[]{:S(2)}, u32[]{:S(2)}) %collective-permute-start.20) | collective-permute-done | bytes 106528 | tf_op jit(solution)/shard_map/ppermute | solution.py:26
  120.1 3.4 %collective-permute-done.24.refs_8_ = bf16[32,768]{1,0:T(8,128)(2,1)S(1)} collective-permute-done((bf16[32,768]{1,0:T(8,128)(2,1)S(1)}, bf16[32,768]{1,0:T(8,128)(2,1)S(1)}, u32[]{:S(2)}, u32[]{:S(2)}) %collective-permute-start.24) | collective-permute-done | bytes 49184 | tf_op jit(solution)/shard_map/ppermute | solution.py:26
  123.6 4.7 %collective-permute-done.27.refs_13_ = bf16[32,1664]{1,0:T(8,128)(2,1)S(1)} collective-permute-done((bf16[32,1664]{1,0:T(8,128)(2,1)S(1)}, bf16[32,1664]{1,0:T(8,128)(2,1)S(1)}, u32[]{:S(2)}, u32[]{:S(2)}) %collective-permute-start.27) | collective-permute-done | bytes 106528 | tf_op jit(solution)/shard_map/ppermute | solution.py:26
  128.3 2.2 %shard_map.108 = (bf16[8,32,1024]{2,1,0:T(8,128)(2,1)S(1)}, f32[8,32,1024]{2,1,0:T(8,128)S(1)}) custom-call(bf16[32,1664]{1,0:T(8,128)(2,1)S(1)} %shard_map.107.refs_0_, bf16[32,1664]{1,0:T(8,128)(2,1)S(1)} %collective-permute-done.15.refs_1_, bf16[32,1664]{1,0:T(8,128)(2,1)S(1)} %collective-permute-done.16.refs_2_, ...), custom_call_target="tpu_custom_call" | custom-call | tf_op jit(solution)/shard_map/pallas_call | solution.py:385
  132.5 14.5 %all_to_all.11.parts = bf16[8,32,1024]{2,1,0:T(8,128)(2,1)S(1)} all-to-all(bf16[8,32,1024]{2,1,0:T(8,128)(2,1)S(1)} %shard_map.109), channel_id=1, replica_groups={{0,2,4,6,8,10,12,14},{1,3,5,7,9,11,13,15},{16,18,20,22,24,26,28,30},{17..., dimensions={0} | all-to-all | bytes 1048576 | tf_op jit(solution)/shard_map/all_to_all | solution.py:50
  (58 shorter events, 33.8 us)
Async XLA Ops:
  1.4 8.7 %collective-permute-start = (bf16[48,1152]{1,0:T(8,128)(2,1)S(1)}, bf16[48,1152]{1,0:T(8,128)(2,1)S(1)}, u32[]{:S(2)}, u32[]{:S(2)}) collective-permute-start(bf16[48,1152]{1,0:T(8,128)(2,1)S(1)} %shard_map.100), channel_id=1, source_target_pairs={{0,0},{1,16},{2,32},{3,48},{4,64},{5,80},{6,96},{7,112},{8,128},{9... | collective-permute-start | bytes 331784 | tf_op jit(solution)/shard_map/ppermute | solution.py:42
  48.4 8.8 %collective-permute-start.2 = (bf16[32,3456]{1,0:T(8,128)(2,1)S(1)}, bf16[32,3456]{1,0:T(8,128)(2,1)S(1)}, u32[]{:S(2)}, u32[]{:S(2)}) collective-permute-start(bf16[32,3456]{1,0:T(8,128)(2,1)S(1)} %get-tuple-element.96), channel_id=1, source_target_pairs={{0,16},{16,0},{32,48},{48,32},{64,80},{80,64},{96,112},{112,96},{1... | collective-permute-start | bytes 663560 | tf_op jit(solution)/shard_map/ppermute | solution.py:26
  50.9 15.7 %collective-permute-start.5 = (bf16[2,32,3456]{2,1,0:T(8,128)(2,1)S(1)}, bf16[2,32,3456]{2,1,0:T(8,128)(2,1)S(1)}, u32[]{:S(2)}, u32[]{:S(2)}) collective-permute-start(bf16[2,32,3456]{2,1,0:T(8,128)(2,1)S(1)} %get-tuple-element.102), channel_id=1, source_target_pairs={{0,16},{16,0},{32,48},{48,32},{64,80},{80,64},{96,112},{112,96},{1... | collective-permute-start | bytes 1327112 | tf_op jit(solution)/shard_map/ppermute | solution.py:26
  57.2 18.9 %collective-permute-start.8 = (bf16[2,32,3456]{2,1,0:T(8,128)(2,1)S(1)}, bf16[2,32,3456]{2,1,0:T(8,128)(2,1)S(1)}, u32[]{:S(2)}, u32[]{:S(2)}) collective-permute-start(bf16[2,32,3456]{2,1,0:T(8,128)(2,1)S(1)} %get-tuple-element.111), channel_id=1, source_target_pairs={{0,16},{16,0},{32,48},{48,32},{64,80},{80,64},{96,112},{112,96},{1... | collective-permute-start | bytes 1327112 | tf_op jit(solution)/shard_map/ppermute | solution.py:26
  59.3 4.8 %collective-permute-start.4 = (bf16[32,1792]{1,0:T(8,128)(2,1)S(1)}, bf16[32,1792]{1,0:T(8,128)(2,1)S(1)}, u32[]{:S(2)}, u32[]{:S(2)}) collective-permute-start(bf16[32,1792]{1,0:T(8,128)(2,1)S(1)} %get-tuple-element.101), channel_id=1, source_target_pairs={{0,224},{16,240},{32,0},{48,16},{64,32},{80,48},{96,64},{112,80},{... | collective-permute-start | bytes 344072 | tf_op jit(solution)/shard_map/ppermute | solution.py:26
  66.8 6.6 %collective-permute-start.6 = (bf16[32,3456]{1,0:T(8,128)(2,1)S(1)}, bf16[32,3456]{1,0:T(8,128)(2,1)S(1)}, u32[]{:S(2)}, u32[]{:S(2)}) collective-permute-start(bf16[32,3456]{1,0:T(8,128)(2,1)S(1)} %get-tuple-element.109), channel_id=1, source_target_pairs={{0,32},{16,48},{32,64},{48,80},{64,96},{80,112},{96,128},{112,144}... | collective-permute-start | bytes 663560 | tf_op jit(solution)/shard_map/ppermute | solution.py:26
  68.2 5.9 %collective-permute-start.7 = (bf16[32,3456]{1,0:T(8,128)(2,1)S(1)}, bf16[32,3456]{1,0:T(8,128)(2,1)S(1)}, u32[]{:S(2)}, u32[]{:S(2)}) collective-permute-start(bf16[32,3456]{1,0:T(8,128)(2,1)S(1)} %get-tuple-element.110), channel_id=1, source_target_pairs={{0,224},{16,240},{32,0},{48,16},{64,32},{80,48},{96,64},{112,80},{... | collective-permute-start | bytes 663560 | tf_op jit(solution)/shard_map/ppermute | solution.py:26
  68.9 16.7 %collective-permute-start.11 = (bf16[2,32,3456]{2,1,0:T(8,128)(2,1)S(1)}, bf16[2,32,3456]{2,1,0:T(8,128)(2,1)S(1)}, u32[]{:S(2)}, u32[]{:S(2)}) collective-permute-start(bf16[2,32,3456]{2,1,0:T(8,128)(2,1)S(1)} %get-tuple-element.120), channel_id=1, source_target_pairs={{0,16},{16,0},{32,48},{48,32},{64,80},{80,64},{96,112},{112,96},{1... | collective-permute-start | bytes 1327112 | tf_op jit(solution)/shard_map/ppermute | solution.py:26
  76.3 9.3 %collective-permute-start.9 = (bf16[32,3456]{1,0:T(8,128)(2,1)S(1)}, bf16[32,3456]{1,0:T(8,128)(2,1)S(1)}, u32[]{:S(2)}, u32[]{:S(2)}) collective-permute-start(bf16[32,3456]{1,0:T(8,128)(2,1)S(1)} %get-tuple-element.118), channel_id=1, source_target_pairs={{0,32},{16,48},{32,64},{48,80},{64,96},{80,112},{96,128},{112,144}... | collective-permute-start | bytes 663560 | tf_op jit(solution)/shard_map/ppermute | solution.py:26
  77.9 7.7 %collective-permute-start.10 = (bf16[32,3456]{1,0:T(8,128)(2,1)S(1)}, bf16[32,3456]{1,0:T(8,128)(2,1)S(1)}, u32[]{:S(2)}, u32[]{:S(2)}) collective-permute-start(bf16[32,3456]{1,0:T(8,128)(2,1)S(1)} %get-tuple-element.119), channel_id=1, source_target_pairs={{0,224},{16,240},{32,0},{48,16},{64,32},{80,48},{96,64},{112,80},{... | collective-permute-start | bytes 663560 | tf_op jit(solution)/shard_map/ppermute | solution.py:26
  78.5 11.3 %collective-permute-start.14 = (bf16[32,3456]{1,0:T(8,128)(2,1)S(1)}, bf16[32,3456]{1,0:T(8,128)(2,1)S(1)}, u32[]{:S(2)}, u32[]{:S(2)}) collective-permute-start(bf16[32,3456]{1,0:T(8,128)(2,1)S(1)} %get-tuple-element.128), channel_id=1, source_target_pairs={{0,16},{16,0},{32,48},{48,32},{64,80},{80,64},{96,112},{112,96},{1... | collective-permute-start | bytes 663560 | tf_op jit(solution)/shard_map/ppermute | solution.py:26
  85.7 6.6 %collective-permute-start.12 = (bf16[32,3456]{1,0:T(8,128)(2,1)S(1)}, bf16[32,3456]{1,0:T(8,128)(2,1)S(1)}, u32[]{:S(2)}, u32[]{:S(2)}) collective-permute-start(bf16[32,3456]{1,0:T(8,128)(2,1)S(1)} %get-tuple-element.126), channel_id=1, source_target_pairs={{0,32},{16,48},{32,64},{48,80},{64,96},{80,112},{96,128},{112,144}... | collective-permute-start | bytes 663560 | tf_op jit(solution)/shard_map/ppermute | solution.py:26
  87.2 6.6 %collective-permute-start.13 = (bf16[32,3456]{1,0:T(8,128)(2,1)S(1)}, bf16[32,3456]{1,0:T(8,128)(2,1)S(1)}, u32[]{:S(2)}, u32[]{:S(2)}) collective-permute-start(bf16[32,3456]{1,0:T(8,128)(2,1)S(1)} %get-tuple-element.127), channel_id=1, source_target_pairs={{0,224},{16,240},{32,0},{48,16},{64,32},{80,48},{96,64},{112,80},{... | collective-permute-start | bytes 663560 | tf_op jit(solution)/shard_map/ppermute | solution.py:26
  94.0 4.8 %collective-permute-start.15 = (bf16[32,1664]{1,0:T(8,128)(2,1)S(1)}, bf16[32,1664]{1,0:T(8,128)(2,1)S(1)}, u32[]{:S(2)}, u32[]{:S(2)}) collective-permute-start(bf16[32,1664]{1,0:T(8,128)(2,1)S(1)} %shard_map.107.refs_0_), channel_id=1, source_target_pairs={{0,32},{16,48},{32,64},{48,80},{64,96},{80,112},{96,128},{112,144}... | collective-permute-start | bytes 319496 | tf_op jit(solution)/shard_map/ppermute | solution.py:26
  96.1 5.9 %collective-permute-start.16 = (bf16[32,1664]{1,0:T(8,128)(2,1)S(1)}, bf16[32,1664]{1,0:T(8,128)(2,1)S(1)}, u32[]{:S(2)}, u32[]{:S(2)}) collective-permute-start(bf16[32,1664]{1,0:T(8,128)(2,1)S(1)} %shard_map.107.refs_0_), channel_id=1, source_target_pairs={{0,224},{16,240},{32,0},{48,16},{64,32},{80,48},{96,64},{112,80},{... | collective-permute-start | bytes 319496 | tf_op jit(solution)/shard_map/ppermute | solution.py:26
  96.1 8.8 %collective-permute-start.19 = (bf16[32,1664]{1,0:T(8,128)(2,1)S(1)}, bf16[32,1664]{1,0:T(8,128)(2,1)S(1)}, u32[]{:S(2)}, u32[]{:S(2)}) collective-permute-start(bf16[32,1664]{1,0:T(8,128)(2,1)S(1)} %shard_map.107.refs_0_), channel_id=1, source_target_pairs={{0,16},{16,0},{32,48},{48,32},{64,80},{80,64},{96,112},{112,96},{1... | collective-permute-start | bytes 319496 | tf_op jit(solution)/shard_map/ppermute | solution.py:26
  102.1 4.8 %collective-permute-start.17 = (bf16[32,1664]{1,0:T(8,128)(2,1)S(1)}, bf16[32,1664]{1,0:T(8,128)(2,1)S(1)}, u32[]{:S(2)}, u32[]{:S(2)}) collective-permute-start(bf16[32,1664]{1,0:T(8,128)(2,1)S(1)} %collective-permute-done.15.refs_1_), channel_id=1, source_target_pairs={{0,32},{16,48},{32,64},{48,80},{64,96},{80,112},{96,128},{112,144}... | collective-permute-start | bytes 319496 | tf_op jit(solution)/shard_map/ppermute | solution.py:26
  104.2 7.0 %collective-permute-start.18 = (bf16[32,1664]{1,0:T(8,128)(2,1)S(1)}, bf16[32,1664]{1,0:T(8,128)(2,1)S(1)}, u32[]{:S(2)}, u32[]{:S(2)}) collective-permute-start(bf16[32,1664]{1,0:T(8,128)(2,1)S(1)} %collective-permute-done.16.refs_2_), channel_id=1, source_target_pairs={{0,224},{16,240},{32,0},{48,16},{64,32},{80,48},{96,64},{112,80},{... | collective-permute-start | bytes 319496 | tf_op jit(solution)/shard_map/ppermute | solution.py:26
  104.2 13.5 %collective-permute-start.22 = (bf16[2,32,1664]{2,1,0:T(8,128)(2,1)S(1)}, bf16[2,32,1664]{2,1,0:T(8,128)(2,1)S(1)}, u32[]{:S(2)}, u32[]{:S(2)}) collective-permute-start(bf16[2,32,1664]{2,1,0:T(8,128)(2,1)S(1)} %pad_maximum_fusion), channel_id=1, source_target_pairs={{0,16},{16,0},{32,48},{48,32},{64,80},{80,64},{96,112},{112,96},{1... | collective-permute-start | bytes 638984 | tf_op jit(solution)/shard_map/ppermute | solution.py:26
  111.2 4.8 %collective-permute-start.20 = (bf16[32,1664]{1,0:T(8,128)(2,1)S(1)}, bf16[32,1664]{1,0:T(8,128)(2,1)S(1)}, u32[]{:S(2)}, u32[]{:S(2)}) collective-permute-start(bf16[32,1664]{1,0:T(8,128)(2,1)S(1)} %collective-permute-done.17.refs_3_), channel_id=1, source_target_pairs={{0,32},{16,48},{32,64},{48,80},{64,96},{80,112},{96,128},{112,144}... | collective-permute-start | bytes 319496 | tf_op jit(solution)/shard_map/ppermute | solution.py:26
  113.3 10.2 %collective-permute-start.25 = (bf16[2,32,1664]{2,1,0:T(8,128)(2,1)S(1)}, bf16[2,32,1664]{2,1,0:T(8,128)(2,1)S(1)}, u32[]{:S(2)}, u32[]{:S(2)}) collective-permute-start(bf16[2,32,1664]{2,1,0:T(8,128)(2,1)S(1)} %pad_maximum_fusion.1), channel_id=1, source_target_pairs={{0,16},{16,0},{32,48},{48,32},{64,80},{80,64},{96,112},{112,96},{1... | collective-permute-start | bytes 638984 | tf_op jit(solution)/shard_map/ppermute | solution.py:26
  117.7 5.8 %collective-permute-start.23 = (bf16[32,896]{1,0:T(8,128)(2,1)S(1)}, bf16[32,896]{1,0:T(8,128)(2,1)S(1)}, u32[]{:S(2)}, u32[]{:S(2)}) collective-permute-start(bf16[32,896]{1,0:T(8,128)(2,1)S(1)} %slice.6), channel_id=1, source_target_pairs={{0,32},{16,48},{32,64},{48,80},{64,96},{80,112},{96,128},{112,144}... | collective-permute-start | bytes 172040 | tf_op jit(solution)/shard_map/ppermute | solution.py:26
  119.8 8.5 %collective-permute-start.26 = (bf16[2,32,1664]{2,1,0:T(8,128)(2,1)S(1)}, bf16[2,32,1664]{2,1,0:T(8,128)(2,1)S(1)}, u32[]{:S(2)}, u32[]{:S(2)}) collective-permute-start(bf16[2,32,1664]{2,1,0:T(8,128)(2,1)S(1)} %pad_maximum_fusion.2), channel_id=1, source_target_pairs={{0,16},{16,0},{32,48},{48,32},{64,80},{80,64},{96,112},{112,96},{1... | collective-permute-start | bytes 638984 | tf_op jit(solution)/shard_map/ppermute | solution.py:26
  123.5 4.8 %collective-permute-start.27 = (bf16[32,1664]{1,0:T(8,128)(2,1)S(1)}, bf16[32,1664]{1,0:T(8,128)(2,1)S(1)}, u32[]{:S(2)}, u32[]{:S(2)}) collective-permute-start(bf16[32,1664]{1,0:T(8,128)(2,1)S(1)} %pad_maximum_fusion.3), channel_id=1, source_target_pairs={{0,16},{16,0},{32,48},{48,32},{64,80},{80,64},{96,112},{112,96},{1... | collective-permute-start | bytes 319496 | tf_op jit(solution)/shard_map/ppermute | solution.py:26
  (7 other events, 133.1 us)

commit v8 on v7

--- a/solution.py
+++ b/solution.py
@@ -59,10 +59,15 @@
     return pltpu.with_memory_space_constraint(value, pltpu.HBM)
 
 
+PAIRS = 8 * ROWS_DEV
+QUERIES = PAIRS + 4 * 16
+ASKED = QUERIES + 4 * 16
+
+
 def softmax(scores, seen):
     scores = jnp.where(seen, scores * F32(HEAD_DIM**-0.5), F32(-1e30))
     exponent = jnp.exp(scores - jnp.max(scores, axis=1, keepdims=True))
-    return (exponent / jnp.sum(exponent, axis=1, keepdims=True)).astype(BF)
+    return (exponent * (F32(1) / jnp.sum(exponent, axis=1, keepdims=True))).astype(BF)
 
 
 def scored(queries, keys):
@@ -102,8 +107,7 @@
     asked = jnp.zeros(shape, jnp.int32)
     for i in range(ROWS_DEV - PREFIX):
         asked = jnp.where(option == i, question_ref[i], asked)
-    out_ref[32:, width:] = asked.astype(F32).astype(BF)
-    out_ref[:32, width:] = jnp.zeros((ROWS_DEV, LANE), BF)
+    out_ref[ASKED : ASKED + 16, :] = asked.astype(F32).astype(BF)
     copies[0].wait()
     copies[1].wait()
     stacked = jnp.concatenate(
@@ -112,25 +116,32 @@
     attention = softmax(scored(stacked, pair[:, :HEAD_DIM]), seen)
     copies[2].wait()
     context = jnp.dot(attention, pair[:, HEAD_DIM:], preferred_element_type=F32).astype(BF)
-    out_ref[32:, : 2 * HEAD_DIM] = pair[:16]
-    out_ref[32:, 2 * HEAD_DIM : 4 * HEAD_DIM] = pair[16:]
+    for i in range(2):
+        for j in range(2):
+            at = PAIRS + (2 * i + j) * 16
+            out_ref[at : at + 16, :] = pair[16 * i : 16 * i + 16, j * HEAD_DIM : (j + 1) * HEAD_DIM]
     last = queries[16:].astype(F32)[PREFIX - 16 :]
     half = width // 2
-    out_ref[32:, half:width] = jnp.concatenate([last[:, :half], last[:, half:]], axis=0).astype(BF)
+    for h in range(heads // 2):
+        first = h * HEAD_DIM
+        tile = [last[:, at : at + HEAD_DIM] for at in (first, first + half)]
+        at = QUERIES + h * 16
+        out_ref[at : at + 16, :] = jnp.concatenate(tile, axis=0).astype(BF)
     copies[3].wait()
     prefix = lax.broadcasted_iota(jnp.int32, (ROWS_DEV, HEAD_DIM), 0) < PREFIX
     for h in range(heads):
         columns = slice(h * HEAD_DIM, (h + 1) * HEAD_DIM)
         mine = context[h * ROWS_DEV : (h + 1) * ROWS_DEV].astype(F32)
         mine = jnp.where(prefix, mine, F32(0))
-        out_ref[:32, columns] = (hidden[:, columns].astype(F32) + mine).astype(BF)
+        at = slice(h * ROWS_DEV, (h + 1) * ROWS_DEV)
+        out_ref[at, :] = (hidden[:, columns].astype(F32) + mine).astype(BF)
 
 
 def prepare(prefix_len, question, queries, hidden_in, key_cache, value_cache):
     rows, width = queries.shape
     return pl.pallas_call(
         prepare_kernel,
-        out_shape=in_vmem(((rows + 16, width + LANE), BF)),
+        out_shape=in_vmem(((ASKED + 16, LANE), BF)),
         in_specs=[HBM] * 6,
         out_specs=VMEM,
         scratch_shapes=[
@@ -181,64 +192,51 @@
     blocks = [(ref, i) for ref in (mine_ref, theirs_ref) for i in range(ZN)]
     options = ROWS_DEV - PREFIX
 
-    def gathered(lanes):
-        return jnp.concatenate([ref[i, n:, lanes] for ref, i in blocks], axis=0)
-
-    def unfolded(first):
-        low, high = slice(first, first + HEAD_DIM), slice(first + 2 * HEAD_DIM, first + 3 * HEAD_DIM)
-        return jnp.concatenate(
-            [ref[i, n:, lanes] for ref, i in blocks for lanes in (low, high)], axis=0
-        )
-
-    keys, values = unfolded(0), unfolded(HEAD_DIM)
-    shape = (16 * len(blocks), n * len(blocks))
-    asked = gathered(slice(width, width + LANE)).astype(F32).astype(jnp.int32)
-    asked = jnp.concatenate([asked] * (shape[1] // LANE), axis=1)
-    place = lax.broadcasted_iota(jnp.int32, shape, 1)
+    def gathered(*parts):
+        return jnp.concatenate([ref[i, at : at + 16, :] for ref, i in blocks for at in parts], axis=0)
+
+    keys, values = gathered(PAIRS, PAIRS + 32), gathered(PAIRS + 16, PAIRS + 48)
+    total = n * len(blocks)
+    place = lax.broadcasted_iota(jnp.int32, (8, total), 1)
     order = place >> 5
-    row = lax.broadcasted_iota(jnp.int32, shape, 0)
-    owner = ((order & (ZN - 1)) << 1) + ((order >> 3) ^ core)
-    live = jnp.zeros(shape, jnp.int32)
+    live = jnp.zeros(place.shape, jnp.int32)
     for i in range(len(blocks)):
         live = jnp.where(order == i, length_ref[((i & (ZN - 1)) << 1) + ((i >> 3) ^ core)], live)
-    seen = (owner == asked) & ((place & (n - 1)) < live)
-    seen = seen | (place == (row >> 4) * n + PREFIX + (row & (options - 1)))
+    owner = ((order & (ZN - 1)) << 1) + ((order >> 3) ^ core)
+    owner = jnp.where((place & (n - 1)) < live, owner, -1)
+    asked = gathered(ASKED).astype(F32).astype(jnp.int32)
+    row = lax.broadcasted_iota(jnp.int32, (asked.shape[0], 1), 0)
+    itself = (row >> 4) * n + PREFIX + (row & (options - 1))
+    seen = (jnp.tile(owner, (asked.shape[0] // 8, 1)) == jnp.tile(asked, (1, total // LANE))) | (
+        jnp.tile(place, (asked.shape[0] // 8, 1)) == itself
+    )
     contexts = []
     for h in range(half // HEAD_DIM):
-        queries = gathered(slice(half + h * HEAD_DIM, half + (h + 1) * HEAD_DIM))
-        attention = softmax(scored(queries, keys), seen)
+        attention = softmax(scored(gathered(QUERIES + h * 16), keys), seen)
         context = jnp.dot(attention, values, preferred_element_type=F32)
         contexts.append(context.astype(BF).astype(F32))
     fetch.wait()
     scale = gain[...].reshape(1, width)
     for k, (ref, i) in enumerate(blocks):
-        at = k * 16
-        added = jnp.concatenate(
-            [context[at : at + options] for context in contexts]
-            + [context[at + options : at + 16] for context in contexts],
-            axis=1,
-        )
-        added = jnp.concatenate([jnp.zeros((16 - options, width), F32), added], axis=0)
-        first = ref[i, :16, :width]
-        last = (ref[i, 16:n, :width].astype(F32) + added).astype(BF)
-        if ref is mine_ref:
-            residual[i, :16] = first
-            residual[i, 16:] = last
         s = (i - z) & (ZN - 1)
         j = flip if ref is mine_ref else 1 - flip
         position = ZN + s
         for index, (target, _) in enumerate(ORDER[:ZN]):
             position = jnp.where((s == target) & (j == 1), index, position)
-        at = pl.multiple_of(position * n, n)
-        for part, offset in ((first, 0), (last, 16)):
+        into = pl.ds(pl.multiple_of(position * n, n), n)
+        total = jnp.zeros((n, LANE), F32)
+        for tile in range(width // LANE):
+            lanes = slice(tile * LANE, (tile + 1) * LANE)
+            at = k * 16 + tile // len(contexts) * options
+            added = contexts[tile % len(contexts)][at : at + options]
+            added = jnp.concatenate([jnp.zeros((PREFIX, LANE), F32), added], axis=0)
+            part = (ref[i, tile * n : (tile + 1) * n, :].astype(F32) + added).astype(BF)
+            if ref is mine_ref:
+                residual[i, :, lanes] = part
             x = part.astype(F32)
-            into = pl.ds(pl.multiple_of(at + offset, 16), 16)
-            rows[into, :] = (x * scale).astype(BF)
-            square = x * x
-            total = square[:, :LANE]
-            for lane in range(1, width // LANE):
-                total = total + square[:, lane * LANE : (lane + 1) * LANE]
-            squares[into, :] = total.astype(BF)
+            rows[into, lanes] = (x * scale[:, lanes]).astype(BF)
+            total = total + x * x
+        squares[into, :] = total.astype(BF)
     own_ref[...] = residual[mp_index >> 1]
     early = slice(0, FIRST * n)
     ready = lambda ref: (fetch_gate if ref is gate_ref else fetch_up).wait()

time: 148 us -> 146 us (0.986)
  no operation moved by 1% of the time
where the time goes in v8:
time: 146 us
  waiting for transfers between devices  56.6 us (39%)
  blocking collectives  44.7 us (31%)
  starting transfers between devices  31.6 us (22%)
  Pallas kernels  12.9 us (9%)
    ppermute x28, waiting for transfers between devices, permute(): return lax.ppermute(value, axis, [(i, target(i)) for i in range(count)])  51.1 us
    all_to_all x2, blocking collectives, over_plane(): lax.all_to_all(value, 'mp', 0, 0, axis_index_groups=PLANE, tiled=True)  44.7 us
    ppermute x28, starting transfers between devices, permute(): return lax.ppermute(value, axis, [(i, target(i)) for i in range(count)])  28.6 us
    ppermute x1, waiting for transfers between devices, transpose_mesh(): lax.ppermute(value, ('batch', 'mp'), [(b * 16 + m, m * 16 + b) for b in r...  5.44 us
    pallas_call x1, Pallas kernels, project(): pl.pallas_call(first_kernel, out_shape=in_vmem(((n, width), BF), ((all_ro...  4.44 us
    pallas_call x7, Pallas kernels, local(): pl.pallas_call(kernel, out_shape=in_vmem(*shapes), in_specs=[VMEM] * len(...  4.15 us
    ppermute x1, starting transfers between devices, transpose_mesh(): lax.ppermute(value, ('batch', 'mp'), [(b * 16 + m, m * 16 + b) for b in r...  3.03 us
  transfers between devices with their start and end apart: 29, of which 22 were waited for; matrix products, arithmetic and copies ran while one was open for 0% of the time, Pallas kernels for 3%

profile of v8, /device:TPU:32, one launch (start us, length us, event | category | flops | bytes accessed | tf_op | source)
XLA Modules:
  0.0 146.1 jit_solution(15797709070532302945)
XLA Ops:
  1.4 3.0 %collective-permute-start = (bf16[400,128]{1,0:T(8,128)(2,1)S(1)}, bf16[400,128]{1,0:T(8,128)(2,1)S(1)}, u32[]{:S(2)}, u32[]{:S(2)}) collective-permute-start(bf16[400,128]{1,0:T(8,128)(2,1)S(1)} %shard_map.100), channel_id=1, source_target_pairs={{0,0},{1,16},{2,32},{3,48},{4,64},{5,80},{6,96},{7,112},{8,128},{9... | collective-permute-start | bytes 307208 | tf_op jit(solution)/shard_map/ppermute | solution.py:42
  4.5 5.4 %collective-permute-done = bf16[400,128]{1,0:T(8,128)(2,1)S(1)} collective-permute-done((bf16[400,128]{1,0:T(8,128)(2,1)S(1)}, bf16[400,128]{1,0:T(8,128)(2,1)S(1)}, u32[]{:S(2)}, u32[]{:S(2)}) %collective-permute-start) | collective-permute-done | bytes 102432 | tf_op jit(solution)/shard_map/ppermute | solution.py:42
  10.0 30.2 %all_to_all.10.mine_ref = bf16[8,400,128]{2,1,0:T(8,128)(2,1)S(1)} all-to-all(bf16[8,400,128]{2,1,0:T(8,128)(2,1)S(1)} %broadcast_in_dim.2), channel_id=1, replica_groups={{0,2,4,6,8,10,12,14},{1,3,5,7,9,11,13,15},{16,18,20,22,24,26,28,30},{17..., dimensions={0} | all-to-all | bytes 1638400 | tf_op jit(solution)/shard_map/all_to_all | solution.py:50
  40.3 2.3 %collective-permute-done.1.theirs_ref = bf16[8,400,128]{2,1,0:T(8,128)(2,1)S(1)} collective-permute-done((bf16[8,400,128]{2,1,0:T(8,128)(2,1)S(1)}, bf16[8,400,128]{2,1,0:T(8,128)(2,1)S(1)}, u32[]{:S(2)}, u32[]{:S(2)}) %collective-permute-start.1) | collective-permute-done | bytes 819232 | tf_op jit(solution)/shard_map/ppermute | solution.py:26
  42.6 4.4 %shard_map.101 = (bf16[32,1024]{1,0:T(8,128)(2,1)S(1)}, bf16[512,1024]{1,0:T(8,128)(2,1)S(1)}, bf16[512,128]{1,0:T(8,128)(2,1)S(1)}, bf16[1024,1664]{1,0:T(8,128...) custom-call(s32[16]{0:T(128)S(1)} %copy-done.1, ...), custom_call_target="tpu_custom_call" | custom-call | tf_op jit(solution)/shard_map/pallas_call | solution.py:263
  47.0 2.7 %collective-permute-start.2 = (bf16[32,3456]{1,0:T(8,128)(2,1)S(1)}, bf16[32,3456]{1,0:T(8,128)(2,1)S(1)}, u32[]{:S(2)}, u32[]{:S(2)}) collective-permute-start(bf16[32,3456]{1,0:T(8,128)(2,1)S(1)} %get-tuple-element.96), channel_id=1, source_target_pairs={{0,16},{16,0},{32,48},{48,32},{64,80},{80,64},{96,112},{112,96},{1... | collective-permute-start | bytes 663560 | tf_op jit(solution)/shard_map/ppermute | solution.py:26
  49.8 3.3 %shard_map.102 = (bf16[2,32,3456]{2,1,0:T(8,128)(2,1)S(1)}, bf16[2,32,3456]{2,1,0:T(8,128)(2,1)S(1)}, bf16[32,3456]{1,0:T(8,128)(2,1)S(1)}, bf16[32,3456]{1,0:T(...) custom-call(bf16[512,1024]{1,0:T(8,128)(2,1)S(1)} %get-tuple-element, ...), custom_call_target="tpu_custom_call" | custom-call | flops 2944401408 | bytes 7077888 | tf_op jit(solution)/shard_map/pallas_call | solution.py:342
  53.1 2.8 %collective-permute-done.2.x = bf16[32,3456]{1,0:T(8,128)(2,1)S(1)} collective-permute-done((bf16[32,3456]{1,0:T(8,128)(2,1)S(1)}, bf16[32,3456]{1,0:T(8,128)(2,1)S(1)}, u32[]{:S(2)}, u32[]{:S(2)}) %collective-permute-start.2) | collective-permute-done | bytes 221216 | tf_op jit(solution)/shard_map/ppermute | solution.py:26
  56.0 2.1 %collective-permute-start.8 = (bf16[2,32,3456]{2,1,0:T(8,128)(2,1)S(1)}, bf16[2,32,3456]{2,1,0:T(8,128)(2,1)S(1)}, u32[]{:S(2)}, u32[]{:S(2)}) collective-permute-start(bf16[2,32,3456]{2,1,0:T(8,128)(2,1)S(1)} %get-tuple-element.111), channel_id=1, source_target_pairs={{0,16},{16,0},{32,48},{48,32},{64,80},{80,64},{96,112},{112,96},{1... | collective-permute-start | bytes 1327112 | tf_op jit(solution)/shard_map/ppermute | solution.py:26
  60.2 2.7 %collective-permute-done.3.up = bf16[32,1664]{1,0:T(8,128)(2,1)S(1)} collective-permute-done((bf16[32,1664]{1,0:T(8,128)(2,1)S(1)}, bf16[32,1664]{1,0:T(8,128)(2,1)S(1)}, u32[]{:S(2)}, u32[]{:S(2)}) %collective-permute-start.3) | collective-permute-done | bytes 106528 | tf_op jit(solution)/shard_map/ppermute | solution.py:26
  62.9 2.5 %collective-permute-done.5.x = bf16[2,32,3456]{2,1,0:T(8,128)(2,1)S(1)} collective-permute-done((bf16[2,32,3456]{2,1,0:T(8,128)(2,1)S(1)}, bf16[2,32,3456]{2,1,0:T(8,128)(2,1)S(1)}, u32[]{:S(2)}, u32[]{:S(2)}) %collective-permute-start.5) | collective-permute-done | bytes 442400 | tf_op jit(solution)/shard_map/ppermute | solution.py:26
  69.7 2.4 %collective-permute-done.6.up = bf16[32,3456]{1,0:T(8,128)(2,1)S(1)} collective-permute-done((bf16[32,3456]{1,0:T(8,128)(2,1)S(1)}, bf16[32,3456]{1,0:T(8,128)(2,1)S(1)}, u32[]{:S(2)}, u32[]{:S(2)}) %collective-permute-start.6) | collective-permute-done | bytes 221216 | tf_op jit(solution)/shard_map/ppermute | solution.py:26
  72.8 2.1 %collective-permute-done.8.x = bf16[2,32,3456]{2,1,0:T(8,128)(2,1)S(1)} collective-permute-done((bf16[2,32,3456]{2,1,0:T(8,128)(2,1)S(1)}, bf16[2,32,3456]{2,1,0:T(8,128)(2,1)S(1)}, u32[]{:S(2)}, u32[]{:S(2)}) %collective-permute-start.8) | collective-permute-done | bytes 442400 | tf_op jit(solution)/shard_map/ppermute | solution.py:26
  79.4 5.0 %collective-permute-done.11.x = bf16[2,32,3456]{2,1,0:T(8,128)(2,1)S(1)} collective-permute-done((bf16[2,32,3456]{2,1,0:T(8,128)(2,1)S(1)}, bf16[2,32,3456]{2,1,0:T(8,128)(2,1)S(1)}, u32[]{:S(2)}, u32[]{:S(2)}) %collective-permute-start.11) | collective-permute-done | bytes 442400 | tf_op jit(solution)/shard_map/ppermute | solution.py:26
  88.6 2.5 %collective-permute-done.12.up = bf16[32,3456]{1,0:T(8,128)(2,1)S(1)} collective-permute-done((bf16[32,3456]{1,0:T(8,128)(2,1)S(1)}, bf16[32,3456]{1,0:T(8,128)(2,1)S(1)}, u32[]{:S(2)}, u32[]{:S(2)}) %collective-permute-start.12) | collective-permute-done | bytes 221216 | tf_op jit(solution)/shard_map/ppermute | solution.py:26
  92.7 2.1 %collective-permute-start.15 = (bf16[32,1664]{1,0:T(8,128)(2,1)S(1)}, bf16[32,1664]{1,0:T(8,128)(2,1)S(1)}, u32[]{:S(2)}, u32[]{:S(2)}) collective-permute-start(bf16[32,1664]{1,0:T(8,128)(2,1)S(1)} %shard_map.107.refs_0_), channel_id=1, source_target_pairs={{0,32},{16,48},{32,64},{48,80},{64,96},{80,112},{96,128},{112,144}... | collective-permute-start | bytes 319496 | tf_op jit(solution)/shard_map/ppermute | solution.py:26
  97.4 3.1 %collective-permute-done.16.refs_2_ = bf16[32,1664]{1,0:T(8,128)(2,1)S(1)} collective-permute-done((bf16[32,1664]{1,0:T(8,128)(2,1)S(1)}, bf16[32,1664]{1,0:T(8,128)(2,1)S(1)}, u32[]{:S(2)}, u32[]{:S(2)}) %collective-permute-start.16) | collective-permute-done | bytes 106528 | tf_op jit(solution)/shard_map/ppermute | solution.py:26
  100.6 2.1 %collective-permute-start.17 = (bf16[32,1664]{1,0:T(8,128)(2,1)S(1)}, bf16[32,1664]{1,0:T(8,128)(2,1)S(1)}, u32[]{:S(2)}, u32[]{:S(2)}) collective-permute-start(bf16[32,1664]{1,0:T(8,128)(2,1)S(1)} %collective-permute-done.15.refs_1_), channel_id=1, source_target_pairs={{0,32},{16,48},{32,64},{48,80},{64,96},{80,112},{96,128},{112,144}... | collective-permute-start | bytes 319496 | tf_op jit(solution)/shard_map/ppermute | solution.py:26
  105.4 4.1 %collective-permute-done.18.refs_4_ = bf16[32,1664]{1,0:T(8,128)(2,1)S(1)} collective-permute-done((bf16[32,1664]{1,0:T(8,128)(2,1)S(1)}, bf16[32,1664]{1,0:T(8,128)(2,1)S(1)}, u32[]{:S(2)}, u32[]{:S(2)}) %collective-permute-start.18) | collective-permute-done | bytes 106528 | tf_op jit(solution)/shard_map/ppermute | solution.py:26
  111.6 2.6 %collective-permute-done.20.refs_5_ = bf16[32,1664]{1,0:T(8,128)(2,1)S(1)} collective-permute-done((bf16[32,1664]{1,0:T(8,128)(2,1)S(1)}, bf16[32,1664]{1,0:T(8,128)(2,1)S(1)}, u32[]{:S(2)}, u32[]{:S(2)}) %collective-permute-start.20) | collective-permute-done | bytes 106528 | tf_op jit(solution)/shard_map/ppermute | solution.py:26
  118.5 3.3 %collective-permute-done.24.refs_8_ = bf16[32,768]{1,0:T(8,128)(2,1)S(1)} collective-permute-done((bf16[32,768]{1,0:T(8,128)(2,1)S(1)}, bf16[32,768]{1,0:T(8,128)(2,1)S(1)}, u32[]{:S(2)}, u32[]{:S(2)}) %collective-permute-start.24) | collective-permute-done | bytes 49184 | tf_op jit(solution)/shard_map/ppermute | solution.py:26
  122.0 4.7 %collective-permute-done.27.refs_13_ = bf16[32,1664]{1,0:T(8,128)(2,1)S(1)} collective-permute-done((bf16[32,1664]{1,0:T(8,128)(2,1)S(1)}, bf16[32,1664]{1,0:T(8,128)(2,1)S(1)}, u32[]{:S(2)}, u32[]{:S(2)}) %collective-permute-start.27) | collective-permute-done | bytes 106528 | tf_op jit(solution)/shard_map/ppermute | solution.py:26
  126.7 2.2 %shard_map.108 = (bf16[8,32,1024]{2,1,0:T(8,128)(2,1)S(1)}, f32[8,32,1024]{2,1,0:T(8,128)S(1)}) custom-call(bf16[32,1664]{1,0:T(8,128)(2,1)S(1)} %shard_map.107.refs_0_, bf16[32,1664]{1,0:T(8,128)(2,1)S(1)} %collective-permute-done.15.refs_1_, bf16[32,1664]{1,0:T(8,128)(2,1)S(1)} %collective-permute-done.16.refs_2_, ...), custom_call_target="tpu_custom_call" | custom-call | tf_op jit(solution)/shard_map/pallas_call | solution.py:383
  130.9 14.4 %all_to_all.11.parts = bf16[8,32,1024]{2,1,0:T(8,128)(2,1)S(1)} all-to-all(bf16[8,32,1024]{2,1,0:T(8,128)(2,1)S(1)} %shard_map.109), channel_id=1, replica_groups={{0,2,4,6,8,10,12,14},{1,3,5,7,9,11,13,15},{16,18,20,22,24,26,28,30},{17..., dimensions={0} | all-to-all | bytes 1048576 | tf_op jit(solution)/shard_map/all_to_all | solution.py:50
  (58 shorter events, 33.8 us)
Async XLA Ops:
  1.4 8.5 %collective-permute-start = (bf16[400,128]{1,0:T(8,128)(2,1)S(1)}, bf16[400,128]{1,0:T(8,128)(2,1)S(1)}, u32[]{:S(2)}, u32[]{:S(2)}) collective-permute-start(bf16[400,128]{1,0:T(8,128)(2,1)S(1)} %shard_map.100), channel_id=1, source_target_pairs={{0,0},{1,16},{2,32},{3,48},{4,64},{5,80},{6,96},{7,112},{8,128},{9... | collective-permute-start | bytes 307208 | tf_op jit(solution)/shard_map/ppermute | solution.py:42
  47.0 8.9 %collective-permute-start.2 = (bf16[32,3456]{1,0:T(8,128)(2,1)S(1)}, bf16[32,3456]{1,0:T(8,128)(2,1)S(1)}, u32[]{:S(2)}, u32[]{:S(2)}) collective-permute-start(bf16[32,3456]{1,0:T(8,128)(2,1)S(1)} %get-tuple-element.96), channel_id=1, source_target_pairs={{0,16},{16,0},{32,48},{48,32},{64,80},{80,64},{96,112},{112,96},{1... | collective-permute-start | bytes 663560 | tf_op jit(solution)/shard_map/ppermute | solution.py:26
  49.7 15.7 %collective-permute-start.5 = (bf16[2,32,3456]{2,1,0:T(8,128)(2,1)S(1)}, bf16[2,32,3456]{2,1,0:T(8,128)(2,1)S(1)}, u32[]{:S(2)}, u32[]{:S(2)}) collective-permute-start(bf16[2,32,3456]{2,1,0:T(8,128)(2,1)S(1)} %get-tuple-element.102), channel_id=1, source_target_pairs={{0,16},{16,0},{32,48},{48,32},{64,80},{80,64},{96,112},{112,96},{1... | collective-permute-start | bytes 1327112 | tf_op jit(solution)/shard_map/ppermute | solution.py:26
  56.0 18.9 %collective-permute-start.8 = (bf16[2,32,3456]{2,1,0:T(8,128)(2,1)S(1)}, bf16[2,32,3456]{2,1,0:T(8,128)(2,1)S(1)}, u32[]{:S(2)}, u32[]{:S(2)}) collective-permute-start(bf16[2,32,3456]{2,1,0:T(8,128)(2,1)S(1)} %get-tuple-element.111), channel_id=1, source_target_pairs={{0,16},{16,0},{32,48},{48,32},{64,80},{80,64},{96,112},{112,96},{1... | collective-permute-start | bytes 1327112 | tf_op jit(solution)/shard_map/ppermute | solution.py:26
  58.1 4.8 %collective-permute-start.4 = (bf16[32,1792]{1,0:T(8,128)(2,1)S(1)}, bf16[32,1792]{1,0:T(8,128)(2,1)S(1)}, u32[]{:S(2)}, u32[]{:S(2)}) collective-permute-start(bf16[32,1792]{1,0:T(8,128)(2,1)S(1)} %get-tuple-element.101), channel_id=1, source_target_pairs={{0,224},{16,240},{32,0},{48,16},{64,32},{80,48},{96,64},{112,80},{... | collective-permute-start | bytes 344072 | tf_op jit(solution)/shard_map/ppermute | solution.py:26
  65.5 6.5 %collective-permute-start.6 = (bf16[32,3456]{1,0:T(8,128)(2,1)S(1)}, bf16[32,3456]{1,0:T(8,128)(2,1)S(1)}, u32[]{:S(2)}, u32[]{:S(2)}) collective-permute-start(bf16[32,3456]{1,0:T(8,128)(2,1)S(1)} %get-tuple-element.109), channel_id=1, source_target_pairs={{0,32},{16,48},{32,64},{48,80},{64,96},{80,112},{96,128},{112,144}... | collective-permute-start | bytes 663560 | tf_op jit(solution)/shard_map/ppermute | solution.py:26
  66.8 5.9 %collective-permute-start.7 = (bf16[32,3456]{1,0:T(8,128)(2,1)S(1)}, bf16[32,3456]{1,0:T(8,128)(2,1)S(1)}, u32[]{:S(2)}, u32[]{:S(2)}) collective-permute-start(bf16[32,3456]{1,0:T(8,128)(2,1)S(1)} %get-tuple-element.110), channel_id=1, source_target_pairs={{0,224},{16,240},{32,0},{48,16},{64,32},{80,48},{96,64},{112,80},{... | collective-permute-start | bytes 663560 | tf_op jit(solution)/shard_map/ppermute | solution.py:26
  67.7 16.7 %collective-permute-start.11 = (bf16[2,32,3456]{2,1,0:T(8,128)(2,1)S(1)}, bf16[2,32,3456]{2,1,0:T(8,128)(2,1)S(1)}, u32[]{:S(2)}, u32[]{:S(2)}) collective-permute-start(bf16[2,32,3456]{2,1,0:T(8,128)(2,1)S(1)} %get-tuple-element.120), channel_id=1, source_target_pairs={{0,16},{16,0},{32,48},{48,32},{64,80},{80,64},{96,112},{112,96},{1... | collective-permute-start | bytes 1327112 | tf_op jit(solution)/shard_map/ppermute | solution.py:26
  75.1 9.3 %collective-permute-start.9 = (bf16[32,3456]{1,0:T(8,128)(2,1)S(1)}, bf16[32,3456]{1,0:T(8,128)(2,1)S(1)}, u32[]{:S(2)}, u32[]{:S(2)}) collective-permute-start(bf16[32,3456]{1,0:T(8,128)(2,1)S(1)} %get-tuple-element.118), channel_id=1, source_target_pairs={{0,32},{16,48},{32,64},{48,80},{64,96},{80,112},{96,128},{112,144}... | collective-permute-start | bytes 663560 | tf_op jit(solution)/shard_map/ppermute | solution.py:26
  76.5 7.8 %collective-permute-start.10 = (bf16[32,3456]{1,0:T(8,128)(2,1)S(1)}, bf16[32,3456]{1,0:T(8,128)(2,1)S(1)}, u32[]{:S(2)}, u32[]{:S(2)}) collective-permute-start(bf16[32,3456]{1,0:T(8,128)(2,1)S(1)} %get-tuple-element.119), channel_id=1, source_target_pairs={{0,224},{16,240},{32,0},{48,16},{64,32},{80,48},{96,64},{112,80},{... | collective-permute-start | bytes 663560 | tf_op jit(solution)/shard_map/ppermute | solution.py:26
  77.3 11.3 %collective-permute-start.14 = (bf16[32,3456]{1,0:T(8,128)(2,1)S(1)}, bf16[32,3456]{1,0:T(8,128)(2,1)S(1)}, u32[]{:S(2)}, u32[]{:S(2)}) collective-permute-start(bf16[32,3456]{1,0:T(8,128)(2,1)S(1)} %get-tuple-element.128), channel_id=1, source_target_pairs={{0,16},{16,0},{32,48},{48,32},{64,80},{80,64},{96,112},{112,96},{1... | collective-permute-start | bytes 663560 | tf_op jit(solution)/shard_map/ppermute | solution.py:26
  84.5 6.5 %collective-permute-start.12 = (bf16[32,3456]{1,0:T(8,128)(2,1)S(1)}, bf16[32,3456]{1,0:T(8,128)(2,1)S(1)}, u32[]{:S(2)}, u32[]{:S(2)}) collective-permute-start(bf16[32,3456]{1,0:T(8,128)(2,1)S(1)} %get-tuple-element.126), channel_id=1, source_target_pairs={{0,32},{16,48},{32,64},{48,80},{64,96},{80,112},{96,128},{112,144}... | collective-permute-start | bytes 663560 | tf_op jit(solution)/shard_map/ppermute | solution.py:26
  85.8 6.6 %collective-permute-start.13 = (bf16[32,3456]{1,0:T(8,128)(2,1)S(1)}, bf16[32,3456]{1,0:T(8,128)(2,1)S(1)}, u32[]{:S(2)}, u32[]{:S(2)}) collective-permute-start(bf16[32,3456]{1,0:T(8,128)(2,1)S(1)} %get-tuple-element.127), channel_id=1, source_target_pairs={{0,224},{16,240},{32,0},{48,16},{64,32},{80,48},{96,64},{112,80},{... | collective-permute-start | bytes 663560 | tf_op jit(solution)/shard_map/ppermute | solution.py:26
  92.7 4.8 %collective-permute-start.15 = (bf16[32,1664]{1,0:T(8,128)(2,1)S(1)}, bf16[32,1664]{1,0:T(8,128)(2,1)S(1)}, u32[]{:S(2)}, u32[]{:S(2)}) collective-permute-start(bf16[32,1664]{1,0:T(8,128)(2,1)S(1)} %shard_map.107.refs_0_), channel_id=1, source_target_pairs={{0,32},{16,48},{32,64},{48,80},{64,96},{80,112},{96,128},{112,144}... | collective-permute-start | bytes 319496 | tf_op jit(solution)/shard_map/ppermute | solution.py:26
  94.8 5.8 %collective-permute-start.16 = (bf16[32,1664]{1,0:T(8,128)(2,1)S(1)}, bf16[32,1664]{1,0:T(8,128)(2,1)S(1)}, u32[]{:S(2)}, u32[]{:S(2)}) collective-permute-start(bf16[32,1664]{1,0:T(8,128)(2,1)S(1)} %shard_map.107.refs_0_), channel_id=1, source_target_pairs={{0,224},{16,240},{32,0},{48,16},{64,32},{80,48},{96,64},{112,80},{... | collective-permute-start | bytes 319496 | tf_op jit(solution)/shard_map/ppermute | solution.py:26
  94.8 9.0 %collective-permute-start.19 = (bf16[32,1664]{1,0:T(8,128)(2,1)S(1)}, bf16[32,1664]{1,0:T(8,128)(2,1)S(1)}, u32[]{:S(2)}, u32[]{:S(2)}) collective-permute-start(bf16[32,1664]{1,0:T(8,128)(2,1)S(1)} %shard_map.107.refs_0_), channel_id=1, source_target_pairs={{0,16},{16,0},{32,48},{48,32},{64,80},{80,64},{96,112},{112,96},{1... | collective-permute-start | bytes 319496 | tf_op jit(solution)/shard_map/ppermute | solution.py:26
  100.6 4.8 %collective-permute-start.17 = (bf16[32,1664]{1,0:T(8,128)(2,1)S(1)}, bf16[32,1664]{1,0:T(8,128)(2,1)S(1)}, u32[]{:S(2)}, u32[]{:S(2)}) collective-permute-start(bf16[32,1664]{1,0:T(8,128)(2,1)S(1)} %collective-permute-done.15.refs_1_), channel_id=1, source_target_pairs={{0,32},{16,48},{32,64},{48,80},{64,96},{80,112},{96,128},{112,144}... | collective-permute-start | bytes 319496 | tf_op jit(solution)/shard_map/ppermute | solution.py:26
  102.7 6.8 %collective-permute-start.18 = (bf16[32,1664]{1,0:T(8,128)(2,1)S(1)}, bf16[32,1664]{1,0:T(8,128)(2,1)S(1)}, u32[]{:S(2)}, u32[]{:S(2)}) collective-permute-start(bf16[32,1664]{1,0:T(8,128)(2,1)S(1)} %collective-permute-done.16.refs_2_), channel_id=1, source_target_pairs={{0,224},{16,240},{32,0},{48,16},{64,32},{80,48},{96,64},{112,80},{... | collective-permute-start | bytes 319496 | tf_op jit(solution)/shard_map/ppermute | solution.py:26
  102.7 13.4 %collective-permute-start.22 = (bf16[2,32,1664]{2,1,0:T(8,128)(2,1)S(1)}, bf16[2,32,1664]{2,1,0:T(8,128)(2,1)S(1)}, u32[]{:S(2)}, u32[]{:S(2)}) collective-permute-start(bf16[2,32,1664]{2,1,0:T(8,128)(2,1)S(1)} %pad_maximum_fusion), channel_id=1, source_target_pairs={{0,16},{16,0},{32,48},{48,32},{64,80},{80,64},{96,112},{112,96},{1... | collective-permute-start | bytes 638984 | tf_op jit(solution)/shard_map/ppermute | solution.py:26
  109.5 4.8 %collective-permute-start.20 = (bf16[32,1664]{1,0:T(8,128)(2,1)S(1)}, bf16[32,1664]{1,0:T(8,128)(2,1)S(1)}, u32[]{:S(2)}, u32[]{:S(2)}) collective-permute-start(bf16[32,1664]{1,0:T(8,128)(2,1)S(1)} %collective-permute-done.17.refs_3_), channel_id=1, source_target_pairs={{0,32},{16,48},{32,64},{48,80},{64,96},{80,112},{96,128},{112,144}... | collective-permute-start | bytes 319496 | tf_op jit(solution)/shard_map/ppermute | solution.py:26
  111.6 10.3 %collective-permute-start.25 = (bf16[2,32,1664]{2,1,0:T(8,128)(2,1)S(1)}, bf16[2,32,1664]{2,1,0:T(8,128)(2,1)S(1)}, u32[]{:S(2)}, u32[]{:S(2)}) collective-permute-start(bf16[2,32,1664]{2,1,0:T(8,128)(2,1)S(1)} %pad_maximum_fusion.1), channel_id=1, source_target_pairs={{0,16},{16,0},{32,48},{48,32},{64,80},{80,64},{96,112},{112,96},{1... | collective-permute-start | bytes 638984 | tf_op jit(solution)/shard_map/ppermute | solution.py:26
  116.1 5.8 %collective-permute-start.23 = (bf16[32,896]{1,0:T(8,128)(2,1)S(1)}, bf16[32,896]{1,0:T(8,128)(2,1)S(1)}, u32[]{:S(2)}, u32[]{:S(2)}) collective-permute-start(bf16[32,896]{1,0:T(8,128)(2,1)S(1)} %slice.6), channel_id=1, source_target_pairs={{0,32},{16,48},{32,64},{48,80},{64,96},{80,112},{96,128},{112,144}... | collective-permute-start | bytes 172040 | tf_op jit(solution)/shard_map/ppermute | solution.py:26
  118.2 8.5 %collective-permute-start.26 = (bf16[2,32,1664]{2,1,0:T(8,128)(2,1)S(1)}, bf16[2,32,1664]{2,1,0:T(8,128)(2,1)S(1)}, u32[]{:S(2)}, u32[]{:S(2)}) collective-permute-start(bf16[2,32,1664]{2,1,0:T(8,128)(2,1)S(1)} %pad_maximum_fusion.2), channel_id=1, source_target_pairs={{0,16},{16,0},{32,48},{48,32},{64,80},{80,64},{96,112},{112,96},{1... | collective-permute-start | bytes 638984 | tf_op jit(solution)/shard_map/ppermute | solution.py:26
  121.9 4.8 %collective-permute-start.27 = (bf16[32,1664]{1,0:T(8,128)(2,1)S(1)}, bf16[32,1664]{1,0:T(8,128)(2,1)S(1)}, u32[]{:S(2)}, u32[]{:S(2)}) collective-permute-start(bf16[32,1664]{1,0:T(8,128)(2,1)S(1)} %pad_maximum_fusion.3), channel_id=1, source_target_pairs={{0,16},{16,0},{32,48},{48,32},{64,80},{80,64},{96,112},{112,96},{1... | collective-permute-start | bytes 319496 | tf_op jit(solution)/shard_map/ppermute | solution.py:26
  (7 other events, 131.2 us)

commit v9 on v8

--- a/solution.py
+++ b/solution.py
@@ -64,10 +64,12 @@
 ASKED = QUERIES + 4 * 16
 
 
-def softmax(scores, seen):
+def mixed(scores, seen, values):
     scores = jnp.where(seen, scores * F32(HEAD_DIM**-0.5), F32(-1e30))
-    exponent = jnp.exp(scores - jnp.max(scores, axis=1, keepdims=True))
-    return (exponent * (F32(1) / jnp.sum(exponent, axis=1, keepdims=True))).astype(BF)
+    weights = jnp.exp(scores - jnp.max(scores, axis=1, keepdims=True)).astype(BF)
+    both = jnp.concatenate([values, jnp.ones(values.shape, BF)], axis=1)
+    product = jnp.dot(weights, both, preferred_element_type=F32)
+    return (product[:, :HEAD_DIM] / product[:, HEAD_DIM:]).astype(BF)
 
 
 def scored(queries, keys):
@@ -113,9 +115,8 @@
     stacked = jnp.concatenate(
         [queries[:, h * HEAD_DIM : (h + 1) * HEAD_DIM] for h in range(heads)], axis=0
     )
-    attention = softmax(scored(stacked, pair[:, :HEAD_DIM]), seen)
     copies[2].wait()
-    context = jnp.dot(attention, pair[:, HEAD_DIM:], preferred_element_type=F32).astype(BF)
+    context = mixed(scored(stacked, pair[:, :HEAD_DIM]), seen, pair[:, HEAD_DIM:])
     for i in range(2):
         for j in range(2):
             at = PAIRS + (2 * i + j) * 16
@@ -163,10 +164,9 @@
 FIRST = 3
 
 
-def products(rows, squares, gate_ref, up_ref, ready):
+def products(rows, squares, gate_ref, up_ref):
     tiles = gate_ref.shape[1] // LANE
     for base, ref in ((0, gate_ref), (tiles, up_ref)):
-        ready(ref)
         for t in range(0, tiles, 2):
             lanes = slice(t * LANE, min(t + 2, tiles) * LANE)
             product = jnp.dot(rows[...], ref[:, lanes], preferred_element_type=F32).astype(BF)
@@ -174,20 +174,16 @@
     yield slice(2 * tiles * LANE, (2 * tiles + 1) * LANE), squares[...]
 
 
-def first_kernel(length_ref, gain_ref, mine_ref, theirs_ref, gate_hbm, up_hbm, *refs):
-    own_ref, rows, squares, gate_ref, up_ref, far_ref, next_ref, residual, gain, sems = refs
+def first_kernel(length_ref, gain_ref, mine_ref, theirs_ref, gate_ref, up_ref, *refs):
+    own_ref, rows, squares, far_ref, next_ref, residual, gain, sem = refs
     n = ROWS_DEV
     width = own_ref.shape[1]
     half = width // 2
     batch_index, mp_index = lax.axis_index("batch"), lax.axis_index("mp")
     z, core = batch_index >> 1, mp_index & 1
     flip = (batch_index & 1) ^ core
-    fetch = pltpu.make_async_copy(gain_ref.at[pl.ds(batch_index * width, width)], gain, sems.at[0])
-    fetch_gate = pltpu.make_async_copy(gate_hbm, gate_ref, sems.at[1])
-    fetch_up = pltpu.make_async_copy(up_hbm, up_ref, sems.at[2])
+    fetch = pltpu.make_async_copy(gain_ref.at[pl.ds(batch_index * width, width)], gain, sem)
     fetch.start()
-    fetch_gate.start()
-    fetch_up.start()
 
     blocks = [(ref, i) for ref in (mine_ref, theirs_ref) for i in range(ZN)]
     options = ROWS_DEV - PREFIX
@@ -212,9 +208,8 @@
     )
     contexts = []
     for h in range(half // HEAD_DIM):
-        attention = softmax(scored(gathered(QUERIES + h * 16), keys), seen)
-        context = jnp.dot(attention, values, preferred_element_type=F32)
-        contexts.append(context.astype(BF).astype(F32))
+        context = mixed(scored(gathered(QUERIES + h * 16), keys), seen, values)
+        contexts.append(context.astype(F32))
     fetch.wait()
     scale = gain[...].reshape(1, width)
     for k, (ref, i) in enumerate(blocks):
@@ -239,8 +234,7 @@
         squares[into, :] = total.astype(BF)
     own_ref[...] = residual[mp_index >> 1]
     early = slice(0, FIRST * n)
-    ready = lambda ref: (fetch_gate if ref is gate_ref else fetch_up).wait()
-    for lanes, value in products(rows.at[early], squares.at[early], gate_ref, up_ref, ready):
+    for lanes, value in products(rows.at[early], squares.at[early], gate_ref, up_ref):
         far_ref[:, lanes] = value[:n]
         next_ref[0, :, lanes] = value[n : 2 * n]
         next_ref[1, :, lanes] = value[2 * n :]
@@ -250,9 +244,32 @@
     n = ROWS_DEV
     into = [give2.at[0], give2.at[1], give1.at[0], give1.at[1], give0, *kept]
     late = slice(FIRST * n, len(ORDER) * n)
-    for lanes, value in products(rows.at[late], squares.at[late], gate_ref, up_ref, lambda ref: None):
+    for lanes, value in products(rows.at[late], squares.at[late], gate_ref, up_ref):
         for i, ref in enumerate(into):
             ref[:, lanes] = value[i * n : (i + 1) * n]
+
+
+def fetch_kernel(gate_hbm, up_hbm, gate_ref, up_ref, sems):
+    copies = (
+        pltpu.make_async_copy(gate_hbm, gate_ref, sems.at[0]),
+        pltpu.make_async_copy(up_hbm, up_ref, sems.at[1]),
+    )
+    for copy in copies:
+        copy.start()
+    for copy in copies:
+        copy.wait()
+
+
+def fetch(gate_weight, up_weight):
+    return pl.pallas_call(
+        fetch_kernel,
+        out_shape=in_vmem((gate_weight.shape, BF), (up_weight.shape, BF)),
+        in_specs=[HBM, HBM],
+        out_specs=(VMEM, VMEM),
+        scratch_shapes=[pltpu.SemaphoreType.DMA((2,))],
+        compiler_params=PARAMS,
+        cost_estimate=cost(1, *gate_weight.shape),
+    )(in_hbm(gate_weight), in_hbm(up_weight))
 
 
 def project(prefix_len, norm_gain, mine, theirs, gate_weight, up_weight):
@@ -260,33 +277,31 @@
     n = ROWS_DEV
     part = (n, 2 * hidden_width + LANE)
     all_rows = len(ORDER) * n
-    own, rows, squares, gate, up, far, following = pl.pallas_call(
+    own, rows, squares, far, following = pl.pallas_call(
         first_kernel,
         out_shape=in_vmem(
             ((n, width), BF),
             ((all_rows, width), BF),
             ((all_rows, LANE), BF),
-            (gate_weight.shape, BF),
-            (up_weight.shape, BF),
             (part, BF),
             ((2, *part), BF),
         ),
-        in_specs=[SMEM, HBM, VMEM, VMEM, HBM, HBM],
-        out_specs=(VMEM,) * 7,
+        in_specs=[SMEM, HBM, VMEM, VMEM, VMEM, VMEM],
+        out_specs=(VMEM,) * 5,
         scratch_shapes=[
             pltpu.VMEM((ZN, n, width), BF),
             pltpu.VMEM((width,), F32),
-            pltpu.SemaphoreType.DMA((3,)),
+            pltpu.SemaphoreType.DMA(()),
         ],
         compiler_params=PARAMS,
-    )(prefix_len, in_hbm(norm_gain), mine, theirs, in_hbm(gate_weight), in_hbm(up_weight))
+    )(prefix_len, in_hbm(norm_gain), mine, theirs, gate_weight, up_weight)
     give2, give1, give0, *kept = local(
         rest_kernel,
         [((2, *part), BF)] * 2 + [(part, BF)] * 9,
         rows,
         squares,
-        gate,
-        up,
+        gate_weight,
+        up_weight,
         cost=cost((len(ORDER) - FIRST) * n, width, part[1]),
     )
     return own, [give0, give1, give2, following, far], kept
@@ -421,7 +436,8 @@
     hidden_width = gate_weight.shape[1]
 
     sent = prepare(prefix_len, question, queries, hidden_in, key_cache, value_cache)
-    came = transpose_mesh(sent)
+    sent, gate_weight, up_weight = after(sent, gate_weight, up_weight)
+    came, gate_weight, up_weight = after(transpose_mesh(sent), *fetch(gate_weight, up_weight))
     mine = over_plane(jnp.broadcast_to(came[None], (ZN, *came.shape)))
     theirs = core_pair(mine)
     own, give, kept = project(prefix_len, norm_gain, mine, theirs, gate_weight, up_weight)

time: 146 us -> 145 us (level)
  waiting for transfers between devices: 56.6 us -> 53.7 us
  Pallas kernels: 12.9 us -> 14.7 us
    ppermute x1, waiting for transfers between devices: 5.44 us -> 2.41 us  [transpose_mesh(): lax.ppermute(value, ('batch', 'mp'), [(b * 16 + m, m * 16 + b) for b in r...]
    pallas_call x0 -> x1, Pallas kernels: none -> 3.02 us  [fetch(): pl.pallas_call(fetch_kernel, out_shape=in_vmem((gate_weight.shape, BF), (...]
  transfers between devices with their start and end apart: 29 -> 29, of which waited for: 22 -> 22; matrix products, arithmetic and copies ran while one was open for 0% -> 0% of each run, Pallas kernels for 3% -> 5%
where the time goes in v9:
time: 145 us
  waiting for transfers between devices  53.7 us (37%)
  blocking collectives  44.7 us (31%)
  starting transfers between devices  31.5 us (22%)
  Pallas kernels  14.7 us (10%)
    ppermute x28, waiting for transfers between devices, permute(): return lax.ppermute(value, axis, [(i, target(i)) for i in range(count)])  51.3 us
    all_to_all x2, blocking collectives, over_plane(): lax.all_to_all(value, 'mp', 0, 0, axis_index_groups=PLANE, tiled=True)  44.7 us
    ppermute x28, starting transfers between devices, permute(): return lax.ppermute(value, axis, [(i, target(i)) for i in range(count)])  28.4 us
    pallas_call x7, Pallas kernels, local(): pl.pallas_call(kernel, out_shape=in_vmem(*shapes), in_specs=[VMEM] * len(...  4.14 us
    pallas_call x1, Pallas kernels, project(): pl.pallas_call(first_kernel, out_shape=in_vmem(((n, width), BF), ((all_ro...  3.38 us
    ppermute x1, starting transfers between devices, transpose_mesh(): lax.ppermute(value, ('batch', 'mp'), [(b * 16 + m, m * 16 + b) for b in r...  3.03 us
    pallas_call x1, Pallas kernels, fetch(): pl.pallas_call(fetch_kernel, out_shape=in_vmem((gate_weight.shape, BF), (...  3.02 us
  transfers between devices with their start and end apart: 29, of which 22 were waited for; matrix products, arithmetic and copies ran while one was open for 0% of the time, Pallas kernels for 5%

profile of v9, /device:TPU:32, one launch (start us, length us, event | category | flops | bytes accessed | tf_op | source)
XLA Modules:
  0.0 144.9 jit_solution(17085009788184885258)
XLA Ops:
  1.3 3.0 %collective-permute-start = (bf16[400,128]{1,0:T(8,128)(2,1)S(1)}, bf16[400,128]{1,0:T(8,128)(2,1)S(1)}, u32[]{:S(2)}, u32[]{:S(2)}) collective-permute-start(bf16[400,128]{1,0:T(8,128)(2,1)S(1)} %shard_map.100), channel_id=1, source_target_pairs={{0,0},{1,16},{2,32},{3,48},{4,64},{5,80},{6,96},{7,112},{8,128},{9... | collective-permute-start | bytes 307208 | tf_op jit(solution)/shard_map/ppermute | solution.py:42
  4.4 3.0 %shard_map.101 = (bf16[1024,1664]{1,0:T(8,128)(2,1)S(1)}, bf16[1024,1664]{1,0:T(8,128)(2,1)S(1)}) custom-call(bf16[1024,1664]{1,0:T(8,128)(2,1)} %gate_hbm, bf16[1024,1664]{1,0:T(8,128)(2,1)} %up_hbm), custom_call_target="tpu_custom_call" | custom-call | flops 3407872 | bytes 3407872 | tf_op jit(solution)/shard_map/pallas_call | solution.py:264
  7.4 2.4 %collective-permute-done = bf16[400,128]{1,0:T(8,128)(2,1)S(1)} collective-permute-done((bf16[400,128]{1,0:T(8,128)(2,1)S(1)}, bf16[400,128]{1,0:T(8,128)(2,1)S(1)}, u32[]{:S(2)}, u32[]{:S(2)}) %collective-permute-start) | collective-permute-done | bytes 102432 | tf_op jit(solution)/shard_map/ppermute | solution.py:42
  9.9 30.2 %all_to_all.10.mine_ref = bf16[8,400,128]{2,1,0:T(8,128)(2,1)S(1)} all-to-all(bf16[8,400,128]{2,1,0:T(8,128)(2,1)S(1)} %broadcast_in_dim.2), channel_id=1, replica_groups={{0,2,4,6,8,10,12,14},{1,3,5,7,9,11,13,15},{16,18,20,22,24,26,28,30},{17..., dimensions={0} | all-to-all | bytes 1638400 | tf_op jit(solution)/shard_map/all_to_all | solution.py:50
  40.2 2.3 %collective-permute-done.1.theirs_ref = bf16[8,400,128]{2,1,0:T(8,128)(2,1)S(1)} collective-permute-done((bf16[8,400,128]{2,1,0:T(8,128)(2,1)S(1)}, bf16[8,400,128]{2,1,0:T(8,128)(2,1)S(1)}, u32[]{:S(2)}, u32[]{:S(2)}) %collective-permute-start.1) | collective-permute-done | bytes 819232 | tf_op jit(solution)/shard_map/ppermute | solution.py:26
  42.5 3.4 %shard_map.102 = (bf16[32,1024]{1,0:T(8,128)(2,1)S(1)}, bf16[512,1024]{1,0:T(8,128)(2,1)S(1)}, bf16[512,128]{1,0:T(8,128)(2,1)S(1)}, bf16[32,3456]{1,0:T(8,128)(2,1)S(1)}, bf16[2,32,3456]{2,1,0:T(8,128)(2,1)S(1)}) custom-call(s32[16]{0:T(128)S(1)} %copy-done.1, f32[16384]{0:T(1024)} %gain_ref.1, bf16[8,400,128]{2,1,0:T(8,128)(2,1)S(1)} %all_to_all.10.mine_ref, ...), custom_call_target="tpu_custom_call" | custom-call | tf_op jit(solution)/shard_map/pallas_call | solution.py:280
  45.9 2.7 %collective-permute-start.2 = (bf16[32,3456]{1,0:T(8,128)(2,1)S(1)}, bf16[32,3456]{1,0:T(8,128)(2,1)S(1)}, u32[]{:S(2)}, u32[]{:S(2)}) collective-permute-start(bf16[32,3456]{1,0:T(8,128)(2,1)S(1)} %get-tuple-element.108), channel_id=1, source_target_pairs={{0,16},{16,0},{32,48},{48,32},{64,80},{80,64},{96,112},{112,96},{1... | collective-permute-start | bytes 663560 | tf_op jit(solution)/shard_map/ppermute | solution.py:26
  48.7 3.3 %shard_map.103 = (bf16[2,32,3456]{2,1,0:T(8,128)(2,1)S(1)}, bf16[2,32,3456]{2,1,0:T(8,128)(2,1)S(1)}, bf16[32,3456]{1,0:T(8,128)(2,1)S(1)}, bf16[32,3456]{1,0:T(...) custom-call(bf16[512,1024]{1,0:T(8,128)(2,1)S(1)} %get-tuple-element, ...), custom_call_target="tpu_custom_call" | custom-call | flops 2944401408 | bytes 7077888 | tf_op jit(solution)/shard_map/pallas_call | solution.py:357
  51.9 2.8 %collective-permute-done.2.x = bf16[32,3456]{1,0:T(8,128)(2,1)S(1)} collective-permute-done((bf16[32,3456]{1,0:T(8,128)(2,1)S(1)}, bf16[32,3456]{1,0:T(8,128)(2,1)S(1)}, u32[]{:S(2)}, u32[]{:S(2)}) %collective-permute-start.2) | collective-permute-done | bytes 221216 | tf_op jit(solution)/shard_map/ppermute | solution.py:26
  54.8 2.1 %collective-permute-start.8 = (bf16[2,32,3456]{2,1,0:T(8,128)(2,1)S(1)}, bf16[2,32,3456]{2,1,0:T(8,128)(2,1)S(1)}, u32[]{:S(2)}, u32[]{:S(2)}) collective-permute-start(bf16[2,32,3456]{2,1,0:T(8,128)(2,1)S(1)} %get-tuple-element.123), channel_id=1, source_target_pairs={{0,16},{16,0},{32,48},{48,32},{64,80},{80,64},{96,112},{112,96},{1... | collective-permute-start | bytes 1327112 | tf_op jit(solution)/shard_map/ppermute | solution.py:26
  59.0 2.7 %collective-permute-done.3.up = bf16[32,1664]{1,0:T(8,128)(2,1)S(1)} collective-permute-done((bf16[32,1664]{1,0:T(8,128)(2,1)S(1)}, bf16[32,1664]{1,0:T(8,128)(2,1)S(1)}, u32[]{:S(2)}, u32[]{:S(2)}) %collective-permute-start.3) | collective-permute-done | bytes 106528 | tf_op jit(solution)/shard_map/ppermute | solution.py:26
  61.8 2.5 %collective-permute-done.5.x = bf16[2,32,3456]{2,1,0:T(8,128)(2,1)S(1)} collective-permute-done((bf16[2,32,3456]{2,1,0:T(8,128)(2,1)S(1)}, bf16[2,32,3456]{2,1,0:T(8,128)(2,1)S(1)}, u32[]{:S(2)}, u32[]{:S(2)}) %collective-permute-start.5) | collective-permute-done | bytes 442400 | tf_op jit(solution)/shard_map/ppermute | solution.py:26
  68.6 5.2 %collective-permute-done.8.x = bf16[2,32,3456]{2,1,0:T(8,128)(2,1)S(1)} collective-permute-done((bf16[2,32,3456]{2,1,0:T(8,128)(2,1)S(1)}, bf16[2,32,3456]{2,1,0:T(8,128)(2,1)S(1)}, u32[]{:S(2)}, u32[]{:S(2)}) %collective-permute-start.8) | collective-permute-done | bytes 442400 | tf_op jit(solution)/shard_map/ppermute | solution.py:26
  78.1 2.4 %collective-permute-done.9.up = bf16[32,3456]{1,0:T(8,128)(2,1)S(1)} collective-permute-done((bf16[32,3456]{1,0:T(8,128)(2,1)S(1)}, bf16[32,3456]{1,0:T(8,128)(2,1)S(1)}, u32[]{:S(2)}, u32[]{:S(2)}) %collective-permute-start.9) | collective-permute-done | bytes 221216 | tf_op jit(solution)/shard_map/ppermute | solution.py:26
  87.5 2.5 %collective-permute-done.12.up = bf16[32,3456]{1,0:T(8,128)(2,1)S(1)} collective-permute-done((bf16[32,3456]{1,0:T(8,128)(2,1)S(1)}, bf16[32,3456]{1,0:T(8,128)(2,1)S(1)}, u32[]{:S(2)}, u32[]{:S(2)}) %collective-permute-start.12) | collective-permute-done | bytes 221216 | tf_op jit(solution)/shard_map/ppermute | solution.py:26
  91.3 2.1 %collective-permute-start.15 = (bf16[32,1664]{1,0:T(8,128)(2,1)S(1)}, bf16[32,1664]{1,0:T(8,128)(2,1)S(1)}, u32[]{:S(2)}, u32[]{:S(2)}) collective-permute-start(bf16[32,1664]{1,0:T(8,128)(2,1)S(1)} %shard_map.108.refs_0_), channel_id=1, source_target_pairs={{0,32},{16,48},{32,64},{48,80},{64,96},{80,112},{96,128},{112,144}... | collective-permute-start | bytes 319496 | tf_op jit(solution)/shard_map/ppermute | solution.py:26
  96.1 3.3 %collective-permute-done.16.refs_2_ = bf16[32,1664]{1,0:T(8,128)(2,1)S(1)} collective-permute-done((bf16[32,1664]{1,0:T(8,128)(2,1)S(1)}, bf16[32,1664]{1,0:T(8,128)(2,1)S(1)}, u32[]{:S(2)}, u32[]{:S(2)}) %collective-permute-start.16) | collective-permute-done | bytes 106528 | tf_op jit(solution)/shard_map/ppermute | solution.py:26
  99.4 2.1 %collective-permute-start.17 = (bf16[32,1664]{1,0:T(8,128)(2,1)S(1)}, bf16[32,1664]{1,0:T(8,128)(2,1)S(1)}, u32[]{:S(2)}, u32[]{:S(2)}) collective-permute-start(bf16[32,1664]{1,0:T(8,128)(2,1)S(1)} %collective-permute-done.15.refs_1_), channel_id=1, source_target_pairs={{0,32},{16,48},{32,64},{48,80},{64,96},{80,112},{96,128},{112,144}... | collective-permute-start | bytes 319496 | tf_op jit(solution)/shard_map/ppermute | solution.py:26
  104.2 4.1 %collective-permute-done.18.refs_4_ = bf16[32,1664]{1,0:T(8,128)(2,1)S(1)} collective-permute-done((bf16[32,1664]{1,0:T(8,128)(2,1)S(1)}, bf16[32,1664]{1,0:T(8,128)(2,1)S(1)}, u32[]{:S(2)}, u32[]{:S(2)}) %collective-permute-start.18) | collective-permute-done | bytes 106528 | tf_op jit(solution)/shard_map/ppermute | solution.py:26
  110.5 2.6 %collective-permute-done.20.refs_5_ = bf16[32,1664]{1,0:T(8,128)(2,1)S(1)} collective-permute-done((bf16[32,1664]{1,0:T(8,128)(2,1)S(1)}, bf16[32,1664]{1,0:T(8,128)(2,1)S(1)}, u32[]{:S(2)}, u32[]{:S(2)}) %collective-permute-start.20) | collective-permute-done | bytes 106528 | tf_op jit(solution)/shard_map/ppermute | solution.py:26
  117.4 3.3 %collective-permute-done.24.refs_8_ = bf16[32,768]{1,0:T(8,128)(2,1)S(1)} collective-permute-done((bf16[32,768]{1,0:T(8,128)(2,1)S(1)}, bf16[32,768]{1,0:T(8,128)(2,1)S(1)}, u32[]{:S(2)}, u32[]{:S(2)}) %collective-permute-start.24) | collective-permute-done | bytes 49184 | tf_op jit(solution)/shard_map/ppermute | solution.py:26
  120.8 4.7 %collective-permute-done.27.refs_13_ = bf16[32,1664]{1,0:T(8,128)(2,1)S(1)} collective-permute-done((bf16[32,1664]{1,0:T(8,128)(2,1)S(1)}, bf16[32,1664]{1,0:T(8,128)(2,1)S(1)}, u32[]{:S(2)}, u32[]{:S(2)}) %collective-permute-start.27) | collective-permute-done | bytes 106528 | tf_op jit(solution)/shard_map/ppermute | solution.py:26
  125.5 2.2 %shard_map.109 = (bf16[8,32,1024]{2,1,0:T(8,128)(2,1)S(1)}, f32[8,32,1024]{2,1,0:T(8,128)S(1)}) custom-call(bf16[32,1664]{1,0:T(8,128)(2,1)S(1)} %shard_map.108.refs_0_, bf16[32,1664]{1,0:T(8,128)(2,1)S(1)} %collective-permute-done.15.refs_1_, bf16[32,1664]{1,0:T(8,128)(2,1)S(1)} %collective-permute-done.16.refs_2_, ...), custom_call_target="tpu_custom_call" | custom-call | tf_op jit(solution)/shard_map/pallas_call | solution.py:398
  129.8 14.4 %all_to_all.11.parts = bf16[8,32,1024]{2,1,0:T(8,128)(2,1)S(1)} all-to-all(bf16[8,32,1024]{2,1,0:T(8,128)(2,1)S(1)} %shard_map.110), channel_id=1, replica_groups={{0,2,4,6,8,10,12,14},{1,3,5,7,9,11,13,15},{16,18,20,22,24,26,28,30},{17..., dimensions={0} | all-to-all | bytes 1048576 | tf_op jit(solution)/shard_map/all_to_all | solution.py:50
  (59 shorter events, 35.4 us)
Async XLA Ops:
  1.3 8.5 %collective-permute-start = (bf16[400,128]{1,0:T(8,128)(2,1)S(1)}, bf16[400,128]{1,0:T(8,128)(2,1)S(1)}, u32[]{:S(2)}, u32[]{:S(2)}) collective-permute-start(bf16[400,128]{1,0:T(8,128)(2,1)S(1)} %shard_map.100), channel_id=1, source_target_pairs={{0,0},{1,16},{2,32},{3,48},{4,64},{5,80},{6,96},{7,112},{8,128},{9... | collective-permute-start | bytes 307208 | tf_op jit(solution)/shard_map/ppermute | solution.py:42
  45.9 8.9 %collective-permute-start.2 = (bf16[32,3456]{1,0:T(8,128)(2,1)S(1)}, bf16[32,3456]{1,0:T(8,128)(2,1)S(1)}, u32[]{:S(2)}, u32[]{:S(2)}) collective-permute-start(bf16[32,3456]{1,0:T(8,128)(2,1)S(1)} %get-tuple-element.108), channel_id=1, source_target_pairs={{0,16},{16,0},{32,48},{48,32},{64,80},{80,64},{96,112},{112,96},{1... | collective-permute-start | bytes 663560 | tf_op jit(solution)/shard_map/ppermute | solution.py:26
  48.6 15.7 %collective-permute-start.5 = (bf16[2,32,3456]{2,1,0:T(8,128)(2,1)S(1)}, bf16[2,32,3456]{2,1,0:T(8,128)(2,1)S(1)}, u32[]{:S(2)}, u32[]{:S(2)}) collective-permute-start(bf16[2,32,3456]{2,1,0:T(8,128)(2,1)S(1)} %get-tuple-element.114), channel_id=1, source_target_pairs={{0,16},{16,0},{32,48},{48,32},{64,80},{80,64},{96,112},{112,96},{1... | collective-permute-start | bytes 1327112 | tf_op jit(solution)/shard_map/ppermute | solution.py:26
  54.8 18.9 %collective-permute-start.8 = (bf16[2,32,3456]{2,1,0:T(8,128)(2,1)S(1)}, bf16[2,32,3456]{2,1,0:T(8,128)(2,1)S(1)}, u32[]{:S(2)}, u32[]{:S(2)}) collective-permute-start(bf16[2,32,3456]{2,1,0:T(8,128)(2,1)S(1)} %get-tuple-element.123), channel_id=1, source_target_pairs={{0,16},{16,0},{32,48},{48,32},{64,80},{80,64},{96,112},{112,96},{1... | collective-permute-start | bytes 1327112 | tf_op jit(solution)/shard_map/ppermute | solution.py:26
  57.0 4.8 %collective-permute-start.4 = (bf16[32,1792]{1,0:T(8,128)(2,1)S(1)}, bf16[32,1792]{1,0:T(8,128)(2,1)S(1)}, u32[]{:S(2)}, u32[]{:S(2)}) collective-permute-start(bf16[32,1792]{1,0:T(8,128)(2,1)S(1)} %get-tuple-element.113), channel_id=1, source_target_pairs={{0,224},{16,240},{32,0},{48,16},{64,32},{80,48},{96,64},{112,80},{... | collective-permute-start | bytes 344072 | tf_op jit(solution)/shard_map/ppermute | solution.py:26
  64.4 9.3 %collective-permute-start.6 = (bf16[32,3456]{1,0:T(8,128)(2,1)S(1)}, bf16[32,3456]{1,0:T(8,128)(2,1)S(1)}, u32[]{:S(2)}, u32[]{:S(2)}) collective-permute-start(bf16[32,3456]{1,0:T(8,128)(2,1)S(1)} %get-tuple-element.121), channel_id=1, source_target_pairs={{0,32},{16,48},{32,64},{48,80},{64,96},{80,112},{96,128},{112,144}... | collective-permute-start | bytes 663560 | tf_op jit(solution)/shard_map/ppermute | solution.py:26
  65.7 8.1 %collective-permute-start.7 = (bf16[32,3456]{1,0:T(8,128)(2,1)S(1)}, bf16[32,3456]{1,0:T(8,128)(2,1)S(1)}, u32[]{:S(2)}, u32[]{:S(2)}) collective-permute-start(bf16[32,3456]{1,0:T(8,128)(2,1)S(1)} %get-tuple-element.122), channel_id=1, source_target_pairs={{0,224},{16,240},{32,0},{48,16},{64,32},{80,48},{96,64},{112,80},{... | collective-permute-start | bytes 663560 | tf_op jit(solution)/shard_map/ppermute | solution.py:26
  66.5 16.7 %collective-permute-start.11 = (bf16[2,32,3456]{2,1,0:T(8,128)(2,1)S(1)}, bf16[2,32,3456]{2,1,0:T(8,128)(2,1)S(1)}, u32[]{:S(2)}, u32[]{:S(2)}) collective-permute-start(bf16[2,32,3456]{2,1,0:T(8,128)(2,1)S(1)} %get-tuple-element.132), channel_id=1, source_target_pairs={{0,16},{16,0},{32,48},{48,32},{64,80},{80,64},{96,112},{112,96},{1... | collective-permute-start | bytes 1327112 | tf_op jit(solution)/shard_map/ppermute | solution.py:26
  73.9 6.6 %collective-permute-start.9 = (bf16[32,3456]{1,0:T(8,128)(2,1)S(1)}, bf16[32,3456]{1,0:T(8,128)(2,1)S(1)}, u32[]{:S(2)}, u32[]{:S(2)}) collective-permute-start(bf16[32,3456]{1,0:T(8,128)(2,1)S(1)} %get-tuple-element.130), channel_id=1, source_target_pairs={{0,32},{16,48},{32,64},{48,80},{64,96},{80,112},{96,128},{112,144}... | collective-permute-start | bytes 663560 | tf_op jit(solution)/shard_map/ppermute | solution.py:26
  75.2 6.4 %collective-permute-start.10 = (bf16[32,3456]{1,0:T(8,128)(2,1)S(1)}, bf16[32,3456]{1,0:T(8,128)(2,1)S(1)}, u32[]{:S(2)}, u32[]{:S(2)}) collective-permute-start(bf16[32,3456]{1,0:T(8,128)(2,1)S(1)} %get-tuple-element.131), channel_id=1, source_target_pairs={{0,224},{16,240},{32,0},{48,16},{64,32},{80,48},{96,64},{112,80},{... | collective-permute-start | bytes 663560 | tf_op jit(solution)/shard_map/ppermute | solution.py:26
  76.0 11.4 %collective-permute-start.14 = (bf16[32,3456]{1,0:T(8,128)(2,1)S(1)}, bf16[32,3456]{1,0:T(8,128)(2,1)S(1)}, u32[]{:S(2)}, u32[]{:S(2)}) collective-permute-start(bf16[32,3456]{1,0:T(8,128)(2,1)S(1)} %get-tuple-element.140), channel_id=1, source_target_pairs={{0,16},{16,0},{32,48},{48,32},{64,80},{80,64},{96,112},{112,96},{1... | collective-permute-start | bytes 663560 | tf_op jit(solution)/shard_map/ppermute | solution.py:26
  83.4 6.6 %collective-permute-start.12 = (bf16[32,3456]{1,0:T(8,128)(2,1)S(1)}, bf16[32,3456]{1,0:T(8,128)(2,1)S(1)}, u32[]{:S(2)}, u32[]{:S(2)}) collective-permute-start(bf16[32,3456]{1,0:T(8,128)(2,1)S(1)} %get-tuple-element.138), channel_id=1, source_target_pairs={{0,32},{16,48},{32,64},{48,80},{64,96},{80,112},{96,128},{112,144}... | collective-permute-start | bytes 663560 | tf_op jit(solution)/shard_map/ppermute | solution.py:26
  84.7 6.4 %collective-permute-start.13 = (bf16[32,3456]{1,0:T(8,128)(2,1)S(1)}, bf16[32,3456]{1,0:T(8,128)(2,1)S(1)}, u32[]{:S(2)}, u32[]{:S(2)}) collective-permute-start(bf16[32,3456]{1,0:T(8,128)(2,1)S(1)} %get-tuple-element.139), channel_id=1, source_target_pairs={{0,224},{16,240},{32,0},{48,16},{64,32},{80,48},{96,64},{112,80},{... | collective-permute-start | bytes 663560 | tf_op jit(solution)/shard_map/ppermute | solution.py:26
  91.3 4.8 %collective-permute-start.15 = (bf16[32,1664]{1,0:T(8,128)(2,1)S(1)}, bf16[32,1664]{1,0:T(8,128)(2,1)S(1)}, u32[]{:S(2)}, u32[]{:S(2)}) collective-permute-start(bf16[32,1664]{1,0:T(8,128)(2,1)S(1)} %shard_map.108.refs_0_), channel_id=1, source_target_pairs={{0,32},{16,48},{32,64},{48,80},{64,96},{80,112},{96,128},{112,144}... | collective-permute-start | bytes 319496 | tf_op jit(solution)/shard_map/ppermute | solution.py:26
  93.5 5.9 %collective-permute-start.16 = (bf16[32,1664]{1,0:T(8,128)(2,1)S(1)}, bf16[32,1664]{1,0:T(8,128)(2,1)S(1)}, u32[]{:S(2)}, u32[]{:S(2)}) collective-permute-start(bf16[32,1664]{1,0:T(8,128)(2,1)S(1)} %shard_map.108.refs_0_), channel_id=1, source_target_pairs={{0,224},{16,240},{32,0},{48,16},{64,32},{80,48},{96,64},{112,80},{... | collective-permute-start | bytes 319496 | tf_op jit(solution)/shard_map/ppermute | solution.py:26
  93.5 9.1 %collective-permute-start.19 = (bf16[32,1664]{1,0:T(8,128)(2,1)S(1)}, bf16[32,1664]{1,0:T(8,128)(2,1)S(1)}, u32[]{:S(2)}, u32[]{:S(2)}) collective-permute-start(bf16[32,1664]{1,0:T(8,128)(2,1)S(1)} %shard_map.108.refs_0_), channel_id=1, source_target_pairs={{0,16},{16,0},{32,48},{48,32},{64,80},{80,64},{96,112},{112,96},{1... | collective-permute-start | bytes 319496 | tf_op jit(solution)/shard_map/ppermute | solution.py:26
  99.4 4.8 %collective-permute-start.17 = (bf16[32,1664]{1,0:T(8,128)(2,1)S(1)}, bf16[32,1664]{1,0:T(8,128)(2,1)S(1)}, u32[]{:S(2)}, u32[]{:S(2)}) collective-permute-start(bf16[32,1664]{1,0:T(8,128)(2,1)S(1)} %collective-permute-done.15.refs_1_), channel_id=1, source_target_pairs={{0,32},{16,48},{32,64},{48,80},{64,96},{80,112},{96,128},{112,144}... | collective-permute-start | bytes 319496 | tf_op jit(solution)/shard_map/ppermute | solution.py:26
  101.5 6.8 %collective-permute-start.18 = (bf16[32,1664]{1,0:T(8,128)(2,1)S(1)}, bf16[32,1664]{1,0:T(8,128)(2,1)S(1)}, u32[]{:S(2)}, u32[]{:S(2)}) collective-permute-start(bf16[32,1664]{1,0:T(8,128)(2,1)S(1)} %collective-permute-done.16.refs_2_), channel_id=1, source_target_pairs={{0,224},{16,240},{32,0},{48,16},{64,32},{80,48},{96,64},{112,80},{... | collective-permute-start | bytes 319496 | tf_op jit(solution)/shard_map/ppermute | solution.py:26
  101.5 13.4 %collective-permute-start.22 = (bf16[2,32,1664]{2,1,0:T(8,128)(2,1)S(1)}, bf16[2,32,1664]{2,1,0:T(8,128)(2,1)S(1)}, u32[]{:S(2)}, u32[]{:S(2)}) collective-permute-start(bf16[2,32,1664]{2,1,0:T(8,128)(2,1)S(1)} %pad_maximum_fusion), channel_id=1, source_target_pairs={{0,16},{16,0},{32,48},{48,32},{64,80},{80,64},{96,112},{112,96},{1... | collective-permute-start | bytes 638984 | tf_op jit(solution)/shard_map/ppermute | solution.py:26
  108.3 4.8 %collective-permute-start.20 = (bf16[32,1664]{1,0:T(8,128)(2,1)S(1)}, bf16[32,1664]{1,0:T(8,128)(2,1)S(1)}, u32[]{:S(2)}, u32[]{:S(2)}) collective-permute-start(bf16[32,1664]{1,0:T(8,128)(2,1)S(1)} %collective-permute-done.17.refs_3_), channel_id=1, source_target_pairs={{0,32},{16,48},{32,64},{48,80},{64,96},{80,112},{96,128},{112,144}... | collective-permute-start | bytes 319496 | tf_op jit(solution)/shard_map/ppermute | solution.py:26
  110.5 10.3 %collective-permute-start.25 = (bf16[2,32,1664]{2,1,0:T(8,128)(2,1)S(1)}, bf16[2,32,1664]{2,1,0:T(8,128)(2,1)S(1)}, u32[]{:S(2)}, u32[]{:S(2)}) collective-permute-start(bf16[2,32,1664]{2,1,0:T(8,128)(2,1)S(1)} %pad_maximum_fusion.1), channel_id=1, source_target_pairs={{0,16},{16,0},{32,48},{48,32},{64,80},{80,64},{96,112},{112,96},{1... | collective-permute-start | bytes 638984 | tf_op jit(solution)/shard_map/ppermute | solution.py:26
  115.0 5.8 %collective-permute-start.23 = (bf16[32,896]{1,0:T(8,128)(2,1)S(1)}, bf16[32,896]{1,0:T(8,128)(2,1)S(1)}, u32[]{:S(2)}, u32[]{:S(2)}) collective-permute-start(bf16[32,896]{1,0:T(8,128)(2,1)S(1)} %slice.6), channel_id=1, source_target_pairs={{0,32},{16,48},{32,64},{48,80},{64,96},{80,112},{96,128},{112,144}... | collective-permute-start | bytes 172040 | tf_op jit(solution)/shard_map/ppermute | solution.py:26
  117.1 8.5 %collective-permute-start.26 = (bf16[2,32,1664]{2,1,0:T(8,128)(2,1)S(1)}, bf16[2,32,1664]{2,1,0:T(8,128)(2,1)S(1)}, u32[]{:S(2)}, u32[]{:S(2)}) collective-permute-start(bf16[2,32,1664]{2,1,0:T(8,128)(2,1)S(1)} %pad_maximum_fusion.2), channel_id=1, source_target_pairs={{0,16},{16,0},{32,48},{48,32},{64,80},{80,64},{96,112},{112,96},{1... | collective-permute-start | bytes 638984 | tf_op jit(solution)/shard_map/ppermute | solution.py:26
  120.7 4.8 %collective-permute-start.27 = (bf16[32,1664]{1,0:T(8,128)(2,1)S(1)}, bf16[32,1664]{1,0:T(8,128)(2,1)S(1)}, u32[]{:S(2)}, u32[]{:S(2)}) collective-permute-start(bf16[32,1664]{1,0:T(8,128)(2,1)S(1)} %pad_maximum_fusion.3), channel_id=1, source_target_pairs={{0,16},{16,0},{32,48},{48,32},{64,80},{80,64},{96,112},{112,96},{1... | collective-permute-start | bytes 319496 | tf_op jit(solution)/shard_map/ppermute | solution.py:26
  (7 other events, 129.8 us)

commit v10 on v9

--- a/solution.py
+++ b/solution.py
@@ -28,6 +28,18 @@
 
 def along_z(value, step):
     return permute(value, "batch", lambda i: (i + 2 * step) % 16)
+
+
+def mirrored(value, step):
+    return lax.ppermute(
+        value,
+        ("batch", "mp"),
+        [
+            (b * 16 + m, (b + 2 * step * (1 - 2 * (m % 2))) % 16 * 16 + m)
+            for b in range(16)
+            for m in range(16)
+        ],
+    )
 
 
 def x_pair(value):
@@ -374,7 +386,7 @@
     partners = {0: x0, 7: x1.at[0], 1: x1.at[1], 6: x2.at[0], 2: x2.at[1], 5: x3.at[0], 3: x3.at[1], FAR: x4}
     for s in range(ZN):
         for j, found in enumerate((ours, partners)):
-            target = (z + s) & (ZN - 1)
+            target = (z + s * (1 - 2 * (mp_index & 1))) & (ZN - 1)
             other = (flip + j) & 1
             at = pl.ds(pl.multiple_of((1 - other) * ZN * n + target * n, n), n)
             if s in found:
@@ -471,7 +483,7 @@
     blocks, partners = [hidden], []
     for step in range(3):
         up, down, across = after(up, down, across)
-        up, down, came = along_z(up, 1), along_z(down, -1), x_pair(across)
+        up, down, came = mirrored(up, 1), mirrored(down, -1), x_pair(across)
         if partners:
             up, down, partners[-1] = after(up, down, partners[-1])
         else:
@@ -481,7 +493,7 @@
         across = jnp.stack([up, down])
     half = (hidden_width // LANE + 1) // 2 * LANE
     up, down, across = after(up[:, :half], down[:, half:], across)
-    up, down, came = along_z(up, 1), along_z(down, -1), x_pair(across)
+    up, down, came = mirrored(up, 1), mirrored(down, -1), x_pair(across)
     up, down, partners[-1] = after(up, down, partners[-1])
     partners += [came, x_pair(jnp.concatenate([up, down], axis=1))]
     blocks += [up, down, *partners]

time: 145 us -> 144 us (level)
  waiting for transfers between devices: 53.7 us -> 49.8 us
  starting transfers between devices: 31.5 us -> 34.6 us
    ppermute x28 -> x20, waiting for transfers between devices: 51.3 us -> 31.8 us  [permute(): return lax.ppermute(value, axis, [(i, target(i)) for i in range(count)])]
    ppermute x0 -> x8, waiting for transfers between devices: none -> 15.6 us  [mirrored(): lax.ppermute(value, ('batch', 'mp'), [(b * 16 + m, (b + 2 * step * (1 - 2...]
    ppermute x0 -> x8, starting transfers between devices: none -> 8.87 us  [mirrored(): lax.ppermute(value, ('batch', 'mp'), [(b * 16 + m, (b + 2 * step * (1 - 2...]
    ppermute x28 -> x20, starting transfers between devices: 28.4 us -> 22.7 us  [permute(): return lax.ppermute(value, axis, [(i, target(i)) for i in range(count)])]
where the time goes in v10:
time: 144 us
  waiting for transfers between devices  49.8 us (35%)
  blocking collectives  44.7 us (31%)
  starting transfers between devices  34.6 us (24%)
  Pallas kernels  14.7 us (10%)
    all_to_all x2, blocking collectives, over_plane(): lax.all_to_all(value, 'mp', 0, 0, axis_index_groups=PLANE, tiled=True)  44.7 us
    ppermute x20, waiting for transfers between devices, permute(): return lax.ppermute(value, axis, [(i, target(i)) for i in range(count)])  31.8 us
    ppermute x20, starting transfers between devices, permute(): return lax.ppermute(value, axis, [(i, target(i)) for i in range(count)])  22.7 us
    ppermute x8, waiting for transfers between devices, mirrored(): lax.ppermute(value, ('batch', 'mp'), [(b * 16 + m, (b + 2 * step * (1 - 2...  15.6 us
    ppermute x8, starting transfers between devices, mirrored(): lax.ppermute(value, ('batch', 'mp'), [(b * 16 + m, (b + 2 * step * (1 - 2...  8.87 us
    pallas_call x7, Pallas kernels, local(): pl.pallas_call(kernel, out_shape=in_vmem(*shapes), in_specs=[VMEM] * len(...  4.14 us
    pallas_call x1, Pallas kernels, project(): pl.pallas_call(first_kernel, out_shape=in_vmem(((n, width), BF), ((all_ro...  3.38 us
    ppermute x1, starting transfers between devices, transpose_mesh(): lax.ppermute(value, ('batch', 'mp'), [(b * 16 + m, m * 16 + b) for b in r...  3.03 us
  transfers between devices with their start and end apart: 29, of which 22 were waited for; matrix products, arithmetic and copies ran while one was open for 0% of the time, Pallas kernels for 5%

profile of v10, /device:TPU:32, one launch (start us, length us, event | category | flops | bytes accessed | tf_op | source)
XLA Modules:
  0.0 144.2 jit_solution(4800775070953692629)
XLA Ops:
  1.3 3.0 %collective-permute-start = (bf16[400,128]{1,0:T(8,128)(2,1)S(1)}, bf16[400,128]{1,0:T(8,128)(2,1)S(1)}, u32[]{:S(2)}, u32[]{:S(2)}) collective-permute-start(bf16[400,128]{1,0:T(8,128)(2,1)S(1)} %shard_map.100), channel_id=1, source_target_pairs={{0,0},{1,16},{2,32},{3,48},{4,64},{5,80},{6,96},{7,112},{8,128},{9... | collective-permute-start | bytes 307208 | tf_op jit(solution)/shard_map/ppermute | solution.py:54
  4.4 3.0 %shard_map.101 = (bf16[1024,1664]{1,0:T(8,128)(2,1)S(1)}, bf16[1024,1664]{1,0:T(8,128)(2,1)S(1)}) custom-call(bf16[1024,1664]{1,0:T(8,128)(2,1)} %gate_hbm, bf16[1024,1664]{1,0:T(8,128)(2,1)} %up_hbm), custom_call_target="tpu_custom_call" | custom-call | flops 3407872 | bytes 3407872 | tf_op jit(solution)/shard_map/pallas_call | solution.py:276
  7.4 2.4 %collective-permute-done = bf16[400,128]{1,0:T(8,128)(2,1)S(1)} collective-permute-done((bf16[400,128]{1,0:T(8,128)(2,1)S(1)}, bf16[400,128]{1,0:T(8,128)(2,1)S(1)}, u32[]{:S(2)}, u32[]{:S(2)}) %collective-permute-start) | collective-permute-done | bytes 102432 | tf_op jit(solution)/shard_map/ppermute | solution.py:54
  9.9 30.2 %all_to_all.10.mine_ref = bf16[8,400,128]{2,1,0:T(8,128)(2,1)S(1)} all-to-all(bf16[8,400,128]{2,1,0:T(8,128)(2,1)S(1)} %broadcast_in_dim.2), channel_id=1, replica_groups={{0,2,4,6,8,10,12,14},{1,3,5,7,9,11,13,15},{16,18,20,22,24,26,28,30},{17..., dimensions={0} | all-to-all | bytes 1638400 | tf_op jit(solution)/shard_map/all_to_all | solution.py:62
  40.2 2.3 %collective-permute-done.1.theirs_ref = bf16[8,400,128]{2,1,0:T(8,128)(2,1)S(1)} collective-permute-done((bf16[8,400,128]{2,1,0:T(8,128)(2,1)S(1)}, bf16[8,400,128]{2,1,0:T(8,128)(2,1)S(1)}, u32[]{:S(2)}, u32[]{:S(2)}) %collective-permute-start.1) | collective-permute-done | bytes 819232 | tf_op jit(solution)/shard_map/ppermute | solution.py:26
  42.5 3.4 %shard_map.102 = (bf16[32,1024]{1,0:T(8,128)(2,1)S(1)}, bf16[512,1024]{1,0:T(8,128)(2,1)S(1)}, bf16[512,128]{1,0:T(8,128)(2,1)S(1)}, bf16[32,3456]{1,0:T(8,128)(2,1)S(1)}, bf16[2,32,3456]{2,1,0:T(8,128)(2,1)S(1)}) custom-call(s32[16]{0:T(128)S(1)} %copy-done.1, f32[16384]{0:T(1024)} %gain_ref.1, bf16[8,400,128]{2,1,0:T(8,128)(2,1)S(1)} %all_to_all.10.mine_ref, ...), custom_call_target="tpu_custom_call" | custom-call | tf_op jit(solution)/shard_map/pallas_call | solution.py:292
  45.9 2.7 %collective-permute-start.2 = (bf16[32,3456]{1,0:T(8,128)(2,1)S(1)}, bf16[32,3456]{1,0:T(8,128)(2,1)S(1)}, u32[]{:S(2)}, u32[]{:S(2)}) collective-permute-start(bf16[32,3456]{1,0:T(8,128)(2,1)S(1)} %get-tuple-element.108), channel_id=1, source_target_pairs={{0,16},{16,0},{32,48},{48,32},{64,80},{80,64},{96,112},{112,96},{1... | collective-permute-start | bytes 663560 | tf_op jit(solution)/shard_map/ppermute | solution.py:26
  48.7 3.3 %shard_map.103 = (bf16[2,32,3456]{2,1,0:T(8,128)(2,1)S(1)}, bf16[2,32,3456]{2,1,0:T(8,128)(2,1)S(1)}, bf16[32,3456]{1,0:T(8,128)(2,1)S(1)}, bf16[32,3456]{1,0:T(...) custom-call(bf16[512,1024]{1,0:T(8,128)(2,1)S(1)} %get-tuple-element, ...), custom_call_target="tpu_custom_call" | custom-call | flops 2944401408 | bytes 7077888 | tf_op jit(solution)/shard_map/pallas_call | solution.py:369
  51.9 2.8 %collective-permute-done.2.x = bf16[32,3456]{1,0:T(8,128)(2,1)S(1)} collective-permute-done((bf16[32,3456]{1,0:T(8,128)(2,1)S(1)}, bf16[32,3456]{1,0:T(8,128)(2,1)S(1)}, u32[]{:S(2)}, u32[]{:S(2)}) %collective-permute-start.2) | collective-permute-done | bytes 221216 | tf_op jit(solution)/shard_map/ppermute | solution.py:26
  54.8 2.1 %collective-permute-start.8 = (bf16[2,32,3456]{2,1,0:T(8,128)(2,1)S(1)}, bf16[2,32,3456]{2,1,0:T(8,128)(2,1)S(1)}, u32[]{:S(2)}, u32[]{:S(2)}) collective-permute-start(bf16[2,32,3456]{2,1,0:T(8,128)(2,1)S(1)} %get-tuple-element.123), channel_id=1, source_target_pairs={{0,16},{16,0},{32,48},{48,32},{64,80},{80,64},{96,112},{112,96},{1... | collective-permute-start | bytes 1327112 | tf_op jit(solution)/shard_map/ppermute | solution.py:26
  59.0 2.7 %collective-permute-done.3.up = bf16[32,1664]{1,0:T(8,128)(2,1)S(1)} collective-permute-done((bf16[32,1664]{1,0:T(8,128)(2,1)S(1)}, bf16[32,1664]{1,0:T(8,128)(2,1)S(1)}, u32[]{:S(2)}, u32[]{:S(2)}) %collective-permute-start.3) | collective-permute-done | bytes 106528 | tf_op jit(solution)/shard_map/ppermute | solution.py:26
  61.8 2.5 %collective-permute-done.5.x = bf16[2,32,3456]{2,1,0:T(8,128)(2,1)S(1)} collective-permute-done((bf16[2,32,3456]{2,1,0:T(8,128)(2,1)S(1)}, bf16[2,32,3456]{2,1,0:T(8,128)(2,1)S(1)}, u32[]{:S(2)}, u32[]{:S(2)}) %collective-permute-start.5) | collective-permute-done | bytes 442400 | tf_op jit(solution)/shard_map/ppermute | solution.py:26
  68.6 5.2 %collective-permute-done.8.x = bf16[2,32,3456]{2,1,0:T(8,128)(2,1)S(1)} collective-permute-done((bf16[2,32,3456]{2,1,0:T(8,128)(2,1)S(1)}, bf16[2,32,3456]{2,1,0:T(8,128)(2,1)S(1)}, u32[]{:S(2)}, u32[]{:S(2)}) %collective-permute-start.8) | collective-permute-done | bytes 442400 | tf_op jit(solution)/shard_map/ppermute | solution.py:26
  78.1 2.4 %collective-permute-done.9.up = bf16[32,3456]{1,0:T(8,128)(2,1)S(1)} collective-permute-done((bf16[32,3456]{1,0:T(8,128)(2,1)S(1)}, bf16[32,3456]{1,0:T(8,128)(2,1)S(1)}, u32[]{:S(2)}, u32[]{:S(2)}) %collective-permute-start.9) | collective-permute-done | bytes 221216 | tf_op jit(solution)/shard_map/ppermute | solution.py:26
  87.5 2.5 %collective-permute-done.12.up = bf16[32,3456]{1,0:T(8,128)(2,1)S(1)} collective-permute-done((bf16[32,3456]{1,0:T(8,128)(2,1)S(1)}, bf16[32,3456]{1,0:T(8,128)(2,1)S(1)}, u32[]{:S(2)}, u32[]{:S(2)}) %collective-permute-start.12) | collective-permute-done | bytes 221216 | tf_op jit(solution)/shard_map/ppermute | solution.py:26
  91.3 2.1 %collective-permute-start.15 = (bf16[32,1664]{1,0:T(8,128)(2,1)S(1)}, bf16[32,1664]{1,0:T(8,128)(2,1)S(1)}, u32[]{:S(2)}, u32[]{:S(2)}) collective-permute-start(bf16[32,1664]{1,0:T(8,128)(2,1)S(1)} %shard_map.108.refs_0_), channel_id=1, source_target_pairs={{0,32},{1,225},{2,34},{3,227},{4,36},{5,229},{6,38},{7,231},{8,40}... | collective-permute-start | bytes 319496 | tf_op jit(solution)/shard_map/ppermute | solution.py:34
  96.1 3.3 %collective-permute-done.16.refs_2_ = bf16[32,1664]{1,0:T(8,128)(2,1)S(1)} collective-permute-done((bf16[32,1664]{1,0:T(8,128)(2,1)S(1)}, bf16[32,1664]{1,0:T(8,128)(2,1)S(1)}, u32[]{:S(2)}, u32[]{:S(2)}) %collective-permute-start.16) | collective-permute-done | bytes 106528 | tf_op jit(solution)/shard_map/ppermute | solution.py:34
  99.4 2.5 %collective-permute-start.17 = (bf16[32,1664]{1,0:T(8,128)(2,1)S(1)}, bf16[32,1664]{1,0:T(8,128)(2,1)S(1)}, u32[]{:S(2)}, u32[]{:S(2)}) collective-permute-start(bf16[32,1664]{1,0:T(8,128)(2,1)S(1)} %collective-permute-done.15.refs_1_), channel_id=1, source_target_pairs={{0,32},{1,225},{2,34},{3,227},{4,36},{5,229},{6,38},{7,231},{8,40}... | collective-permute-start | bytes 319496 | tf_op jit(solution)/shard_map/ppermute | solution.py:34
  104.9 2.7 %collective-permute-done.18.refs_4_ = bf16[32,1664]{1,0:T(8,128)(2,1)S(1)} collective-permute-done((bf16[32,1664]{1,0:T(8,128)(2,1)S(1)}, bf16[32,1664]{1,0:T(8,128)(2,1)S(1)}, u32[]{:S(2)}, u32[]{:S(2)}) %collective-permute-start.18) | collective-permute-done | bytes 106528 | tf_op jit(solution)/shard_map/ppermute | solution.py:34
  107.6 2.1 %collective-permute-start.20 = (bf16[32,1664]{1,0:T(8,128)(2,1)S(1)}, bf16[32,1664]{1,0:T(8,128)(2,1)S(1)}, u32[]{:S(2)}, u32[]{:S(2)}) collective-permute-start(bf16[32,1664]{1,0:T(8,128)(2,1)S(1)} %collective-permute-done.17.refs_3_), channel_id=1, source_target_pairs={{0,32},{1,225},{2,34},{3,227},{4,36},{5,229},{6,38},{7,231},{8,40}... | collective-permute-start | bytes 319496 | tf_op jit(solution)/shard_map/ppermute | solution.py:34
  117.6 2.4 %collective-permute-done.24.refs_8_ = bf16[32,768]{1,0:T(8,128)(2,1)S(1)} collective-permute-done((bf16[32,768]{1,0:T(8,128)(2,1)S(1)}, bf16[32,768]{1,0:T(8,128)(2,1)S(1)}, u32[]{:S(2)}, u32[]{:S(2)}) %collective-permute-start.24) | collective-permute-done | bytes 49184 | tf_op jit(solution)/shard_map/ppermute | solution.py:34
  121.2 3.5 %collective-permute-done.27.refs_13_ = bf16[32,1664]{1,0:T(8,128)(2,1)S(1)} collective-permute-done((bf16[32,1664]{1,0:T(8,128)(2,1)S(1)}, bf16[32,1664]{1,0:T(8,128)(2,1)S(1)}, u32[]{:S(2)}, u32[]{:S(2)}) %collective-permute-start.27) | collective-permute-done | bytes 106528 | tf_op jit(solution)/shard_map/ppermute | solution.py:26
  124.8 2.2 %shard_map.109 = (bf16[8,32,1024]{2,1,0:T(8,128)(2,1)S(1)}, f32[8,32,1024]{2,1,0:T(8,128)S(1)}) custom-call(bf16[32,1664]{1,0:T(8,128)(2,1)S(1)} %shard_map.108.refs_0_, bf16[32,1664]{1,0:T(8,128)(2,1)S(1)} %collective-permute-done.15.refs_1_, bf16[32,1664]{1,0:T(8,128)(2,1)S(1)} %collective-permute-done.16.refs_2_, ...), custom_call_target="tpu_custom_call" | custom-call | tf_op jit(solution)/shard_map/pallas_call | solution.py:410
  129.0 14.4 %all_to_all.11.parts = bf16[8,32,1024]{2,1,0:T(8,128)(2,1)S(1)} all-to-all(bf16[8,32,1024]{2,1,0:T(8,128)(2,1)S(1)} %shard_map.110), channel_id=1, replica_groups={{0,2,4,6,8,10,12,14},{1,3,5,7,9,11,13,15},{16,18,20,22,24,26,28,30},{17..., dimensions={0} | all-to-all | bytes 1048576 | tf_op jit(solution)/shard_map/all_to_all | solution.py:62
  (59 shorter events, 38.2 us)
Async XLA Ops:
  1.3 8.5 %collective-permute-start = (bf16[400,128]{1,0:T(8,128)(2,1)S(1)}, bf16[400,128]{1,0:T(8,128)(2,1)S(1)}, u32[]{:S(2)}, u32[]{:S(2)}) collective-permute-start(bf16[400,128]{1,0:T(8,128)(2,1)S(1)} %shard_map.100), channel_id=1, source_target_pairs={{0,0},{1,16},{2,32},{3,48},{4,64},{5,80},{6,96},{7,112},{8,128},{9... | collective-permute-start | bytes 307208 | tf_op jit(solution)/shard_map/ppermute | solution.py:54
  45.9 8.9 %collective-permute-start.2 = (bf16[32,3456]{1,0:T(8,128)(2,1)S(1)}, bf16[32,3456]{1,0:T(8,128)(2,1)S(1)}, u32[]{:S(2)}, u32[]{:S(2)}) collective-permute-start(bf16[32,3456]{1,0:T(8,128)(2,1)S(1)} %get-tuple-element.108), channel_id=1, source_target_pairs={{0,16},{16,0},{32,48},{48,32},{64,80},{80,64},{96,112},{112,96},{1... | collective-permute-start | bytes 663560 | tf_op jit(solution)/shard_map/ppermute | solution.py:26
  48.6 15.7 %collective-permute-start.5 = (bf16[2,32,3456]{2,1,0:T(8,128)(2,1)S(1)}, bf16[2,32,3456]{2,1,0:T(8,128)(2,1)S(1)}, u32[]{:S(2)}, u32[]{:S(2)}) collective-permute-start(bf16[2,32,3456]{2,1,0:T(8,128)(2,1)S(1)} %get-tuple-element.114), channel_id=1, source_target_pairs={{0,16},{16,0},{32,48},{48,32},{64,80},{80,64},{96,112},{112,96},{1... | collective-permute-start | bytes 1327112 | tf_op jit(solution)/shard_map/ppermute | solution.py:26
  54.8 18.9 %collective-permute-start.8 = (bf16[2,32,3456]{2,1,0:T(8,128)(2,1)S(1)}, bf16[2,32,3456]{2,1,0:T(8,128)(2,1)S(1)}, u32[]{:S(2)}, u32[]{:S(2)}) collective-permute-start(bf16[2,32,3456]{2,1,0:T(8,128)(2,1)S(1)} %get-tuple-element.123), channel_id=1, source_target_pairs={{0,16},{16,0},{32,48},{48,32},{64,80},{80,64},{96,112},{112,96},{1... | collective-permute-start | bytes 1327112 | tf_op jit(solution)/shard_map/ppermute | solution.py:26
  57.0 4.8 %collective-permute-start.4 = (bf16[32,1792]{1,0:T(8,128)(2,1)S(1)}, bf16[32,1792]{1,0:T(8,128)(2,1)S(1)}, u32[]{:S(2)}, u32[]{:S(2)}) collective-permute-start(bf16[32,1792]{1,0:T(8,128)(2,1)S(1)} %get-tuple-element.113), channel_id=1, source_target_pairs={{0,224},{16,240},{32,0},{48,16},{64,32},{80,48},{96,64},{112,80},{... | collective-permute-start | bytes 344072 | tf_op jit(solution)/shard_map/ppermute | solution.py:26
  64.4 9.3 %collective-permute-start.6 = (bf16[32,3456]{1,0:T(8,128)(2,1)S(1)}, bf16[32,3456]{1,0:T(8,128)(2,1)S(1)}, u32[]{:S(2)}, u32[]{:S(2)}) collective-permute-start(bf16[32,3456]{1,0:T(8,128)(2,1)S(1)} %get-tuple-element.121), channel_id=1, source_target_pairs={{0,32},{16,48},{32,64},{48,80},{64,96},{80,112},{96,128},{112,144}... | collective-permute-start | bytes 663560 | tf_op jit(solution)/shard_map/ppermute | solution.py:26
  65.7 8.1 %collective-permute-start.7 = (bf16[32,3456]{1,0:T(8,128)(2,1)S(1)}, bf16[32,3456]{1,0:T(8,128)(2,1)S(1)}, u32[]{:S(2)}, u32[]{:S(2)}) collective-permute-start(bf16[32,3456]{1,0:T(8,128)(2,1)S(1)} %get-tuple-element.122), channel_id=1, source_target_pairs={{0,224},{16,240},{32,0},{48,16},{64,32},{80,48},{96,64},{112,80},{... | collective-permute-start | bytes 663560 | tf_op jit(solution)/shard_map/ppermute | solution.py:26
  66.5 16.7 %collective-permute-start.11 = (bf16[2,32,3456]{2,1,0:T(8,128)(2,1)S(1)}, bf16[2,32,3456]{2,1,0:T(8,128)(2,1)S(1)}, u32[]{:S(2)}, u32[]{:S(2)}) collective-permute-start(bf16[2,32,3456]{2,1,0:T(8,128)(2,1)S(1)} %get-tuple-element.132), channel_id=1, source_target_pairs={{0,16},{16,0},{32,48},{48,32},{64,80},{80,64},{96,112},{112,96},{1... | collective-permute-start | bytes 1327112 | tf_op jit(solution)/shard_map/ppermute | solution.py:26
  73.9 6.6 %collective-permute-start.9 = (bf16[32,3456]{1,0:T(8,128)(2,1)S(1)}, bf16[32,3456]{1,0:T(8,128)(2,1)S(1)}, u32[]{:S(2)}, u32[]{:S(2)}) collective-permute-start(bf16[32,3456]{1,0:T(8,128)(2,1)S(1)} %get-tuple-element.130), channel_id=1, source_target_pairs={{0,32},{16,48},{32,64},{48,80},{64,96},{80,112},{96,128},{112,144}... | collective-permute-start | bytes 663560 | tf_op jit(solution)/shard_map/ppermute | solution.py:26
  75.2 6.4 %collective-permute-start.10 = (bf16[32,3456]{1,0:T(8,128)(2,1)S(1)}, bf16[32,3456]{1,0:T(8,128)(2,1)S(1)}, u32[]{:S(2)}, u32[]{:S(2)}) collective-permute-start(bf16[32,3456]{1,0:T(8,128)(2,1)S(1)} %get-tuple-element.131), channel_id=1, source_target_pairs={{0,224},{16,240},{32,0},{48,16},{64,32},{80,48},{96,64},{112,80},{... | collective-permute-start | bytes 663560 | tf_op jit(solution)/shard_map/ppermute | solution.py:26
  76.0 11.4 %collective-permute-start.14 = (bf16[32,3456]{1,0:T(8,128)(2,1)S(1)}, bf16[32,3456]{1,0:T(8,128)(2,1)S(1)}, u32[]{:S(2)}, u32[]{:S(2)}) collective-permute-start(bf16[32,3456]{1,0:T(8,128)(2,1)S(1)} %get-tuple-element.140), channel_id=1, source_target_pairs={{0,16},{16,0},{32,48},{48,32},{64,80},{80,64},{96,112},{112,96},{1... | collective-permute-start | bytes 663560 | tf_op jit(solution)/shard_map/ppermute | solution.py:26
  83.4 6.6 %collective-permute-start.12 = (bf16[32,3456]{1,0:T(8,128)(2,1)S(1)}, bf16[32,3456]{1,0:T(8,128)(2,1)S(1)}, u32[]{:S(2)}, u32[]{:S(2)}) collective-permute-start(bf16[32,3456]{1,0:T(8,128)(2,1)S(1)} %get-tuple-element.138), channel_id=1, source_target_pairs={{0,32},{16,48},{32,64},{48,80},{64,96},{80,112},{96,128},{112,144}... | collective-permute-start | bytes 663560 | tf_op jit(solution)/shard_map/ppermute | solution.py:26
  84.7 6.4 %collective-permute-start.13 = (bf16[32,3456]{1,0:T(8,128)(2,1)S(1)}, bf16[32,3456]{1,0:T(8,128)(2,1)S(1)}, u32[]{:S(2)}, u32[]{:S(2)}) collective-permute-start(bf16[32,3456]{1,0:T(8,128)(2,1)S(1)} %get-tuple-element.139), channel_id=1, source_target_pairs={{0,224},{16,240},{32,0},{48,16},{64,32},{80,48},{96,64},{112,80},{... | collective-permute-start | bytes 663560 | tf_op jit(solution)/shard_map/ppermute | solution.py:26
  91.3 4.8 %collective-permute-start.15 = (bf16[32,1664]{1,0:T(8,128)(2,1)S(1)}, bf16[32,1664]{1,0:T(8,128)(2,1)S(1)}, u32[]{:S(2)}, u32[]{:S(2)}) collective-permute-start(bf16[32,1664]{1,0:T(8,128)(2,1)S(1)} %shard_map.108.refs_0_), channel_id=1, source_target_pairs={{0,32},{1,225},{2,34},{3,227},{4,36},{5,229},{6,38},{7,231},{8,40}... | collective-permute-start | bytes 319496 | tf_op jit(solution)/shard_map/ppermute | solution.py:34
  93.5 5.9 %collective-permute-start.16 = (bf16[32,1664]{1,0:T(8,128)(2,1)S(1)}, bf16[32,1664]{1,0:T(8,128)(2,1)S(1)}, u32[]{:S(2)}, u32[]{:S(2)}) collective-permute-start(bf16[32,1664]{1,0:T(8,128)(2,1)S(1)} %shard_map.108.refs_0_), channel_id=1, source_target_pairs={{0,224},{1,33},{2,226},{3,35},{4,228},{5,37},{6,230},{7,39},{8,232... | collective-permute-start | bytes 319496 | tf_op jit(solution)/shard_map/ppermute | solution.py:34
  93.5 9.5 %collective-permute-start.19 = (bf16[32,1664]{1,0:T(8,128)(2,1)S(1)}, bf16[32,1664]{1,0:T(8,128)(2,1)S(1)}, u32[]{:S(2)}, u32[]{:S(2)}) collective-permute-start(bf16[32,1664]{1,0:T(8,128)(2,1)S(1)} %shard_map.108.refs_0_), channel_id=1, source_target_pairs={{0,16},{16,0},{32,48},{48,32},{64,80},{80,64},{96,112},{112,96},{1... | collective-permute-start | bytes 319496 | tf_op jit(solution)/shard_map/ppermute | solution.py:26
  99.4 5.5 %collective-permute-start.17 = (bf16[32,1664]{1,0:T(8,128)(2,1)S(1)}, bf16[32,1664]{1,0:T(8,128)(2,1)S(1)}, u32[]{:S(2)}, u32[]{:S(2)}) collective-permute-start(bf16[32,1664]{1,0:T(8,128)(2,1)S(1)} %collective-permute-done.15.refs_1_), channel_id=1, source_target_pairs={{0,32},{1,225},{2,34},{3,227},{4,36},{5,229},{6,38},{7,231},{8,40}... | collective-permute-start | bytes 319496 | tf_op jit(solution)/shard_map/ppermute | solution.py:34
  102.0 5.6 %collective-permute-start.18 = (bf16[32,1664]{1,0:T(8,128)(2,1)S(1)}, bf16[32,1664]{1,0:T(8,128)(2,1)S(1)}, u32[]{:S(2)}, u32[]{:S(2)}) collective-permute-start(bf16[32,1664]{1,0:T(8,128)(2,1)S(1)} %collective-permute-done.16.refs_2_), channel_id=1, source_target_pairs={{0,224},{1,33},{2,226},{3,35},{4,228},{5,37},{6,230},{7,39},{8,232... | collective-permute-start | bytes 319496 | tf_op jit(solution)/shard_map/ppermute | solution.py:34
  102.0 12.5 %collective-permute-start.22 = (bf16[2,32,1664]{2,1,0:T(8,128)(2,1)S(1)}, bf16[2,32,1664]{2,1,0:T(8,128)(2,1)S(1)}, u32[]{:S(2)}, u32[]{:S(2)}) collective-permute-start(bf16[2,32,1664]{2,1,0:T(8,128)(2,1)S(1)} %pad_maximum_fusion), channel_id=1, source_target_pairs={{0,16},{16,0},{32,48},{48,32},{64,80},{80,64},{96,112},{112,96},{1... | collective-permute-start | bytes 638984 | tf_op jit(solution)/shard_map/ppermute | solution.py:26
  107.6 4.8 %collective-permute-start.20 = (bf16[32,1664]{1,0:T(8,128)(2,1)S(1)}, bf16[32,1664]{1,0:T(8,128)(2,1)S(1)}, u32[]{:S(2)}, u32[]{:S(2)}) collective-permute-start(bf16[32,1664]{1,0:T(8,128)(2,1)S(1)} %collective-permute-done.17.refs_3_), channel_id=1, source_target_pairs={{0,32},{1,225},{2,34},{3,227},{4,36},{5,229},{6,38},{7,231},{8,40}... | collective-permute-start | bytes 319496 | tf_op jit(solution)/shard_map/ppermute | solution.py:34
  109.7 10.2 %collective-permute-start.25 = (bf16[2,32,1664]{2,1,0:T(8,128)(2,1)S(1)}, bf16[2,32,1664]{2,1,0:T(8,128)(2,1)S(1)}, u32[]{:S(2)}, u32[]{:S(2)}) collective-permute-start(bf16[2,32,1664]{2,1,0:T(8,128)(2,1)S(1)} %pad_maximum_fusion.1), channel_id=1, source_target_pairs={{0,16},{16,0},{32,48},{48,32},{64,80},{80,64},{96,112},{112,96},{1... | collective-permute-start | bytes 638984 | tf_op jit(solution)/shard_map/ppermute | solution.py:26
  114.5 5.5 %collective-permute-start.23 = (bf16[32,896]{1,0:T(8,128)(2,1)S(1)}, bf16[32,896]{1,0:T(8,128)(2,1)S(1)}, u32[]{:S(2)}, u32[]{:S(2)}) collective-permute-start(bf16[32,896]{1,0:T(8,128)(2,1)S(1)} %slice.6), channel_id=1, source_target_pairs={{0,32},{1,225},{2,34},{3,227},{4,36},{5,229},{6,38},{7,231},{8,40}... | collective-permute-start | bytes 172040 | tf_op jit(solution)/shard_map/ppermute | solution.py:34
  116.6 8.2 %collective-permute-start.26 = (bf16[2,32,1664]{2,1,0:T(8,128)(2,1)S(1)}, bf16[2,32,1664]{2,1,0:T(8,128)(2,1)S(1)}, u32[]{:S(2)}, u32[]{:S(2)}) collective-permute-start(bf16[2,32,1664]{2,1,0:T(8,128)(2,1)S(1)} %pad_maximum_fusion.2), channel_id=1, source_target_pairs={{0,16},{16,0},{32,48},{48,32},{64,80},{80,64},{96,112},{112,96},{1... | collective-permute-start | bytes 638984 | tf_op jit(solution)/shard_map/ppermute | solution.py:26
  120.0 4.8 %collective-permute-start.27 = (bf16[32,1664]{1,0:T(8,128)(2,1)S(1)}, bf16[32,1664]{1,0:T(8,128)(2,1)S(1)}, u32[]{:S(2)}, u32[]{:S(2)}) collective-permute-start(bf16[32,1664]{1,0:T(8,128)(2,1)S(1)} %pad_maximum_fusion.3), channel_id=1, source_target_pairs={{0,16},{16,0},{32,48},{48,32},{64,80},{80,64},{96,112},{112,96},{1... | collective-permute-start | bytes 319496 | tf_op jit(solution)/shard_map/ppermute | solution.py:26
  (7 other events, 129.0 us)

commit v11 on v10

--- a/solution.py
+++ b/solution.py
@@ -376,44 +376,51 @@
     )(*args)
 
 
-def down_kernel(*refs):
+def down_kernel(kept, *refs):
     own, up1, down1, up2, down2, up3, down3, up4, down4, x0, x1, x2, x3, x4, down_ref = refs[:15]
-    give, keep, rows = refs[15:]
+    out, rows = refs[15:]
     n = ROWS_DEV
     batch_index, mp_index = lax.axis_index("batch"), lax.axis_index("mp")
     z, flip = batch_index >> 1, (batch_index ^ mp_index) & 1
     ours = {0: own, 1: down1, 2: down2, 3: down3, 5: up3, 6: up2, 7: up1}
     partners = {0: x0, 7: x1.at[0], 1: x1.at[1], 6: x2.at[0], 2: x2.at[1], 5: x3.at[0], 3: x3.at[1], FAR: x4}
-    for s in range(ZN):
-        for j, found in enumerate((ours, partners)):
+
+    def collect(found):
+        for s in range(ZN):
             target = (z + s * (1 - 2 * (mp_index & 1))) & (ZN - 1)
-            other = (flip + j) & 1
-            at = pl.ds(pl.multiple_of((1 - other) * ZN * n + target * n, n), n)
+            at = pl.ds(pl.multiple_of(target * n, n), n)
             if s in found:
                 rows[at, :] = found[s][...]
             else:
                 rows[at, : up4.shape[1]] = up4[...]
                 rows[at, up4.shape[1] :] = down4[...]
+
+    @pl.when(flip != kept)
+    def _():
+        collect(ours)
+
+    @pl.when(flip == kept)
+    def _():
+        collect(partners)
+
     step = 2 * LANE
     for i in range(0, down_ref.shape[1], step):
         lanes = slice(i, i + step)
         product = jnp.dot(rows[...], down_ref[:, lanes], preferred_element_type=F32)
         for target in range(ZN):
-            give[target, :, lanes] = product[target * n : (target + 1) * n].astype(BF)
-            at = (ZN + target) * n
-            keep[target, :, lanes] = product[at : at + n]
-
-
-def project_down(blocks, down_weight):
+            out[target, :, lanes] = product[target * n : (target + 1) * n].astype(out.dtype)
+
+
+def project_down(blocks, down_weight, kept):
     hidden_width, width = down_weight.shape
-    shape = (ZN, ROWS_DEV, width)
     return pl.pallas_call(
-        down_kernel,
-        out_shape=in_vmem((shape, BF), (shape, F32)),
+        lambda *refs: down_kernel(kept, *refs),
+        out_shape=in_vmem(((ZN, ROWS_DEV, width), F32 if kept else BF)),
         in_specs=[VMEM] * (len(blocks) + 1),
-        out_specs=(VMEM, VMEM),
-        scratch_shapes=[pltpu.VMEM((2 * ZN * ROWS_DEV, hidden_width), BF)],
+        out_specs=VMEM,
+        scratch_shapes=[pltpu.VMEM((ZN * ROWS_DEV, hidden_width), BF)],
         compiler_params=PARAMS,
+        cost_estimate=cost(ZN * ROWS_DEV, hidden_width, width),
     )(*blocks, down_weight)
 
 
@@ -497,7 +504,9 @@
     up, down, partners[-1] = after(up, down, partners[-1])
     partners += [came, x_pair(jnp.concatenate([up, down], axis=1))]
     blocks += [up, down, *partners]
-    send, keep = project_down(blocks, down_weight)
+    send = project_down(blocks, down_weight, 0)
+    send, down_weight = after(send, down_weight)
+    keep = project_down(blocks, down_weight, 1)
     held = local(add_core_kernel, [(keep.shape, BF)], keep, core_pair(send))
     parts = over_plane(held)
     return pl.pallas_call(

time: 144 us -> 143 us (level)
  transfers between devices with their start and end apart: 29 -> 29, of which waited for: 22 -> 22; matrix products, arithmetic and copies ran while one was open for 0% -> 0% of each run, Pallas kernels for 5% -> 6%
where the time goes in v11:
time: 143 us
  waiting for transfers between devices  48.6 us (34%)
  blocking collectives  44.7 us (31%)
  starting transfers between devices  34.6 us (24%)
  Pallas kernels  14.9 us (10%)
    all_to_all x2, blocking collectives, over_plane(): lax.all_to_all(value, 'mp', 0, 0, axis_index_groups=PLANE, tiled=True)  44.7 us
    ppermute x20, waiting for transfers between devices, permute(): return lax.ppermute(value, axis, [(i, target(i)) for i in range(count)])  30.6 us
    ppermute x20, starting transfers between devices, permute(): return lax.ppermute(value, axis, [(i, target(i)) for i in range(count)])  22.7 us
    ppermute x8, waiting for transfers between devices, mirrored(): lax.ppermute(value, ('batch', 'mp'), [(b * 16 + m, (b + 2 * step * (1 - 2...  15.6 us
    ppermute x8, starting transfers between devices, mirrored(): lax.ppermute(value, ('batch', 'mp'), [(b * 16 + m, (b + 2 * step * (1 - 2...  8.87 us
    pallas_call x7, Pallas kernels, local(): pl.pallas_call(kernel, out_shape=in_vmem(*shapes), in_specs=[VMEM] * len(...  4.13 us
    pallas_call x1, Pallas kernels, project(): pl.pallas_call(first_kernel, out_shape=in_vmem(((n, width), BF), ((all_ro...  3.38 us
    ppermute x1, starting transfers between devices, transpose_mesh(): lax.ppermute(value, ('batch', 'mp'), [(b * 16 + m, m * 16 + b) for b in r...  3.03 us
  transfers between devices with their start and end apart: 29, of which 22 were waited for; matrix products, arithmetic and copies ran while one was open for 0% of the time, Pallas kernels for 6%

profile of v11, /device:TPU:32, one launch (start us, length us, event | category | flops | bytes accessed | tf_op | source)
XLA Modules:
  0.0 143.2 jit_solution(10581765366471516430)
XLA Ops:
  1.3 3.0 %collective-permute-start = (bf16[400,128]{1,0:T(8,128)(2,1)S(1)}, bf16[400,128]{1,0:T(8,128)(2,1)S(1)}, u32[]{:S(2)}, u32[]{:S(2)}) collective-permute-start(bf16[400,128]{1,0:T(8,128)(2,1)S(1)} %shard_map.100), channel_id=1, source_target_pairs={{0,0},{1,16},{2,32},{3,48},{4,64},{5,80},{6,96},{7,112},{8,128},{9... | collective-permute-start | bytes 307208 | tf_op jit(solution)/shard_map/ppermute | solution.py:54
  4.4 3.0 %shard_map.101 = (bf16[1024,1664]{1,0:T(8,128)(2,1)S(1)}, bf16[1024,1664]{1,0:T(8,128)(2,1)S(1)}) custom-call(bf16[1024,1664]{1,0:T(8,128)(2,1)} %gate_hbm, bf16[1024,1664]{1,0:T(8,128)(2,1)} %up_hbm), custom_call_target="tpu_custom_call" | custom-call | flops 3407872 | bytes 3407872 | tf_op jit(solution)/shard_map/pallas_call | solution.py:276
  7.4 2.4 %collective-permute-done = bf16[400,128]{1,0:T(8,128)(2,1)S(1)} collective-permute-done((bf16[400,128]{1,0:T(8,128)(2,1)S(1)}, bf16[400,128]{1,0:T(8,128)(2,1)S(1)}, u32[]{:S(2)}, u32[]{:S(2)}) %collective-permute-start) | collective-permute-done | bytes 102432 | tf_op jit(solution)/shard_map/ppermute | solution.py:54
  9.9 30.2 %all_to_all.10.mine_ref = bf16[8,400,128]{2,1,0:T(8,128)(2,1)S(1)} all-to-all(bf16[8,400,128]{2,1,0:T(8,128)(2,1)S(1)} %broadcast_in_dim.2), channel_id=1, replica_groups={{0,2,4,6,8,10,12,14},{1,3,5,7,9,11,13,15},{16,18,20,22,24,26,28,30},{17..., dimensions={0} | all-to-all | bytes 1638400 | tf_op jit(solution)/shard_map/all_to_all | solution.py:62
  40.2 2.3 %collective-permute-done.1.theirs_ref = bf16[8,400,128]{2,1,0:T(8,128)(2,1)S(1)} collective-permute-done((bf16[8,400,128]{2,1,0:T(8,128)(2,1)S(1)}, bf16[8,400,128]{2,1,0:T(8,128)(2,1)S(1)}, u32[]{:S(2)}, u32[]{:S(2)}) %collective-permute-start.1) | collective-permute-done | bytes 819232 | tf_op jit(solution)/shard_map/ppermute | solution.py:26
  42.5 3.4 %shard_map.102 = (bf16[32,1024]{1,0:T(8,128)(2,1)S(1)}, bf16[512,1024]{1,0:T(8,128)(2,1)S(1)}, bf16[512,128]{1,0:T(8,128)(2,1)S(1)}, bf16[32,3456]{1,0:T(8,128)(2,1)S(1)}, bf16[2,32,3456]{2,1,0:T(8,128)(2,1)S(1)}) custom-call(s32[16]{0:T(128)S(1)} %copy-done.1, f32[16384]{0:T(1024)} %gain_ref.1, bf16[8,400,128]{2,1,0:T(8,128)(2,1)S(1)} %all_to_all.10.mine_ref, ...), custom_call_target="tpu_custom_call" | custom-call | tf_op jit(solution)/shard_map/pallas_call | solution.py:292
  45.9 2.7 %collective-permute-start.2 = (bf16[32,3456]{1,0:T(8,128)(2,1)S(1)}, bf16[32,3456]{1,0:T(8,128)(2,1)S(1)}, u32[]{:S(2)}, u32[]{:S(2)}) collective-permute-start(bf16[32,3456]{1,0:T(8,128)(2,1)S(1)} %get-tuple-element.108), channel_id=1, source_target_pairs={{0,16},{16,0},{32,48},{48,32},{64,80},{80,64},{96,112},{112,96},{1... | collective-permute-start | bytes 663560 | tf_op jit(solution)/shard_map/ppermute | solution.py:26
  48.7 3.3 %shard_map.103 = (bf16[2,32,3456]{2,1,0:T(8,128)(2,1)S(1)}, bf16[2,32,3456]{2,1,0:T(8,128)(2,1)S(1)}, bf16[32,3456]{1,0:T(8,128)(2,1)S(1)}, bf16[32,3456]{1,0:T(...) custom-call(bf16[512,1024]{1,0:T(8,128)(2,1)S(1)} %get-tuple-element, ...), custom_call_target="tpu_custom_call" | custom-call | flops 2944401408 | bytes 7077888 | tf_op jit(solution)/shard_map/pallas_call | solution.py:369
  51.9 2.8 %collective-permute-done.2.x = bf16[32,3456]{1,0:T(8,128)(2,1)S(1)} collective-permute-done((bf16[32,3456]{1,0:T(8,128)(2,1)S(1)}, bf16[32,3456]{1,0:T(8,128)(2,1)S(1)}, u32[]{:S(2)}, u32[]{:S(2)}) %collective-permute-start.2) | collective-permute-done | bytes 221216 | tf_op jit(solution)/shard_map/ppermute | solution.py:26
  54.8 2.1 %collective-permute-start.8 = (bf16[2,32,3456]{2,1,0:T(8,128)(2,1)S(1)}, bf16[2,32,3456]{2,1,0:T(8,128)(2,1)S(1)}, u32[]{:S(2)}, u32[]{:S(2)}) collective-permute-start(bf16[2,32,3456]{2,1,0:T(8,128)(2,1)S(1)} %get-tuple-element.123), channel_id=1, source_target_pairs={{0,16},{16,0},{32,48},{48,32},{64,80},{80,64},{96,112},{112,96},{1... | collective-permute-start | bytes 1327112 | tf_op jit(solution)/shard_map/ppermute | solution.py:26
  59.0 2.7 %collective-permute-done.3.up = bf16[32,1664]{1,0:T(8,128)(2,1)S(1)} collective-permute-done((bf16[32,1664]{1,0:T(8,128)(2,1)S(1)}, bf16[32,1664]{1,0:T(8,128)(2,1)S(1)}, u32[]{:S(2)}, u32[]{:S(2)}) %collective-permute-start.3) | collective-permute-done | bytes 106528 | tf_op jit(solution)/shard_map/ppermute | solution.py:26
  61.8 2.5 %collective-permute-done.5.x = bf16[2,32,3456]{2,1,0:T(8,128)(2,1)S(1)} collective-permute-done((bf16[2,32,3456]{2,1,0:T(8,128)(2,1)S(1)}, bf16[2,32,3456]{2,1,0:T(8,128)(2,1)S(1)}, u32[]{:S(2)}, u32[]{:S(2)}) %collective-permute-start.5) | collective-permute-done | bytes 442400 | tf_op jit(solution)/shard_map/ppermute | solution.py:26
  66.5 2.1 %collective-permute-start.11 = (bf16[2,32,3456]{2,1,0:T(8,128)(2,1)S(1)}, bf16[2,32,3456]{2,1,0:T(8,128)(2,1)S(1)}, u32[]{:S(2)}, u32[]{:S(2)}) collective-permute-start(bf16[2,32,3456]{2,1,0:T(8,128)(2,1)S(1)} %get-tuple-element.132), channel_id=1, source_target_pairs={{0,16},{16,0},{32,48},{48,32},{64,80},{80,64},{96,112},{112,96},{1... | collective-permute-start | bytes 1327112 | tf_op jit(solution)/shard_map/ppermute | solution.py:26
  68.6 5.2 %collective-permute-done.8.x = bf16[2,32,3456]{2,1,0:T(8,128)(2,1)S(1)} collective-permute-done((bf16[2,32,3456]{2,1,0:T(8,128)(2,1)S(1)}, bf16[2,32,3456]{2,1,0:T(8,128)(2,1)S(1)}, u32[]{:S(2)}, u32[]{:S(2)}) %collective-permute-start.8) | collective-permute-done | bytes 442400 | tf_op jit(solution)/shard_map/ppermute | solution.py:26
  78.1 2.4 %collective-permute-done.9.up = bf16[32,3456]{1,0:T(8,128)(2,1)S(1)} collective-permute-done((bf16[32,3456]{1,0:T(8,128)(2,1)S(1)}, bf16[32,3456]{1,0:T(8,128)(2,1)S(1)}, u32[]{:S(2)}, u32[]{:S(2)}) %collective-permute-start.9) | collective-permute-done | bytes 221216 | tf_op jit(solution)/shard_map/ppermute | solution.py:26
  87.5 2.5 %collective-permute-done.12.up = bf16[32,3456]{1,0:T(8,128)(2,1)S(1)} collective-permute-done((bf16[32,3456]{1,0:T(8,128)(2,1)S(1)}, bf16[32,3456]{1,0:T(8,128)(2,1)S(1)}, u32[]{:S(2)}, u32[]{:S(2)}) %collective-permute-start.12) | collective-permute-done | bytes 221216 | tf_op jit(solution)/shard_map/ppermute | solution.py:26
  91.3 2.1 %collective-permute-start.15 = (bf16[32,1664]{1,0:T(8,128)(2,1)S(1)}, bf16[32,1664]{1,0:T(8,128)(2,1)S(1)}, u32[]{:S(2)}, u32[]{:S(2)}) collective-permute-start(bf16[32,1664]{1,0:T(8,128)(2,1)S(1)} %shard_map.108.refs_0_), channel_id=1, source_target_pairs={{0,32},{1,225},{2,34},{3,227},{4,36},{5,229},{6,38},{7,231},{8,40}... | collective-permute-start | bytes 319496 | tf_op jit(solution)/shard_map/ppermute | solution.py:34
  96.1 3.3 %collective-permute-done.16.refs_2_ = bf16[32,1664]{1,0:T(8,128)(2,1)S(1)} collective-permute-done((bf16[32,1664]{1,0:T(8,128)(2,1)S(1)}, bf16[32,1664]{1,0:T(8,128)(2,1)S(1)}, u32[]{:S(2)}, u32[]{:S(2)}) %collective-permute-start.16) | collective-permute-done | bytes 106528 | tf_op jit(solution)/shard_map/ppermute | solution.py:34
  99.4 2.5 %collective-permute-start.17 = (bf16[32,1664]{1,0:T(8,128)(2,1)S(1)}, bf16[32,1664]{1,0:T(8,128)(2,1)S(1)}, u32[]{:S(2)}, u32[]{:S(2)}) collective-permute-start(bf16[32,1664]{1,0:T(8,128)(2,1)S(1)} %collective-permute-done.15.refs_1_), channel_id=1, source_target_pairs={{0,32},{1,225},{2,34},{3,227},{4,36},{5,229},{6,38},{7,231},{8,40}... | collective-permute-start | bytes 319496 | tf_op jit(solution)/shard_map/ppermute | solution.py:34
  104.9 2.7 %collective-permute-done.18.refs_4_ = bf16[32,1664]{1,0:T(8,128)(2,1)S(1)} collective-permute-done((bf16[32,1664]{1,0:T(8,128)(2,1)S(1)}, bf16[32,1664]{1,0:T(8,128)(2,1)S(1)}, u32[]{:S(2)}, u32[]{:S(2)}) %collective-permute-start.18) | collective-permute-done | bytes 106528 | tf_op jit(solution)/shard_map/ppermute | solution.py:34
  107.6 2.1 %collective-permute-start.20 = (bf16[32,1664]{1,0:T(8,128)(2,1)S(1)}, bf16[32,1664]{1,0:T(8,128)(2,1)S(1)}, u32[]{:S(2)}, u32[]{:S(2)}) collective-permute-start(bf16[32,1664]{1,0:T(8,128)(2,1)S(1)} %collective-permute-done.17.refs_3_), channel_id=1, source_target_pairs={{0,32},{1,225},{2,34},{3,227},{4,36},{5,229},{6,38},{7,231},{8,40}... | collective-permute-start | bytes 319496 | tf_op jit(solution)/shard_map/ppermute | solution.py:34
  117.6 2.4 %collective-permute-done.24.refs_8_ = bf16[32,768]{1,0:T(8,128)(2,1)S(1)} collective-permute-done((bf16[32,768]{1,0:T(8,128)(2,1)S(1)}, bf16[32,768]{1,0:T(8,128)(2,1)S(1)}, u32[]{:S(2)}, u32[]{:S(2)}) %collective-permute-start.24) | collective-permute-done | bytes 49184 | tf_op jit(solution)/shard_map/ppermute | solution.py:34
  121.2 3.5 %collective-permute-done.27.refs_13_ = bf16[32,1664]{1,0:T(8,128)(2,1)S(1)} collective-permute-done((bf16[32,1664]{1,0:T(8,128)(2,1)S(1)}, bf16[32,1664]{1,0:T(8,128)(2,1)S(1)}, u32[]{:S(2)}, u32[]{:S(2)}) %collective-permute-start.27) | collective-permute-done | bytes 106528 | tf_op jit(solution)/shard_map/ppermute | solution.py:26
  128.0 14.4 %all_to_all.11.parts = bf16[8,32,1024]{2,1,0:T(8,128)(2,1)S(1)} all-to-all(bf16[8,32,1024]{2,1,0:T(8,128)(2,1)S(1)} %shard_map.111), channel_id=1, replica_groups={{0,2,4,6,8,10,12,14},{1,3,5,7,9,11,13,15},{16,18,20,22,24,26,28,30},{17..., dimensions={0} | all-to-all | bytes 1048576 | tf_op jit(solution)/shard_map/all_to_all | solution.py:62
  (60 shorter events, 37.3 us)
Async XLA Ops:
  1.3 8.5 %collective-permute-start = (bf16[400,128]{1,0:T(8,128)(2,1)S(1)}, bf16[400,128]{1,0:T(8,128)(2,1)S(1)}, u32[]{:S(2)}, u32[]{:S(2)}) collective-permute-start(bf16[400,128]{1,0:T(8,128)(2,1)S(1)} %shard_map.100), channel_id=1, source_target_pairs={{0,0},{1,16},{2,32},{3,48},{4,64},{5,80},{6,96},{7,112},{8,128},{9... | collective-permute-start | bytes 307208 | tf_op jit(solution)/shard_map/ppermute | solution.py:54
  45.9 8.9 %collective-permute-start.2 = (bf16[32,3456]{1,0:T(8,128)(2,1)S(1)}, bf16[32,3456]{1,0:T(8,128)(2,1)S(1)}, u32[]{:S(2)}, u32[]{:S(2)}) collective-permute-start(bf16[32,3456]{1,0:T(8,128)(2,1)S(1)} %get-tuple-element.108), channel_id=1, source_target_pairs={{0,16},{16,0},{32,48},{48,32},{64,80},{80,64},{96,112},{112,96},{1... | collective-permute-start | bytes 663560 | tf_op jit(solution)/shard_map/ppermute | solution.py:26
  48.6 15.7 %collective-permute-start.5 = (bf16[2,32,3456]{2,1,0:T(8,128)(2,1)S(1)}, bf16[2,32,3456]{2,1,0:T(8,128)(2,1)S(1)}, u32[]{:S(2)}, u32[]{:S(2)}) collective-permute-start(bf16[2,32,3456]{2,1,0:T(8,128)(2,1)S(1)} %get-tuple-element.114), channel_id=1, source_target_pairs={{0,16},{16,0},{32,48},{48,32},{64,80},{80,64},{96,112},{112,96},{1... | collective-permute-start | bytes 1327112 | tf_op jit(solution)/shard_map/ppermute | solution.py:26
  54.8 18.9 %collective-permute-start.8 = (bf16[2,32,3456]{2,1,0:T(8,128)(2,1)S(1)}, bf16[2,32,3456]{2,1,0:T(8,128)(2,1)S(1)}, u32[]{:S(2)}, u32[]{:S(2)}) collective-permute-start(bf16[2,32,3456]{2,1,0:T(8,128)(2,1)S(1)} %get-tuple-element.123), channel_id=1, source_target_pairs={{0,16},{16,0},{32,48},{48,32},{64,80},{80,64},{96,112},{112,96},{1... | collective-permute-start | bytes 1327112 | tf_op jit(solution)/shard_map/ppermute | solution.py:26
  57.0 4.8 %collective-permute-start.4 = (bf16[32,1792]{1,0:T(8,128)(2,1)S(1)}, bf16[32,1792]{1,0:T(8,128)(2,1)S(1)}, u32[]{:S(2)}, u32[]{:S(2)}) collective-permute-start(bf16[32,1792]{1,0:T(8,128)(2,1)S(1)} %get-tuple-element.113), channel_id=1, source_target_pairs={{0,224},{16,240},{32,0},{48,16},{64,32},{80,48},{96,64},{112,80},{... | collective-permute-start | bytes 344072 | tf_op jit(solution)/shard_map/ppermute | solution.py:26
  64.4 9.3 %collective-permute-start.6 = (bf16[32,3456]{1,0:T(8,128)(2,1)S(1)}, bf16[32,3456]{1,0:T(8,128)(2,1)S(1)}, u32[]{:S(2)}, u32[]{:S(2)}) collective-permute-start(bf16[32,3456]{1,0:T(8,128)(2,1)S(1)} %get-tuple-element.121), channel_id=1, source_target_pairs={{0,32},{16,48},{32,64},{48,80},{64,96},{80,112},{96,128},{112,144}... | collective-permute-start | bytes 663560 | tf_op jit(solution)/shard_map/ppermute | solution.py:26
  65.7 8.1 %collective-permute-start.7 = (bf16[32,3456]{1,0:T(8,128)(2,1)S(1)}, bf16[32,3456]{1,0:T(8,128)(2,1)S(1)}, u32[]{:S(2)}, u32[]{:S(2)}) collective-permute-start(bf16[32,3456]{1,0:T(8,128)(2,1)S(1)} %get-tuple-element.122), channel_id=1, source_target_pairs={{0,224},{16,240},{32,0},{48,16},{64,32},{80,48},{96,64},{112,80},{... | collective-permute-start | bytes 663560 | tf_op jit(solution)/shard_map/ppermute | solution.py:26
  66.5 16.7 %collective-permute-start.11 = (bf16[2,32,3456]{2,1,0:T(8,128)(2,1)S(1)}, bf16[2,32,3456]{2,1,0:T(8,128)(2,1)S(1)}, u32[]{:S(2)}, u32[]{:S(2)}) collective-permute-start(bf16[2,32,3456]{2,1,0:T(8,128)(2,1)S(1)} %get-tuple-element.132), channel_id=1, source_target_pairs={{0,16},{16,0},{32,48},{48,32},{64,80},{80,64},{96,112},{112,96},{1... | collective-permute-start | bytes 1327112 | tf_op jit(solution)/shard_map/ppermute | solution.py:26
  73.9 6.6 %collective-permute-start.9 = (bf16[32,3456]{1,0:T(8,128)(2,1)S(1)}, bf16[32,3456]{1,0:T(8,128)(2,1)S(1)}, u32[]{:S(2)}, u32[]{:S(2)}) collective-permute-start(bf16[32,3456]{1,0:T(8,128)(2,1)S(1)} %get-tuple-element.130), channel_id=1, source_target_pairs={{0,32},{16,48},{32,64},{48,80},{64,96},{80,112},{96,128},{112,144}... | collective-permute-start | bytes 663560 | tf_op jit(solution)/shard_map/ppermute | solution.py:26
  75.2 6.4 %collective-permute-start.10 = (bf16[32,3456]{1,0:T(8,128)(2,1)S(1)}, bf16[32,3456]{1,0:T(8,128)(2,1)S(1)}, u32[]{:S(2)}, u32[]{:S(2)}) collective-permute-start(bf16[32,3456]{1,0:T(8,128)(2,1)S(1)} %get-tuple-element.131), channel_id=1, source_target_pairs={{0,224},{16,240},{32,0},{48,16},{64,32},{80,48},{96,64},{112,80},{... | collective-permute-start | bytes 663560 | tf_op jit(solution)/shard_map/ppermute | solution.py:26
  76.0 11.4 %collective-permute-start.14 = (bf16[32,3456]{1,0:T(8,128)(2,1)S(1)}, bf16[32,3456]{1,0:T(8,128)(2,1)S(1)}, u32[]{:S(2)}, u32[]{:S(2)}) collective-permute-start(bf16[32,3456]{1,0:T(8,128)(2,1)S(1)} %get-tuple-element.140), channel_id=1, source_target_pairs={{0,16},{16,0},{32,48},{48,32},{64,80},{80,64},{96,112},{112,96},{1... | collective-permute-start | bytes 663560 | tf_op jit(solution)/shard_map/ppermute | solution.py:26
  83.4 6.6 %collective-permute-start.12 = (bf16[32,3456]{1,0:T(8,128)(2,1)S(1)}, bf16[32,3456]{1,0:T(8,128)(2,1)S(1)}, u32[]{:S(2)}, u32[]{:S(2)}) collective-permute-start(bf16[32,3456]{1,0:T(8,128)(2,1)S(1)} %get-tuple-element.138), channel_id=1, source_target_pairs={{0,32},{16,48},{32,64},{48,80},{64,96},{80,112},{96,128},{112,144}... | collective-permute-start | bytes 663560 | tf_op jit(solution)/shard_map/ppermute | solution.py:26
  84.7 6.4 %collective-permute-start.13 = (bf16[32,3456]{1,0:T(8,128)(2,1)S(1)}, bf16[32,3456]{1,0:T(8,128)(2,1)S(1)}, u32[]{:S(2)}, u32[]{:S(2)}) collective-permute-start(bf16[32,3456]{1,0:T(8,128)(2,1)S(1)} %get-tuple-element.139), channel_id=1, source_target_pairs={{0,224},{16,240},{32,0},{48,16},{64,32},{80,48},{96,64},{112,80},{... | collective-permute-start | bytes 663560 | tf_op jit(solution)/shard_map/ppermute | solution.py:26
  91.3 4.8 %collective-permute-start.15 = (bf16[32,1664]{1,0:T(8,128)(2,1)S(1)}, bf16[32,1664]{1,0:T(8,128)(2,1)S(1)}, u32[]{:S(2)}, u32[]{:S(2)}) collective-permute-start(bf16[32,1664]{1,0:T(8,128)(2,1)S(1)} %shard_map.108.refs_0_), channel_id=1, source_target_pairs={{0,32},{1,225},{2,34},{3,227},{4,36},{5,229},{6,38},{7,231},{8,40}... | collective-permute-start | bytes 319496 | tf_op jit(solution)/shard_map/ppermute | solution.py:34
  93.5 5.9 %collective-permute-start.16 = (bf16[32,1664]{1,0:T(8,128)(2,1)S(1)}, bf16[32,1664]{1,0:T(8,128)(2,1)S(1)}, u32[]{:S(2)}, u32[]{:S(2)}) collective-permute-start(bf16[32,1664]{1,0:T(8,128)(2,1)S(1)} %shard_map.108.refs_0_), channel_id=1, source_target_pairs={{0,224},{1,33},{2,226},{3,35},{4,228},{5,37},{6,230},{7,39},{8,232... | collective-permute-start | bytes 319496 | tf_op jit(solution)/shard_map/ppermute | solution.py:34
  93.5 9.5 %collective-permute-start.19 = (bf16[32,1664]{1,0:T(8,128)(2,1)S(1)}, bf16[32,1664]{1,0:T(8,128)(2,1)S(1)}, u32[]{:S(2)}, u32[]{:S(2)}) collective-permute-start(bf16[32,1664]{1,0:T(8,128)(2,1)S(1)} %shard_map.108.refs_0_), channel_id=1, source_target_pairs={{0,16},{16,0},{32,48},{48,32},{64,80},{80,64},{96,112},{112,96},{1... | collective-permute-start | bytes 319496 | tf_op jit(solution)/shard_map/ppermute | solution.py:26
  99.4 5.5 %collective-permute-start.17 = (bf16[32,1664]{1,0:T(8,128)(2,1)S(1)}, bf16[32,1664]{1,0:T(8,128)(2,1)S(1)}, u32[]{:S(2)}, u32[]{:S(2)}) collective-permute-start(bf16[32,1664]{1,0:T(8,128)(2,1)S(1)} %collective-permute-done.15.refs_1_), channel_id=1, source_target_pairs={{0,32},{1,225},{2,34},{3,227},{4,36},{5,229},{6,38},{7,231},{8,40}... | collective-permute-start | bytes 319496 | tf_op jit(solution)/shard_map/ppermute | solution.py:34
  102.0 5.6 %collective-permute-start.18 = (bf16[32,1664]{1,0:T(8,128)(2,1)S(1)}, bf16[32,1664]{1,0:T(8,128)(2,1)S(1)}, u32[]{:S(2)}, u32[]{:S(2)}) collective-permute-start(bf16[32,1664]{1,0:T(8,128)(2,1)S(1)} %collective-permute-done.16.refs_2_), channel_id=1, source_target_pairs={{0,224},{1,33},{2,226},{3,35},{4,228},{5,37},{6,230},{7,39},{8,232... | collective-permute-start | bytes 319496 | tf_op jit(solution)/shard_map/ppermute | solution.py:34
  102.0 12.5 %collective-permute-start.22 = (bf16[2,32,1664]{2,1,0:T(8,128)(2,1)S(1)}, bf16[2,32,1664]{2,1,0:T(8,128)(2,1)S(1)}, u32[]{:S(2)}, u32[]{:S(2)}) collective-permute-start(bf16[2,32,1664]{2,1,0:T(8,128)(2,1)S(1)} %pad_maximum_fusion), channel_id=1, source_target_pairs={{0,16},{16,0},{32,48},{48,32},{64,80},{80,64},{96,112},{112,96},{1... | collective-permute-start | bytes 638984 | tf_op jit(solution)/shard_map/ppermute | solution.py:26
  107.6 4.8 %collective-permute-start.20 = (bf16[32,1664]{1,0:T(8,128)(2,1)S(1)}, bf16[32,1664]{1,0:T(8,128)(2,1)S(1)}, u32[]{:S(2)}, u32[]{:S(2)}) collective-permute-start(bf16[32,1664]{1,0:T(8,128)(2,1)S(1)} %collective-permute-done.17.refs_3_), channel_id=1, source_target_pairs={{0,32},{1,225},{2,34},{3,227},{4,36},{5,229},{6,38},{7,231},{8,40}... | collective-permute-start | bytes 319496 | tf_op jit(solution)/shard_map/ppermute | solution.py:34
  109.7 10.2 %collective-permute-start.25 = (bf16[2,32,1664]{2,1,0:T(8,128)(2,1)S(1)}, bf16[2,32,1664]{2,1,0:T(8,128)(2,1)S(1)}, u32[]{:S(2)}, u32[]{:S(2)}) collective-permute-start(bf16[2,32,1664]{2,1,0:T(8,128)(2,1)S(1)} %pad_maximum_fusion.1), channel_id=1, source_target_pairs={{0,16},{16,0},{32,48},{48,32},{64,80},{80,64},{96,112},{112,96},{1... | collective-permute-start | bytes 638984 | tf_op jit(solution)/shard_map/ppermute | solution.py:26
  114.5 5.5 %collective-permute-start.23 = (bf16[32,896]{1,0:T(8,128)(2,1)S(1)}, bf16[32,896]{1,0:T(8,128)(2,1)S(1)}, u32[]{:S(2)}, u32[]{:S(2)}) collective-permute-start(bf16[32,896]{1,0:T(8,128)(2,1)S(1)} %slice.6), channel_id=1, source_target_pairs={{0,32},{1,225},{2,34},{3,227},{4,36},{5,229},{6,38},{7,231},{8,40}... | collective-permute-start | bytes 172040 | tf_op jit(solution)/shard_map/ppermute | solution.py:34
  116.6 8.2 %collective-permute-start.26 = (bf16[2,32,1664]{2,1,0:T(8,128)(2,1)S(1)}, bf16[2,32,1664]{2,1,0:T(8,128)(2,1)S(1)}, u32[]{:S(2)}, u32[]{:S(2)}) collective-permute-start(bf16[2,32,1664]{2,1,0:T(8,128)(2,1)S(1)} %pad_maximum_fusion.2), channel_id=1, source_target_pairs={{0,16},{16,0},{32,48},{48,32},{64,80},{80,64},{96,112},{112,96},{1... | collective-permute-start | bytes 638984 | tf_op jit(solution)/shard_map/ppermute | solution.py:26
  120.0 4.8 %collective-permute-start.27 = (bf16[32,1664]{1,0:T(8,128)(2,1)S(1)}, bf16[32,1664]{1,0:T(8,128)(2,1)S(1)}, u32[]{:S(2)}, u32[]{:S(2)}) collective-permute-start(bf16[32,1664]{1,0:T(8,128)(2,1)S(1)} %pad_maximum_fusion.3), channel_id=1, source_target_pairs={{0,16},{16,0},{32,48},{48,32},{64,80},{80,64},{96,112},{112,96},{1... | collective-permute-start | bytes 319496 | tf_op jit(solution)/shard_map/ppermute | solution.py:26
  (7 other events, 129.0 us)
